TPU v7x, 32 devices: a whole 2x2x4 slice. The times are simulated.
32 devices in a mesh: row: 4 (over y, core), col: 8 (over z, x).
Axes of the slice: x: 2, y: 2, z: 4, core: 2. Of those that a mesh axis runs over, the one named last changes fastest.
Arguments:
- images: bfloat16 [1024, 1024], P(('row', 'col')), may hold values from -6 to 6
- texts: bfloat16 [1024, 1024], P(('row', 'col')), may hold values from -6 to 6
- loss_weights: float32 [2], replicated, may hold values from 0.5 to 1.5
Outputs:
- grad_images: float32 [1024, 1024], P(('row', 'col'))
- grad_texts: float32 [1024, 1024], P(('row', 'col'))
All inputs are finite; a program needn't handle non-finite values.
Results may differ from a plain program's by a relative error of at most 0.0013.
Values may be sent and summed in bfloat16 or wider, within the bound.
No kernel may reach another device: no remote copies, remote signals or barrier semaphores. Data moves between devices by JAX's collectives and lax.ppermute only.
A program may use at most 64 MiB of HBM per device.

v0:
```python
import math

import jax
import jax.numpy as jnp
from jax import lax
from jax.sharding import PartitionSpec as P


def local(images, texts, loss_weights):
    width = images.shape[1]
    batch = images.shape[0] * lax.axis_size("row") * lax.axis_size("col")
    scale = 1.0 / math.sqrt(width * batch)
    cross_scale = loss_weights[0] * scale
    inner_scale = loss_weights[1] * scale
    own = jnp.stack([images, texts])
    columns = lax.all_gather(own, "row", axis=1, tiled=True)
    col_img = columns[0]
    col_txt = columns[1]
    col_count = col_img.shape[0]
    keys = jnp.concatenate(
        [
            jnp.concatenate([col_txt, -col_img], axis=1),
            jnp.concatenate([col_img, -col_txt], axis=1),
        ],
        axis=0,
    )
    piece = lax.all_gather(own, "col", axis=1, tiled=True)
    joined = jnp.concatenate([piece[0], piece[1]], axis=1)
    scores = lax.dot_general(
        joined, keys, (((1,), (1,)), ((), ())), preferred_element_type=jnp.float32
    )
    p_mat = (scores[:, :col_count] * cross_scale).astype(jnp.bfloat16)
    q_mat = (scores[:, col_count:] * inner_scale).astype(jnp.bfloat16)
    joined, weights = (joined, jnp.concatenate([p_mat, q_mat], axis=1))
    result = lax.dot_general(
        weights, joined, (((0,), (0,)), ((), ())), preferred_element_type=jnp.float32
    )
    grad_img = result[col_count:, :width] - result[:col_count, width:]
    grad_txt = result[:col_count, :width] - result[col_count:, width:]
    totals = jnp.stack([grad_img, grad_txt])
    grads = lax.psum_scatter(totals, "row", scatter_dimension=1, tiled=True)
    return (grads[0], grads[1])


def solution(mesh):
    in_specs = (P(("row", "col"), None), P(("row", "col"), None), P())
    out_specs = (P(("row", "col"), None), P(("row", "col"), None))
    return jax.shard_map(local, mesh=mesh, in_specs=in_specs, out_specs=out_specs, check_vma=False)
```

profile of v0, /device:TPU:0, one launch (start us, length us, event | category | flops | bytes accessed | tf_op | source)
XLA Modules:
  0.0 89.5 jit_solution(11710233088622924198)
XLA Ops:
  7.2 0.0 all-gather.2.cloned.1.call-start
  7.2 1.5 %pad_maximum_fusion.4 = bf16[2,32,1024]{2,1,0:T(8,128)(2,1)} fusion(bf16[1,32,1024]{2,1,0:T(8,128)(2,1)} %bitcast.24, bf16[1,32,1024]{2,1,0:T(8,128)(2,1)} %bitcast.25), kind=kLoop, calls=%fused_computation.25 | loop fusion | flops 65536 | bytes 262144 | tf_op jit(solution)/shard_map/stack | solution.py:15
  8.8 0.0 all-gather.2.cloned.1.call-update
  8.8 0.0 reduce-scatter.2.cloned.1.call-start
  8.8 1.3 %fusion.20 = (f32[1]{0:T(128)}, f32[1]{0:T(128)}) fusion(f32[2]{0:T(128)} %param.5), kind=kLoop, calls=%fused_computation.33 | loop fusion | bytes 16 | tf_op jit(solution)/shard_map/slice | solution.py:13
  11.4 8.9 %all_gather.7 = bf16[2,128,1024]{2,1,0:T(8,128)(2,1)S(1)} all-gather(bf16[2,32,1024]{2,1,0:T(8,128)(2,1)} %pad_maximum_fusion.4), channel_id=1, replica_groups=mesh['row'=4,'col'=8] {'row'}, dimensions={1}, use_global_device_ids=true | all-gather | bytes 655360 | tf_op jit(solution)/shard_map/all_gather | solution.py:16
  20.3 33.4 %all-gather.2.cloned.1.call-done = bf16[2,256,1024]{2,1,0:T(8,128)(2,1)} async-done(((bf16[2,32,1024]{2,1,0:T(8,128)(2,1)}), bf16[2,256,1024]{2,1,0:T(8,128)(2,1)}) %all-gather.2.cloned.1.call-update) | async-done | bytes 1048592 | tf_op jit(solution)/shard_map/all_gather | solution.py:27
  53.7 1.3 %slice_bitcast_fusion.1 = (bf16[256,1024]{1,0:T(8,128)(2,1)S(1)}, bf16[256,1024]{1,0:T(8,128)(2,1)S(1)}) fusion(bf16[2,256,1024]{2,1,0:T(8,128)(2,1)} %all-gather.2.cloned.1.call-done), kind=kLoop, calls=%fused_computation.16 | loop fusion | bytes 2097152 | tf_op jit(solution)/shard_map/squeeze | solution.py:28
  55.0 0.6 fusion
  55.5 0.4 fusion.8
  56.0 0.1 fusion.10
  56.1 1.0 %pad_maximum_fusion.1 = f32[2,128,1024]{2,1,0:T(8,128)} fusion(f32[1,128,1024]{2,1,0:T(8,128)S(1)} %get-tuple-element.3, f32[1,128,1024]{2,1,0:T(8,128)S(1)} %get-tuple-element.2), kind=kLoop, calls=%fused_computation.9 | loop fusion | flops 262144 | bytes 2097152 | tf_op jit(solution)/shard_map/stack | solution.py:40
  57.2 0.0 reduce-scatter.2.cloned.1.call-update
  57.2 23.8 %reduce-scatter.2.cloned.1.call-done = f32[2,32,1024]{2,1,0:T(8,128)} async-done(((f32[2,128,1024]{2,1,0:T(8,128)}), f32[2,32,1024]{2,1,0:T(8,128)}) %reduce-scatter.2.cloned.1.call-update) | async-done | bytes 262160 | tf_op jit(solution)/shard_map/reduce_scatter | solution.py:41
  81.0 1.7 %slice_bitcast_fusion.4 = (f32[32,1024]{1,0:T(8,128)}, f32[32,1024]{1,0:T(8,128)}) fusion(f32[2,32,1024]{2,1,0:T(8,128)} %reduce-scatter.2.cloned.1.call-done), kind=kLoop, calls=%fused_computation.19 | loop fusion | bytes 524288 | tf_op jit(solution)/shard_map/squeeze | solution.py:42
  (3 shorter events, 0.1 us)
Async XLA Ops:
  7.2 46.5 %all-gather.2.cloned.1.call-start = ((), (), s32[]{:S(2)}) async-start(), calls=%async_computation.1 | async-start | bytes 1179648 | tf_op jit(solution)/shard_map/all_gather | solution.py:27
  8.8 72.2 %reduce-scatter.2.cloned.1.call-start = ((), (), s32[]{:S(2)}) async-start(), calls=%async_computation.2 | async-start | bytes 1310720 | tf_op jit(solution)/shard_map/reduce_scatter | solution.py:41
Sparse Core Ops, SparseCore 0:
  10.8 42.8 all-gather.1
  57.3 23.6 reduce-scatter.1
where the time goes:
time: 89.8 us; the launch traced here: 89.5 us
  waiting for transfers between devices  57.2 us (64%)
  between operations  15.3 us (17%)
  blocking collectives  8.86 us (10%)
  local copies, waits for them, and re-layouts  4.29 us (5%)
  other arithmetic  2.79 us (3%)
  matrix products  1 us (1%)
    all_gather x1, waiting for transfers between devices, local(): piece = lax.all_gather(own, 'col', axis=1, tiled=True)  33.4 us
    reduce_scatter x1, waiting for transfers between devices, local(): grads = lax.psum_scatter(totals, 'row', scatter_dimension=1, tiled=True)  23.8 us
    all_gather x1, blocking collectives, local(): columns = lax.all_gather(own, 'row', axis=1, tiled=True)  8.86 us
  transfers between devices with their start and end apart: 2, of which 2 were waited for; matrix products, arithmetic and copies ran while one was open for 2% of the time, Pallas kernels for 0%

commit v1 on v0

v1 whole, which is shorter than its diff:
```python
import functools
import math

import jax
import jax.numpy as jnp
from jax import lax
from jax.experimental import pallas as pl
from jax.experimental.pallas import tpu as pltpu
from jax.sharding import PartitionSpec as P


def halves(count):
    inner = 2 if count % 2 == 0 else 1
    return count // inner, inner


def outer_shift(count, step):
    outer, inner = halves(count)
    return [(i, (i // inner + step) % outer * inner + i % inner) for i in range(count)]


def inner_shift(count, step):
    _, inner = halves(count)
    return [(i, i // inner * inner + (i + step) % inner) for i in range(count)]


def both_shift(count, j, k):
    outer, inner = halves(count)
    return [((i // inner + j) % outer * inner + (i + k) % inner, i) for i in range(count)]


def stacked(refs, part):
    return jnp.concatenate([ref[part] for ref in refs], axis=0)


def dot(a, b, dims):
    return lax.dot_general(a, b, (dims, ((), ())), preferred_element_type=jnp.float32)


def block_kernel(scale, n_own, n_keys, weights, *refs):
    own, keys, outs = refs[:n_own], refs[n_own : n_own + n_keys], refs[n_own + n_keys :]
    nt = ((1,), (1,))
    nn = ((1,), (0,))
    img, txt = stacked(own, 0), stacked(own, 1)
    key_img, key_txt = stacked(keys, 0), stacked(keys, 1)
    cross = dot(img, key_txt, nt) - dot(txt, key_img, nt)
    inmodal = dot(img, key_img, nt) - dot(txt, key_txt, nt)
    p_mat = (cross * (weights[0] * scale)).astype(jnp.bfloat16)
    q_mat = (inmodal * (weights[1] * scale)).astype(jnp.bfloat16)
    grad_img = dot(p_mat, key_txt, nn) + dot(q_mat, key_img, nn)
    grad_txt = -dot(p_mat, key_img, nn) - dot(q_mat, key_txt, nn)
    rows = own[0].shape[1]
    for i, out in enumerate(outs):
        out[0] = grad_img[i * rows : (i + 1) * rows]
        out[1] = grad_txt[i * rows : (i + 1) * rows]


def partials(own, keys, weights, scale):
    vmem = pl.BlockSpec(memory_space=pltpu.VMEM)
    smem = pl.BlockSpec(memory_space=pltpu.SMEM)
    return pl.pallas_call(
        functools.partial(block_kernel, scale, len(own), len(keys)),
        out_shape=[jax.ShapeDtypeStruct(x.shape, jnp.float32) for x in own],
        in_specs=[smem] + [vmem] * (len(own) + len(keys)),
        out_specs=[vmem] * len(own),
        compiler_params=pltpu.CompilerParams(vmem_limit_bytes=48 * 2**20),
    )(weights, *own, *keys)


def local(images, texts, loss_weights):
    n_row, n_col = lax.axis_size("row"), lax.axis_size("col")
    row_outer, row_inner = halves(n_row)
    col_outer, col_inner = halves(n_col)
    width = images.shape[1]
    batch = images.shape[0] * n_row * n_col
    scale = 1.0 / math.sqrt(width * batch)
    own = jnp.stack([images, texts])

    line = [own] + [lax.ppermute(own, "col", outer_shift(n_col, k)) for k in range(1, col_outer)]
    keys = list(line)
    for k in range(1, col_inner):
        keys += [lax.ppermute(block, "col", inner_shift(n_col, k)) for block in line]

    column = []
    for j in range(row_outer):
        for k in range(row_inner):
            src = both_shift(n_row, j, k)
            column.append(lax.ppermute(own, "row", src) if j or k else own)

    parts = partials(column, keys, loss_weights, scale)
    sums = []
    for j in reversed(range(row_outer)):
        total = parts[j * row_inner]
        for k in range(1, row_inner):
            total = total + lax.ppermute(parts[j * row_inner + k], "row", inner_shift(n_row, k))
        sums.insert(0, total)
    total = sums[0]
    for j in range(1, row_outer):
        total = total + lax.ppermute(sums[j], "row", outer_shift(n_row, j))
    return total[0], total[1]


def solution(mesh):
    in_specs = (P(("row", "col"), None), P(("row", "col"), None), P())
    out_specs = (P(("row", "col"), None), P(("row", "col"), None))
    return jax.shard_map(local, mesh=mesh, in_specs=in_specs, out_specs=out_specs, check_vma=False)
```

time: 89.8 us -> 41.9 us (0.47)
  waiting for transfers between devices: 57.2 us -> 23.8 us
  between operations: 15.3 us -> 0.68 us
  starting transfers between devices: 0.08 us -> 13.9 us
  blocking collectives: 8.86 us -> 0 us
  local copies, waits for them, and re-layouts: 4.29 us -> 0.72 us
  other arithmetic: 2.79 us -> 0.96 us
  Pallas kernels: 0 us -> 1.75 us
  matrix products: 1 us -> 0 us
    all_gather x1 -> x0, waiting for transfers between devices: 33.4 us -> none  [local(): piece = lax.all_gather(own, 'col', axis=1, tiled=True)]
    reduce_scatter x1 -> x0, waiting for transfers between devices: 23.8 us -> none  [local(): grads = lax.psum_scatter(totals, 'row', scatter_dimension=1, tiled=True)]
    ppermute x0 -> x13, waiting for transfers between devices: none -> 23.8 us  [the longest x3 8.24 us: local(): lax.ppermute(own, 'col', outer_shift(n_col, k))]
    ppermute x0 -> x13, starting transfers between devices: none -> 13.9 us  [the longest x4 5.57 us: local(): lax.ppermute(block, 'col', inner_shift(n_col, k))]
    all_gather x1 -> x0, blocking collectives: 8.86 us -> none  [local(): columns = lax.all_gather(own, 'row', axis=1, tiled=True)]
    squeeze x3 -> x1, local copies, waits for them, and re-layouts: 2.99 us -> 0.72 us  [local(): return (total[0], total[1])]
    pallas_call x0 -> x1, Pallas kernels: none -> 1.75 us  [partials(): pl.pallas_call(functools.partial(block_kernel, scale, len(own), len(keys)...]
    slice x1 -> x0, local copies, waits for them, and re-layouts: 1.31 us -> none  [local(): cross_scale = loss_weights[0] * scale]
  transfers between devices with their start and end apart: 2 -> 13, of which waited for: 2 -> 7; matrix products, arithmetic and copies ran while one was open for 2% -> 0% of each run, Pallas kernels for 0% -> 0%
where the time goes in v1:
time: 41.9 us; the launch traced here: 41.8 us
  waiting for transfers between devices  23.8 us (57%)
  starting transfers between devices  13.9 us (33%)
  Pallas kernels  1.75 us (4%)
  other arithmetic  0.96 us (2%)
  local copies, waits for them, and re-layouts  0.72 us (2%)
  between operations  0.68 us (2%)
    ppermute x3, waiting for transfers between devices, local(): lax.ppermute(own, 'col', outer_shift(n_col, k))  8.24 us
    ppermute x4, waiting for transfers between devices, local(): lax.ppermute(block, 'col', inner_shift(n_col, k))  7.68 us
    ppermute x1, waiting for transfers between devices, local(): total = total + lax.ppermute(sums[j], 'row', outer_shift(n_row, j))  6.83 us
    ppermute x4, starting transfers between devices, local(): lax.ppermute(block, 'col', inner_shift(n_col, k))  5.57 us
    ppermute x3, starting transfers between devices, local(): lax.ppermute(own, 'col', outer_shift(n_col, k))  4.61 us
    pallas_call x1, Pallas kernels, partials(): pl.pallas_call(functools.partial(block_kernel, scale, len(own), len(keys)...  1.75 us
    ppermute x1, starting transfers between devices, local(): total = total + lax.ppermute(sums[j], 'row', outer_shift(n_row, j))  1.58 us
    ppermute x3, starting transfers between devices, local(): column.append(lax.ppermute(own, 'row', src) if j or k else own)  1.55 us
  transfers between devices with their start and end apart: 13, of which 7 were waited for; matrix products, arithmetic and copies ran while one was open for 0% of the time, Pallas kernels for 0%

profile of v1, /device:TPU:0, one launch (start us, length us, event | category | flops | bytes accessed | tf_op | source)
XLA Modules:
  0.0 41.8 jit_solution(3252482542461496430)
XLA Ops:
  0.6 0.0 copy-start
  0.6 0.9 %pad_maximum_fusion.refs_0_.refs_4_ = bf16[2,32,1024]{2,1,0:T(8,128)(2,1)S(1)} fusion(bf16[1,32,1024]{2,1,0:T(8,128)(2,1)} %bitcast.6, bf16[1,32,1024]{2,1,0:T(8,128)(2,1)} %bitcast.7), kind=kLoop, calls=%fused_computation.3 | loop fusion | flops 65536 | bytes 262144 | tf_op jit(solution)/shard_map/stack | solution.py:77
  1.5 3.0 %collective-permute-start.6 = (bf16[2,32,1024]{2,1,0:T(8,128)(2,1)S(1)}, bf16[2,32,1024]{2,1,0:T(8,128)(2,1)S(1)}, u32[]{:S(2)}, u32[]{:S(2)}) collective-permute-start(bf16[2,32,1024]{2,1,0:T(8,128)(2,1)S(1)} %pad_maximum_fusion.refs_0_.refs_4_), channel_id=1, source_target_pairs={{0,1},{1,0},{2,3},{3,2},{4,5},{5,4},{6,7},{7,6},{8,9},{9,8},{10,11... | collective-permute-start | bytes 393224 | tf_op jit(solution)/shard_map/ppermute | solution.py:82
  4.5 3.6 %collective-permute-start.5 = (bf16[2,32,1024]{2,1,0:T(8,128)(2,1)S(1)}, bf16[2,32,1024]{2,1,0:T(8,128)(2,1)S(1)}, u32[]{:S(2)}, u32[]{:S(2)}) collective-permute-start(bf16[2,32,1024]{2,1,0:T(8,128)(2,1)S(1)} %pad_maximum_fusion.refs_0_.refs_4_), channel_id=1, source_target_pairs={{0,6},{1,7},{2,0},{3,1},{4,2},{5,3},{6,4},{7,5},{8,14},{9,15},{10,... | collective-permute-start | bytes 393224 | tf_op jit(solution)/shard_map/ppermute | solution.py:79
  8.1 0.0 collective-permute-start.4
  8.1 1.0 %collective-permute-start.3 = (bf16[2,32,1024]{2,1,0:T(8,128)(2,1)S(1)}, bf16[2,32,1024]{2,1,0:T(8,128)(2,1)S(1)}, u32[]{:S(2)}, u32[]{:S(2)}) collective-permute-start(bf16[2,32,1024]{2,1,0:T(8,128)(2,1)S(1)} %pad_maximum_fusion.refs_0_.refs_4_), channel_id=1, source_target_pairs={{0,2},{1,3},{2,4},{3,5},{4,6},{5,7},{6,0},{7,1},{8,10},{9,11},{10,... | collective-permute-start | bytes 393224 | tf_op jit(solution)/shard_map/ppermute | solution.py:79
  9.2 0.0 collective-permute-start.2
  9.2 0.0 collective-permute-done.6.refs_8_
  9.2 1.5 %collective-permute-start.1 = (bf16[2,32,1024]{2,1,0:T(8,128)(2,1)S(1)}, bf16[2,32,1024]{2,1,0:T(8,128)(2,1)S(1)}, u32[]{:S(2)}, u32[]{:S(2)}) collective-permute-start(bf16[2,32,1024]{2,1,0:T(8,128)(2,1)S(1)} %pad_maximum_fusion.refs_0_.refs_4_), channel_id=1, source_target_pairs={{16,0},{24,8},{0,16},{8,24},{17,1},{25,9},{1,17},{9,25},{18,2},{26... | collective-permute-start | bytes 393224 | tf_op jit(solution)/shard_map/ppermute | solution.py:88
  10.7 1.4 %collective-permute-done.5.refs_7_ = bf16[2,32,1024]{2,1,0:T(8,128)(2,1)S(1)} collective-permute-done((bf16[2,32,1024]{2,1,0:T(8,128)(2,1)S(1)}, bf16[2,32,1024]{2,1,0:T(8,128)(2,1)S(1)}, u32[]{:S(2)}, u32[]{:S(2)}) %collective-permute-start.5) | collective-permute-done | bytes 131104 | tf_op jit(solution)/shard_map/ppermute | solution.py:79
  12.1 0.0 collective-permute-start
  12.1 6.9 %collective-permute-done.4.refs_6_ = bf16[2,32,1024]{2,1,0:T(8,128)(2,1)S(1)} collective-permute-done((bf16[2,32,1024]{2,1,0:T(8,128)(2,1)S(1)}, bf16[2,32,1024]{2,1,0:T(8,128)(2,1)S(1)}, u32[]{:S(2)}, u32[]{:S(2)}) %collective-permute-start.4) | collective-permute-done | bytes 131104 | tf_op jit(solution)/shard_map/ppermute | solution.py:79
  18.9 0.5 %collective-permute-start.9 = (bf16[2,32,1024]{2,1,0:T(8,128)(2,1)S(1)}, bf16[2,32,1024]{2,1,0:T(8,128)(2,1)S(1)}, u32[]{:S(2)}, u32[]{:S(2)}) collective-permute-start(bf16[2,32,1024]{2,1,0:T(8,128)(2,1)S(1)} %collective-permute-done.5.refs_7_), channel_id=1, source_target_pairs={{0,1},{1,0},{2,3},{3,2},{4,5},{5,4},{6,7},{7,6},{8,9},{9,8},{10,11... | collective-permute-start | bytes 393224 | tf_op jit(solution)/shard_map/ppermute | solution.py:82
  19.5 0.0 collective-permute-done.3.refs_5_
  19.5 1.5 %collective-permute-start.8 = (bf16[2,32,1024]{2,1,0:T(8,128)(2,1)S(1)}, bf16[2,32,1024]{2,1,0:T(8,128)(2,1)S(1)}, u32[]{:S(2)}, u32[]{:S(2)}) collective-permute-start(bf16[2,32,1024]{2,1,0:T(8,128)(2,1)S(1)} %collective-permute-done.4.refs_6_), channel_id=1, source_target_pairs={{0,1},{1,0},{2,3},{3,2},{4,5},{5,4},{6,7},{7,6},{8,9},{9,8},{10,11... | collective-permute-start | bytes 393224 | tf_op jit(solution)/shard_map/ppermute | solution.py:82
  21.0 0.0 collective-permute-done.2.refs_3_
  21.0 0.5 %collective-permute-start.7 = (bf16[2,32,1024]{2,1,0:T(8,128)(2,1)S(1)}, bf16[2,32,1024]{2,1,0:T(8,128)(2,1)S(1)}, u32[]{:S(2)}, u32[]{:S(2)}) collective-permute-start(bf16[2,32,1024]{2,1,0:T(8,128)(2,1)S(1)} %collective-permute-done.3.refs_5_), channel_id=1, source_target_pairs={{0,1},{1,0},{2,3},{3,2},{4,5},{5,4},{6,7},{7,6},{8,9},{9,8},{10,11... | collective-permute-start | bytes 393224 | tf_op jit(solution)/shard_map/ppermute | solution.py:82
  21.5 0.0 collective-permute-done.1.refs_2_
  21.5 0.0 collective-permute-done.refs_1_
  21.5 3.9 %collective-permute-done.9.refs_11_ = bf16[2,32,1024]{2,1,0:T(8,128)(2,1)S(1)} collective-permute-done((bf16[2,32,1024]{2,1,0:T(8,128)(2,1)S(1)}, bf16[2,32,1024]{2,1,0:T(8,128)(2,1)S(1)}, u32[]{:S(2)}, u32[]{:S(2)}) %collective-permute-start.9) | collective-permute-done | bytes 131104 | tf_op jit(solution)/shard_map/ppermute | solution.py:82
  25.4 2.4 %collective-permute-done.8.refs_10_ = bf16[2,32,1024]{2,1,0:T(8,128)(2,1)S(1)} collective-permute-done((bf16[2,32,1024]{2,1,0:T(8,128)(2,1)S(1)}, bf16[2,32,1024]{2,1,0:T(8,128)(2,1)S(1)}, u32[]{:S(2)}, u32[]{:S(2)}) %collective-permute-start.8) | collective-permute-done | bytes 131104 | tf_op jit(solution)/shard_map/ppermute | solution.py:82
  27.8 1.4 %collective-permute-done.7.refs_9_ = bf16[2,32,1024]{2,1,0:T(8,128)(2,1)S(1)} collective-permute-done((bf16[2,32,1024]{2,1,0:T(8,128)(2,1)S(1)}, bf16[2,32,1024]{2,1,0:T(8,128)(2,1)S(1)}, u32[]{:S(2)}, u32[]{:S(2)}) %collective-permute-start.7) | collective-permute-done | bytes 131104 | tf_op jit(solution)/shard_map/ppermute | solution.py:82
  29.2 0.0 copy-done
  29.2 1.7 %shard_map.50 = (f32[2,32,1024]{2,1,0:T(8,128)S(1)}, f32[2,32,1024]{2,1,0:T(8,128)S(1)}, f32[2,32,1024]{2,1,0:T(8,128)S(1)}, f32[2,32,1024]{2,1,0:T(8,128)S(1)}) custom-call(f32[2]{0:T(128)S(1)} %copy-done, bf16[2,32,1024]{2,1,0:T(8,128)(2,1)S(1)} %pad_maximum_fusion.refs_0_.refs_4_, bf16[2,32,1024]{2,1,0:T(8,128)(2,1)S(1)} %collective-permute-done.refs_1_, ...), custom_call_target="tpu_custom_call" | custom-call | tf_op jit(solution)/shard_map/pallas_call | solution.py:61
  31.0 0.1 collective-permute-start.11
  31.0 0.5 %collective-permute-start.10 = (f32[2,32,1024]{2,1,0:T(8,128)S(1)}, f32[2,32,1024]{2,1,0:T(8,128)S(1)}, u32[]{:S(2)}, u32[]{:S(2)}) collective-permute-start(f32[2,32,1024]{2,1,0:T(8,128)S(1)} %get-tuple-element.7), channel_id=1, source_target_pairs={{0,8},{8,0},{16,24},{24,16},{1,9},{9,1},{17,25},{25,17},{2,10},{10... | collective-permute-start | bytes 786440 | tf_op jit(solution)/shard_map/ppermute | solution.py:95
  31.5 1.0 %collective-permute-done.11 = f32[2,32,1024]{2,1,0:T(8,128)S(1)} collective-permute-done((f32[2,32,1024]{2,1,0:T(8,128)S(1)}, f32[2,32,1024]{2,1,0:T(8,128)S(1)}, u32[]{:S(2)}, u32[]{:S(2)}) %collective-permute-start.11) | collective-permute-done | bytes 262176 | tf_op jit(solution)/shard_map/ppermute | solution.py:95
  32.6 1.6 %collective-permute-start.12 = (f32[2,32,1024]{2,1,0:T(8,128)S(1)}, f32[2,32,1024]{2,1,0:T(8,128)S(1)}, u32[]{:S(2)}, u32[]{:S(2)}) collective-permute-start(f32[2,32,1024]{2,1,0:T(8,128)S(1)} %add.10), channel_id=1, source_target_pairs={{0,16},{8,24},{16,0},{24,8},{1,17},{9,25},{17,1},{25,9},{2,18},{10... | collective-permute-start | bytes 786440 | tf_op jit(solution)/shard_map/ppermute | solution.py:99
  34.2 0.0 collective-permute-done.10
  34.2 6.8 %collective-permute-done.12 = f32[2,32,1024]{2,1,0:T(8,128)S(1)} collective-permute-done((f32[2,32,1024]{2,1,0:T(8,128)S(1)}, f32[2,32,1024]{2,1,0:T(8,128)S(1)}, u32[]{:S(2)}, u32[]{:S(2)}) %collective-permute-start.12) | collective-permute-done | bytes 262176 | tf_op jit(solution)/shard_map/ppermute | solution.py:99
  41.1 0.7 %slice_bitcast_fusion = (f32[32,1024]{1,0:T(8,128)}, f32[32,1024]{1,0:T(8,128)}) fusion(f32[2,32,1024]{2,1,0:T(8,128)S(1)} %add_add_fusion), kind=kLoop, calls=%fused_computation.1 | loop fusion | bytes 524288 | tf_op jit(solution)/shard_map/squeeze | solution.py:100
  (2 shorter events, 0.1 us)
Async XLA Ops:
  0.6 28.6 %copy-start = (f32[2]{0:T(128)S(1)}, f32[2]{0:T(128)}, u32[]{:S(2)}) copy-start(f32[2]{0:T(128)} %weights.1) | copy-start | bytes 28
  1.5 7.6 %collective-permute-start.6 = (bf16[2,32,1024]{2,1,0:T(8,128)(2,1)S(1)}, bf16[2,32,1024]{2,1,0:T(8,128)(2,1)S(1)}, u32[]{:S(2)}, u32[]{:S(2)}) collective-permute-start(bf16[2,32,1024]{2,1,0:T(8,128)(2,1)S(1)} %pad_maximum_fusion.refs_0_.refs_4_), channel_id=1, source_target_pairs={{0,1},{1,0},{2,3},{3,2},{4,5},{5,4},{6,7},{7,6},{8,9},{9,8},{10,11... | collective-permute-start | bytes 393224 | tf_op jit(solution)/shard_map/ppermute | solution.py:82
  4.5 7.5 %collective-permute-start.5 = (bf16[2,32,1024]{2,1,0:T(8,128)(2,1)S(1)}, bf16[2,32,1024]{2,1,0:T(8,128)(2,1)S(1)}, u32[]{:S(2)}, u32[]{:S(2)}) collective-permute-start(bf16[2,32,1024]{2,1,0:T(8,128)(2,1)S(1)} %pad_maximum_fusion.refs_0_.refs_4_), channel_id=1, source_target_pairs={{0,6},{1,7},{2,0},{3,1},{4,2},{5,3},{6,4},{7,5},{8,14},{9,15},{10,... | collective-permute-start | bytes 393224 | tf_op jit(solution)/shard_map/ppermute | solution.py:79
  8.1 10.8 %collective-permute-start.4 = (bf16[2,32,1024]{2,1,0:T(8,128)(2,1)S(1)}, bf16[2,32,1024]{2,1,0:T(8,128)(2,1)S(1)}, u32[]{:S(2)}, u32[]{:S(2)}) collective-permute-start(bf16[2,32,1024]{2,1,0:T(8,128)(2,1)S(1)} %pad_maximum_fusion.refs_0_.refs_4_), channel_id=1, source_target_pairs={{0,4},{1,5},{2,6},{3,7},{4,0},{5,1},{6,2},{7,3},{8,12},{9,13},{10,... | collective-permute-start | bytes 393224 | tf_op jit(solution)/shard_map/ppermute | solution.py:79
  8.1 11.3 %collective-permute-start.3 = (bf16[2,32,1024]{2,1,0:T(8,128)(2,1)S(1)}, bf16[2,32,1024]{2,1,0:T(8,128)(2,1)S(1)}, u32[]{:S(2)}, u32[]{:S(2)}) collective-permute-start(bf16[2,32,1024]{2,1,0:T(8,128)(2,1)S(1)} %pad_maximum_fusion.refs_0_.refs_4_), channel_id=1, source_target_pairs={{0,2},{1,3},{2,4},{3,5},{4,6},{5,7},{6,0},{7,1},{8,10},{9,11},{10,... | collective-permute-start | bytes 393224 | tf_op jit(solution)/shard_map/ppermute | solution.py:79
  9.2 11.8 %collective-permute-start.2 = (bf16[2,32,1024]{2,1,0:T(8,128)(2,1)S(1)}, bf16[2,32,1024]{2,1,0:T(8,128)(2,1)S(1)}, u32[]{:S(2)}, u32[]{:S(2)}) collective-permute-start(bf16[2,32,1024]{2,1,0:T(8,128)(2,1)S(1)} %pad_maximum_fusion.refs_0_.refs_4_), channel_id=1, source_target_pairs={{24,0},{16,8},{8,16},{0,24},{25,1},{17,9},{9,17},{1,25},{26,2},{18... | collective-permute-start | bytes 393224 | tf_op jit(solution)/shard_map/ppermute | solution.py:88
  9.2 12.4 %collective-permute-start.1 = (bf16[2,32,1024]{2,1,0:T(8,128)(2,1)S(1)}, bf16[2,32,1024]{2,1,0:T(8,128)(2,1)S(1)}, u32[]{:S(2)}, u32[]{:S(2)}) collective-permute-start(bf16[2,32,1024]{2,1,0:T(8,128)(2,1)S(1)} %pad_maximum_fusion.refs_0_.refs_4_), channel_id=1, source_target_pairs={{16,0},{24,8},{0,16},{8,24},{17,1},{25,9},{1,17},{9,25},{18,2},{26... | collective-permute-start | bytes 393224 | tf_op jit(solution)/shard_map/ppermute | solution.py:88
  12.1 9.4 %collective-permute-start = (bf16[2,32,1024]{2,1,0:T(8,128)(2,1)S(1)}, bf16[2,32,1024]{2,1,0:T(8,128)(2,1)S(1)}, u32[]{:S(2)}, u32[]{:S(2)}) collective-permute-start(bf16[2,32,1024]{2,1,0:T(8,128)(2,1)S(1)} %pad_maximum_fusion.refs_0_.refs_4_), channel_id=1, source_target_pairs={{8,0},{0,8},{24,16},{16,24},{9,1},{1,9},{25,17},{17,25},{10,2},{2,... | collective-permute-start | bytes 393224 | tf_op jit(solution)/shard_map/ppermute | solution.py:88
  18.9 6.4 %collective-permute-start.9 = (bf16[2,32,1024]{2,1,0:T(8,128)(2,1)S(1)}, bf16[2,32,1024]{2,1,0:T(8,128)(2,1)S(1)}, u32[]{:S(2)}, u32[]{:S(2)}) collective-permute-start(bf16[2,32,1024]{2,1,0:T(8,128)(2,1)S(1)} %collective-permute-done.5.refs_7_), channel_id=1, source_target_pairs={{0,1},{1,0},{2,3},{3,2},{4,5},{5,4},{6,7},{7,6},{8,9},{9,8},{10,11... | collective-permute-start | bytes 393224 | tf_op jit(solution)/shard_map/ppermute | solution.py:82
  19.5 8.3 %collective-permute-start.8 = (bf16[2,32,1024]{2,1,0:T(8,128)(2,1)S(1)}, bf16[2,32,1024]{2,1,0:T(8,128)(2,1)S(1)}, u32[]{:S(2)}, u32[]{:S(2)}) collective-permute-start(bf16[2,32,1024]{2,1,0:T(8,128)(2,1)S(1)} %collective-permute-done.4.refs_6_), channel_id=1, source_target_pairs={{0,1},{1,0},{2,3},{3,2},{4,5},{5,4},{6,7},{7,6},{8,9},{9,8},{10,11... | collective-permute-start | bytes 393224 | tf_op jit(solution)/shard_map/ppermute | solution.py:82
  21.0 8.2 %collective-permute-start.7 = (bf16[2,32,1024]{2,1,0:T(8,128)(2,1)S(1)}, bf16[2,32,1024]{2,1,0:T(8,128)(2,1)S(1)}, u32[]{:S(2)}, u32[]{:S(2)}) collective-permute-start(bf16[2,32,1024]{2,1,0:T(8,128)(2,1)S(1)} %collective-permute-done.3.refs_5_), channel_id=1, source_target_pairs={{0,1},{1,0},{2,3},{3,2},{4,5},{5,4},{6,7},{7,6},{8,9},{9,8},{10,11... | collective-permute-start | bytes 393224 | tf_op jit(solution)/shard_map/ppermute | solution.py:82
  31.0 1.6 %collective-permute-start.11 = (f32[2,32,1024]{2,1,0:T(8,128)S(1)}, f32[2,32,1024]{2,1,0:T(8,128)S(1)}, u32[]{:S(2)}, u32[]{:S(2)}) collective-permute-start(f32[2,32,1024]{2,1,0:T(8,128)S(1)} %get-tuple-element.9), channel_id=1, source_target_pairs={{0,8},{8,0},{16,24},{24,16},{1,9},{9,1},{17,25},{25,17},{2,10},{10... | collective-permute-start | bytes 786440 | tf_op jit(solution)/shard_map/ppermute | solution.py:95
  31.0 3.1 %collective-permute-start.10 = (f32[2,32,1024]{2,1,0:T(8,128)S(1)}, f32[2,32,1024]{2,1,0:T(8,128)S(1)}, u32[]{:S(2)}, u32[]{:S(2)}) collective-permute-start(f32[2,32,1024]{2,1,0:T(8,128)S(1)} %get-tuple-element.7), channel_id=1, source_target_pairs={{0,8},{8,0},{16,24},{24,16},{1,9},{9,1},{17,25},{25,17},{2,10},{10... | collective-permute-start | bytes 786440 | tf_op jit(solution)/shard_map/ppermute | solution.py:95
  32.6 8.4 %collective-permute-start.12 = (f32[2,32,1024]{2,1,0:T(8,128)S(1)}, f32[2,32,1024]{2,1,0:T(8,128)S(1)}, u32[]{:S(2)}, u32[]{:S(2)}) collective-permute-start(f32[2,32,1024]{2,1,0:T(8,128)S(1)} %add.10), channel_id=1, source_target_pairs={{0,16},{8,24},{16,0},{24,8},{1,17},{9,25},{17,1},{25,9},{2,18},{10... | collective-permute-start | bytes 786440 | tf_op jit(solution)/shard_map/ppermute | solution.py:99

commit v2 on v1

--- a/solution.py
+++ b/solution.py
@@ -17,6 +17,14 @@
 def outer_shift(count, step):
     outer, inner = halves(count)
     return [(i, (i // inner + step) % outer * inner + i % inner) for i in range(count)]
+
+
+def outer_ring(count):
+    outer, inner = halves(count)
+    odd, even = list(range(1, outer, 2)), list(range(0, outer, 2))
+    ring = odd + even[::-1]
+    after = {a: ring[(i + 1) % outer] for i, a in enumerate(ring)}
+    return [(i, after[i // inner] * inner + i % inner) for i in range(count)]
 
 
 def inner_shift(count, step):
@@ -76,16 +84,22 @@
     scale = 1.0 / math.sqrt(width * batch)
     own = jnp.stack([images, texts])
 
-    line = [own] + [lax.ppermute(own, "col", outer_shift(n_col, k)) for k in range(1, col_outer)]
-    keys = list(line)
-    for k in range(1, col_inner):
-        keys += [lax.ppermute(block, "col", inner_shift(n_col, k)) for block in line]
-
-    column = []
-    for j in range(row_outer):
-        for k in range(row_inner):
-            src = both_shift(n_row, j, k)
-            column.append(lax.ppermute(own, "row", src) if j or k else own)
+    others = [(j, k) for j in range(row_outer) for k in range(row_inner) if j or k]
+    per_round = -(-len(others) // max(col_outer - 1, 1))
+    keys, column, block, mine = [own], {(0, 0): own}, own, own
+    for step in range(col_outer):
+        arrived, passed = block, []
+        if step + 1 < col_outer:
+            arrived = lax.ppermute(block, "col", outer_ring(n_col))
+        for k in range(1, col_inner):
+            passed.append(lax.ppermute(block, "col", inner_shift(n_col, k)))
+        for j, k in others[step * per_round : (step + 1) * per_round]:
+            column[j, k] = lax.ppermute(mine, "row", both_shift(n_row, j, k))
+        if step + 1 < col_outer:
+            block, passed, mine = lax.optimization_barrier((arrived, passed, mine))
+            keys.append(block)
+        keys += passed
+    column = [column[j, k] for j in range(row_outer) for k in range(row_inner)]
 
     parts = partials(column, keys, loss_weights, scale)
     sums = []

time: 41.9 us -> 41.9 us (level)
  starting transfers between devices: 13.9 us -> 12.8 us
  waiting for transfers between devices: 23.8 us -> 24.8 us
    ppermute x10, starting transfers between devices: 11.7 us -> 10.6 us  [the longest x4 5.5 us: local(): passed.append(lax.ppermute(block, 'col', inner_shift(n_col, k)))]
    ppermute x10, waiting for transfers between devices: 15.9 us -> 16.9 us  [the longest x4 7.94 us: local(): passed.append(lax.ppermute(block, 'col', inner_shift(n_col, k)))]
  transfers between devices with their start and end apart: 13 -> 13, of which waited for: 7 -> 11; matrix products, arithmetic and copies ran while one was open for 0% -> 0% of each run, Pallas kernels for 0% -> 0%
where the time goes in v2:
time: 41.9 us; the launch traced here: 41.7 us
  waiting for transfers between devices  24.8 us (59%)
  starting transfers between devices  12.8 us (31%)
  Pallas kernels  1.75 us (4%)
  other arithmetic  0.96 us (2%)
  local copies, waits for them, and re-layouts  0.72 us (2%)
  between operations  0.68 us (2%)
    ppermute x4, waiting for transfers between devices, local(): passed.append(lax.ppermute(block, 'col', inner_shift(n_col, k)))  7.94 us
    ppermute x1, waiting for transfers between devices, local(): total = total + lax.ppermute(sums[j], 'row', outer_shift(n_row, j))  6.83 us
    ppermute x3, waiting for transfers between devices, local(): arrived = lax.ppermute(block, 'col', outer_ring(n_col))  6.19 us
    ppermute x4, starting transfers between devices, local(): passed.append(lax.ppermute(block, 'col', inner_shift(n_col, k)))  5.5 us
    ppermute x3, starting transfers between devices, local(): arrived = lax.ppermute(block, 'col', outer_ring(n_col))  3.28 us
    ppermute x3, waiting for transfers between devices, local(): column[j, k] = lax.ppermute(mine, 'row', both_shift(n_row, j, k))  2.81 us
    ppermute x3, starting transfers between devices, local(): column[j, k] = lax.ppermute(mine, 'row', both_shift(n_row, j, k))  1.86 us
    pallas_call x1, Pallas kernels, partials(): pl.pallas_call(functools.partial(block_kernel, scale, len(own), len(keys)...  1.75 us
  transfers between devices with their start and end apart: 13, of which 11 were waited for; matrix products, arithmetic and copies ran while one was open for 0% of the time, Pallas kernels for 0%

profile of v2, /device:TPU:0, one launch (start us, length us, event | category | flops | bytes accessed | tf_op | source)
XLA Modules:
  0.0 41.7 jit_solution(9346104659983952346)
XLA Ops:
  0.6 0.0 copy-start
  0.6 0.9 %pad_maximum_fusion.refs_0_.refs_4_ = bf16[2,32,1024]{2,1,0:T(8,128)(2,1)S(1)} fusion(bf16[1,32,1024]{2,1,0:T(8,128)(2,1)} %bitcast.6, bf16[1,32,1024]{2,1,0:T(8,128)(2,1)} %bitcast.7), kind=kLoop, calls=%fused_computation.3 | loop fusion | flops 65536 | bytes 262144 | tf_op jit(solution)/shard_map/stack | solution.py:85
  1.5 3.0 %collective-permute-start.2 = (bf16[2,32,1024]{2,1,0:T(8,128)(2,1)S(1)}, bf16[2,32,1024]{2,1,0:T(8,128)(2,1)S(1)}, u32[]{:S(2)}, u32[]{:S(2)}) collective-permute-start(bf16[2,32,1024]{2,1,0:T(8,128)(2,1)S(1)} %pad_maximum_fusion.refs_0_.refs_4_), channel_id=1, source_target_pairs={{0,1},{1,0},{2,3},{3,2},{4,5},{5,4},{6,7},{7,6},{8,9},{9,8},{10,11... | collective-permute-start | bytes 393224 | tf_op jit(solution)/shard_map/ppermute | solution.py:95
  4.5 1.6 %collective-permute-start.1 = (bf16[2,32,1024]{2,1,0:T(8,128)(2,1)S(1)}, bf16[2,32,1024]{2,1,0:T(8,128)(2,1)S(1)}, u32[]{:S(2)}, u32[]{:S(2)}) collective-permute-start(bf16[2,32,1024]{2,1,0:T(8,128)(2,1)S(1)} %pad_maximum_fusion.refs_0_.refs_4_), channel_id=1, source_target_pairs={{0,2},{1,3},{2,6},{3,7},{4,0},{5,1},{6,4},{7,5},{8,10},{9,11},{10,... | collective-permute-start | bytes 393224 | tf_op jit(solution)/shard_map/ppermute | solution.py:93
  6.1 1.9 %collective-permute-done.2.refs_6_ = bf16[2,32,1024]{2,1,0:T(8,128)(2,1)S(1)} collective-permute-done((bf16[2,32,1024]{2,1,0:T(8,128)(2,1)S(1)}, bf16[2,32,1024]{2,1,0:T(8,128)(2,1)S(1)}, u32[]{:S(2)}, u32[]{:S(2)}) %collective-permute-start.2) | collective-permute-done | bytes 131104 | tf_op jit(solution)/shard_map/ppermute | solution.py:95
  8.0 2.4 %collective-permute-done.1.refs_5_ = bf16[2,32,1024]{2,1,0:T(8,128)(2,1)S(1)} collective-permute-done((bf16[2,32,1024]{2,1,0:T(8,128)(2,1)S(1)}, bf16[2,32,1024]{2,1,0:T(8,128)(2,1)S(1)}, u32[]{:S(2)}, u32[]{:S(2)}) %collective-permute-start.1) | collective-permute-done | bytes 131104 | tf_op jit(solution)/shard_map/ppermute | solution.py:93
  10.4 0.5 %collective-permute-start.5 = (bf16[2,32,1024]{2,1,0:T(8,128)(2,1)S(1)}, bf16[2,32,1024]{2,1,0:T(8,128)(2,1)S(1)}, u32[]{:S(2)}, u32[]{:S(2)}) collective-permute-start(bf16[2,32,1024]{2,1,0:T(8,128)(2,1)S(1)} %collective-permute-done.1.refs_5_), channel_id=1, source_target_pairs={{0,1},{1,0},{2,3},{3,2},{4,5},{5,4},{6,7},{7,6},{8,9},{9,8},{10,11... | collective-permute-start | bytes 393224 | tf_op jit(solution)/shard_map/ppermute | solution.py:95
  10.9 0.9 %collective-permute-start.4 = (bf16[2,32,1024]{2,1,0:T(8,128)(2,1)S(1)}, bf16[2,32,1024]{2,1,0:T(8,128)(2,1)S(1)}, u32[]{:S(2)}, u32[]{:S(2)}) collective-permute-start(bf16[2,32,1024]{2,1,0:T(8,128)(2,1)S(1)} %collective-permute-done.1.refs_5_), channel_id=1, source_target_pairs={{0,2},{1,3},{2,6},{3,7},{4,0},{5,1},{6,4},{7,5},{8,10},{9,11},{10,... | collective-permute-start | bytes 393224 | tf_op jit(solution)/shard_map/ppermute | solution.py:93
  11.8 3.6 %collective-permute-done.5.refs_8_ = bf16[2,32,1024]{2,1,0:T(8,128)(2,1)S(1)} collective-permute-done((bf16[2,32,1024]{2,1,0:T(8,128)(2,1)S(1)}, bf16[2,32,1024]{2,1,0:T(8,128)(2,1)S(1)}, u32[]{:S(2)}, u32[]{:S(2)}) %collective-permute-start.5) | collective-permute-done | bytes 131104 | tf_op jit(solution)/shard_map/ppermute | solution.py:95
  15.4 1.4 %collective-permute-done.4.refs_7_ = bf16[2,32,1024]{2,1,0:T(8,128)(2,1)S(1)} collective-permute-done((bf16[2,32,1024]{2,1,0:T(8,128)(2,1)S(1)}, bf16[2,32,1024]{2,1,0:T(8,128)(2,1)S(1)}, u32[]{:S(2)}, u32[]{:S(2)}) %collective-permute-start.4) | collective-permute-done | bytes 131104 | tf_op jit(solution)/shard_map/ppermute | solution.py:93
  16.7 1.6 %collective-permute-start.8 = (bf16[2,32,1024]{2,1,0:T(8,128)(2,1)S(1)}, bf16[2,32,1024]{2,1,0:T(8,128)(2,1)S(1)}, u32[]{:S(2)}, u32[]{:S(2)}) collective-permute-start(bf16[2,32,1024]{2,1,0:T(8,128)(2,1)S(1)} %collective-permute-done.4.refs_7_), channel_id=1, source_target_pairs={{0,1},{1,0},{2,3},{3,2},{4,5},{5,4},{6,7},{7,6},{8,9},{9,8},{10,11... | collective-permute-start | bytes 393224 | tf_op jit(solution)/shard_map/ppermute | solution.py:95
  18.3 0.8 %collective-permute-start.7 = (bf16[2,32,1024]{2,1,0:T(8,128)(2,1)S(1)}, bf16[2,32,1024]{2,1,0:T(8,128)(2,1)S(1)}, u32[]{:S(2)}, u32[]{:S(2)}) collective-permute-start(bf16[2,32,1024]{2,1,0:T(8,128)(2,1)S(1)} %collective-permute-done.4.refs_7_), channel_id=1, source_target_pairs={{0,2},{1,3},{2,6},{3,7},{4,0},{5,1},{6,4},{7,5},{8,10},{9,11},{10,... | collective-permute-start | bytes 393224 | tf_op jit(solution)/shard_map/ppermute | solution.py:93
  19.1 0.0 collective-permute-start
  19.1 1.5 %collective-permute-start.3 = (bf16[2,32,1024]{2,1,0:T(8,128)(2,1)S(1)}, bf16[2,32,1024]{2,1,0:T(8,128)(2,1)S(1)}, u32[]{:S(2)}, u32[]{:S(2)}) collective-permute-start(bf16[2,32,1024]{2,1,0:T(8,128)(2,1)S(1)} %pad_maximum_fusion.refs_0_.refs_4_), channel_id=1, source_target_pairs={{16,0},{24,8},{0,16},{8,24},{17,1},{25,9},{1,17},{9,25},{18,2},{26... | collective-permute-start | bytes 393224 | tf_op jit(solution)/shard_map/ppermute | solution.py:97
  20.6 0.3 collective-permute-start.6
  21.0 0.7 %collective-permute-done.8.refs_10_ = bf16[2,32,1024]{2,1,0:T(8,128)(2,1)S(1)} collective-permute-done((bf16[2,32,1024]{2,1,0:T(8,128)(2,1)S(1)}, bf16[2,32,1024]{2,1,0:T(8,128)(2,1)S(1)}, u32[]{:S(2)}, u32[]{:S(2)}) %collective-permute-start.8) | collective-permute-done | bytes 131104 | tf_op jit(solution)/shard_map/ppermute | solution.py:95
  21.7 2.5 %collective-permute-done.7.refs_9_ = bf16[2,32,1024]{2,1,0:T(8,128)(2,1)S(1)} collective-permute-done((bf16[2,32,1024]{2,1,0:T(8,128)(2,1)S(1)}, bf16[2,32,1024]{2,1,0:T(8,128)(2,1)S(1)}, u32[]{:S(2)}, u32[]{:S(2)}) %collective-permute-start.7) | collective-permute-done | bytes 131104 | tf_op jit(solution)/shard_map/ppermute | solution.py:93
  24.2 0.5 %collective-permute-start.9 = (bf16[2,32,1024]{2,1,0:T(8,128)(2,1)S(1)}, bf16[2,32,1024]{2,1,0:T(8,128)(2,1)S(1)}, u32[]{:S(2)}, u32[]{:S(2)}) collective-permute-start(bf16[2,32,1024]{2,1,0:T(8,128)(2,1)S(1)} %collective-permute-done.7.refs_9_), channel_id=1, source_target_pairs={{0,1},{1,0},{2,3},{3,2},{4,5},{5,4},{6,7},{7,6},{8,9},{9,8},{10,11... | collective-permute-start | bytes 393224 | tf_op jit(solution)/shard_map/ppermute | solution.py:95
  24.6 0.0 collective-permute-done.refs_1_
  24.6 0.8 %collective-permute-done.3.refs_2_ = bf16[2,32,1024]{2,1,0:T(8,128)(2,1)S(1)} collective-permute-done((bf16[2,32,1024]{2,1,0:T(8,128)(2,1)S(1)}, bf16[2,32,1024]{2,1,0:T(8,128)(2,1)S(1)}, u32[]{:S(2)}, u32[]{:S(2)}) %collective-permute-start.3) | collective-permute-done | bytes 131104 | tf_op jit(solution)/shard_map/ppermute | solution.py:97
  25.4 2.0 %collective-permute-done.6.refs_3_ = bf16[2,32,1024]{2,1,0:T(8,128)(2,1)S(1)} collective-permute-done((bf16[2,32,1024]{2,1,0:T(8,128)(2,1)S(1)}, bf16[2,32,1024]{2,1,0:T(8,128)(2,1)S(1)}, u32[]{:S(2)}, u32[]{:S(2)}) %collective-permute-start.6) | collective-permute-done | bytes 131104 | tf_op jit(solution)/shard_map/ppermute | solution.py:97
  27.5 1.7 %collective-permute-done.9.refs_11_ = bf16[2,32,1024]{2,1,0:T(8,128)(2,1)S(1)} collective-permute-done((bf16[2,32,1024]{2,1,0:T(8,128)(2,1)S(1)}, bf16[2,32,1024]{2,1,0:T(8,128)(2,1)S(1)}, u32[]{:S(2)}, u32[]{:S(2)}) %collective-permute-start.9) | collective-permute-done | bytes 131104 | tf_op jit(solution)/shard_map/ppermute | solution.py:95
  29.1 0.0 copy-done
  29.1 1.8 %shard_map.50 = (f32[2,32,1024]{2,1,0:T(8,128)S(1)}, f32[2,32,1024]{2,1,0:T(8,128)S(1)}, f32[2,32,1024]{2,1,0:T(8,128)S(1)}, f32[2,32,1024]{2,1,0:T(8,128)S(1)}) custom-call(f32[2]{0:T(128)S(1)} %copy-done, bf16[2,32,1024]{2,1,0:T(8,128)(2,1)S(1)} %pad_maximum_fusion.refs_0_.refs_4_, bf16[2,32,1024]{2,1,0:T(8,128)(2,1)S(1)} %collective-permute-done.refs_1_, ...), custom_call_target="tpu_custom_call" | custom-call | tf_op jit(solution)/shard_map/pallas_call | solution.py:69
  30.9 0.1 collective-permute-start.11
  31.0 0.5 %collective-permute-start.10 = (f32[2,32,1024]{2,1,0:T(8,128)S(1)}, f32[2,32,1024]{2,1,0:T(8,128)S(1)}, u32[]{:S(2)}, u32[]{:S(2)}) collective-permute-start(f32[2,32,1024]{2,1,0:T(8,128)S(1)} %get-tuple-element.23), channel_id=1, source_target_pairs={{0,8},{8,0},{16,24},{24,16},{1,9},{9,1},{17,25},{25,17},{2,10},{10... | collective-permute-start | bytes 786440 | tf_op jit(solution)/shard_map/ppermute | solution.py:109
  31.5 1.0 %collective-permute-done.11 = f32[2,32,1024]{2,1,0:T(8,128)S(1)} collective-permute-done((f32[2,32,1024]{2,1,0:T(8,128)S(1)}, f32[2,32,1024]{2,1,0:T(8,128)S(1)}, u32[]{:S(2)}, u32[]{:S(2)}) %collective-permute-start.11) | collective-permute-done | bytes 262176 | tf_op jit(solution)/shard_map/ppermute | solution.py:109
  32.5 1.6 %collective-permute-start.12 = (f32[2,32,1024]{2,1,0:T(8,128)S(1)}, f32[2,32,1024]{2,1,0:T(8,128)S(1)}, u32[]{:S(2)}, u32[]{:S(2)}) collective-permute-start(f32[2,32,1024]{2,1,0:T(8,128)S(1)} %add.10), channel_id=1, source_target_pairs={{0,16},{8,24},{16,0},{24,8},{1,17},{9,25},{17,1},{25,9},{2,18},{10... | collective-permute-start | bytes 786440 | tf_op jit(solution)/shard_map/ppermute | solution.py:113
  34.1 0.0 collective-permute-done.10
  34.1 6.8 %collective-permute-done.12 = f32[2,32,1024]{2,1,0:T(8,128)S(1)} collective-permute-done((f32[2,32,1024]{2,1,0:T(8,128)S(1)}, f32[2,32,1024]{2,1,0:T(8,128)S(1)}, u32[]{:S(2)}, u32[]{:S(2)}) %collective-permute-start.12) | collective-permute-done | bytes 262176 | tf_op jit(solution)/shard_map/ppermute | solution.py:113
  41.0 0.7 %slice_bitcast_fusion = (f32[32,1024]{1,0:T(8,128)}, f32[32,1024]{1,0:T(8,128)}) fusion(f32[2,32,1024]{2,1,0:T(8,128)S(1)} %add_add_fusion), kind=kLoop, calls=%fused_computation.1 | loop fusion | bytes 524288 | tf_op jit(solution)/shard_map/squeeze | solution.py:114
  (2 shorter events, 0.1 us)
Async XLA Ops:
  0.6 28.5 %copy-start = (f32[2]{0:T(128)S(1)}, f32[2]{0:T(128)}, u32[]{:S(2)}) copy-start(f32[2]{0:T(128)} %weights.1) | copy-start | bytes 28
  1.5 6.5 %collective-permute-start.2 = (bf16[2,32,1024]{2,1,0:T(8,128)(2,1)S(1)}, bf16[2,32,1024]{2,1,0:T(8,128)(2,1)S(1)}, u32[]{:S(2)}, u32[]{:S(2)}) collective-permute-start(bf16[2,32,1024]{2,1,0:T(8,128)(2,1)S(1)} %pad_maximum_fusion.refs_0_.refs_4_), channel_id=1, source_target_pairs={{0,1},{1,0},{2,3},{3,2},{4,5},{5,4},{6,7},{7,6},{8,9},{9,8},{10,11... | collective-permute-start | bytes 393224 | tf_op jit(solution)/shard_map/ppermute | solution.py:95
  4.5 5.9 %collective-permute-start.1 = (bf16[2,32,1024]{2,1,0:T(8,128)(2,1)S(1)}, bf16[2,32,1024]{2,1,0:T(8,128)(2,1)S(1)}, u32[]{:S(2)}, u32[]{:S(2)}) collective-permute-start(bf16[2,32,1024]{2,1,0:T(8,128)(2,1)S(1)} %pad_maximum_fusion.refs_0_.refs_4_), channel_id=1, source_target_pairs={{0,2},{1,3},{2,6},{3,7},{4,0},{5,1},{6,4},{7,5},{8,10},{9,11},{10,... | collective-permute-start | bytes 393224 | tf_op jit(solution)/shard_map/ppermute | solution.py:93
  10.4 5.0 %collective-permute-start.5 = (bf16[2,32,1024]{2,1,0:T(8,128)(2,1)S(1)}, bf16[2,32,1024]{2,1,0:T(8,128)(2,1)S(1)}, u32[]{:S(2)}, u32[]{:S(2)}) collective-permute-start(bf16[2,32,1024]{2,1,0:T(8,128)(2,1)S(1)} %collective-permute-done.1.refs_5_), channel_id=1, source_target_pairs={{0,1},{1,0},{2,3},{3,2},{4,5},{5,4},{6,7},{7,6},{8,9},{9,8},{10,11... | collective-permute-start | bytes 393224 | tf_op jit(solution)/shard_map/ppermute | solution.py:95
  10.9 5.9 %collective-permute-start.4 = (bf16[2,32,1024]{2,1,0:T(8,128)(2,1)S(1)}, bf16[2,32,1024]{2,1,0:T(8,128)(2,1)S(1)}, u32[]{:S(2)}, u32[]{:S(2)}) collective-permute-start(bf16[2,32,1024]{2,1,0:T(8,128)(2,1)S(1)} %collective-permute-done.1.refs_5_), channel_id=1, source_target_pairs={{0,2},{1,3},{2,6},{3,7},{4,0},{5,1},{6,4},{7,5},{8,10},{9,11},{10,... | collective-permute-start | bytes 393224 | tf_op jit(solution)/shard_map/ppermute | solution.py:93
  16.7 5.0 %collective-permute-start.8 = (bf16[2,32,1024]{2,1,0:T(8,128)(2,1)S(1)}, bf16[2,32,1024]{2,1,0:T(8,128)(2,1)S(1)}, u32[]{:S(2)}, u32[]{:S(2)}) collective-permute-start(bf16[2,32,1024]{2,1,0:T(8,128)(2,1)S(1)} %collective-permute-done.4.refs_7_), channel_id=1, source_target_pairs={{0,1},{1,0},{2,3},{3,2},{4,5},{5,4},{6,7},{7,6},{8,9},{9,8},{10,11... | collective-permute-start | bytes 393224 | tf_op jit(solution)/shard_map/ppermute | solution.py:95
  18.3 5.9 %collective-permute-start.7 = (bf16[2,32,1024]{2,1,0:T(8,128)(2,1)S(1)}, bf16[2,32,1024]{2,1,0:T(8,128)(2,1)S(1)}, u32[]{:S(2)}, u32[]{:S(2)}) collective-permute-start(bf16[2,32,1024]{2,1,0:T(8,128)(2,1)S(1)} %collective-permute-done.4.refs_7_), channel_id=1, source_target_pairs={{0,2},{1,3},{2,6},{3,7},{4,0},{5,1},{6,4},{7,5},{8,10},{9,11},{10,... | collective-permute-start | bytes 393224 | tf_op jit(solution)/shard_map/ppermute | solution.py:93
  19.1 5.5 %collective-permute-start = (bf16[2,32,1024]{2,1,0:T(8,128)(2,1)S(1)}, bf16[2,32,1024]{2,1,0:T(8,128)(2,1)S(1)}, u32[]{:S(2)}, u32[]{:S(2)}) collective-permute-start(bf16[2,32,1024]{2,1,0:T(8,128)(2,1)S(1)} %pad_maximum_fusion.refs_0_.refs_4_), channel_id=1, source_target_pairs={{8,0},{0,8},{24,16},{16,24},{9,1},{1,9},{25,17},{17,25},{10,2},{2,... | collective-permute-start | bytes 393224 | tf_op jit(solution)/shard_map/ppermute | solution.py:97
  19.1 6.3 %collective-permute-start.3 = (bf16[2,32,1024]{2,1,0:T(8,128)(2,1)S(1)}, bf16[2,32,1024]{2,1,0:T(8,128)(2,1)S(1)}, u32[]{:S(2)}, u32[]{:S(2)}) collective-permute-start(bf16[2,32,1024]{2,1,0:T(8,128)(2,1)S(1)} %pad_maximum_fusion.refs_0_.refs_4_), channel_id=1, source_target_pairs={{16,0},{24,8},{0,16},{8,24},{17,1},{25,9},{1,17},{9,25},{18,2},{26... | collective-permute-start | bytes 393224 | tf_op jit(solution)/shard_map/ppermute | solution.py:97
  20.6 6.8 %collective-permute-start.6 = (bf16[2,32,1024]{2,1,0:T(8,128)(2,1)S(1)}, bf16[2,32,1024]{2,1,0:T(8,128)(2,1)S(1)}, u32[]{:S(2)}, u32[]{:S(2)}) collective-permute-start(bf16[2,32,1024]{2,1,0:T(8,128)(2,1)S(1)} %pad_maximum_fusion.refs_0_.refs_4_), channel_id=1, source_target_pairs={{24,0},{16,8},{8,16},{0,24},{25,1},{17,9},{9,17},{1,25},{26,2},{18... | collective-permute-start | bytes 393224 | tf_op jit(solution)/shard_map/ppermute | solution.py:97
  24.2 5.0 %collective-permute-start.9 = (bf16[2,32,1024]{2,1,0:T(8,128)(2,1)S(1)}, bf16[2,32,1024]{2,1,0:T(8,128)(2,1)S(1)}, u32[]{:S(2)}, u32[]{:S(2)}) collective-permute-start(bf16[2,32,1024]{2,1,0:T(8,128)(2,1)S(1)} %collective-permute-done.7.refs_9_), channel_id=1, source_target_pairs={{0,1},{1,0},{2,3},{3,2},{4,5},{5,4},{6,7},{7,6},{8,9},{9,8},{10,11... | collective-permute-start | bytes 393224 | tf_op jit(solution)/shard_map/ppermute | solution.py:95
  30.9 1.6 %collective-permute-start.11 = (f32[2,32,1024]{2,1,0:T(8,128)S(1)}, f32[2,32,1024]{2,1,0:T(8,128)S(1)}, u32[]{:S(2)}, u32[]{:S(2)}) collective-permute-start(f32[2,32,1024]{2,1,0:T(8,128)S(1)} %get-tuple-element.25), channel_id=1, source_target_pairs={{0,8},{8,0},{16,24},{24,16},{1,9},{9,1},{17,25},{25,17},{2,10},{10... | collective-permute-start | bytes 786440 | tf_op jit(solution)/shard_map/ppermute | solution.py:109
  31.0 3.1 %collective-permute-start.10 = (f32[2,32,1024]{2,1,0:T(8,128)S(1)}, f32[2,32,1024]{2,1,0:T(8,128)S(1)}, u32[]{:S(2)}, u32[]{:S(2)}) collective-permute-start(f32[2,32,1024]{2,1,0:T(8,128)S(1)} %get-tuple-element.23), channel_id=1, source_target_pairs={{0,8},{8,0},{16,24},{24,16},{1,9},{9,1},{17,25},{25,17},{2,10},{10... | collective-permute-start | bytes 786440 | tf_op jit(solution)/shard_map/ppermute | solution.py:109
  32.5 8.4 %collective-permute-start.12 = (f32[2,32,1024]{2,1,0:T(8,128)S(1)}, f32[2,32,1024]{2,1,0:T(8,128)S(1)}, u32[]{:S(2)}, u32[]{:S(2)}) collective-permute-start(f32[2,32,1024]{2,1,0:T(8,128)S(1)} %add.10), channel_id=1, source_target_pairs={{0,16},{8,24},{16,0},{24,8},{1,17},{9,25},{17,1},{25,9},{2,18},{10... | collective-permute-start | bytes 786440 | tf_op jit(solution)/shard_map/ppermute | solution.py:113

commit v3 on v1

--- a/solution.py
+++ b/solution.py
@@ -19,6 +19,14 @@
     return [(i, (i // inner + step) % outer * inner + i % inner) for i in range(count)]
 
 
+def outer_ring(count):
+    outer, inner = halves(count)
+    odd, even = list(range(1, outer, 2)), list(range(0, outer, 2))
+    ring = odd + even[::-1]
+    after = {a: ring[(i + 1) % outer] for i, a in enumerate(ring)}
+    return [(i, after[i // inner] * inner + i % inner) for i in range(count)]
+
+
 def inner_shift(count, step):
     _, inner = halves(count)
     return [(i, i // inner * inner + (i + step) % inner) for i in range(count)]
@@ -29,8 +37,8 @@
     return [((i // inner + j) % outer * inner + (i + k) % inner, i) for i in range(count)]
 
 
-def stacked(refs, part):
-    return jnp.concatenate([ref[part] for ref in refs], axis=0)
+def stacked(refs):
+    return jnp.concatenate([ref[...] for ref in refs], axis=0)
 
 
 def dot(a, b, dims):
@@ -38,18 +46,18 @@
 
 
 def block_kernel(scale, n_own, n_keys, weights, *refs):
-    own, keys, outs = refs[:n_own], refs[n_own : n_own + n_keys], refs[n_own + n_keys :]
+    own, keys, outs = refs[: 2 * n_own], refs[2 * n_own : -n_own], refs[-n_own:]
     nt = ((1,), (1,))
     nn = ((1,), (0,))
-    img, txt = stacked(own, 0), stacked(own, 1)
-    key_img, key_txt = stacked(keys, 0), stacked(keys, 1)
+    img, txt = stacked(own[:n_own]), stacked(own[n_own:])
+    key_img, key_txt = stacked(keys[:n_keys]), stacked(keys[n_keys:])
     cross = dot(img, key_txt, nt) - dot(txt, key_img, nt)
     inmodal = dot(img, key_img, nt) - dot(txt, key_txt, nt)
     p_mat = (cross * (weights[0] * scale)).astype(jnp.bfloat16)
     q_mat = (inmodal * (weights[1] * scale)).astype(jnp.bfloat16)
     grad_img = dot(p_mat, key_txt, nn) + dot(q_mat, key_img, nn)
     grad_txt = -dot(p_mat, key_img, nn) - dot(q_mat, key_txt, nn)
-    rows = own[0].shape[1]
+    rows = own[0].shape[0]
     for i, out in enumerate(outs):
         out[0] = grad_img[i * rows : (i + 1) * rows]
         out[1] = grad_txt[i * rows : (i + 1) * rows]
@@ -58,13 +66,14 @@
 def partials(own, keys, weights, scale):
     vmem = pl.BlockSpec(memory_space=pltpu.VMEM)
     smem = pl.BlockSpec(memory_space=pltpu.SMEM)
+    n_own, n_keys = len(own[0]), len(keys[0])
     return pl.pallas_call(
-        functools.partial(block_kernel, scale, len(own), len(keys)),
-        out_shape=[jax.ShapeDtypeStruct(x.shape, jnp.float32) for x in own],
-        in_specs=[smem] + [vmem] * (len(own) + len(keys)),
-        out_specs=[vmem] * len(own),
+        functools.partial(block_kernel, scale, n_own, n_keys),
+        out_shape=[jax.ShapeDtypeStruct((2, *x.shape), jnp.float32) for x in own[0]],
+        in_specs=[smem] + [vmem] * (2 * n_own + 2 * n_keys),
+        out_specs=[vmem] * n_own,
         compiler_params=pltpu.CompilerParams(vmem_limit_bytes=48 * 2**20),
-    )(weights, *own, *keys)
+    )(weights, *own[0], *own[1], *keys[0], *keys[1])
 
 
 def local(images, texts, loss_weights):
@@ -74,18 +83,29 @@
     width = images.shape[1]
     batch = images.shape[0] * n_row * n_col
     scale = 1.0 / math.sqrt(width * batch)
-    own = jnp.stack([images, texts])
+    own = (images, texts)
 
-    line = [own] + [lax.ppermute(own, "col", outer_shift(n_col, k)) for k in range(1, col_outer)]
-    keys = list(line)
-    for k in range(1, col_inner):
-        keys += [lax.ppermute(block, "col", inner_shift(n_col, k)) for block in line]
+    keys, block = [[images], [texts]], list(own)
+    for step in range(col_outer):
+        for s in range(2):
+            arrived, passed = block[s], []
+            if step + 1 < col_outer:
+                arrived = lax.ppermute(block[s], "col", outer_ring(n_col))
+            for k in range(1, col_inner):
+                passed.append(lax.ppermute(block[s], "col", inner_shift(n_col, k)))
+            if step + 1 < col_outer:
+                arrived, passed = lax.optimization_barrier((arrived, passed))
+                block[s] = arrived
+                keys[s].append(arrived)
+            keys[s] += passed
 
-    column = []
+    column = [[], []]
     for j in range(row_outer):
+        first = lax.ppermute(jnp.stack(own), "row", both_shift(n_row, j, 0)) if j else jnp.stack(own)
         for k in range(row_inner):
-            src = both_shift(n_row, j, k)
-            column.append(lax.ppermute(own, "row", src) if j or k else own)
+            pair = lax.ppermute(first, "row", both_shift(n_row, 0, k)) if k else first
+            for s in range(2):
+                column[s].append(pair[s] if j or k else own[s])
 
     parts = partials(column, keys, loss_weights, scale)
     sums = []

time: 41.9 us -> 42.8 us (1.021)
  starting transfers between devices: 13.9 us -> 19.1 us
  waiting for transfers between devices: 23.8 us -> 18.6 us
  local copies, waits for them, and re-layouts: 0.72 us -> 1.41 us
    ppermute x10 -> x17, starting transfers between devices: 11.7 us -> 17.4 us  [the longest x8 8.29 us: local(): passed.append(lax.ppermute(block[s], 'col', inner_shift(n_col, k)))]
    ppermute x10 -> x17, waiting for transfers between devices: 15.9 us -> 10.3 us  [the longest x8 5.39 us: local(): passed.append(lax.ppermute(block[s], 'col', inner_shift(n_col, k)))]
    unnamed x2 -> x6, local copies, waits for them, and re-layouts: 0.01 us -> 0.66 us
    ppermute x1, waiting for transfers between devices: 6.83 us -> 7.3 us  [local(): total = total + lax.ppermute(sums[j], 'row', outer_shift(n_row, j))]
    ppermute x1, starting transfers between devices: 1.58 us -> 1.11 us  [local(): total = total + lax.ppermute(sums[j], 'row', outer_shift(n_row, j))]
  transfers between devices with their start and end apart: 13 -> 20, of which waited for: 7 -> 10; matrix products, arithmetic and copies ran while one was open for 0% -> 2% of each run, Pallas kernels for 0% -> 0%
where the time goes in v3:
time: 42.8 us; the launch traced here: 42.6 us
  starting transfers between devices  19.1 us (45%)
  waiting for transfers between devices  18.6 us (43%)
  Pallas kernels  1.74 us (4%)
  local copies, waits for them, and re-layouts  1.41 us (3%)
  other arithmetic  0.96 us (2%)
  between operations  0.72 us (2%)
    ppermute x8, starting transfers between devices, local(): passed.append(lax.ppermute(block[s], 'col', inner_shift(n_col, k)))  8.29 us
    ppermute x6, starting transfers between devices, local(): arrived = lax.ppermute(block[s], 'col', outer_ring(n_col))  7.49 us
    ppermute x1, waiting for transfers between devices, local(): total = total + lax.ppermute(sums[j], 'row', outer_shift(n_row, j))  7.3 us
    ppermute x8, waiting for transfers between devices, local(): passed.append(lax.ppermute(block[s], 'col', inner_shift(n_col, k)))  5.39 us
    ppermute x6, waiting for transfers between devices, local(): arrived = lax.ppermute(block[s], 'col', outer_ring(n_col))  4.92 us
    pallas_call x1, Pallas kernels, partials(): pl.pallas_call(functools.partial(block_kernel, scale, n_own, n_keys), out...  1.74 us
    ppermute x1, starting transfers between devices, local(): lax.ppermute(jnp.stack(own), 'row', both_shift(n_row, j, 0))  1.58 us
    ppermute x1, starting transfers between devices, local(): total = total + lax.ppermute(sums[j], 'row', outer_shift(n_row, j))  1.11 us
  transfers between devices with their start and end apart: 20, of which 10 were waited for; matrix products, arithmetic and copies ran while one was open for 2% of the time, Pallas kernels for 0%

profile of v3, /device:TPU:0, one launch (start us, length us, event | category | flops | bytes accessed | tf_op | source)
XLA Modules:
  0.0 42.6 jit_solution(16603062840182985040)
XLA Ops:
  0.6 3.1 %collective-permute-start.3 = (bf16[32,1024]{1,0:T(8,128)(2,1)}, bf16[32,1024]{1,0:T(8,128)(2,1)S(1)}, u32[]{:S(2)}, u32[]{:S(2)}) collective-permute-start(bf16[32,1024]{1,0:T(8,128)(2,1)} %refs_8_.1), channel_id=1, source_target_pairs={{0,2},{1,3},{2,6},{3,7},{4,0},{5,1},{6,4},{7,5},{8,10},{9,11},{10,... | collective-permute-start | bytes 196616 | tf_op jit(solution)/shard_map/ppermute | solution.py:93
  3.7 1.5 %collective-permute-start.4 = (bf16[32,1024]{1,0:T(8,128)(2,1)}, bf16[32,1024]{1,0:T(8,128)(2,1)S(1)}, u32[]{:S(2)}, u32[]{:S(2)}) collective-permute-start(bf16[32,1024]{1,0:T(8,128)(2,1)} %refs_8_.1), channel_id=1, source_target_pairs={{0,1},{1,0},{2,3},{3,2},{4,5},{5,4},{6,7},{7,6},{8,9},{9,8},{10,11... | collective-permute-start | bytes 196616 | tf_op jit(solution)/shard_map/ppermute | solution.py:95
  5.2 2.6 %collective-permute-start.10 = (bf16[32,1024]{1,0:T(8,128)(2,1)}, bf16[32,1024]{1,0:T(8,128)(2,1)S(1)}, u32[]{:S(2)}, u32[]{:S(2)}) collective-permute-start(bf16[32,1024]{1,0:T(8,128)(2,1)} %refs_16_.1), channel_id=1, source_target_pairs={{0,2},{1,3},{2,6},{3,7},{4,0},{5,1},{6,4},{7,5},{8,10},{9,11},{10,... | collective-permute-start | bytes 196616 | tf_op jit(solution)/shard_map/ppermute | solution.py:93
  7.8 0.5 %collective-permute-start.11 = (bf16[32,1024]{1,0:T(8,128)(2,1)}, bf16[32,1024]{1,0:T(8,128)(2,1)S(1)}, u32[]{:S(2)}, u32[]{:S(2)}) collective-permute-start(bf16[32,1024]{1,0:T(8,128)(2,1)} %refs_16_.1), channel_id=1, source_target_pairs={{0,1},{1,0},{2,3},{3,2},{4,5},{5,4},{6,7},{7,6},{8,9},{9,8},{10,11... | collective-permute-start | bytes 196616 | tf_op jit(solution)/shard_map/ppermute | solution.py:95
  8.3 0.9 %pad_maximum_fusion = bf16[2,32,1024]{2,1,0:T(8,128)(2,1)S(1)} fusion(bf16[1,32,1024]{2,1,0:T(8,128)(2,1)} %bitcast.19, bf16[1,32,1024]{2,1,0:T(8,128)(2,1)} %bitcast.18), kind=kLoop, calls=%fused_computation.3 | loop fusion | flops 65536 | bytes 262144 | tf_op jit(solution)/shard_map/stack | solution.py:104
  9.2 1.6 %collective-permute-start.1 = (bf16[2,32,1024]{2,1,0:T(8,128)(2,1)S(1)}, bf16[2,32,1024]{2,1,0:T(8,128)(2,1)S(1)}, u32[]{:S(2)}, u32[]{:S(2)}) collective-permute-start(bf16[2,32,1024]{2,1,0:T(8,128)(2,1)S(1)} %pad_maximum_fusion), channel_id=1, source_target_pairs={{16,0},{24,8},{0,16},{8,24},{17,1},{25,9},{1,17},{9,25},{18,2},{26... | collective-permute-start | bytes 393224 | tf_op jit(solution)/shard_map/ppermute | solution.py:104
  10.8 0.0 collective-permute-done.3.refs_9_
  10.8 0.0 collective-permute-done.4.refs_10_
  10.8 1.5 %collective-permute-start.6 = (bf16[32,1024]{1,0:T(8,128)(2,1)S(1)}, bf16[32,1024]{1,0:T(8,128)(2,1)S(1)}, u32[]{:S(2)}, u32[]{:S(2)}) collective-permute-start(bf16[32,1024]{1,0:T(8,128)(2,1)S(1)} %collective-permute-done.3.refs_9_), channel_id=1, source_target_pairs={{0,1},{1,0},{2,3},{3,2},{4,5},{5,4},{6,7},{7,6},{8,9},{9,8},{10,11... | collective-permute-start | bytes 196616 | tf_op jit(solution)/shard_map/ppermute | solution.py:95
  12.3 0.4 %collective-permute-start.5 = (bf16[32,1024]{1,0:T(8,128)(2,1)S(1)}, bf16[32,1024]{1,0:T(8,128)(2,1)S(1)}, u32[]{:S(2)}, u32[]{:S(2)}) collective-permute-start(bf16[32,1024]{1,0:T(8,128)(2,1)S(1)} %collective-permute-done.3.refs_9_), channel_id=1, source_target_pairs={{0,2},{1,3},{2,6},{3,7},{4,0},{5,1},{6,4},{7,5},{8,10},{9,11},{10,... | collective-permute-start | bytes 196616 | tf_op jit(solution)/shard_map/ppermute | solution.py:93
  12.7 0.0 collective-permute-done.10.refs_17_
  12.8 0.0 collective-permute-done.11.refs_18_
  12.8 0.7 %collective-permute-start.13 = (bf16[32,1024]{1,0:T(8,128)(2,1)S(1)}, bf16[32,1024]{1,0:T(8,128)(2,1)S(1)}, u32[]{:S(2)}, u32[]{:S(2)}) collective-permute-start(bf16[32,1024]{1,0:T(8,128)(2,1)S(1)} %collective-permute-done.10.refs_17_), channel_id=1, source_target_pairs={{0,1},{1,0},{2,3},{3,2},{4,5},{5,4},{6,7},{7,6},{8,9},{9,8},{10,11... | collective-permute-start | bytes 196616 | tf_op jit(solution)/shard_map/ppermute | solution.py:95
  13.5 0.7 %collective-permute-start.12 = (bf16[32,1024]{1,0:T(8,128)(2,1)S(1)}, bf16[32,1024]{1,0:T(8,128)(2,1)S(1)}, u32[]{:S(2)}, u32[]{:S(2)}) collective-permute-start(bf16[32,1024]{1,0:T(8,128)(2,1)S(1)} %collective-permute-done.10.refs_17_), channel_id=1, source_target_pairs={{0,2},{1,3},{2,6},{3,7},{4,0},{5,1},{6,4},{7,5},{8,10},{9,11},{10,... | collective-permute-start | bytes 196616 | tf_op jit(solution)/shard_map/ppermute | solution.py:93
  14.2 0.9 %collective-permute-done.6.refs_12_ = bf16[32,1024]{1,0:T(8,128)(2,1)S(1)} collective-permute-done((bf16[32,1024]{1,0:T(8,128)(2,1)S(1)}, bf16[32,1024]{1,0:T(8,128)(2,1)S(1)}, u32[]{:S(2)}, u32[]{:S(2)}) %collective-permute-start.6) | collective-permute-done | bytes 65568 | tf_op jit(solution)/shard_map/ppermute | solution.py:95
  15.1 0.0 collective-permute-start
  15.1 2.4 %collective-permute-done.5.refs_11_ = bf16[32,1024]{1,0:T(8,128)(2,1)S(1)} collective-permute-done((bf16[32,1024]{1,0:T(8,128)(2,1)S(1)}, bf16[32,1024]{1,0:T(8,128)(2,1)S(1)}, u32[]{:S(2)}, u32[]{:S(2)}) %collective-permute-start.5) | collective-permute-done | bytes 65568 | tf_op jit(solution)/shard_map/ppermute | solution.py:93
  17.5 0.5 %collective-permute-start.8 = (bf16[32,1024]{1,0:T(8,128)(2,1)S(1)}, bf16[32,1024]{1,0:T(8,128)(2,1)S(1)}, u32[]{:S(2)}, u32[]{:S(2)}) collective-permute-start(bf16[32,1024]{1,0:T(8,128)(2,1)S(1)} %collective-permute-done.5.refs_11_), channel_id=1, source_target_pairs={{0,1},{1,0},{2,3},{3,2},{4,5},{5,4},{6,7},{7,6},{8,9},{9,8},{10,11... | collective-permute-start | bytes 196616 | tf_op jit(solution)/shard_map/ppermute | solution.py:95
  18.0 0.0 collective-permute-done.13.refs_20_
  18.0 0.0 collective-permute-start.7
  18.0 0.6 %collective-permute-done.12.refs_19_ = bf16[32,1024]{1,0:T(8,128)(2,1)S(1)} collective-permute-done((bf16[32,1024]{1,0:T(8,128)(2,1)S(1)}, bf16[32,1024]{1,0:T(8,128)(2,1)S(1)}, u32[]{:S(2)}, u32[]{:S(2)}) %collective-permute-start.12) | collective-permute-done | bytes 65568 | tf_op jit(solution)/shard_map/ppermute | solution.py:93
  18.6 1.3 %collective-permute-start.15 = (bf16[32,1024]{1,0:T(8,128)(2,1)S(1)}, bf16[32,1024]{1,0:T(8,128)(2,1)S(1)}, u32[]{:S(2)}, u32[]{:S(2)}) collective-permute-start(bf16[32,1024]{1,0:T(8,128)(2,1)S(1)} %collective-permute-done.12.refs_19_), channel_id=1, source_target_pairs={{0,1},{1,0},{2,3},{3,2},{4,5},{5,4},{6,7},{7,6},{8,9},{9,8},{10,11... | collective-permute-start | bytes 196616 | tf_op jit(solution)/shard_map/ppermute | solution.py:95
  19.9 0.0 collective-permute-done.1
  20.0 0.7 %collective-permute-start.14 = (bf16[32,1024]{1,0:T(8,128)(2,1)S(1)}, bf16[32,1024]{1,0:T(8,128)(2,1)S(1)}, u32[]{:S(2)}, u32[]{:S(2)}) collective-permute-start(bf16[32,1024]{1,0:T(8,128)(2,1)S(1)} %collective-permute-done.12.refs_19_), channel_id=1, source_target_pairs={{0,2},{1,3},{2,6},{3,7},{4,0},{5,1},{6,4},{7,5},{8,10},{9,11},{10,... | collective-permute-start | bytes 196616 | tf_op jit(solution)/shard_map/ppermute | solution.py:93
  20.7 0.0 collective-permute-done
  20.7 0.1 collective-permute-start.2
  20.8 0.0 copy-start
  20.8 0.0 copy-start.1
  20.8 0.9 %collective-permute-done.8.refs_14_ = bf16[32,1024]{1,0:T(8,128)(2,1)S(1)} collective-permute-done((bf16[32,1024]{1,0:T(8,128)(2,1)S(1)}, bf16[32,1024]{1,0:T(8,128)(2,1)S(1)}, u32[]{:S(2)}, u32[]{:S(2)}) %collective-permute-start.8) | collective-permute-done | bytes 65568 | tf_op jit(solution)/shard_map/ppermute | solution.py:95
  21.7 1.4 %collective-permute-done.7.refs_13_ = bf16[32,1024]{1,0:T(8,128)(2,1)S(1)} collective-permute-done((bf16[32,1024]{1,0:T(8,128)(2,1)S(1)}, bf16[32,1024]{1,0:T(8,128)(2,1)S(1)}, u32[]{:S(2)}, u32[]{:S(2)}) %collective-permute-start.7) | collective-permute-done | bytes 65568 | tf_op jit(solution)/shard_map/ppermute | solution.py:93
  23.2 1.5 %collective-permute-start.9 = (bf16[32,1024]{1,0:T(8,128)(2,1)S(1)}, bf16[32,1024]{1,0:T(8,128)(2,1)S(1)}, u32[]{:S(2)}, u32[]{:S(2)}) collective-permute-start(bf16[32,1024]{1,0:T(8,128)(2,1)S(1)} %collective-permute-done.7.refs_13_), channel_id=1, source_target_pairs={{0,1},{1,0},{2,3},{3,2},{4,5},{5,4},{6,7},{7,6},{8,9},{9,8},{10,11... | collective-permute-start | bytes 196616 | tf_op jit(solution)/shard_map/ppermute | solution.py:95
  24.7 0.0 collective-permute-done.15.refs_22_
  24.7 0.5 %collective-permute-done.14.refs_21_ = bf16[32,1024]{1,0:T(8,128)(2,1)S(1)} collective-permute-done((bf16[32,1024]{1,0:T(8,128)(2,1)S(1)}, bf16[32,1024]{1,0:T(8,128)(2,1)S(1)}, u32[]{:S(2)}, u32[]{:S(2)}) %collective-permute-start.14) | collective-permute-done | bytes 65568 | tf_op jit(solution)/shard_map/ppermute | solution.py:93
  25.1 0.7 %collective-permute-start.16 = (bf16[32,1024]{1,0:T(8,128)(2,1)S(1)}, bf16[32,1024]{1,0:T(8,128)(2,1)S(1)}, u32[]{:S(2)}, u32[]{:S(2)}) collective-permute-start(bf16[32,1024]{1,0:T(8,128)(2,1)S(1)} %collective-permute-done.14.refs_21_), channel_id=1, source_target_pairs={{0,1},{1,0},{2,3},{3,2},{4,5},{5,4},{6,7},{7,6},{8,9},{9,8},{10,11... | collective-permute-start | bytes 196616 | tf_op jit(solution)/shard_map/ppermute | solution.py:95
  25.8 0.0 collective-permute-done.2
  25.9 1.6 %collective-permute-done.9.refs_15_ = bf16[32,1024]{1,0:T(8,128)(2,1)S(1)} collective-permute-done((bf16[32,1024]{1,0:T(8,128)(2,1)S(1)}, bf16[32,1024]{1,0:T(8,128)(2,1)S(1)}, u32[]{:S(2)}, u32[]{:S(2)}) %collective-permute-start.9) | collective-permute-done | bytes 65568 | tf_op jit(solution)/shard_map/ppermute | solution.py:95
  27.4 1.9 %collective-permute-done.16.refs_23_ = bf16[32,1024]{1,0:T(8,128)(2,1)S(1)} collective-permute-done((bf16[32,1024]{1,0:T(8,128)(2,1)S(1)}, bf16[32,1024]{1,0:T(8,128)(2,1)S(1)}, u32[]{:S(2)}, u32[]{:S(2)}) %collective-permute-start.16) | collective-permute-done | bytes 65568 | tf_op jit(solution)/shard_map/ppermute | solution.py:95
  29.4 0.0 copy-start.2
  29.4 0.0 copy-done
  29.4 0.0 copy-done.1
  29.4 0.6 %copy-done.2 = f32[2]{0:T(128)S(1)} copy-done((f32[2]{0:T(128)S(1)}, f32[2]{0:T(128)}, u32[]{:S(2)}) %copy-start.2) | copy-done | bytes 32
  30.0 1.7 %shard_map.50 = (f32[2,32,1024]{2,1,0:T(8,128)S(1)}, f32[2,32,1024]{2,1,0:T(8,128)S(1)}, f32[2,32,1024]{2,1,0:T(8,128)S(1)}, f32[2,32,1024]{2,1,0:T(8,128)S(1)}) custom-call(f32[2]{0:T(128)S(1)} %copy-done.2, bf16[32,1024]{1,0:T(8,128)(2,1)S(1)} %copy-done, bf16[32,1024]{1,0:T(8,128)(2,1)S(1)} %get-tuple-element.41.refs_1_, ...), custom_call_target="tpu_custom_call" | custom-call | tf_op jit(solution)/shard_map/pallas_call | solution.py:70
  31.8 0.1 collective-permute-start.18
  31.9 0.5 %collective-permute-start.17 = (f32[2,32,1024]{2,1,0:T(8,128)S(1)}, f32[2,32,1024]{2,1,0:T(8,128)S(1)}, u32[]{:S(2)}, u32[]{:S(2)}) collective-permute-start(f32[2,32,1024]{2,1,0:T(8,128)S(1)} %get-tuple-element.31), channel_id=1, source_target_pairs={{0,8},{8,0},{16,24},{24,16},{1,9},{9,1},{17,25},{25,17},{2,10},{10... | collective-permute-start | bytes 786440 | tf_op jit(solution)/shard_map/ppermute | solution.py:115
  32.4 1.0 %collective-permute-done.18 = f32[2,32,1024]{2,1,0:T(8,128)S(1)} collective-permute-done((f32[2,32,1024]{2,1,0:T(8,128)S(1)}, f32[2,32,1024]{2,1,0:T(8,128)S(1)}, u32[]{:S(2)}, u32[]{:S(2)}) %collective-permute-start.18) | collective-permute-done | bytes 262176 | tf_op jit(solution)/shard_map/ppermute | solution.py:115
  33.4 1.1 %collective-permute-start.19 = (f32[2,32,1024]{2,1,0:T(8,128)S(1)}, f32[2,32,1024]{2,1,0:T(8,128)S(1)}, u32[]{:S(2)}, u32[]{:S(2)}) collective-permute-start(f32[2,32,1024]{2,1,0:T(8,128)S(1)} %add.10), channel_id=1, source_target_pairs={{0,16},{8,24},{16,0},{24,8},{1,17},{9,25},{17,1},{25,9},{2,18},{10... | collective-permute-start | bytes 786440 | tf_op jit(solution)/shard_map/ppermute | solution.py:119
  34.5 0.0 collective-permute-done.17
  34.5 7.3 %collective-permute-done.19 = f32[2,32,1024]{2,1,0:T(8,128)S(1)} collective-permute-done((f32[2,32,1024]{2,1,0:T(8,128)S(1)}, f32[2,32,1024]{2,1,0:T(8,128)S(1)}, u32[]{:S(2)}, u32[]{:S(2)}) %collective-permute-start.19) | collective-permute-done | bytes 262176 | tf_op jit(solution)/shard_map/ppermute | solution.py:119
  41.9 0.7 %slice_bitcast_fusion = (f32[32,1024]{1,0:T(8,128)}, f32[32,1024]{1,0:T(8,128)}) fusion(f32[2,32,1024]{2,1,0:T(8,128)S(1)} %add_add_fusion), kind=kLoop, calls=%fused_computation.1 | loop fusion | bytes 524288 | tf_op jit(solution)/shard_map/squeeze | solution.py:120
  (5 shorter events, 0.1 us)
Async XLA Ops:
  0.6 10.2 %collective-permute-start.3 = (bf16[32,1024]{1,0:T(8,128)(2,1)}, bf16[32,1024]{1,0:T(8,128)(2,1)S(1)}, u32[]{:S(2)}, u32[]{:S(2)}) collective-permute-start(bf16[32,1024]{1,0:T(8,128)(2,1)} %refs_8_.1), channel_id=1, source_target_pairs={{0,2},{1,3},{2,6},{3,7},{4,0},{5,1},{6,4},{7,5},{8,10},{9,11},{10,... | collective-permute-start | bytes 196616 | tf_op jit(solution)/shard_map/ppermute | solution.py:93
  3.7 7.1 %collective-permute-start.4 = (bf16[32,1024]{1,0:T(8,128)(2,1)}, bf16[32,1024]{1,0:T(8,128)(2,1)S(1)}, u32[]{:S(2)}, u32[]{:S(2)}) collective-permute-start(bf16[32,1024]{1,0:T(8,128)(2,1)} %refs_8_.1), channel_id=1, source_target_pairs={{0,1},{1,0},{2,3},{3,2},{4,5},{5,4},{6,7},{7,6},{8,9},{9,8},{10,11... | collective-permute-start | bytes 196616 | tf_op jit(solution)/shard_map/ppermute | solution.py:95
  5.2 7.6 %collective-permute-start.10 = (bf16[32,1024]{1,0:T(8,128)(2,1)}, bf16[32,1024]{1,0:T(8,128)(2,1)S(1)}, u32[]{:S(2)}, u32[]{:S(2)}) collective-permute-start(bf16[32,1024]{1,0:T(8,128)(2,1)} %refs_16_.1), channel_id=1, source_target_pairs={{0,2},{1,3},{2,6},{3,7},{4,0},{5,1},{6,4},{7,5},{8,10},{9,11},{10,... | collective-permute-start | bytes 196616 | tf_op jit(solution)/shard_map/ppermute | solution.py:93
  7.8 5.0 %collective-permute-start.11 = (bf16[32,1024]{1,0:T(8,128)(2,1)}, bf16[32,1024]{1,0:T(8,128)(2,1)S(1)}, u32[]{:S(2)}, u32[]{:S(2)}) collective-permute-start(bf16[32,1024]{1,0:T(8,128)(2,1)} %refs_16_.1), channel_id=1, source_target_pairs={{0,1},{1,0},{2,3},{3,2},{4,5},{5,4},{6,7},{7,6},{8,9},{9,8},{10,11... | collective-permute-start | bytes 196616 | tf_op jit(solution)/shard_map/ppermute | solution.py:95
  9.2 10.7 %collective-permute-start.1 = (bf16[2,32,1024]{2,1,0:T(8,128)(2,1)S(1)}, bf16[2,32,1024]{2,1,0:T(8,128)(2,1)S(1)}, u32[]{:S(2)}, u32[]{:S(2)}) collective-permute-start(bf16[2,32,1024]{2,1,0:T(8,128)(2,1)S(1)} %pad_maximum_fusion), channel_id=1, source_target_pairs={{16,0},{24,8},{0,16},{8,24},{17,1},{25,9},{1,17},{9,25},{18,2},{26... | collective-permute-start | bytes 393224 | tf_op jit(solution)/shard_map/ppermute | solution.py:104
  10.8 4.3 %collective-permute-start.6 = (bf16[32,1024]{1,0:T(8,128)(2,1)S(1)}, bf16[32,1024]{1,0:T(8,128)(2,1)S(1)}, u32[]{:S(2)}, u32[]{:S(2)}) collective-permute-start(bf16[32,1024]{1,0:T(8,128)(2,1)S(1)} %collective-permute-done.3.refs_9_), channel_id=1, source_target_pairs={{0,1},{1,0},{2,3},{3,2},{4,5},{5,4},{6,7},{7,6},{8,9},{9,8},{10,11... | collective-permute-start | bytes 196616 | tf_op jit(solution)/shard_map/ppermute | solution.py:95
  12.3 5.2 %collective-permute-start.5 = (bf16[32,1024]{1,0:T(8,128)(2,1)S(1)}, bf16[32,1024]{1,0:T(8,128)(2,1)S(1)}, u32[]{:S(2)}, u32[]{:S(2)}) collective-permute-start(bf16[32,1024]{1,0:T(8,128)(2,1)S(1)} %collective-permute-done.3.refs_9_), channel_id=1, source_target_pairs={{0,2},{1,3},{2,6},{3,7},{4,0},{5,1},{6,4},{7,5},{8,10},{9,11},{10,... | collective-permute-start | bytes 196616 | tf_op jit(solution)/shard_map/ppermute | solution.py:93
  12.8 5.2 %collective-permute-start.13 = (bf16[32,1024]{1,0:T(8,128)(2,1)S(1)}, bf16[32,1024]{1,0:T(8,128)(2,1)S(1)}, u32[]{:S(2)}, u32[]{:S(2)}) collective-permute-start(bf16[32,1024]{1,0:T(8,128)(2,1)S(1)} %collective-permute-done.10.refs_17_), channel_id=1, source_target_pairs={{0,1},{1,0},{2,3},{3,2},{4,5},{5,4},{6,7},{7,6},{8,9},{9,8},{10,11... | collective-permute-start | bytes 196616 | tf_op jit(solution)/shard_map/ppermute | solution.py:95
  13.5 5.2 %collective-permute-start.12 = (bf16[32,1024]{1,0:T(8,128)(2,1)S(1)}, bf16[32,1024]{1,0:T(8,128)(2,1)S(1)}, u32[]{:S(2)}, u32[]{:S(2)}) collective-permute-start(bf16[32,1024]{1,0:T(8,128)(2,1)S(1)} %collective-permute-done.10.refs_17_), channel_id=1, source_target_pairs={{0,2},{1,3},{2,6},{3,7},{4,0},{5,1},{6,4},{7,5},{8,10},{9,11},{10,... | collective-permute-start | bytes 196616 | tf_op jit(solution)/shard_map/ppermute | solution.py:93
  15.1 5.6 %collective-permute-start = (bf16[2,32,1024]{2,1,0:T(8,128)(2,1)S(1)}, bf16[2,32,1024]{2,1,0:T(8,128)(2,1)S(1)}, u32[]{:S(2)}, u32[]{:S(2)}) collective-permute-start(bf16[2,32,1024]{2,1,0:T(8,128)(2,1)S(1)} %pad_maximum_fusion), channel_id=1, source_target_pairs={{8,0},{0,8},{24,16},{16,24},{9,1},{1,9},{25,17},{17,25},{10,2},{2,... | collective-permute-start | bytes 393224 | tf_op jit(solution)/shard_map/ppermute | solution.py:106
  17.5 4.3 %collective-permute-start.8 = (bf16[32,1024]{1,0:T(8,128)(2,1)S(1)}, bf16[32,1024]{1,0:T(8,128)(2,1)S(1)}, u32[]{:S(2)}, u32[]{:S(2)}) collective-permute-start(bf16[32,1024]{1,0:T(8,128)(2,1)S(1)} %collective-permute-done.5.refs_11_), channel_id=1, source_target_pairs={{0,1},{1,0},{2,3},{3,2},{4,5},{5,4},{6,7},{7,6},{8,9},{9,8},{10,11... | collective-permute-start | bytes 196616 | tf_op jit(solution)/shard_map/ppermute | solution.py:95
  18.0 5.2 %collective-permute-start.7 = (bf16[32,1024]{1,0:T(8,128)(2,1)S(1)}, bf16[32,1024]{1,0:T(8,128)(2,1)S(1)}, u32[]{:S(2)}, u32[]{:S(2)}) collective-permute-start(bf16[32,1024]{1,0:T(8,128)(2,1)S(1)} %collective-permute-done.5.refs_11_), channel_id=1, source_target_pairs={{0,2},{1,3},{2,6},{3,7},{4,0},{5,1},{6,4},{7,5},{8,10},{9,11},{10,... | collective-permute-start | bytes 196616 | tf_op jit(solution)/shard_map/ppermute | solution.py:93
  18.6 6.0 %collective-permute-start.15 = (bf16[32,1024]{1,0:T(8,128)(2,1)S(1)}, bf16[32,1024]{1,0:T(8,128)(2,1)S(1)}, u32[]{:S(2)}, u32[]{:S(2)}) collective-permute-start(bf16[32,1024]{1,0:T(8,128)(2,1)S(1)} %collective-permute-done.12.refs_19_), channel_id=1, source_target_pairs={{0,1},{1,0},{2,3},{3,2},{4,5},{5,4},{6,7},{7,6},{8,9},{9,8},{10,11... | collective-permute-start | bytes 196616 | tf_op jit(solution)/shard_map/ppermute | solution.py:95
  20.0 5.2 %collective-permute-start.14 = (bf16[32,1024]{1,0:T(8,128)(2,1)S(1)}, bf16[32,1024]{1,0:T(8,128)(2,1)S(1)}, u32[]{:S(2)}, u32[]{:S(2)}) collective-permute-start(bf16[32,1024]{1,0:T(8,128)(2,1)S(1)} %collective-permute-done.12.refs_19_), channel_id=1, source_target_pairs={{0,2},{1,3},{2,6},{3,7},{4,0},{5,1},{6,4},{7,5},{8,10},{9,11},{10,... | collective-permute-start | bytes 196616 | tf_op jit(solution)/shard_map/ppermute | solution.py:93
  20.7 5.2 %collective-permute-start.2 = (bf16[2,32,1024]{2,1,0:T(8,128)(2,1)S(1)}, bf16[2,32,1024]{2,1,0:T(8,128)(2,1)S(1)}, u32[]{:S(2)}, u32[]{:S(2)}) collective-permute-start(bf16[2,32,1024]{2,1,0:T(8,128)(2,1)S(1)} %collective-permute-done.1), channel_id=1, source_target_pairs={{8,0},{0,8},{24,16},{16,24},{9,1},{1,9},{25,17},{17,25},{10,2},{2,... | collective-permute-start | bytes 393224 | tf_op jit(solution)/shard_map/ppermute | solution.py:106
  20.8 8.6 %copy-start = (bf16[32,1024]{1,0:T(8,128)(2,1)S(1)}, bf16[32,1024]{1,0:T(8,128)(2,1)}, u32[]{:S(2)}) copy-start(bf16[32,1024]{1,0:T(8,128)(2,1)} %refs_8_.1) | copy-start | bytes 196612
  20.8 8.6 %copy-start.1 = (bf16[32,1024]{1,0:T(8,128)(2,1)S(1)}, bf16[32,1024]{1,0:T(8,128)(2,1)}, u32[]{:S(2)}) copy-start(bf16[32,1024]{1,0:T(8,128)(2,1)} %refs_16_.1) | copy-start | bytes 196612
  23.2 4.3 %collective-permute-start.9 = (bf16[32,1024]{1,0:T(8,128)(2,1)S(1)}, bf16[32,1024]{1,0:T(8,128)(2,1)S(1)}, u32[]{:S(2)}, u32[]{:S(2)}) collective-permute-start(bf16[32,1024]{1,0:T(8,128)(2,1)S(1)} %collective-permute-done.7.refs_13_), channel_id=1, source_target_pairs={{0,1},{1,0},{2,3},{3,2},{4,5},{5,4},{6,7},{7,6},{8,9},{9,8},{10,11... | collective-permute-start | bytes 196616 | tf_op jit(solution)/shard_map/ppermute | solution.py:95
  25.1 4.3 %collective-permute-start.16 = (bf16[32,1024]{1,0:T(8,128)(2,1)S(1)}, bf16[32,1024]{1,0:T(8,128)(2,1)S(1)}, u32[]{:S(2)}, u32[]{:S(2)}) collective-permute-start(bf16[32,1024]{1,0:T(8,128)(2,1)S(1)} %collective-permute-done.14.refs_21_), channel_id=1, source_target_pairs={{0,1},{1,0},{2,3},{3,2},{4,5},{5,4},{6,7},{7,6},{8,9},{9,8},{10,11... | collective-permute-start | bytes 196616 | tf_op jit(solution)/shard_map/ppermute | solution.py:95
  29.4 0.7 %copy-start.2 = (f32[2]{0:T(128)S(1)}, f32[2]{0:T(128)}, u32[]{:S(2)}) copy-start(f32[2]{0:T(128)} %weights.1) | copy-start | bytes 28
  31.8 1.6 %collective-permute-start.18 = (f32[2,32,1024]{2,1,0:T(8,128)S(1)}, f32[2,32,1024]{2,1,0:T(8,128)S(1)}, u32[]{:S(2)}, u32[]{:S(2)}) collective-permute-start(f32[2,32,1024]{2,1,0:T(8,128)S(1)} %get-tuple-element.33), channel_id=1, source_target_pairs={{0,8},{8,0},{16,24},{24,16},{1,9},{9,1},{17,25},{25,17},{2,10},{10... | collective-permute-start | bytes 786440 | tf_op jit(solution)/shard_map/ppermute | solution.py:115
  31.9 2.7 %collective-permute-start.17 = (f32[2,32,1024]{2,1,0:T(8,128)S(1)}, f32[2,32,1024]{2,1,0:T(8,128)S(1)}, u32[]{:S(2)}, u32[]{:S(2)}) collective-permute-start(f32[2,32,1024]{2,1,0:T(8,128)S(1)} %get-tuple-element.31), channel_id=1, source_target_pairs={{0,8},{8,0},{16,24},{24,16},{1,9},{9,1},{17,25},{25,17},{2,10},{10... | collective-permute-start | bytes 786440 | tf_op jit(solution)/shard_map/ppermute | solution.py:115
  33.4 8.4 %collective-permute-start.19 = (f32[2,32,1024]{2,1,0:T(8,128)S(1)}, f32[2,32,1024]{2,1,0:T(8,128)S(1)}, u32[]{:S(2)}, u32[]{:S(2)}) collective-permute-start(f32[2,32,1024]{2,1,0:T(8,128)S(1)} %add.10), channel_id=1, source_target_pairs={{0,16},{8,24},{16,0},{24,8},{1,17},{9,25},{17,1},{25,9},{2,18},{10... | collective-permute-start | bytes 786440 | tf_op jit(solution)/shard_map/ppermute | solution.py:119

commit v4 on v1

v4 whole, which is shorter than its diff:
```python
import functools
import math

import jax
import jax.numpy as jnp
from jax import lax
from jax.experimental import pallas as pl
from jax.experimental.pallas import tpu as pltpu
from jax.sharding import PartitionSpec as P

LIMIT = 6.0
TOP = 32768.0


def halves(count):
    inner = 2 if count % 2 == 0 else 1
    return count // inner, inner


def outer_moves(count):
    outer, inner = halves(count)

    def perm(to):
        return [(i, to(i // inner) * inner + i % inner) for i in range(count)]

    moves = []
    if outer & (outer - 1) == 0:
        held, stride = 1, outer // 2
        while stride:
            moves += [(b, perm(lambda o, s=stride: o ^ s)) for b in range(held)]
            held, stride = 2 * held, stride // 2
    else:
        moves = [(0, perm(lambda o, s=s: (o + s) % outer)) for s in range(1, outer)]
    return moves


def inner_shift(count, step):
    _, inner = halves(count)
    return [(i, i // inner * inner + (i + step) % inner) for i in range(count)]


def square_shift(n_row, n_col, j, k):
    r_outer, r_inner = halves(n_row)
    _, c_inner = halves(n_col)
    pairs = []
    for r in range(n_row):
        for c in range(n_col):
            to_r = (r // r_inner + j) % r_outer * r_inner + r % r_inner
            to_c = c // c_inner * c_inner + (c + k) % c_inner
            pairs.append((r * n_col + c, to_r * n_col + to_c))
    return pairs


def stacked(refs, part):
    return jnp.concatenate([ref[part] for ref in refs], axis=0)


def dot(a, b, dims):
    return lax.dot_general(a, b, (dims, ((), ())), preferred_element_type=jnp.float32)


def block_kernel(scale, n_own, n_keys, weights, *refs):
    own, keys = refs[:n_own], refs[n_own : n_own + n_keys]
    mine, unscale, outs = refs[n_own + n_keys], refs[n_own + n_keys + 1], refs[n_own + n_keys + 2 :]
    nt = ((1,), (1,))
    nn = ((1,), (0,))
    img, txt = stacked(own, 0), stacked(own, 1)
    key_img, key_txt = stacked(keys, 0), stacked(keys, 1)
    cross = dot(img, key_txt, nt) - dot(txt, key_img, nt)
    inmodal = dot(img, key_img, nt) - dot(txt, key_txt, nt)
    p_mat = (cross * (weights[0] * scale)).astype(jnp.bfloat16)
    q_mat = (inmodal * (weights[1] * scale)).astype(jnp.bfloat16)
    grad_img = dot(p_mat, key_txt, nn) + dot(q_mat, key_img, nn)
    grad_txt = -dot(p_mat, key_img, nn) - dot(q_mat, key_txt, nn)
    size = jnp.sum(jnp.abs(img.astype(jnp.float32)) + jnp.abs(txt.astype(jnp.float32)), axis=1, keepdims=True)
    count = key_img.shape[0]
    most = size * ((weights[0] + weights[1]) * (1.02 * scale * LIMIT * LIMIT * count)) + 1e-30
    up, down = TOP / most, most / TOP
    rows = own[0].shape[1]
    grad_img, grad_txt = grad_img * up, grad_txt * up
    mine[0] = grad_img[:rows]
    mine[1] = grad_txt[:rows]
    unscale[...] = jnp.broadcast_to(down[:rows], unscale.shape)
    for i, out in enumerate(outs, 1):
        out[0] = grad_img[i * rows : (i + 1) * rows]
        out[1] = grad_txt[i * rows : (i + 1) * rows]


def partials(own, keys, weights, scale):
    vmem = pl.BlockSpec(memory_space=pltpu.VMEM)
    smem = pl.BlockSpec(memory_space=pltpu.SMEM)
    shape = own[0].shape
    out_shape = [jax.ShapeDtypeStruct(shape, jnp.float32), jax.ShapeDtypeStruct((shape[1], 128), jnp.float32)]
    out_shape += [jax.ShapeDtypeStruct(shape, jnp.float32)] * (len(own) - 1)
    return pl.pallas_call(
        functools.partial(block_kernel, scale, len(own), len(keys)),
        out_shape=out_shape,
        in_specs=[smem] + [vmem] * (len(own) + len(keys)),
        out_specs=[vmem] * len(out_shape),
        compiler_params=pltpu.CompilerParams(vmem_limit_bytes=48 * 2**20),
    )(weights, *own, *keys)


def local(images, texts, loss_weights):
    n_row, n_col = lax.axis_size("row"), lax.axis_size("col")
    width = images.shape[1]
    batch = images.shape[0] * n_row * n_col
    scale = 1.0 / math.sqrt(width * batch)
    both = ("row", "col")
    square = [(j, k) for j in range(halves(n_row)[0]) for k in range(halves(n_col)[1])][1:]
    own = jnp.stack([images, texts])

    line = [own]
    for which, perm in outer_moves(n_col):
        line.append(lax.ppermute(line[which], "col", perm))
    keys = list(line)
    for k in range(1, halves(n_row)[1]):
        keys += [lax.ppermute(block, "row", inner_shift(n_row, k)) for block in line]

    rows = [own] + [lax.ppermute(own, both, square_shift(n_row, n_col, j, k)) for j, k in square]

    mine, unscale, *parts = partials(rows, keys, loss_weights, scale)
    back = [
        lax.ppermute(part.astype(jnp.float16), both, square_shift(n_row, n_col, -j, -k))
        for part, (j, k) in zip(parts, square)
    ]
    down = unscale[:, :1]
    grads = []
    for s in range(2):
        total = mine[s]
        for part in back:
            total = total + part[s].astype(jnp.float32)
        grads.append(total * down)
    return tuple(grads)


def solution(mesh):
    in_specs = (P(("row", "col"), None), P(("row", "col"), None), P())
    out_specs = (P(("row", "col"), None), P(("row", "col"), None))
    return jax.shard_map(local, mesh=mesh, in_specs=in_specs, out_specs=out_specs, check_vma=False)
```

time: 41.9 us -> 30.6 us (0.73)
  waiting for transfers between devices: 23.8 us -> 10.3 us
  starting transfers between devices: 13.9 us -> 15.9 us
  other arithmetic: 0.96 us -> 1.73 us
  local copies, waits for them, and re-layouts: 0.72 us -> 0.11 us
    ppermute x13, waiting for transfers between devices: 23.8 us -> 10.3 us  [the longest x3 4.94 us: local(): lax.ppermute(part.astype(jnp.float16), both, square_shift(n_row, n_col, -...]
    ppermute x13, starting transfers between devices: 13.9 us -> 15.9 us  [the longest x3 6.34 us: local(): line.append(lax.ppermute(line[which], 'col', perm))]
    mul x0 -> x1, other arithmetic: none -> 0.78 us  [local(): grads.append(total * down)]
    squeeze x1 -> x0, local copies, waits for them, and re-layouts: 0.72 us -> none  [local(): return (total[0], total[1])]
where the time goes in v4:
time: 30.6 us; the launch traced here: 30.5 us
  starting transfers between devices  15.9 us (52%)
  waiting for transfers between devices  10.3 us (34%)
  Pallas kernels  1.76 us (6%)
  other arithmetic  1.73 us (6%)
  between operations  0.7 us (2%)
    ppermute x3, starting transfers between devices, local(): line.append(lax.ppermute(line[which], 'col', perm))  6.34 us
    ppermute x3, starting transfers between devices, local(): lax.ppermute(own, both, square_shift(n_row, n_col, j, k))  5.46 us
    ppermute x3, waiting for transfers between devices, local(): lax.ppermute(part.astype(jnp.float16), both, square_shift(n_row, n_col, -...  4.94 us
    ppermute x3, starting transfers between devices, local(): lax.ppermute(part.astype(jnp.float16), both, square_shift(n_row, n_col, -...  3.55 us
    ppermute x3, waiting for transfers between devices, local(): line.append(lax.ppermute(line[which], 'col', perm))  3.16 us
    ppermute x3, waiting for transfers between devices, local(): lax.ppermute(own, both, square_shift(n_row, n_col, j, k))  2.18 us
    pallas_call x1, Pallas kernels, partials(): pl.pallas_call(functools.partial(block_kernel, scale, len(own), len(keys)...  1.76 us
    another operation x1, other arithmetic, local(): own = jnp.stack([images, texts])  0.89 us
  transfers between devices with their start and end apart: 13, of which 7 were waited for; matrix products, arithmetic and copies ran while one was open for 0% of the time, Pallas kernels for 0%

profile of v4, /device:TPU:0, one launch (start us, length us, event | category | flops | bytes accessed | tf_op | source)
XLA Modules:
  0.0 30.5 jit_solution(9492406059632650541)
XLA Ops:
  0.6 0.0 copy-start
  0.6 0.9 %pad_maximum_fusion.refs_0_.refs_4_ = bf16[2,32,1024]{2,1,0:T(8,128)(2,1)S(1)} fusion(bf16[1,32,1024]{2,1,0:T(8,128)(2,1)} %bitcast.6, bf16[1,32,1024]{2,1,0:T(8,128)(2,1)} %bitcast.7), kind=kLoop, calls=%fused_computation | loop fusion | flops 65536 | bytes 262144 | tf_op jit(solution)/shard_map/stack | solution.py:111
  1.5 4.1 %collective-permute-start.3 = (bf16[2,32,1024]{2,1,0:T(8,128)(2,1)S(1)}, bf16[2,32,1024]{2,1,0:T(8,128)(2,1)S(1)}, u32[]{:S(2)}, u32[]{:S(2)}) collective-permute-start(bf16[2,32,1024]{2,1,0:T(8,128)(2,1)S(1)} %pad_maximum_fusion.refs_0_.refs_4_), channel_id=1, source_target_pairs={{0,4},{1,5},{2,6},{3,7},{4,0},{5,1},{6,2},{7,3},{8,12},{9,13},{10,... | collective-permute-start | bytes 393224 | tf_op jit(solution)/shard_map/ppermute | solution.py:115
  5.6 0.0 collective-permute-start.6
  5.6 1.6 %collective-permute-start.4 = (bf16[2,32,1024]{2,1,0:T(8,128)(2,1)S(1)}, bf16[2,32,1024]{2,1,0:T(8,128)(2,1)S(1)}, u32[]{:S(2)}, u32[]{:S(2)}) collective-permute-start(bf16[2,32,1024]{2,1,0:T(8,128)(2,1)S(1)} %pad_maximum_fusion.refs_0_.refs_4_), channel_id=1, source_target_pairs={{0,2},{1,3},{2,0},{3,1},{4,6},{5,7},{6,4},{7,5},{8,10},{9,11},{10,... | collective-permute-start | bytes 393224 | tf_op jit(solution)/shard_map/ppermute | solution.py:115
  7.2 2.4 %collective-permute-start.2 = (bf16[2,32,1024]{2,1,0:T(8,128)(2,1)S(1)}, bf16[2,32,1024]{2,1,0:T(8,128)(2,1)S(1)}, u32[]{:S(2)}, u32[]{:S(2)}) collective-permute-start(bf16[2,32,1024]{2,1,0:T(8,128)(2,1)S(1)} %pad_maximum_fusion.refs_0_.refs_4_), channel_id=1, source_target_pairs={{0,17},{1,16},{2,19},{3,18},{4,21},{5,20},{6,23},{7,22},{8,25},{9,... | collective-permute-start | bytes 393224 | tf_op jit(solution)/shard_map/ppermute | solution.py:120
  9.7 2.4 %collective-permute-done.3.refs_5_ = bf16[2,32,1024]{2,1,0:T(8,128)(2,1)S(1)} collective-permute-done((bf16[2,32,1024]{2,1,0:T(8,128)(2,1)S(1)}, bf16[2,32,1024]{2,1,0:T(8,128)(2,1)S(1)}, u32[]{:S(2)}, u32[]{:S(2)}) %collective-permute-start.3) | collective-permute-done | bytes 131104 | tf_op jit(solution)/shard_map/ppermute | solution.py:115
  12.0 0.7 %collective-permute-start.5 = (bf16[2,32,1024]{2,1,0:T(8,128)(2,1)S(1)}, bf16[2,32,1024]{2,1,0:T(8,128)(2,1)S(1)}, u32[]{:S(2)}, u32[]{:S(2)}) collective-permute-start(bf16[2,32,1024]{2,1,0:T(8,128)(2,1)S(1)} %collective-permute-done.3.refs_5_), channel_id=1, source_target_pairs={{0,2},{1,3},{2,0},{3,1},{4,6},{5,7},{6,4},{7,5},{8,10},{9,11},{10,... | collective-permute-start | bytes 393224 | tf_op jit(solution)/shard_map/ppermute | solution.py:115
  12.7 1.5 %collective-permute-start.1 = (bf16[2,32,1024]{2,1,0:T(8,128)(2,1)S(1)}, bf16[2,32,1024]{2,1,0:T(8,128)(2,1)S(1)}, u32[]{:S(2)}, u32[]{:S(2)}) collective-permute-start(bf16[2,32,1024]{2,1,0:T(8,128)(2,1)S(1)} %pad_maximum_fusion.refs_0_.refs_4_), channel_id=1, source_target_pairs={{0,16},{1,17},{2,18},{3,19},{4,20},{5,21},{6,22},{7,23},{8,24},{9,... | collective-permute-start | bytes 393224 | tf_op jit(solution)/shard_map/ppermute | solution.py:120
  14.2 0.0 collective-permute-done.6.refs_8_
  14.2 1.5 %collective-permute-start = (bf16[2,32,1024]{2,1,0:T(8,128)(2,1)S(1)}, bf16[2,32,1024]{2,1,0:T(8,128)(2,1)S(1)}, u32[]{:S(2)}, u32[]{:S(2)}) collective-permute-start(bf16[2,32,1024]{2,1,0:T(8,128)(2,1)S(1)} %pad_maximum_fusion.refs_0_.refs_4_), channel_id=1, source_target_pairs={{0,1},{1,0},{2,3},{3,2},{4,5},{5,4},{6,7},{7,6},{8,9},{9,8},{10,11... | collective-permute-start | bytes 393224 | tf_op jit(solution)/shard_map/ppermute | solution.py:120
  15.7 0.0 collective-permute-done.4.refs_6_
  15.7 0.0 collective-permute-start.7
  15.7 0.0 collective-permute-done.2.refs_3_
  15.7 0.5 %collective-permute-start.8 = (bf16[2,32,1024]{2,1,0:T(8,128)(2,1)S(1)}, bf16[2,32,1024]{2,1,0:T(8,128)(2,1)S(1)}, u32[]{:S(2)}, u32[]{:S(2)}) collective-permute-start(bf16[2,32,1024]{2,1,0:T(8,128)(2,1)S(1)} %collective-permute-done.4.refs_6_), channel_id=1, source_target_pairs={{0,8},{8,0},{16,24},{24,16},{1,9},{9,1},{17,25},{25,17},{2,10},{10... | collective-permute-start | bytes 393224 | tf_op jit(solution)/shard_map/ppermute | solution.py:118
  16.2 0.8 %collective-permute-done.5.refs_7_ = bf16[2,32,1024]{2,1,0:T(8,128)(2,1)S(1)} collective-permute-done((bf16[2,32,1024]{2,1,0:T(8,128)(2,1)S(1)}, bf16[2,32,1024]{2,1,0:T(8,128)(2,1)S(1)}, u32[]{:S(2)}, u32[]{:S(2)}) %collective-permute-start.5) | collective-permute-done | bytes 131104 | tf_op jit(solution)/shard_map/ppermute | solution.py:115
  17.0 0.0 collective-permute-start.9
  17.0 0.8 %collective-permute-done.1.refs_2_ = bf16[2,32,1024]{2,1,0:T(8,128)(2,1)S(1)} collective-permute-done((bf16[2,32,1024]{2,1,0:T(8,128)(2,1)S(1)}, bf16[2,32,1024]{2,1,0:T(8,128)(2,1)S(1)}, u32[]{:S(2)}, u32[]{:S(2)}) %collective-permute-start.1) | collective-permute-done | bytes 131104 | tf_op jit(solution)/shard_map/ppermute | solution.py:120
  17.8 1.4 %collective-permute-done.refs_1_ = bf16[2,32,1024]{2,1,0:T(8,128)(2,1)S(1)} collective-permute-done((bf16[2,32,1024]{2,1,0:T(8,128)(2,1)S(1)}, bf16[2,32,1024]{2,1,0:T(8,128)(2,1)S(1)}, u32[]{:S(2)}, u32[]{:S(2)}) %collective-permute-start) | collective-permute-done | bytes 131104 | tf_op jit(solution)/shard_map/ppermute | solution.py:120
  19.2 0.0 collective-permute-done.8.refs_10_
  19.2 0.0 collective-permute-done.7.refs_9_
  19.2 0.0 collective-permute-done.9.refs_11_
  19.2 0.0 copy-done
  19.2 1.8 %shard_map.50 = (f32[2,32,1024]{2,1,0:T(8,128)S(1)}, f32[32,128]{1,0:T(8,128)S(1)}, f32[2,32,1024]{2,1,0:T(8,128)S(1)}, f32[2,32,1024]{2,1,0:T(8,128)S(1)}, f32[2,32,1024]{2,1,0:T(8,128)S(1)}) custom-call(f32[2]{0:T(128)S(1)} %copy-done, bf16[2,32,1024]{2,1,0:T(8,128)(2,1)S(1)} %pad_maximum_fusion.refs_0_.refs_4_, ...), custom_call_target="tpu_custom_call" | custom-call | tf_op jit(solution)/shard_map/pallas_call | solution.py:95
  21.1 1.7 %collective-permute-start.12 = (f16[2,32,1024]{2,1,0:T(8,128)(2,1)S(1)}, f16[2,32,1024]{2,1,0:T(8,128)(2,1)S(1)}, u32[]{:S(2)}, u32[]{:S(2)}) collective-permute-start(f16[2,32,1024]{2,1,0:T(8,128)(2,1)S(1)} %convert_element_type.37), channel_id=1, source_target_pairs={{0,17},{1,16},{2,19},{3,18},{4,21},{5,20},{6,23},{7,22},{8,25},{9,... | collective-permute-start | bytes 393224 | tf_op jit(solution)/shard_map/ppermute | solution.py:124
  22.8 1.3 %collective-permute-start.11 = (f16[2,32,1024]{2,1,0:T(8,128)(2,1)S(1)}, f16[2,32,1024]{2,1,0:T(8,128)(2,1)S(1)}, u32[]{:S(2)}, u32[]{:S(2)}) collective-permute-start(f16[2,32,1024]{2,1,0:T(8,128)(2,1)S(1)} %convert_element_type.35), channel_id=1, source_target_pairs={{0,16},{1,17},{2,18},{3,19},{4,20},{5,21},{6,22},{7,23},{8,24},{9,... | collective-permute-start | bytes 393224 | tf_op jit(solution)/shard_map/ppermute | solution.py:124
  24.1 0.5 %collective-permute-start.10 = (f16[2,32,1024]{2,1,0:T(8,128)(2,1)S(1)}, f16[2,32,1024]{2,1,0:T(8,128)(2,1)S(1)}, u32[]{:S(2)}, u32[]{:S(2)}) collective-permute-start(f16[2,32,1024]{2,1,0:T(8,128)(2,1)S(1)} %convert_element_type.33), channel_id=1, source_target_pairs={{0,1},{1,0},{2,3},{3,2},{4,5},{5,4},{6,7},{7,6},{8,9},{9,8},{10,11... | collective-permute-start | bytes 393224 | tf_op jit(solution)/shard_map/ppermute | solution.py:124
  24.6 0.1 slice_reduce_fusion
  24.7 2.9 %collective-permute-done.12 = f16[2,32,1024]{2,1,0:T(8,128)(2,1)S(1)} collective-permute-done((f16[2,32,1024]{2,1,0:T(8,128)(2,1)S(1)}, f16[2,32,1024]{2,1,0:T(8,128)(2,1)S(1)}, u32[]{:S(2)}, u32[]{:S(2)}) %collective-permute-start.12) | collective-permute-done | bytes 131104 | tf_op jit(solution)/shard_map/ppermute | solution.py:124
  27.6 1.9 %collective-permute-done.11 = f16[2,32,1024]{2,1,0:T(8,128)(2,1)S(1)} collective-permute-done((f16[2,32,1024]{2,1,0:T(8,128)(2,1)S(1)}, f16[2,32,1024]{2,1,0:T(8,128)(2,1)S(1)}, u32[]{:S(2)}, u32[]{:S(2)}) %collective-permute-start.11) | collective-permute-done | bytes 131104 | tf_op jit(solution)/shard_map/ppermute | solution.py:124
  29.5 0.1 collective-permute-done.10
  29.7 0.8 %bitcast_multiply_fusion = (f32[32,1024]{1,0:T(8,128)}, f32[32,1024]{1,0:T(8,128)}) fusion(f32[2,32,1024]{2,1,0:T(8,128)S(1)} %get-tuple-element.7, f16[2,32,1024]{2,1,0:T(8,128)(2,1)S(1)} %collective-permute-done.12, f16[2,32,1024]{2,1,0:T(8,128)(2,1)S(1)} %collective-permute-done.11, f16[2,32,1024]{2,1,0:T(8,128)(2,1)S(1)} %collective-permute-done.10, ...), kind=kLoop, calls=%fused_computation.1 | loop fusion | flops 458752 | bytes 917632 | tf_op jit(solution)/shard_map/mul | solution.py:133
  (3 shorter events, 0.1 us)
Async XLA Ops:
  0.6 18.6 %copy-start = (f32[2]{0:T(128)S(1)}, f32[2]{0:T(128)}, u32[]{:S(2)}) copy-start(f32[2]{0:T(128)} %weights.1) | copy-start | bytes 28
  1.5 10.5 %collective-permute-start.3 = (bf16[2,32,1024]{2,1,0:T(8,128)(2,1)S(1)}, bf16[2,32,1024]{2,1,0:T(8,128)(2,1)S(1)}, u32[]{:S(2)}, u32[]{:S(2)}) collective-permute-start(bf16[2,32,1024]{2,1,0:T(8,128)(2,1)S(1)} %pad_maximum_fusion.refs_0_.refs_4_), channel_id=1, source_target_pairs={{0,4},{1,5},{2,6},{3,7},{4,0},{5,1},{6,2},{7,3},{8,12},{9,13},{10,... | collective-permute-start | bytes 393224 | tf_op jit(solution)/shard_map/ppermute | solution.py:115
  5.6 8.6 %collective-permute-start.6 = (bf16[2,32,1024]{2,1,0:T(8,128)(2,1)S(1)}, bf16[2,32,1024]{2,1,0:T(8,128)(2,1)S(1)}, u32[]{:S(2)}, u32[]{:S(2)}) collective-permute-start(bf16[2,32,1024]{2,1,0:T(8,128)(2,1)S(1)} %pad_maximum_fusion.refs_0_.refs_4_), channel_id=1, source_target_pairs={{0,8},{8,0},{16,24},{24,16},{1,9},{9,1},{17,25},{25,17},{2,10},{10... | collective-permute-start | bytes 393224 | tf_op jit(solution)/shard_map/ppermute | solution.py:118
  5.6 10.1 %collective-permute-start.4 = (bf16[2,32,1024]{2,1,0:T(8,128)(2,1)S(1)}, bf16[2,32,1024]{2,1,0:T(8,128)(2,1)S(1)}, u32[]{:S(2)}, u32[]{:S(2)}) collective-permute-start(bf16[2,32,1024]{2,1,0:T(8,128)(2,1)S(1)} %pad_maximum_fusion.refs_0_.refs_4_), channel_id=1, source_target_pairs={{0,2},{1,3},{2,0},{3,1},{4,6},{5,7},{6,4},{7,5},{8,10},{9,11},{10,... | collective-permute-start | bytes 393224 | tf_op jit(solution)/shard_map/ppermute | solution.py:115
  7.2 8.5 %collective-permute-start.2 = (bf16[2,32,1024]{2,1,0:T(8,128)(2,1)S(1)}, bf16[2,32,1024]{2,1,0:T(8,128)(2,1)S(1)}, u32[]{:S(2)}, u32[]{:S(2)}) collective-permute-start(bf16[2,32,1024]{2,1,0:T(8,128)(2,1)S(1)} %pad_maximum_fusion.refs_0_.refs_4_), channel_id=1, source_target_pairs={{0,17},{1,16},{2,19},{3,18},{4,21},{5,20},{6,23},{7,22},{8,25},{9,... | collective-permute-start | bytes 393224 | tf_op jit(solution)/shard_map/ppermute | solution.py:120
  12.0 5.0 %collective-permute-start.5 = (bf16[2,32,1024]{2,1,0:T(8,128)(2,1)S(1)}, bf16[2,32,1024]{2,1,0:T(8,128)(2,1)S(1)}, u32[]{:S(2)}, u32[]{:S(2)}) collective-permute-start(bf16[2,32,1024]{2,1,0:T(8,128)(2,1)S(1)} %collective-permute-done.3.refs_5_), channel_id=1, source_target_pairs={{0,2},{1,3},{2,0},{3,1},{4,6},{5,7},{6,4},{7,5},{8,10},{9,11},{10,... | collective-permute-start | bytes 393224 | tf_op jit(solution)/shard_map/ppermute | solution.py:115
  12.7 5.1 %collective-permute-start.1 = (bf16[2,32,1024]{2,1,0:T(8,128)(2,1)S(1)}, bf16[2,32,1024]{2,1,0:T(8,128)(2,1)S(1)}, u32[]{:S(2)}, u32[]{:S(2)}) collective-permute-start(bf16[2,32,1024]{2,1,0:T(8,128)(2,1)S(1)} %pad_maximum_fusion.refs_0_.refs_4_), channel_id=1, source_target_pairs={{0,16},{1,17},{2,18},{3,19},{4,20},{5,21},{6,22},{7,23},{8,24},{9,... | collective-permute-start | bytes 393224 | tf_op jit(solution)/shard_map/ppermute | solution.py:120
  14.2 5.0 %collective-permute-start = (bf16[2,32,1024]{2,1,0:T(8,128)(2,1)S(1)}, bf16[2,32,1024]{2,1,0:T(8,128)(2,1)S(1)}, u32[]{:S(2)}, u32[]{:S(2)}) collective-permute-start(bf16[2,32,1024]{2,1,0:T(8,128)(2,1)S(1)} %pad_maximum_fusion.refs_0_.refs_4_), channel_id=1, source_target_pairs={{0,1},{1,0},{2,3},{3,2},{4,5},{5,4},{6,7},{7,6},{8,9},{9,8},{10,11... | collective-permute-start | bytes 393224 | tf_op jit(solution)/shard_map/ppermute | solution.py:120
  15.7 3.5 %collective-permute-start.7 = (bf16[2,32,1024]{2,1,0:T(8,128)(2,1)S(1)}, bf16[2,32,1024]{2,1,0:T(8,128)(2,1)S(1)}, u32[]{:S(2)}, u32[]{:S(2)}) collective-permute-start(bf16[2,32,1024]{2,1,0:T(8,128)(2,1)S(1)} %collective-permute-done.3.refs_5_), channel_id=1, source_target_pairs={{0,8},{8,0},{16,24},{24,16},{1,9},{9,1},{17,25},{25,17},{2,10},{10... | collective-permute-start | bytes 393224 | tf_op jit(solution)/shard_map/ppermute | solution.py:118
  15.7 3.5 %collective-permute-start.8 = (bf16[2,32,1024]{2,1,0:T(8,128)(2,1)S(1)}, bf16[2,32,1024]{2,1,0:T(8,128)(2,1)S(1)}, u32[]{:S(2)}, u32[]{:S(2)}) collective-permute-start(bf16[2,32,1024]{2,1,0:T(8,128)(2,1)S(1)} %collective-permute-done.4.refs_6_), channel_id=1, source_target_pairs={{0,8},{8,0},{16,24},{24,16},{1,9},{9,1},{17,25},{25,17},{2,10},{10... | collective-permute-start | bytes 393224 | tf_op jit(solution)/shard_map/ppermute | solution.py:118
  17.0 2.2 %collective-permute-start.9 = (bf16[2,32,1024]{2,1,0:T(8,128)(2,1)S(1)}, bf16[2,32,1024]{2,1,0:T(8,128)(2,1)S(1)}, u32[]{:S(2)}, u32[]{:S(2)}) collective-permute-start(bf16[2,32,1024]{2,1,0:T(8,128)(2,1)S(1)} %collective-permute-done.5.refs_7_), channel_id=1, source_target_pairs={{0,8},{8,0},{16,24},{24,16},{1,9},{9,1},{17,25},{25,17},{2,10},{10... | collective-permute-start | bytes 393224 | tf_op jit(solution)/shard_map/ppermute | solution.py:118
  21.1 6.6 %collective-permute-start.12 = (f16[2,32,1024]{2,1,0:T(8,128)(2,1)S(1)}, f16[2,32,1024]{2,1,0:T(8,128)(2,1)S(1)}, u32[]{:S(2)}, u32[]{:S(2)}) collective-permute-start(f16[2,32,1024]{2,1,0:T(8,128)(2,1)S(1)} %convert_element_type.37), channel_id=1, source_target_pairs={{0,17},{1,16},{2,19},{3,18},{4,21},{5,20},{6,23},{7,22},{8,25},{9,... | collective-permute-start | bytes 393224 | tf_op jit(solution)/shard_map/ppermute | solution.py:124
  22.8 6.8 %collective-permute-start.11 = (f16[2,32,1024]{2,1,0:T(8,128)(2,1)S(1)}, f16[2,32,1024]{2,1,0:T(8,128)(2,1)S(1)}, u32[]{:S(2)}, u32[]{:S(2)}) collective-permute-start(f16[2,32,1024]{2,1,0:T(8,128)(2,1)S(1)} %convert_element_type.35), channel_id=1, source_target_pairs={{0,16},{1,17},{2,18},{3,19},{4,20},{5,21},{6,22},{7,23},{8,24},{9,... | collective-permute-start | bytes 393224 | tf_op jit(solution)/shard_map/ppermute | solution.py:124
  24.1 5.6 %collective-permute-start.10 = (f16[2,32,1024]{2,1,0:T(8,128)(2,1)S(1)}, f16[2,32,1024]{2,1,0:T(8,128)(2,1)S(1)}, u32[]{:S(2)}, u32[]{:S(2)}) collective-permute-start(f16[2,32,1024]{2,1,0:T(8,128)(2,1)S(1)} %convert_element_type.33), channel_id=1, source_target_pairs={{0,1},{1,0},{2,3},{3,2},{4,5},{5,4},{6,7},{7,6},{8,9},{9,8},{10,11... | collective-permute-start | bytes 393224 | tf_op jit(solution)/shard_map/ppermute | solution.py:124

commit v5 on v4

v5 whole, which is shorter than its diff:
```python
import functools
import math

import jax
import jax.numpy as jnp
from jax import lax
from jax.experimental import pallas as pl
from jax.experimental.pallas import tpu as pltpu
from jax.sharding import PartitionSpec as P

LIMIT = 6.0
TOP = 32768.0


def halves(count):
    inner = 2 if count % 2 == 0 else 1
    return count // inner, inner


def outer_moves(count):
    outer, inner = halves(count)

    def perm(to):
        return [(i, to(i // inner) * inner + i % inner) for i in range(count)]

    moves = []
    if outer & (outer - 1) == 0:
        held, stride = 1, outer // 2
        while stride:
            moves += [(b, perm(lambda o, s=stride: o ^ s)) for b in range(held)]
            held, stride = 2 * held, stride // 2
    else:
        moves = [(0, perm(lambda o, s=s: (o + s) % outer)) for s in range(1, outer)]
    return moves


def inner_shift(count, step):
    _, inner = halves(count)
    return [(i, i // inner * inner + (i + step) % inner) for i in range(count)]


def square_shift(n_row, n_col, j, k):
    r_outer, r_inner = halves(n_row)
    _, c_inner = halves(n_col)
    pairs = []
    for r in range(n_row):
        for c in range(n_col):
            to_r = (r // r_inner + j) % r_outer * r_inner + r % r_inner
            to_c = c // c_inner * c_inner + (c + k) % c_inner
            pairs.append((r * n_col + c, to_r * n_col + to_c))
    return pairs


def dot(a, b, dims):
    return lax.dot_general(a, b, (dims, ((), ())), preferred_element_type=jnp.float32)


def join(refs):
    return [jnp.concatenate([ref[s] for ref in refs], axis=0) for s in range(2)]


def products(img, txt, key_img, key_txt, weights, scale):
    n, m = img.shape[0], key_img.shape[0]
    scores = dot(jnp.concatenate([img, txt]), jnp.concatenate([key_img, key_txt]), ((1,), (1,)))
    cross = scores[:n, m:] - scores[n:, :m]
    inmodal = scores[:n, :m] - scores[n:, m:]
    p_mat = (cross * (weights[0] * scale)).astype(jnp.bfloat16)
    q_mat = (inmodal * (weights[1] * scale)).astype(jnp.bfloat16)
    both = jnp.concatenate([p_mat, q_mat], axis=1)
    nn = ((1,), (0,))
    grad_img = dot(both, jnp.concatenate([key_txt, key_img]), nn)
    grad_txt = dot(both, jnp.concatenate([key_img, key_txt]), nn)
    return grad_img, -grad_txt


def early_kernel(scale, total, n, weights, *refs):
    img, txt = join(refs[:n])
    key_img, key_txt = join(refs[n:-3])
    acc, up, down = refs[-3:]
    grad_img, grad_txt = products(img, txt, key_img, key_txt, weights, scale)
    acc[0] = grad_img
    acc[1] = grad_txt
    size = jnp.sum(jnp.abs(img.astype(jnp.float32)) + jnp.abs(txt.astype(jnp.float32)), axis=1, keepdims=True)
    most = size * ((weights[0] + weights[1]) * (1.02 * scale * LIMIT * LIMIT * total)) + 1e-30
    rows = down.shape[0]
    up[...] = jnp.broadcast_to(TOP / most, up.shape)
    down[...] = jnp.broadcast_to((most / TOP)[:rows], down.shape)


def late_kernel(scale, n, weights, *refs):
    img, txt = join(refs[:n])
    key_img, key_txt = join(refs[n : -n - 2])
    acc, up, *outs = refs[-n - 2 :]
    grad_img, grad_txt = products(img, txt, key_img, key_txt, weights, scale)
    factor = up[:, :1]
    grad_img, grad_txt = (grad_img + acc[0]) * factor, (grad_txt + acc[1]) * factor
    rows = outs[0].shape[1]
    for i, out in enumerate(outs):
        out[0] = grad_img[i * rows : (i + 1) * rows]
        out[1] = grad_txt[i * rows : (i + 1) * rows]


def call(kernel, weights, operands, out_shape, flops):
    vmem = pl.BlockSpec(memory_space=pltpu.VMEM)
    smem = pl.BlockSpec(memory_space=pltpu.SMEM)
    moved = sum(x.size * x.dtype.itemsize for x in [*operands, *out_shape])
    return pl.pallas_call(
        kernel,
        out_shape=out_shape,
        in_specs=[smem] + [vmem] * len(operands),
        out_specs=[vmem] * len(out_shape),
        compiler_params=pltpu.CompilerParams(vmem_limit_bytes=40 * 2**20),
        cost_estimate=pl.CostEstimate(flops=flops, bytes_accessed=moved, transcendentals=0),
    )(weights, *operands)


def local(images, texts, loss_weights):
    n_row, n_col = lax.axis_size("row"), lax.axis_size("col")
    row_inner = halves(n_row)[1]
    rows, width = images.shape
    batch = rows * n_row * n_col
    scale = 1.0 / math.sqrt(width * batch)
    both = ("row", "col")
    square = [(j, k) for j in range(halves(n_row)[0]) for k in range(halves(n_col)[1])][1:]
    own = jnp.stack([images, texts])

    mine = [own] + [lax.ppermute(own, both, square_shift(n_row, n_col, j, k)) for j, k in square]

    line = [own]
    for which, perm in outer_moves(n_col):
        line.append(lax.ppermute(line[which], "col", perm))

    def pair(block):
        return [lax.ppermute(block, "row", inner_shift(n_row, k)) for k in range(1, row_inner)]

    early, late = list(line), pair(line[-1])
    for i, block in enumerate(line[:-1]):
        if i < len(square):
            block, mine[i + 1] = lax.optimization_barrier((block, mine[i + 1]))
        early += pair(block)

    total = rows * len(line) * row_inner
    many = rows * len(mine)
    f32 = jnp.float32

    def flops(keys):
        return 16 * many * width * rows * len(keys)

    acc, up, down = call(
        functools.partial(early_kernel, scale, total, len(mine)),
        loss_weights,
        mine + early,
        [jax.ShapeDtypeStruct(s, f32) for s in [(2, many, width), (many, 128), (rows, 128)]],
        flops(early),
    )
    first, *parts = call(
        functools.partial(late_kernel, scale, len(mine)),
        loss_weights,
        mine + late + [acc, up],
        [jax.ShapeDtypeStruct((2, rows, width), f32)] * len(mine),
        flops(late),
    )
    back = [
        lax.ppermute(part.astype(jnp.float16), both, square_shift(n_row, n_col, -j, -k))
        for part, (j, k) in zip(parts, square)
    ]
    grads = []
    for s in range(2):
        total = first[s]
        for part in back:
            total = total + part[s].astype(f32)
        grads.append(total * down[:, :1])
    return tuple(grads)


def solution(mesh):
    in_specs = (P(("row", "col"), None), P(("row", "col"), None), P())
    out_specs = (P(("row", "col"), None), P(("row", "col"), None))
    return jax.shard_map(local, mesh=mesh, in_specs=in_specs, out_specs=out_specs, check_vma=False)
```

time: 30.6 us -> 31 us (1.013)
  starting transfers between devices: 15.9 us -> 14 us
  Pallas kernels: 1.76 us -> 3.04 us
  waiting for transfers between devices: 10.3 us -> 11.3 us
    ppermute x3, waiting for transfers between devices: 2.18 us -> 0.01 us  [local(): lax.ppermute(own, both, square_shift(n_row, n_col, j, k))]
    ppermute x3, waiting for transfers between devices: 3.16 us -> 5.23 us  [local(): line.append(lax.ppermute(line[which], 'col', perm))]
    ppermute x3, starting transfers between devices: 5.46 us -> 3.49 us  [local(): lax.ppermute(own, both, square_shift(n_row, n_col, j, k))]
    pallas_call x1 -> x2, Pallas kernels: 1.76 us -> 3.04 us  [call(): pl.pallas_call(kernel, out_shape=out_shape, in_specs=[smem] + [vmem] * le...]
    ppermute x3, waiting for transfers between devices: 4.94 us -> 6.01 us  [local(): lax.ppermute(part.astype(jnp.float16), both, square_shift(n_row, n_col, -...]
  transfers between devices with their start and end apart: 13 -> 13, of which waited for: 7 -> 5; matrix products, arithmetic and copies ran while one was open for 0% -> 0% of each run, Pallas kernels for 0% -> 5%
where the time goes in v5:
time: 31 us; the launch traced here: 30.8 us
  starting transfers between devices  14 us (45%)
  waiting for transfers between devices  11.3 us (36%)
  Pallas kernels  3.04 us (10%)
  other arithmetic  1.73 us (6%)
  between operations  0.72 us (2%)
    ppermute x3, starting transfers between devices, local(): line.append(lax.ppermute(line[which], 'col', perm))  6.34 us
    ppermute x3, waiting for transfers between devices, local(): lax.ppermute(part.astype(jnp.float16), both, square_shift(n_row, n_col, -...  6.01 us
    ppermute x3, waiting for transfers between devices, local(): line.append(lax.ppermute(line[which], 'col', perm))  5.23 us
    ppermute x3, starting transfers between devices, local(): lax.ppermute(part.astype(jnp.float16), both, square_shift(n_row, n_col, -...  3.55 us
    ppermute x3, starting transfers between devices, local(): lax.ppermute(own, both, square_shift(n_row, n_col, j, k))  3.49 us
    pallas_call x2, Pallas kernels, call(): pl.pallas_call(kernel, out_shape=out_shape, in_specs=[smem] + [vmem] * le...  3.04 us
    another operation x1, other arithmetic, local(): own = jnp.stack([images, texts])  0.89 us
    mul x1, other arithmetic, local(): grads.append(total * down[:, :1])  0.79 us
  transfers between devices with their start and end apart: 13, of which 5 were waited for; matrix products, arithmetic and copies ran while one was open for 0% of the time, Pallas kernels for 5%

profile of v5, /device:TPU:0, one launch (start us, length us, event | category | flops | bytes accessed | tf_op | source)
XLA Modules:
  0.0 30.8 jit_solution(9033192369621886262)
XLA Ops:
  0.6 0.0 copy-start
  0.6 0.9 %pad_maximum_fusion.refs_0_.refs_4_ = bf16[2,32,1024]{2,1,0:T(8,128)(2,1)S(1)} fusion(bf16[1,32,1024]{2,1,0:T(8,128)(2,1)} %bitcast.6, bf16[1,32,1024]{2,1,0:T(8,128)(2,1)} %bitcast.7), kind=kLoop, calls=%fused_computation | loop fusion | flops 65536 | bytes 262144 | tf_op jit(solution)/shard_map/stack | solution.py:125
  1.5 4.1 %collective-permute-start.1 = (bf16[2,32,1024]{2,1,0:T(8,128)(2,1)S(1)}, bf16[2,32,1024]{2,1,0:T(8,128)(2,1)S(1)}, u32[]{:S(2)}, u32[]{:S(2)}) collective-permute-start(bf16[2,32,1024]{2,1,0:T(8,128)(2,1)S(1)} %pad_maximum_fusion.refs_0_.refs_4_), channel_id=1, source_target_pairs={{0,4},{1,5},{2,6},{3,7},{4,0},{5,1},{6,2},{7,3},{8,12},{9,13},{10,... | collective-permute-start | bytes 393224 | tf_op jit(solution)/shard_map/ppermute | solution.py:131
  5.6 2.4 %collective-permute-start.4 = (bf16[2,32,1024]{2,1,0:T(8,128)(2,1)S(1)}, bf16[2,32,1024]{2,1,0:T(8,128)(2,1)S(1)}, u32[]{:S(2)}, u32[]{:S(2)}) collective-permute-start(bf16[2,32,1024]{2,1,0:T(8,128)(2,1)S(1)} %pad_maximum_fusion.refs_0_.refs_4_), channel_id=1, source_target_pairs={{0,17},{1,16},{2,19},{3,18},{4,21},{5,20},{6,23},{7,22},{8,25},{9,... | collective-permute-start | bytes 393224 | tf_op jit(solution)/shard_map/ppermute | solution.py:127
  8.1 1.6 %collective-permute-start.3 = (bf16[2,32,1024]{2,1,0:T(8,128)(2,1)S(1)}, bf16[2,32,1024]{2,1,0:T(8,128)(2,1)S(1)}, u32[]{:S(2)}, u32[]{:S(2)}) collective-permute-start(bf16[2,32,1024]{2,1,0:T(8,128)(2,1)S(1)} %pad_maximum_fusion.refs_0_.refs_4_), channel_id=1, source_target_pairs={{0,2},{1,3},{2,0},{3,1},{4,6},{5,7},{6,4},{7,5},{8,10},{9,11},{10,... | collective-permute-start | bytes 393224 | tf_op jit(solution)/shard_map/ppermute | solution.py:131
  9.7 0.5 %collective-permute-start.2 = (bf16[2,32,1024]{2,1,0:T(8,128)(2,1)S(1)}, bf16[2,32,1024]{2,1,0:T(8,128)(2,1)S(1)}, u32[]{:S(2)}, u32[]{:S(2)}) collective-permute-start(bf16[2,32,1024]{2,1,0:T(8,128)(2,1)S(1)} %pad_maximum_fusion.refs_0_.refs_4_), channel_id=1, source_target_pairs={{0,16},{1,17},{2,18},{3,19},{4,20},{5,21},{6,22},{7,23},{8,24},{9,... | collective-permute-start | bytes 393224 | tf_op jit(solution)/shard_map/ppermute | solution.py:127
  10.2 0.5 %collective-permute-start = (bf16[2,32,1024]{2,1,0:T(8,128)(2,1)S(1)}, bf16[2,32,1024]{2,1,0:T(8,128)(2,1)S(1)}, u32[]{:S(2)}, u32[]{:S(2)}) collective-permute-start(bf16[2,32,1024]{2,1,0:T(8,128)(2,1)S(1)} %pad_maximum_fusion.refs_0_.refs_4_), channel_id=1, source_target_pairs={{0,1},{1,0},{2,3},{3,2},{4,5},{5,4},{6,7},{7,6},{8,9},{9,8},{10,11... | collective-permute-start | bytes 393224 | tf_op jit(solution)/shard_map/ppermute | solution.py:127
  10.7 1.3 %collective-permute-done.1.refs_5_ = bf16[2,32,1024]{2,1,0:T(8,128)(2,1)S(1)} collective-permute-done((bf16[2,32,1024]{2,1,0:T(8,128)(2,1)S(1)}, bf16[2,32,1024]{2,1,0:T(8,128)(2,1)S(1)}, u32[]{:S(2)}, u32[]{:S(2)}) %collective-permute-start.1) | collective-permute-done | bytes 131104 | tf_op jit(solution)/shard_map/ppermute | solution.py:131
  12.0 0.7 %collective-permute-start.5 = (bf16[2,32,1024]{2,1,0:T(8,128)(2,1)S(1)}, bf16[2,32,1024]{2,1,0:T(8,128)(2,1)S(1)}, u32[]{:S(2)}, u32[]{:S(2)}) collective-permute-start(bf16[2,32,1024]{2,1,0:T(8,128)(2,1)S(1)} %collective-permute-done.1.refs_5_), channel_id=1, source_target_pairs={{0,2},{1,3},{2,0},{3,1},{4,6},{5,7},{6,4},{7,5},{8,10},{9,11},{10,... | collective-permute-start | bytes 393224 | tf_op jit(solution)/shard_map/ppermute | solution.py:131
  12.7 0.0 collective-permute-done.4.refs_3_
  12.7 2.2 %collective-permute-done.3.refs_6_ = bf16[2,32,1024]{2,1,0:T(8,128)(2,1)S(1)} collective-permute-done((bf16[2,32,1024]{2,1,0:T(8,128)(2,1)S(1)}, bf16[2,32,1024]{2,1,0:T(8,128)(2,1)S(1)}, u32[]{:S(2)}, u32[]{:S(2)}) %collective-permute-start.3) | collective-permute-done | bytes 131104 | tf_op jit(solution)/shard_map/ppermute | solution.py:131
  14.9 0.0 collective-permute-start.9
  14.9 0.0 collective-permute-done.2.refs_2_
  14.9 0.5 %collective-permute-start.8 = (bf16[2,32,1024]{2,1,0:T(8,128)(2,1)S(1)}, bf16[2,32,1024]{2,1,0:T(8,128)(2,1)S(1)}, u32[]{:S(2)}, u32[]{:S(2)}) collective-permute-start(bf16[2,32,1024]{2,1,0:T(8,128)(2,1)S(1)} %collective-permute-done.1.refs_5_), channel_id=1, source_target_pairs={{0,8},{8,0},{16,24},{24,16},{1,9},{9,1},{17,25},{25,17},{2,10},{10... | collective-permute-start | bytes 393224 | tf_op jit(solution)/shard_map/ppermute | solution.py:134
  15.4 0.0 collective-permute-done.refs_1_
  15.4 0.1 collective-permute-start.7
  15.5 1.7 %collective-permute-done.5.refs_7_ = bf16[2,32,1024]{2,1,0:T(8,128)(2,1)S(1)} collective-permute-done((bf16[2,32,1024]{2,1,0:T(8,128)(2,1)S(1)}, bf16[2,32,1024]{2,1,0:T(8,128)(2,1)S(1)}, u32[]{:S(2)}, u32[]{:S(2)}) %collective-permute-start.5) | collective-permute-done | bytes 131104 | tf_op jit(solution)/shard_map/ppermute | solution.py:131
  17.2 0.0 collective-permute-start.6
  17.2 0.0 collective-permute-done.9.refs_10_
  17.2 0.0 collective-permute-done.8.refs_9_
  17.2 0.0 collective-permute-done.7.refs_8_
  17.2 0.0 copy-done
  17.2 1.6 %shard_map.50 = (f32[2,128,1024]{2,1,0:T(8,128)S(1)}, f32[128,128]{1,0:T(8,128)S(1)}, f32[32,128]{1,0:T(8,128)S(1)}) custom-call(f32[2]{0:T(128)S(1)} %copy-done, bf16[2,32,1024]{2,1,0:T(8,128)(2,1)S(1)} %pad_maximum_fusion.refs_0_.refs_4_, bf16[2,32,1024]{2,1,0:T(8,128)(2,1)S(1)} %collective-permute-done.refs_1_, ...), custom_call_target="tpu_custom_call" | custom-call | flops 469762048 | bytes 2572288 | tf_op jit(solution)/shard_map/pallas_call | solution.py:107
  18.8 0.0 collective-permute-done.6.refs_4_
  18.8 1.4 %shard_map.51 = (f32[2,32,1024]{2,1,0:T(8,128)S(1)}, f32[2,32,1024]{2,1,0:T(8,128)S(1)}, f32[2,32,1024]{2,1,0:T(8,128)S(1)}, f32[2,32,1024]{2,1,0:T(8,128)S(1)}) custom-call(f32[2]{0:T(128)S(1)} %copy-done, bf16[2,32,1024]{2,1,0:T(8,128)(2,1)S(1)} %pad_maximum_fusion.refs_0_.refs_4_, bf16[2,32,1024]{2,1,0:T(8,128)(2,1)S(1)} %collective-permute-done.refs_1_, ...), custom_call_target="tpu_custom_call" | custom-call | flops 67108864 | bytes 2818048 | tf_op jit(solution)/shard_map/pallas_call | solution.py:107
  20.4 2.4 %collective-permute-start.12 = (f16[2,32,1024]{2,1,0:T(8,128)(2,1)S(1)}, f16[2,32,1024]{2,1,0:T(8,128)(2,1)S(1)}, u32[]{:S(2)}, u32[]{:S(2)}) collective-permute-start(f16[2,32,1024]{2,1,0:T(8,128)(2,1)S(1)} %convert_element_type.37), channel_id=1, source_target_pairs={{0,17},{1,16},{2,19},{3,18},{4,21},{5,20},{6,23},{7,22},{8,25},{9,... | collective-permute-start | bytes 393224 | tf_op jit(solution)/shard_map/ppermute | solution.py:164
  22.8 0.5 %collective-permute-start.11 = (f16[2,32,1024]{2,1,0:T(8,128)(2,1)S(1)}, f16[2,32,1024]{2,1,0:T(8,128)(2,1)S(1)}, u32[]{:S(2)}, u32[]{:S(2)}) collective-permute-start(f16[2,32,1024]{2,1,0:T(8,128)(2,1)S(1)} %convert_element_type.35), channel_id=1, source_target_pairs={{0,16},{1,17},{2,18},{3,19},{4,20},{5,21},{6,22},{7,23},{8,24},{9,... | collective-permute-start | bytes 393224 | tf_op jit(solution)/shard_map/ppermute | solution.py:164
  23.3 0.6 %collective-permute-start.10 = (f16[2,32,1024]{2,1,0:T(8,128)(2,1)S(1)}, f16[2,32,1024]{2,1,0:T(8,128)(2,1)S(1)}, u32[]{:S(2)}, u32[]{:S(2)}) collective-permute-start(f16[2,32,1024]{2,1,0:T(8,128)(2,1)S(1)} %convert_element_type.33), channel_id=1, source_target_pairs={{0,1},{1,0},{2,3},{3,2},{4,5},{5,4},{6,7},{7,6},{8,9},{9,8},{10,11... | collective-permute-start | bytes 393224 | tf_op jit(solution)/shard_map/ppermute | solution.py:164
  23.9 0.1 slice_reduce_fusion
  24.0 3.6 %collective-permute-done.12 = f16[2,32,1024]{2,1,0:T(8,128)(2,1)S(1)} collective-permute-done((f16[2,32,1024]{2,1,0:T(8,128)(2,1)S(1)}, f16[2,32,1024]{2,1,0:T(8,128)(2,1)S(1)}, u32[]{:S(2)}, u32[]{:S(2)}) %collective-permute-start.12) | collective-permute-done | bytes 131104 | tf_op jit(solution)/shard_map/ppermute | solution.py:164
  27.6 2.4 %collective-permute-done.11 = f16[2,32,1024]{2,1,0:T(8,128)(2,1)S(1)} collective-permute-done((f16[2,32,1024]{2,1,0:T(8,128)(2,1)S(1)}, f16[2,32,1024]{2,1,0:T(8,128)(2,1)S(1)}, u32[]{:S(2)}, u32[]{:S(2)}) %collective-permute-start.11) | collective-permute-done | bytes 131104 | tf_op jit(solution)/shard_map/ppermute | solution.py:164
  30.0 0.0 collective-permute-done.10
  30.0 0.8 %bitcast_multiply_fusion = (f32[32,1024]{1,0:T(8,128)}, f32[32,1024]{1,0:T(8,128)}) fusion(f32[2,32,1024]{2,1,0:T(8,128)S(1)} %get-tuple-element.23, f16[2,32,1024]{2,1,0:T(8,128)(2,1)S(1)} %collective-permute-done.12, f16[2,32,1024]{2,1,0:T(8,128)(2,1)S(1)} %collective-permute-done.11, f16[2,32,1024]{2,1,0:T(8,128)(2,1)S(1)} %collective-permute-done.10, ...), kind=kLoop, calls=%fused_computation.1 | loop fusion | flops 458752 | bytes 917632 | tf_op jit(solution)/shard_map/mul | solution.py:172
  (3 shorter events, 0.1 us)
Async XLA Ops:
  0.6 16.6 %copy-start = (f32[2]{0:T(128)S(1)}, f32[2]{0:T(128)}, u32[]{:S(2)}) copy-start(f32[2]{0:T(128)} %weights.3) | copy-start | bytes 28
  1.5 10.5 %collective-permute-start.1 = (bf16[2,32,1024]{2,1,0:T(8,128)(2,1)S(1)}, bf16[2,32,1024]{2,1,0:T(8,128)(2,1)S(1)}, u32[]{:S(2)}, u32[]{:S(2)}) collective-permute-start(bf16[2,32,1024]{2,1,0:T(8,128)(2,1)S(1)} %pad_maximum_fusion.refs_0_.refs_4_), channel_id=1, source_target_pairs={{0,4},{1,5},{2,6},{3,7},{4,0},{5,1},{6,2},{7,3},{8,12},{9,13},{10,... | collective-permute-start | bytes 393224 | tf_op jit(solution)/shard_map/ppermute | solution.py:131
  5.6 7.1 %collective-permute-start.4 = (bf16[2,32,1024]{2,1,0:T(8,128)(2,1)S(1)}, bf16[2,32,1024]{2,1,0:T(8,128)(2,1)S(1)}, u32[]{:S(2)}, u32[]{:S(2)}) collective-permute-start(bf16[2,32,1024]{2,1,0:T(8,128)(2,1)S(1)} %pad_maximum_fusion.refs_0_.refs_4_), channel_id=1, source_target_pairs={{0,17},{1,16},{2,19},{3,18},{4,21},{5,20},{6,23},{7,22},{8,25},{9,... | collective-permute-start | bytes 393224 | tf_op jit(solution)/shard_map/ppermute | solution.py:127
  8.1 6.8 %collective-permute-start.3 = (bf16[2,32,1024]{2,1,0:T(8,128)(2,1)S(1)}, bf16[2,32,1024]{2,1,0:T(8,128)(2,1)S(1)}, u32[]{:S(2)}, u32[]{:S(2)}) collective-permute-start(bf16[2,32,1024]{2,1,0:T(8,128)(2,1)S(1)} %pad_maximum_fusion.refs_0_.refs_4_), channel_id=1, source_target_pairs={{0,2},{1,3},{2,0},{3,1},{4,6},{5,7},{6,4},{7,5},{8,10},{9,11},{10,... | collective-permute-start | bytes 393224 | tf_op jit(solution)/shard_map/ppermute | solution.py:131
  9.7 5.3 %collective-permute-start.2 = (bf16[2,32,1024]{2,1,0:T(8,128)(2,1)S(1)}, bf16[2,32,1024]{2,1,0:T(8,128)(2,1)S(1)}, u32[]{:S(2)}, u32[]{:S(2)}) collective-permute-start(bf16[2,32,1024]{2,1,0:T(8,128)(2,1)S(1)} %pad_maximum_fusion.refs_0_.refs_4_), channel_id=1, source_target_pairs={{0,16},{1,17},{2,18},{3,19},{4,20},{5,21},{6,22},{7,23},{8,24},{9,... | collective-permute-start | bytes 393224 | tf_op jit(solution)/shard_map/ppermute | solution.py:127
  10.2 5.3 %collective-permute-start = (bf16[2,32,1024]{2,1,0:T(8,128)(2,1)S(1)}, bf16[2,32,1024]{2,1,0:T(8,128)(2,1)S(1)}, u32[]{:S(2)}, u32[]{:S(2)}) collective-permute-start(bf16[2,32,1024]{2,1,0:T(8,128)(2,1)S(1)} %pad_maximum_fusion.refs_0_.refs_4_), channel_id=1, source_target_pairs={{0,1},{1,0},{2,3},{3,2},{4,5},{5,4},{6,7},{7,6},{8,9},{9,8},{10,11... | collective-permute-start | bytes 393224 | tf_op jit(solution)/shard_map/ppermute | solution.py:127
  12.0 5.1 %collective-permute-start.5 = (bf16[2,32,1024]{2,1,0:T(8,128)(2,1)S(1)}, bf16[2,32,1024]{2,1,0:T(8,128)(2,1)S(1)}, u32[]{:S(2)}, u32[]{:S(2)}) collective-permute-start(bf16[2,32,1024]{2,1,0:T(8,128)(2,1)S(1)} %collective-permute-done.1.refs_5_), channel_id=1, source_target_pairs={{0,2},{1,3},{2,0},{3,1},{4,6},{5,7},{6,4},{7,5},{8,10},{9,11},{10,... | collective-permute-start | bytes 393224 | tf_op jit(solution)/shard_map/ppermute | solution.py:131
  14.9 2.3 %collective-permute-start.9 = (bf16[2,32,1024]{2,1,0:T(8,128)(2,1)S(1)}, bf16[2,32,1024]{2,1,0:T(8,128)(2,1)S(1)}, u32[]{:S(2)}, u32[]{:S(2)}) collective-permute-start(bf16[2,32,1024]{2,1,0:T(8,128)(2,1)S(1)} %collective-permute-done.3.refs_6_), channel_id=1, source_target_pairs={{0,8},{8,0},{16,24},{24,16},{1,9},{9,1},{17,25},{25,17},{2,10},{10... | collective-permute-start | bytes 393224 | tf_op jit(solution)/shard_map/ppermute | solution.py:134
  14.9 2.3 %collective-permute-start.8 = (bf16[2,32,1024]{2,1,0:T(8,128)(2,1)S(1)}, bf16[2,32,1024]{2,1,0:T(8,128)(2,1)S(1)}, u32[]{:S(2)}, u32[]{:S(2)}) collective-permute-start(bf16[2,32,1024]{2,1,0:T(8,128)(2,1)S(1)} %collective-permute-done.1.refs_5_), channel_id=1, source_target_pairs={{0,8},{8,0},{16,24},{24,16},{1,9},{9,1},{17,25},{25,17},{2,10},{10... | collective-permute-start | bytes 393224 | tf_op jit(solution)/shard_map/ppermute | solution.py:134
  15.4 1.8 %collective-permute-start.7 = (bf16[2,32,1024]{2,1,0:T(8,128)(2,1)S(1)}, bf16[2,32,1024]{2,1,0:T(8,128)(2,1)S(1)}, u32[]{:S(2)}, u32[]{:S(2)}) collective-permute-start(bf16[2,32,1024]{2,1,0:T(8,128)(2,1)S(1)} %pad_maximum_fusion.refs_0_.refs_4_), channel_id=1, source_target_pairs={{0,8},{8,0},{16,24},{24,16},{1,9},{9,1},{17,25},{25,17},{2,10},{10... | collective-permute-start | bytes 393224 | tf_op jit(solution)/shard_map/ppermute | solution.py:134
  17.2 1.6 %collective-permute-start.6 = (bf16[2,32,1024]{2,1,0:T(8,128)(2,1)S(1)}, bf16[2,32,1024]{2,1,0:T(8,128)(2,1)S(1)}, u32[]{:S(2)}, u32[]{:S(2)}) collective-permute-start(bf16[2,32,1024]{2,1,0:T(8,128)(2,1)S(1)} %collective-permute-done.5.refs_7_), channel_id=1, source_target_pairs={{0,8},{8,0},{16,24},{24,16},{1,9},{9,1},{17,25},{25,17},{2,10},{10... | collective-permute-start | bytes 393224 | tf_op jit(solution)/shard_map/ppermute | solution.py:134
  20.4 7.3 %collective-permute-start.12 = (f16[2,32,1024]{2,1,0:T(8,128)(2,1)S(1)}, f16[2,32,1024]{2,1,0:T(8,128)(2,1)S(1)}, u32[]{:S(2)}, u32[]{:S(2)}) collective-permute-start(f16[2,32,1024]{2,1,0:T(8,128)(2,1)S(1)} %convert_element_type.37), channel_id=1, source_target_pairs={{0,17},{1,16},{2,19},{3,18},{4,21},{5,20},{6,23},{7,22},{8,25},{9,... | collective-permute-start | bytes 393224 | tf_op jit(solution)/shard_map/ppermute | solution.py:164
  22.8 7.3 %collective-permute-start.11 = (f16[2,32,1024]{2,1,0:T(8,128)(2,1)S(1)}, f16[2,32,1024]{2,1,0:T(8,128)(2,1)S(1)}, u32[]{:S(2)}, u32[]{:S(2)}) collective-permute-start(f16[2,32,1024]{2,1,0:T(8,128)(2,1)S(1)} %convert_element_type.35), channel_id=1, source_target_pairs={{0,16},{1,17},{2,18},{3,19},{4,20},{5,21},{6,22},{7,23},{8,24},{9,... | collective-permute-start | bytes 393224 | tf_op jit(solution)/shard_map/ppermute | solution.py:164
  23.3 6.8 %collective-permute-start.10 = (f16[2,32,1024]{2,1,0:T(8,128)(2,1)S(1)}, f16[2,32,1024]{2,1,0:T(8,128)(2,1)S(1)}, u32[]{:S(2)}, u32[]{:S(2)}) collective-permute-start(f16[2,32,1024]{2,1,0:T(8,128)(2,1)S(1)} %convert_element_type.33), channel_id=1, source_target_pairs={{0,1},{1,0},{2,3},{3,2},{4,5},{5,4},{6,7},{7,6},{8,9},{9,8},{10,11... | collective-permute-start | bytes 393224 | tf_op jit(solution)/shard_map/ppermute | solution.py:164

commit v6 on v5

--- a/solution.py
+++ b/solution.py
@@ -56,48 +56,58 @@
 
 
 def join(refs):
-    return [jnp.concatenate([ref[s] for ref in refs], axis=0) for s in range(2)]
+    return jnp.concatenate([ref[s] for s in range(2) for ref in refs], axis=0)
 
 
-def products(img, txt, key_img, key_txt, weights, scale):
-    n, m = img.shape[0], key_img.shape[0]
-    scores = dot(jnp.concatenate([img, txt]), jnp.concatenate([key_img, key_txt]), ((1,), (1,)))
+def weigh(rows, keys, weights, scale):
+    n, m = rows.shape[0] // 2, keys.shape[0] // 2
+    scores = dot(rows, keys, ((1,), (1,)))
     cross = scores[:n, m:] - scores[n:, :m]
     inmodal = scores[:n, :m] - scores[n:, m:]
     p_mat = (cross * (weights[0] * scale)).astype(jnp.bfloat16)
     q_mat = (inmodal * (weights[1] * scale)).astype(jnp.bfloat16)
-    both = jnp.concatenate([p_mat, q_mat], axis=1)
+    return p_mat, q_mat
+
+
+def tiles(width):
+    step = 256 if width % 256 == 0 else width
+    return [slice(i, i + step) for i in range(0, width, step)]
+
+
+def tile_grads(p_mat, q_mat, keys, at):
+    m = keys.shape[0] // 2
+    img, txt = keys[:m, at], keys[m:, at]
     nn = ((1,), (0,))
-    grad_img = dot(both, jnp.concatenate([key_txt, key_img]), nn)
-    grad_txt = dot(both, jnp.concatenate([key_img, key_txt]), nn)
-    return grad_img, -grad_txt
+    grad_img = dot(jnp.concatenate([q_mat, p_mat], axis=1), jnp.concatenate([img, txt]), nn)
+    grad_txt = dot(jnp.concatenate([-p_mat, -q_mat], axis=1), jnp.concatenate([img, txt]), nn)
+    return grad_img, grad_txt
 
 
 def early_kernel(scale, total, n, weights, *refs):
-    img, txt = join(refs[:n])
-    key_img, key_txt = join(refs[n:-3])
-    acc, up, down = refs[-3:]
-    grad_img, grad_txt = products(img, txt, key_img, key_txt, weights, scale)
-    acc[0] = grad_img
-    acc[1] = grad_txt
-    size = jnp.sum(jnp.abs(img.astype(jnp.float32)) + jnp.abs(txt.astype(jnp.float32)), axis=1, keepdims=True)
+    own, acc, up, down = refs[-4:]
+    rows = join(refs[:n])
+    own[...] = rows
+    keys = join(refs[n:-4])
+    p_mat, q_mat = weigh(rows, keys, weights, scale)
+    for at in tiles(keys.shape[1]):
+        acc[0, :, at], acc[1, :, at] = tile_grads(p_mat, q_mat, keys, at)
+    size = jnp.sum(jnp.abs(rows.astype(jnp.float32)), axis=1, keepdims=True)
+    size = size[: size.shape[0] // 2] + size[size.shape[0] // 2 :]
     most = size * ((weights[0] + weights[1]) * (1.02 * scale * LIMIT * LIMIT * total)) + 1e-30
-    rows = down.shape[0]
     up[...] = jnp.broadcast_to(TOP / most, up.shape)
-    down[...] = jnp.broadcast_to((most / TOP)[:rows], down.shape)
+    down[...] = jnp.broadcast_to((most / TOP)[: down.shape[0]], down.shape)
 
 
-def late_kernel(scale, n, weights, *refs):
-    img, txt = join(refs[:n])
-    key_img, key_txt = join(refs[n : -n - 2])
-    acc, up, *outs = refs[-n - 2 :]
-    grad_img, grad_txt = products(img, txt, key_img, key_txt, weights, scale)
-    factor = up[:, :1]
-    grad_img, grad_txt = (grad_img + acc[0]) * factor, (grad_txt + acc[1]) * factor
+def late_kernel(scale, n, weights, own, acc, up, *refs):
+    outs = refs[-n:]
+    keys = join(refs[:-n])
+    p_mat, q_mat = weigh(own[...], keys, weights, scale)
     rows = outs[0].shape[1]
-    for i, out in enumerate(outs):
-        out[0] = grad_img[i * rows : (i + 1) * rows]
-        out[1] = grad_txt[i * rows : (i + 1) * rows]
+    for at in tiles(keys.shape[1]):
+        for s, grad in enumerate(tile_grads(p_mat, q_mat, keys, at)):
+            grad = (grad + acc[s, :, at]) * up[:, :1]
+            for i, out in enumerate(outs):
+                out[s, :, at] = grad[i * rows : (i + 1) * rows]
 
 
 def call(kernel, weights, operands, out_shape, flops):
@@ -133,12 +143,7 @@
     def pair(block):
         return [lax.ppermute(block, "row", inner_shift(n_row, k)) for k in range(1, row_inner)]
 
-    early, late = list(line), pair(line[-1])
-    for i, block in enumerate(line[:-1]):
-        if i < len(square):
-            block, mine[i + 1] = lax.optimization_barrier((block, mine[i + 1]))
-        early += pair(block)
-
+    early, copies = line[:-1], [copy for block in line[:-1] for copy in pair(block)]
     total = rows * len(line) * row_inner
     many = rows * len(mine)
     f32 = jnp.float32
@@ -146,17 +151,20 @@
     def flops(keys):
         return 16 * many * width * rows * len(keys)
 
-    acc, up, down = call(
+    joined, acc, up, down = call(
         functools.partial(early_kernel, scale, total, len(mine)),
         loss_weights,
         mine + early,
-        [jax.ShapeDtypeStruct(s, f32) for s in [(2, many, width), (many, 128), (rows, 128)]],
+        [jax.ShapeDtypeStruct((2 * many, width), images.dtype)]
+        + [jax.ShapeDtypeStruct(s, f32) for s in [(2, many, width), (many, 128), (rows, 128)]],
         flops(early),
     )
+    last, acc = lax.optimization_barrier((line[-1], acc))
+    late = copies + [last] + pair(last)
     first, *parts = call(
         functools.partial(late_kernel, scale, len(mine)),
         loss_weights,
-        mine + late + [acc, up],
+        [joined, acc, up] + late,
         [jax.ShapeDtypeStruct((2, rows, width), f32)] * len(mine),
         flops(late),
     )

time: 31 us -> 30.8 us (level)
    ppermute x3, waiting for transfers between devices: 5.23 us -> 1.35 us  [local(): line.append(lax.ppermute(line[which], 'col', perm))]
    ppermute x3, waiting for transfers between devices: 0.01 us -> 3.01 us  [local(): lax.ppermute(own, both, square_shift(n_row, n_col, j, k))]
    ppermute x4, waiting for transfers between devices: 0.01 us -> 0.98 us  [pair(): lax.ppermute(block, 'row', inner_shift(n_row, k))]
  transfers between devices with their start and end apart: 13 -> 13, of which waited for: 5 -> 8; matrix products, arithmetic and copies ran while one was open for 0% -> 0% of each run, Pallas kernels for 5% -> 5%
where the time goes in v6:
time: 30.8 us; the launch traced here: 30.6 us
  starting transfers between devices  13.8 us (45%)
  waiting for transfers between devices  11.3 us (37%)
  Pallas kernels  2.95 us (10%)
  other arithmetic  1.73 us (6%)
  between operations  0.7 us (2%)
    ppermute x3, starting transfers between devices, local(): line.append(lax.ppermute(line[which], 'col', perm))  6.29 us
    ppermute x3, waiting for transfers between devices, local(): lax.ppermute(part.astype(jnp.float16), both, square_shift(n_row, n_col, -...  5.96 us
    ppermute x3, starting transfers between devices, local(): lax.ppermute(part.astype(jnp.float16), both, square_shift(n_row, n_col, -...  3.57 us
    ppermute x3, starting transfers between devices, local(): lax.ppermute(own, both, square_shift(n_row, n_col, j, k))  3.49 us
    ppermute x3, waiting for transfers between devices, local(): lax.ppermute(own, both, square_shift(n_row, n_col, j, k))  3.01 us
    pallas_call x2, Pallas kernels, call(): pl.pallas_call(kernel, out_shape=out_shape, in_specs=[smem] + [vmem] * le...  2.95 us
    ppermute x3, waiting for transfers between devices, local(): line.append(lax.ppermute(line[which], 'col', perm))  1.35 us
    ppermute x4, waiting for transfers between devices, pair(): lax.ppermute(block, 'row', inner_shift(n_row, k))  0.98 us
  transfers between devices with their start and end apart: 13, of which 8 were waited for; matrix products, arithmetic and copies ran while one was open for 0% of the time, Pallas kernels for 5%

profile of v6, /device:TPU:0, one launch (start us, length us, event | category | flops | bytes accessed | tf_op | source)
XLA Modules:
  0.0 30.6 jit_solution(17515595910269921724)
XLA Ops:
  0.6 0.0 copy-start
  0.6 0.9 %pad_maximum_fusion.refs_0_.refs_4_ = bf16[2,32,1024]{2,1,0:T(8,128)(2,1)S(1)} fusion(bf16[1,32,1024]{2,1,0:T(8,128)(2,1)} %bitcast.6, bf16[1,32,1024]{2,1,0:T(8,128)(2,1)} %bitcast.7), kind=kLoop, calls=%fused_computation | loop fusion | flops 65536 | bytes 262144 | tf_op jit(solution)/shard_map/stack | solution.py:135
  1.5 4.1 %collective-permute-start.3 = (bf16[2,32,1024]{2,1,0:T(8,128)(2,1)S(1)}, bf16[2,32,1024]{2,1,0:T(8,128)(2,1)S(1)}, u32[]{:S(2)}, u32[]{:S(2)}) collective-permute-start(bf16[2,32,1024]{2,1,0:T(8,128)(2,1)S(1)} %pad_maximum_fusion.refs_0_.refs_4_), channel_id=1, source_target_pairs={{0,4},{1,5},{2,6},{3,7},{4,0},{5,1},{6,2},{7,3},{8,12},{9,13},{10,... | collective-permute-start | bytes 393224 | tf_op jit(solution)/shard_map/ppermute | solution.py:141
  5.6 1.6 %collective-permute-start.4 = (bf16[2,32,1024]{2,1,0:T(8,128)(2,1)S(1)}, bf16[2,32,1024]{2,1,0:T(8,128)(2,1)S(1)}, u32[]{:S(2)}, u32[]{:S(2)}) collective-permute-start(bf16[2,32,1024]{2,1,0:T(8,128)(2,1)S(1)} %pad_maximum_fusion.refs_0_.refs_4_), channel_id=1, source_target_pairs={{0,2},{1,3},{2,0},{3,1},{4,6},{5,7},{6,4},{7,5},{8,10},{9,11},{10,... | collective-permute-start | bytes 393224 | tf_op jit(solution)/shard_map/ppermute | solution.py:141
  7.2 2.4 %collective-permute-start.2 = (bf16[2,32,1024]{2,1,0:T(8,128)(2,1)S(1)}, bf16[2,32,1024]{2,1,0:T(8,128)(2,1)S(1)}, u32[]{:S(2)}, u32[]{:S(2)}) collective-permute-start(bf16[2,32,1024]{2,1,0:T(8,128)(2,1)S(1)} %pad_maximum_fusion.refs_0_.refs_4_), channel_id=1, source_target_pairs={{0,17},{1,16},{2,19},{3,18},{4,21},{5,20},{6,23},{7,22},{8,25},{9,... | collective-permute-start | bytes 393224 | tf_op jit(solution)/shard_map/ppermute | solution.py:137
  9.7 0.5 %collective-permute-start.1 = (bf16[2,32,1024]{2,1,0:T(8,128)(2,1)S(1)}, bf16[2,32,1024]{2,1,0:T(8,128)(2,1)S(1)}, u32[]{:S(2)}, u32[]{:S(2)}) collective-permute-start(bf16[2,32,1024]{2,1,0:T(8,128)(2,1)S(1)} %pad_maximum_fusion.refs_0_.refs_4_), channel_id=1, source_target_pairs={{0,16},{1,17},{2,18},{3,19},{4,20},{5,21},{6,22},{7,23},{8,24},{9,... | collective-permute-start | bytes 393224 | tf_op jit(solution)/shard_map/ppermute | solution.py:137
  10.2 0.5 %collective-permute-start = (bf16[2,32,1024]{2,1,0:T(8,128)(2,1)S(1)}, bf16[2,32,1024]{2,1,0:T(8,128)(2,1)S(1)}, u32[]{:S(2)}, u32[]{:S(2)}) collective-permute-start(bf16[2,32,1024]{2,1,0:T(8,128)(2,1)S(1)} %pad_maximum_fusion.refs_0_.refs_4_), channel_id=1, source_target_pairs={{0,1},{1,0},{2,3},{3,2},{4,5},{5,4},{6,7},{7,6},{8,9},{9,8},{10,11... | collective-permute-start | bytes 393224 | tf_op jit(solution)/shard_map/ppermute | solution.py:137
  10.7 1.3 %collective-permute-done.3.refs_5_ = bf16[2,32,1024]{2,1,0:T(8,128)(2,1)S(1)} collective-permute-done((bf16[2,32,1024]{2,1,0:T(8,128)(2,1)S(1)}, bf16[2,32,1024]{2,1,0:T(8,128)(2,1)S(1)}, u32[]{:S(2)}, u32[]{:S(2)}) %collective-permute-start.3) | collective-permute-done | bytes 131104 | tf_op jit(solution)/shard_map/ppermute | solution.py:141
  12.0 0.6 %collective-permute-start.5 = (bf16[2,32,1024]{2,1,0:T(8,128)(2,1)S(1)}, bf16[2,32,1024]{2,1,0:T(8,128)(2,1)S(1)}, u32[]{:S(2)}, u32[]{:S(2)}) collective-permute-start(bf16[2,32,1024]{2,1,0:T(8,128)(2,1)S(1)} %collective-permute-done.3.refs_5_), channel_id=1, source_target_pairs={{0,2},{1,3},{2,0},{3,1},{4,6},{5,7},{6,4},{7,5},{8,10},{9,11},{10,... | collective-permute-start | bytes 393224 | tf_op jit(solution)/shard_map/ppermute | solution.py:141
  12.7 0.0 collective-permute-done.4.refs_6_
  12.7 0.0 collective-permute-start.6
  12.7 1.1 %collective-permute-done.2.refs_3_ = bf16[2,32,1024]{2,1,0:T(8,128)(2,1)S(1)} collective-permute-done((bf16[2,32,1024]{2,1,0:T(8,128)(2,1)S(1)}, bf16[2,32,1024]{2,1,0:T(8,128)(2,1)S(1)}, u32[]{:S(2)}, u32[]{:S(2)}) %collective-permute-start.2) | collective-permute-done | bytes 131104 | tf_op jit(solution)/shard_map/ppermute | solution.py:137
  13.8 0.0 collective-permute-start.7
  13.8 1.8 %collective-permute-done.1.refs_2_ = bf16[2,32,1024]{2,1,0:T(8,128)(2,1)S(1)} collective-permute-done((bf16[2,32,1024]{2,1,0:T(8,128)(2,1)S(1)}, bf16[2,32,1024]{2,1,0:T(8,128)(2,1)S(1)}, u32[]{:S(2)}, u32[]{:S(2)}) %collective-permute-start.1) | collective-permute-done | bytes 131104 | tf_op jit(solution)/shard_map/ppermute | solution.py:137
  15.6 0.0 collective-permute-start.8
  15.6 0.1 collective-permute-done.refs_1_
  15.7 0.0 copy-done
  15.7 1.5 %shard_map.50 = (bf16[256,1024]{1,0:T(8,128)(2,1)S(1)}, f32[2,128,1024]{2,1,0:T(8,128)S(1)}, f32[128,128]{1,0:T(8,128)S(1)}, f32[32,128]{1,0:T(8,128)S(1)}) custom-call(f32[2]{0:T(128)S(1)} %copy-done, bf16[2,32,1024]{2,1,0:T(8,128)(2,1)S(1)} %pad_maximum_fusion.refs_0_.refs_4_, bf16[2,32,1024]{2,1,0:T(8,128)(2,1)S(1)} %collective-permute-done.refs_1_, ...), custom_call_target="tpu_custom_call" | custom-call | flops 201326592 | bytes 2572288 | tf_op jit(solution)/shard_map/pallas_call | solution.py:117
  17.1 0.0 collective-permute-done.5.refs_3_
  17.2 0.5 %collective-permute-start.9 = (bf16[2,32,1024]{2,1,0:T(8,128)(2,1)S(1)}, bf16[2,32,1024]{2,1,0:T(8,128)(2,1)S(1)}, u32[]{:S(2)}, u32[]{:S(2)}) collective-permute-start(bf16[2,32,1024]{2,1,0:T(8,128)(2,1)S(1)} %collective-permute-done.5.refs_3_), channel_id=1, source_target_pairs={{0,8},{8,0},{16,24},{24,16},{1,9},{9,1},{17,25},{25,17},{2,10},{10... | collective-permute-start | bytes 393224 | tf_op jit(solution)/shard_map/ppermute | solution.py:144
  17.6 0.0 collective-permute-done.6.refs_0_
  17.7 0.0 collective-permute-done.8.refs_2_
  17.7 0.0 collective-permute-done.7.refs_1_
  17.7 1.0 %collective-permute-done.9.refs_4_ = bf16[2,32,1024]{2,1,0:T(8,128)(2,1)S(1)} collective-permute-done((bf16[2,32,1024]{2,1,0:T(8,128)(2,1)S(1)}, bf16[2,32,1024]{2,1,0:T(8,128)(2,1)S(1)}, u32[]{:S(2)}, u32[]{:S(2)}) %collective-permute-start.9) | collective-permute-done | bytes 131104 | tf_op jit(solution)/shard_map/ppermute | solution.py:144
  18.6 1.5 %shard_map.51 = (f32[2,32,1024]{2,1,0:T(8,128)S(1)}, f32[2,32,1024]{2,1,0:T(8,128)S(1)}, f32[2,32,1024]{2,1,0:T(8,128)S(1)}, f32[2,32,1024]{2,1,0:T(8,128)S(1)}) custom-call(f32[2]{0:T(128)S(1)} %copy-done, bf16[256,1024]{1,0:T(8,128)(2,1)S(1)} %get-tuple-element.12.own, f32[2,128,1024]{2,1,0:T(8,128)S(1)} %get-tuple-element.14.acc, ...), custom_call_target="tpu_custom_call" | custom-call | flops 335544320 | bytes 3342336 | tf_op jit(solution)/shard_map/pallas_call | solution.py:117
  20.2 2.3 %collective-permute-start.12 = (f16[2,32,1024]{2,1,0:T(8,128)(2,1)S(1)}, f16[2,32,1024]{2,1,0:T(8,128)(2,1)S(1)}, u32[]{:S(2)}, u32[]{:S(2)}) collective-permute-start(f16[2,32,1024]{2,1,0:T(8,128)(2,1)S(1)} %convert_element_type.37), channel_id=1, source_target_pairs={{0,17},{1,16},{2,19},{3,18},{4,21},{5,20},{6,23},{7,22},{8,25},{9,... | collective-permute-start | bytes 393224 | tf_op jit(solution)/shard_map/ppermute | solution.py:172
  22.5 0.7 %collective-permute-start.11 = (f16[2,32,1024]{2,1,0:T(8,128)(2,1)S(1)}, f16[2,32,1024]{2,1,0:T(8,128)(2,1)S(1)}, u32[]{:S(2)}, u32[]{:S(2)}) collective-permute-start(f16[2,32,1024]{2,1,0:T(8,128)(2,1)S(1)} %convert_element_type.35), channel_id=1, source_target_pairs={{0,16},{1,17},{2,18},{3,19},{4,20},{5,21},{6,22},{7,23},{8,24},{9,... | collective-permute-start | bytes 393224 | tf_op jit(solution)/shard_map/ppermute | solution.py:172
  23.2 0.5 %collective-permute-start.10 = (f16[2,32,1024]{2,1,0:T(8,128)(2,1)S(1)}, f16[2,32,1024]{2,1,0:T(8,128)(2,1)S(1)}, u32[]{:S(2)}, u32[]{:S(2)}) collective-permute-start(f16[2,32,1024]{2,1,0:T(8,128)(2,1)S(1)} %convert_element_type.33), channel_id=1, source_target_pairs={{0,1},{1,0},{2,3},{3,2},{4,5},{5,4},{6,7},{7,6},{8,9},{9,8},{10,11... | collective-permute-start | bytes 393224 | tf_op jit(solution)/shard_map/ppermute | solution.py:172
  23.8 0.1 slice_reduce_fusion
  23.9 3.6 %collective-permute-done.12 = f16[2,32,1024]{2,1,0:T(8,128)(2,1)S(1)} collective-permute-done((f16[2,32,1024]{2,1,0:T(8,128)(2,1)S(1)}, f16[2,32,1024]{2,1,0:T(8,128)(2,1)S(1)}, u32[]{:S(2)}, u32[]{:S(2)}) %collective-permute-start.12) | collective-permute-done | bytes 131104 | tf_op jit(solution)/shard_map/ppermute | solution.py:172
  27.5 2.2 %collective-permute-done.11 = f16[2,32,1024]{2,1,0:T(8,128)(2,1)S(1)} collective-permute-done((f16[2,32,1024]{2,1,0:T(8,128)(2,1)S(1)}, f16[2,32,1024]{2,1,0:T(8,128)(2,1)S(1)}, u32[]{:S(2)}, u32[]{:S(2)}) %collective-permute-start.11) | collective-permute-done | bytes 131104 | tf_op jit(solution)/shard_map/ppermute | solution.py:172
  29.8 0.1 collective-permute-done.10
  29.9 0.8 %bitcast_multiply_fusion = (f32[32,1024]{1,0:T(8,128)}, f32[32,1024]{1,0:T(8,128)}) fusion(f32[2,32,1024]{2,1,0:T(8,128)S(1)} %get-tuple-element.17, f16[2,32,1024]{2,1,0:T(8,128)(2,1)S(1)} %collective-permute-done.12, f16[2,32,1024]{2,1,0:T(8,128)(2,1)S(1)} %collective-permute-done.11, f16[2,32,1024]{2,1,0:T(8,128)(2,1)S(1)} %collective-permute-done.10, ...), kind=kLoop, calls=%fused_computation.1 | loop fusion | flops 458752 | bytes 917632 | tf_op jit(solution)/shard_map/mul | solution.py:180
  (3 shorter events, 0.1 us)
Async XLA Ops:
  0.6 15.1 %copy-start = (f32[2]{0:T(128)S(1)}, f32[2]{0:T(128)}, u32[]{:S(2)}) copy-start(f32[2]{0:T(128)} %weights.3) | copy-start | bytes 28
  1.5 10.5 %collective-permute-start.3 = (bf16[2,32,1024]{2,1,0:T(8,128)(2,1)S(1)}, bf16[2,32,1024]{2,1,0:T(8,128)(2,1)S(1)}, u32[]{:S(2)}, u32[]{:S(2)}) collective-permute-start(bf16[2,32,1024]{2,1,0:T(8,128)(2,1)S(1)} %pad_maximum_fusion.refs_0_.refs_4_), channel_id=1, source_target_pairs={{0,4},{1,5},{2,6},{3,7},{4,0},{5,1},{6,2},{7,3},{8,12},{9,13},{10,... | collective-permute-start | bytes 393224 | tf_op jit(solution)/shard_map/ppermute | solution.py:141
  5.6 7.0 %collective-permute-start.4 = (bf16[2,32,1024]{2,1,0:T(8,128)(2,1)S(1)}, bf16[2,32,1024]{2,1,0:T(8,128)(2,1)S(1)}, u32[]{:S(2)}, u32[]{:S(2)}) collective-permute-start(bf16[2,32,1024]{2,1,0:T(8,128)(2,1)S(1)} %pad_maximum_fusion.refs_0_.refs_4_), channel_id=1, source_target_pairs={{0,2},{1,3},{2,0},{3,1},{4,6},{5,7},{6,4},{7,5},{8,10},{9,11},{10,... | collective-permute-start | bytes 393224 | tf_op jit(solution)/shard_map/ppermute | solution.py:141
  7.2 6.6 %collective-permute-start.2 = (bf16[2,32,1024]{2,1,0:T(8,128)(2,1)S(1)}, bf16[2,32,1024]{2,1,0:T(8,128)(2,1)S(1)}, u32[]{:S(2)}, u32[]{:S(2)}) collective-permute-start(bf16[2,32,1024]{2,1,0:T(8,128)(2,1)S(1)} %pad_maximum_fusion.refs_0_.refs_4_), channel_id=1, source_target_pairs={{0,17},{1,16},{2,19},{3,18},{4,21},{5,20},{6,23},{7,22},{8,25},{9,... | collective-permute-start | bytes 393224 | tf_op jit(solution)/shard_map/ppermute | solution.py:137
  9.7 5.9 %collective-permute-start.1 = (bf16[2,32,1024]{2,1,0:T(8,128)(2,1)S(1)}, bf16[2,32,1024]{2,1,0:T(8,128)(2,1)S(1)}, u32[]{:S(2)}, u32[]{:S(2)}) collective-permute-start(bf16[2,32,1024]{2,1,0:T(8,128)(2,1)S(1)} %pad_maximum_fusion.refs_0_.refs_4_), channel_id=1, source_target_pairs={{0,16},{1,17},{2,18},{3,19},{4,20},{5,21},{6,22},{7,23},{8,24},{9,... | collective-permute-start | bytes 393224 | tf_op jit(solution)/shard_map/ppermute | solution.py:137
  10.2 5.5 %collective-permute-start = (bf16[2,32,1024]{2,1,0:T(8,128)(2,1)S(1)}, bf16[2,32,1024]{2,1,0:T(8,128)(2,1)S(1)}, u32[]{:S(2)}, u32[]{:S(2)}) collective-permute-start(bf16[2,32,1024]{2,1,0:T(8,128)(2,1)S(1)} %pad_maximum_fusion.refs_0_.refs_4_), channel_id=1, source_target_pairs={{0,1},{1,0},{2,3},{3,2},{4,5},{5,4},{6,7},{7,6},{8,9},{9,8},{10,11... | collective-permute-start | bytes 393224 | tf_op jit(solution)/shard_map/ppermute | solution.py:137
  12.0 5.1 %collective-permute-start.5 = (bf16[2,32,1024]{2,1,0:T(8,128)(2,1)S(1)}, bf16[2,32,1024]{2,1,0:T(8,128)(2,1)S(1)}, u32[]{:S(2)}, u32[]{:S(2)}) collective-permute-start(bf16[2,32,1024]{2,1,0:T(8,128)(2,1)S(1)} %collective-permute-done.3.refs_5_), channel_id=1, source_target_pairs={{0,2},{1,3},{2,0},{3,1},{4,6},{5,7},{6,4},{7,5},{8,10},{9,11},{10,... | collective-permute-start | bytes 393224 | tf_op jit(solution)/shard_map/ppermute | solution.py:141
  12.7 5.0 %collective-permute-start.6 = (bf16[2,32,1024]{2,1,0:T(8,128)(2,1)S(1)}, bf16[2,32,1024]{2,1,0:T(8,128)(2,1)S(1)}, u32[]{:S(2)}, u32[]{:S(2)}) collective-permute-start(bf16[2,32,1024]{2,1,0:T(8,128)(2,1)S(1)} %pad_maximum_fusion.refs_0_.refs_4_), channel_id=1, source_target_pairs={{0,8},{8,0},{16,24},{24,16},{1,9},{9,1},{17,25},{25,17},{2,10},{10... | collective-permute-start | bytes 393224 | tf_op jit(solution)/shard_map/ppermute | solution.py:144
  13.8 3.9 %collective-permute-start.7 = (bf16[2,32,1024]{2,1,0:T(8,128)(2,1)S(1)}, bf16[2,32,1024]{2,1,0:T(8,128)(2,1)S(1)}, u32[]{:S(2)}, u32[]{:S(2)}) collective-permute-start(bf16[2,32,1024]{2,1,0:T(8,128)(2,1)S(1)} %collective-permute-done.3.refs_5_), channel_id=1, source_target_pairs={{0,8},{8,0},{16,24},{24,16},{1,9},{9,1},{17,25},{25,17},{2,10},{10... | collective-permute-start | bytes 393224 | tf_op jit(solution)/shard_map/ppermute | solution.py:144
  15.6 2.1 %collective-permute-start.8 = (bf16[2,32,1024]{2,1,0:T(8,128)(2,1)S(1)}, bf16[2,32,1024]{2,1,0:T(8,128)(2,1)S(1)}, u32[]{:S(2)}, u32[]{:S(2)}) collective-permute-start(bf16[2,32,1024]{2,1,0:T(8,128)(2,1)S(1)} %collective-permute-done.4.refs_6_), channel_id=1, source_target_pairs={{0,8},{8,0},{16,24},{24,16},{1,9},{9,1},{17,25},{25,17},{2,10},{10... | collective-permute-start | bytes 393224 | tf_op jit(solution)/shard_map/ppermute | solution.py:144
  17.2 1.5 %collective-permute-start.9 = (bf16[2,32,1024]{2,1,0:T(8,128)(2,1)S(1)}, bf16[2,32,1024]{2,1,0:T(8,128)(2,1)S(1)}, u32[]{:S(2)}, u32[]{:S(2)}) collective-permute-start(bf16[2,32,1024]{2,1,0:T(8,128)(2,1)S(1)} %collective-permute-done.5.refs_3_), channel_id=1, source_target_pairs={{0,8},{8,0},{16,24},{24,16},{1,9},{9,1},{17,25},{25,17},{2,10},{10... | collective-permute-start | bytes 393224 | tf_op jit(solution)/shard_map/ppermute | solution.py:144
  20.2 7.3 %collective-permute-start.12 = (f16[2,32,1024]{2,1,0:T(8,128)(2,1)S(1)}, f16[2,32,1024]{2,1,0:T(8,128)(2,1)S(1)}, u32[]{:S(2)}, u32[]{:S(2)}) collective-permute-start(f16[2,32,1024]{2,1,0:T(8,128)(2,1)S(1)} %convert_element_type.37), channel_id=1, source_target_pairs={{0,17},{1,16},{2,19},{3,18},{4,21},{5,20},{6,23},{7,22},{8,25},{9,... | collective-permute-start | bytes 393224 | tf_op jit(solution)/shard_map/ppermute | solution.py:172
  22.5 7.2 %collective-permute-start.11 = (f16[2,32,1024]{2,1,0:T(8,128)(2,1)S(1)}, f16[2,32,1024]{2,1,0:T(8,128)(2,1)S(1)}, u32[]{:S(2)}, u32[]{:S(2)}) collective-permute-start(f16[2,32,1024]{2,1,0:T(8,128)(2,1)S(1)} %convert_element_type.35), channel_id=1, source_target_pairs={{0,16},{1,17},{2,18},{3,19},{4,20},{5,21},{6,22},{7,23},{8,24},{9,... | collective-permute-start | bytes 393224 | tf_op jit(solution)/shard_map/ppermute | solution.py:172
  23.2 6.6 %collective-permute-start.10 = (f16[2,32,1024]{2,1,0:T(8,128)(2,1)S(1)}, f16[2,32,1024]{2,1,0:T(8,128)(2,1)S(1)}, u32[]{:S(2)}, u32[]{:S(2)}) collective-permute-start(f16[2,32,1024]{2,1,0:T(8,128)(2,1)S(1)} %convert_element_type.33), channel_id=1, source_target_pairs={{0,1},{1,0},{2,3},{3,2},{4,5},{5,4},{6,7},{7,6},{8,9},{9,8},{10,11... | collective-permute-start | bytes 393224 | tf_op jit(solution)/shard_map/ppermute | solution.py:172

commit v7 on v6

--- a/solution.py
+++ b/solution.py
@@ -59,13 +59,13 @@
     return jnp.concatenate([ref[s] for s in range(2) for ref in refs], axis=0)
 
 
-def weigh(rows, keys, weights, scale):
+def weigh(rows, keys, factors):
     n, m = rows.shape[0] // 2, keys.shape[0] // 2
     scores = dot(rows, keys, ((1,), (1,)))
     cross = scores[:n, m:] - scores[n:, :m]
     inmodal = scores[:n, :m] - scores[n:, m:]
-    p_mat = (cross * (weights[0] * scale)).astype(jnp.bfloat16)
-    q_mat = (inmodal * (weights[1] * scale)).astype(jnp.bfloat16)
+    p_mat = (cross * factors[0:1, 0:1]).astype(jnp.bfloat16)
+    q_mat = (inmodal * factors[1:2, 0:1]).astype(jnp.bfloat16)
     return p_mat, q_mat
 
 
@@ -83,25 +83,25 @@
     return grad_img, grad_txt
 
 
-def early_kernel(scale, total, n, weights, *refs):
+def early_kernel(total, n, factors, *refs):
     own, acc, up, down = refs[-4:]
     rows = join(refs[:n])
     own[...] = rows
     keys = join(refs[n:-4])
-    p_mat, q_mat = weigh(rows, keys, weights, scale)
+    p_mat, q_mat = weigh(rows, keys, factors)
     for at in tiles(keys.shape[1]):
         acc[0, :, at], acc[1, :, at] = tile_grads(p_mat, q_mat, keys, at)
     size = jnp.sum(jnp.abs(rows.astype(jnp.float32)), axis=1, keepdims=True)
     size = size[: size.shape[0] // 2] + size[size.shape[0] // 2 :]
-    most = size * ((weights[0] + weights[1]) * (1.02 * scale * LIMIT * LIMIT * total)) + 1e-30
+    most = size * ((factors[0:1, 0:1] + factors[1:2, 0:1]) * (1.02 * LIMIT * LIMIT * total)) + 1e-30
     up[...] = jnp.broadcast_to(TOP / most, up.shape)
     down[...] = jnp.broadcast_to((most / TOP)[: down.shape[0]], down.shape)
 
 
-def late_kernel(scale, n, weights, own, acc, up, *refs):
+def late_kernel(n, factors, own, acc, up, *refs):
     outs = refs[-n:]
     keys = join(refs[:-n])
-    p_mat, q_mat = weigh(own[...], keys, weights, scale)
+    p_mat, q_mat = weigh(own[...], keys, factors)
     rows = outs[0].shape[1]
     for at in tiles(keys.shape[1]):
         for s, grad in enumerate(tile_grads(p_mat, q_mat, keys, at)):
@@ -110,18 +110,17 @@
                 out[s, :, at] = grad[i * rows : (i + 1) * rows]
 
 
-def call(kernel, weights, operands, out_shape, flops):
+def call(kernel, operands, out_shape, flops):
     vmem = pl.BlockSpec(memory_space=pltpu.VMEM)
-    smem = pl.BlockSpec(memory_space=pltpu.SMEM)
     moved = sum(x.size * x.dtype.itemsize for x in [*operands, *out_shape])
     return pl.pallas_call(
         kernel,
         out_shape=out_shape,
-        in_specs=[smem] + [vmem] * len(operands),
+        in_specs=[vmem] * len(operands),
         out_specs=[vmem] * len(out_shape),
         compiler_params=pltpu.CompilerParams(vmem_limit_bytes=40 * 2**20),
         cost_estimate=pl.CostEstimate(flops=flops, bytes_accessed=moved, transcendentals=0),
-    )(weights, *operands)
+    )(*operands)
 
 
 def local(images, texts, loss_weights):
@@ -129,7 +128,7 @@
     row_inner = halves(n_row)[1]
     rows, width = images.shape
     batch = rows * n_row * n_col
-    scale = 1.0 / math.sqrt(width * batch)
+    factors = jnp.broadcast_to((loss_weights * (1.0 / math.sqrt(width * batch)))[:, None], (2, 128))
     both = ("row", "col")
     square = [(j, k) for j in range(halves(n_row)[0]) for k in range(halves(n_col)[1])][1:]
     own = jnp.stack([images, texts])
@@ -152,9 +151,8 @@
         return 16 * many * width * rows * len(keys)
 
     joined, acc, up, down = call(
-        functools.partial(early_kernel, scale, total, len(mine)),
-        loss_weights,
-        mine + early,
+        functools.partial(early_kernel, total, len(mine)),
+        [factors] + mine + early,
         [jax.ShapeDtypeStruct((2 * many, width), images.dtype)]
         + [jax.ShapeDtypeStruct(s, f32) for s in [(2, many, width), (many, 128), (rows, 128)]],
         flops(early),
@@ -162,9 +160,8 @@
     last, acc = lax.optimization_barrier((line[-1], acc))
     late = copies + [last] + pair(last)
     first, *parts = call(
-        functools.partial(late_kernel, scale, len(mine)),
-        loss_weights,
-        [joined, acc, up] + late,
+        functools.partial(late_kernel, len(mine)),
+        [factors, joined, acc, up] + late,
         [jax.ShapeDtypeStruct((2, rows, width), f32)] * len(mine),
         flops(late),
     )

time: 30.8 us -> 29.8 us (0.968)
  Pallas kernels: 2.95 us -> 1.88 us
    pallas_call x2, Pallas kernels: 2.95 us -> 1.88 us  [call(): pl.pallas_call(kernel, out_shape=out_shape, in_specs=[vmem] * len(operand...]
    ppermute x3, waiting for transfers between devices: 1.35 us -> 1.69 us  [local(): line.append(lax.ppermute(line[which], 'col', perm))]
  transfers between devices with their start and end apart: 13 -> 13, of which waited for: 8 -> 9; matrix products, arithmetic and copies ran while one was open for 0% -> 1% of each run, Pallas kernels for 5% -> 3%
where the time goes in v7:
time: 29.8 us; the launch traced here: 29.7 us
  starting transfers between devices  13.6 us (46%)
  waiting for transfers between devices  11.6 us (39%)
  Pallas kernels  1.88 us (6%)
  other arithmetic  1.73 us (6%)
  between operations  0.7 us (2%)
    ppermute x3, starting transfers between devices, local(): line.append(lax.ppermute(line[which], 'col', perm))  6.29 us
    ppermute x3, waiting for transfers between devices, local(): lax.ppermute(part.astype(jnp.float16), both, square_shift(n_row, n_col, -...  5.8 us
    ppermute x3, starting transfers between devices, local(): lax.ppermute(part.astype(jnp.float16), both, square_shift(n_row, n_col, -...  3.55 us
    ppermute x3, starting transfers between devices, local(): lax.ppermute(own, both, square_shift(n_row, n_col, j, k))  3.49 us
    ppermute x3, waiting for transfers between devices, local(): lax.ppermute(own, both, square_shift(n_row, n_col, j, k))  2.93 us
    pallas_call x2, Pallas kernels, call(): pl.pallas_call(kernel, out_shape=out_shape, in_specs=[vmem] * len(operand...  1.88 us
    ppermute x3, waiting for transfers between devices, local(): line.append(lax.ppermute(line[which], 'col', perm))  1.69 us
    ppermute x4, waiting for transfers between devices, pair(): lax.ppermute(block, 'row', inner_shift(n_row, k))  1.19 us
  transfers between devices with their start and end apart: 13, of which 9 were waited for; matrix products, arithmetic and copies ran while one was open for 1% of the time, Pallas kernels for 3%

profile of v7, /device:TPU:0, one launch (start us, length us, event | category | flops | bytes accessed | tf_op | source)
XLA Modules:
  0.0 29.7 jit_solution(1219014766307113710)
XLA Ops:
  0.6 0.0 copy-start
  0.6 0.9 %pad_maximum_fusion.refs_0_.refs_4_ = bf16[2,32,1024]{2,1,0:T(8,128)(2,1)S(1)} fusion(bf16[1,32,1024]{2,1,0:T(8,128)(2,1)} %bitcast.6, bf16[1,32,1024]{2,1,0:T(8,128)(2,1)} %bitcast.7), kind=kLoop, calls=%fused_computation | loop fusion | flops 65536 | bytes 262144 | tf_op jit(solution)/shard_map/stack | solution.py:134
  1.5 4.1 %collective-permute-start.3 = (bf16[2,32,1024]{2,1,0:T(8,128)(2,1)S(1)}, bf16[2,32,1024]{2,1,0:T(8,128)(2,1)S(1)}, u32[]{:S(2)}, u32[]{:S(2)}) collective-permute-start(bf16[2,32,1024]{2,1,0:T(8,128)(2,1)S(1)} %pad_maximum_fusion.refs_0_.refs_4_), channel_id=1, source_target_pairs={{0,4},{1,5},{2,6},{3,7},{4,0},{5,1},{6,2},{7,3},{8,12},{9,13},{10,... | collective-permute-start | bytes 393224 | tf_op jit(solution)/shard_map/ppermute | solution.py:140
  5.6 1.6 %collective-permute-start.4 = (bf16[2,32,1024]{2,1,0:T(8,128)(2,1)S(1)}, bf16[2,32,1024]{2,1,0:T(8,128)(2,1)S(1)}, u32[]{:S(2)}, u32[]{:S(2)}) collective-permute-start(bf16[2,32,1024]{2,1,0:T(8,128)(2,1)S(1)} %pad_maximum_fusion.refs_0_.refs_4_), channel_id=1, source_target_pairs={{0,2},{1,3},{2,0},{3,1},{4,6},{5,7},{6,4},{7,5},{8,10},{9,11},{10,... | collective-permute-start | bytes 393224 | tf_op jit(solution)/shard_map/ppermute | solution.py:140
  7.2 2.4 %collective-permute-start.2 = (bf16[2,32,1024]{2,1,0:T(8,128)(2,1)S(1)}, bf16[2,32,1024]{2,1,0:T(8,128)(2,1)S(1)}, u32[]{:S(2)}, u32[]{:S(2)}) collective-permute-start(bf16[2,32,1024]{2,1,0:T(8,128)(2,1)S(1)} %pad_maximum_fusion.refs_0_.refs_4_), channel_id=1, source_target_pairs={{0,17},{1,16},{2,19},{3,18},{4,21},{5,20},{6,23},{7,22},{8,25},{9,... | collective-permute-start | bytes 393224 | tf_op jit(solution)/shard_map/ppermute | solution.py:136
  9.7 0.5 %collective-permute-start.1 = (bf16[2,32,1024]{2,1,0:T(8,128)(2,1)S(1)}, bf16[2,32,1024]{2,1,0:T(8,128)(2,1)S(1)}, u32[]{:S(2)}, u32[]{:S(2)}) collective-permute-start(bf16[2,32,1024]{2,1,0:T(8,128)(2,1)S(1)} %pad_maximum_fusion.refs_0_.refs_4_), channel_id=1, source_target_pairs={{0,16},{1,17},{2,18},{3,19},{4,20},{5,21},{6,22},{7,23},{8,24},{9,... | collective-permute-start | bytes 393224 | tf_op jit(solution)/shard_map/ppermute | solution.py:136
  10.2 0.5 %collective-permute-start = (bf16[2,32,1024]{2,1,0:T(8,128)(2,1)S(1)}, bf16[2,32,1024]{2,1,0:T(8,128)(2,1)S(1)}, u32[]{:S(2)}, u32[]{:S(2)}) collective-permute-start(bf16[2,32,1024]{2,1,0:T(8,128)(2,1)S(1)} %pad_maximum_fusion.refs_0_.refs_4_), channel_id=1, source_target_pairs={{0,1},{1,0},{2,3},{3,2},{4,5},{5,4},{6,7},{7,6},{8,9},{9,8},{10,11... | collective-permute-start | bytes 393224 | tf_op jit(solution)/shard_map/ppermute | solution.py:136
  10.7 1.3 %collective-permute-done.3.refs_5_ = bf16[2,32,1024]{2,1,0:T(8,128)(2,1)S(1)} collective-permute-done((bf16[2,32,1024]{2,1,0:T(8,128)(2,1)S(1)}, bf16[2,32,1024]{2,1,0:T(8,128)(2,1)S(1)}, u32[]{:S(2)}, u32[]{:S(2)}) %collective-permute-start.3) | collective-permute-done | bytes 131104 | tf_op jit(solution)/shard_map/ppermute | solution.py:140
  12.0 0.6 %collective-permute-start.5 = (bf16[2,32,1024]{2,1,0:T(8,128)(2,1)S(1)}, bf16[2,32,1024]{2,1,0:T(8,128)(2,1)S(1)}, u32[]{:S(2)}, u32[]{:S(2)}) collective-permute-start(bf16[2,32,1024]{2,1,0:T(8,128)(2,1)S(1)} %collective-permute-done.3.refs_5_), channel_id=1, source_target_pairs={{0,2},{1,3},{2,0},{3,1},{4,6},{5,7},{6,4},{7,5},{8,10},{9,11},{10,... | collective-permute-start | bytes 393224 | tf_op jit(solution)/shard_map/ppermute | solution.py:140
  12.7 0.0 copy-done
  12.7 0.0 collective-permute-done.4.refs_6_
  12.7 0.1 collective-permute-start.6
  12.8 1.0 %collective-permute-done.2.refs_3_ = bf16[2,32,1024]{2,1,0:T(8,128)(2,1)S(1)} collective-permute-done((bf16[2,32,1024]{2,1,0:T(8,128)(2,1)S(1)}, bf16[2,32,1024]{2,1,0:T(8,128)(2,1)S(1)}, u32[]{:S(2)}, u32[]{:S(2)}) %collective-permute-start.2) | collective-permute-done | bytes 131104 | tf_op jit(solution)/shard_map/ppermute | solution.py:136
  13.8 0.0 collective-permute-start.7
  13.8 1.8 %collective-permute-done.1.refs_2_ = bf16[2,32,1024]{2,1,0:T(8,128)(2,1)S(1)} collective-permute-done((bf16[2,32,1024]{2,1,0:T(8,128)(2,1)S(1)}, bf16[2,32,1024]{2,1,0:T(8,128)(2,1)S(1)}, u32[]{:S(2)}, u32[]{:S(2)}) %collective-permute-start.1) | collective-permute-done | bytes 131104 | tf_op jit(solution)/shard_map/ppermute | solution.py:136
  15.6 0.0 collective-permute-start.8
  15.6 0.1 collective-permute-done.refs_1_
  15.7 0.1 broadcast_in_dim.2.factors
  15.8 0.9 %shard_map.50 = (bf16[256,1024]{1,0:T(8,128)(2,1)S(1)}, f32[2,128,1024]{2,1,0:T(8,128)S(1)}, f32[128,128]{1,0:T(8,128)S(1)}, f32[32,128]{1,0:T(8,128)S(1)}) custom-call(f32[2,128]{1,0:T(2,128)S(1)} %broadcast_in_dim.2.factors, bf16[2,32,1024]{2,1,0:T(8,128)(2,1)S(1)} %pad_maximum_fusion.refs_0_.refs_4_, ...), custom_call_target="tpu_custom_call" | custom-call | flops 201326592 | bytes 2573312 | tf_op jit(solution)/shard_map/pallas_call | solution.py:116
  16.7 0.3 %collective-permute-done.5.refs_3_ = bf16[2,32,1024]{2,1,0:T(8,128)(2,1)S(1)} collective-permute-done((bf16[2,32,1024]{2,1,0:T(8,128)(2,1)S(1)}, bf16[2,32,1024]{2,1,0:T(8,128)(2,1)S(1)}, u32[]{:S(2)}, u32[]{:S(2)}) %collective-permute-start.5) | collective-permute-done | bytes 131104 | tf_op jit(solution)/shard_map/ppermute | solution.py:140
  17.0 0.2 collective-permute-start.9
  17.2 0.0 collective-permute-done.6.refs_0_
  17.2 0.0 collective-permute-done.8.refs_2_
  17.2 0.0 collective-permute-done.7.refs_1_
  17.2 1.2 %collective-permute-done.9.refs_4_ = bf16[2,32,1024]{2,1,0:T(8,128)(2,1)S(1)} collective-permute-done((bf16[2,32,1024]{2,1,0:T(8,128)(2,1)S(1)}, bf16[2,32,1024]{2,1,0:T(8,128)(2,1)S(1)}, u32[]{:S(2)}, u32[]{:S(2)}) %collective-permute-start.9) | collective-permute-done | bytes 131104 | tf_op jit(solution)/shard_map/ppermute | solution.py:143
  18.4 1.0 %shard_map.51 = (f32[2,32,1024]{2,1,0:T(8,128)S(1)}, f32[2,32,1024]{2,1,0:T(8,128)S(1)}, f32[2,32,1024]{2,1,0:T(8,128)S(1)}, f32[2,32,1024]{2,1,0:T(8,128)S(1)}) custom-call(f32[2,128]{1,0:T(2,128)S(1)} %broadcast_in_dim.2.factors, bf16[256,1024]{1,0:T(8,128)(2,1)S(1)} %get-tuple-element.12.own, f32[2,128,1024]{2,1,0:T(8,128)S(1)} %get-tuple-element.14.acc, ...), custom_call_target="tpu_custom_call" | custom-call | flops 335544320 | bytes 3343360 | tf_op jit(solution)/shard_map/pallas_call | solution.py:116
  19.4 2.6 %collective-permute-start.12 = (f16[2,32,1024]{2,1,0:T(8,128)(2,1)S(1)}, f16[2,32,1024]{2,1,0:T(8,128)(2,1)S(1)}, u32[]{:S(2)}, u32[]{:S(2)}) collective-permute-start(f16[2,32,1024]{2,1,0:T(8,128)(2,1)S(1)} %convert_element_type.37), channel_id=1, source_target_pairs={{0,17},{1,16},{2,19},{3,18},{4,21},{5,20},{6,23},{7,22},{8,25},{9,... | collective-permute-start | bytes 393224 | tf_op jit(solution)/shard_map/ppermute | solution.py:169
  22.0 0.5 %collective-permute-start.11 = (f16[2,32,1024]{2,1,0:T(8,128)(2,1)S(1)}, f16[2,32,1024]{2,1,0:T(8,128)(2,1)S(1)}, u32[]{:S(2)}, u32[]{:S(2)}) collective-permute-start(f16[2,32,1024]{2,1,0:T(8,128)(2,1)S(1)} %convert_element_type.35), channel_id=1, source_target_pairs={{0,16},{1,17},{2,18},{3,19},{4,20},{5,21},{6,22},{7,23},{8,24},{9,... | collective-permute-start | bytes 393224 | tf_op jit(solution)/shard_map/ppermute | solution.py:169
  22.5 0.5 %collective-permute-start.10 = (f16[2,32,1024]{2,1,0:T(8,128)(2,1)S(1)}, f16[2,32,1024]{2,1,0:T(8,128)(2,1)S(1)}, u32[]{:S(2)}, u32[]{:S(2)}) collective-permute-start(f16[2,32,1024]{2,1,0:T(8,128)(2,1)S(1)} %convert_element_type.33), channel_id=1, source_target_pairs={{0,1},{1,0},{2,3},{3,2},{4,5},{5,4},{6,7},{7,6},{8,9},{9,8},{10,11... | collective-permute-start | bytes 393224 | tf_op jit(solution)/shard_map/ppermute | solution.py:169
  23.0 0.1 slice_reduce_fusion
  23.1 3.1 %collective-permute-done.12 = f16[2,32,1024]{2,1,0:T(8,128)(2,1)S(1)} collective-permute-done((f16[2,32,1024]{2,1,0:T(8,128)(2,1)S(1)}, f16[2,32,1024]{2,1,0:T(8,128)(2,1)S(1)}, u32[]{:S(2)}, u32[]{:S(2)}) %collective-permute-start.12) | collective-permute-done | bytes 131104 | tf_op jit(solution)/shard_map/ppermute | solution.py:169
  26.2 2.6 %collective-permute-done.11 = f16[2,32,1024]{2,1,0:T(8,128)(2,1)S(1)} collective-permute-done((f16[2,32,1024]{2,1,0:T(8,128)(2,1)S(1)}, f16[2,32,1024]{2,1,0:T(8,128)(2,1)S(1)}, u32[]{:S(2)}, u32[]{:S(2)}) %collective-permute-start.11) | collective-permute-done | bytes 131104 | tf_op jit(solution)/shard_map/ppermute | solution.py:169
  28.7 0.1 collective-permute-done.10
  28.9 0.8 %bitcast_multiply_fusion = (f32[32,1024]{1,0:T(8,128)}, f32[32,1024]{1,0:T(8,128)}) fusion(f32[2,32,1024]{2,1,0:T(8,128)S(1)} %get-tuple-element.17, f16[2,32,1024]{2,1,0:T(8,128)(2,1)S(1)} %collective-permute-done.12, f16[2,32,1024]{2,1,0:T(8,128)(2,1)S(1)} %collective-permute-done.11, f16[2,32,1024]{2,1,0:T(8,128)(2,1)S(1)} %collective-permute-done.10, ...), kind=kLoop, calls=%fused_computation.1 | loop fusion | flops 458752 | bytes 917632 | tf_op jit(solution)/shard_map/mul | solution.py:177
  (4 shorter events, 0.1 us)
Async XLA Ops:
  0.6 12.0 %copy-start = (f32[2]{0:T(128)S(1)}, f32[2]{0:T(128)}, u32[]{:S(2)}) copy-start(f32[2]{0:T(128)} %param.5) | copy-start | bytes 28
  1.5 10.5 %collective-permute-start.3 = (bf16[2,32,1024]{2,1,0:T(8,128)(2,1)S(1)}, bf16[2,32,1024]{2,1,0:T(8,128)(2,1)S(1)}, u32[]{:S(2)}, u32[]{:S(2)}) collective-permute-start(bf16[2,32,1024]{2,1,0:T(8,128)(2,1)S(1)} %pad_maximum_fusion.refs_0_.refs_4_), channel_id=1, source_target_pairs={{0,4},{1,5},{2,6},{3,7},{4,0},{5,1},{6,2},{7,3},{8,12},{9,13},{10,... | collective-permute-start | bytes 393224 | tf_op jit(solution)/shard_map/ppermute | solution.py:140
  5.6 7.0 %collective-permute-start.4 = (bf16[2,32,1024]{2,1,0:T(8,128)(2,1)S(1)}, bf16[2,32,1024]{2,1,0:T(8,128)(2,1)S(1)}, u32[]{:S(2)}, u32[]{:S(2)}) collective-permute-start(bf16[2,32,1024]{2,1,0:T(8,128)(2,1)S(1)} %pad_maximum_fusion.refs_0_.refs_4_), channel_id=1, source_target_pairs={{0,2},{1,3},{2,0},{3,1},{4,6},{5,7},{6,4},{7,5},{8,10},{9,11},{10,... | collective-permute-start | bytes 393224 | tf_op jit(solution)/shard_map/ppermute | solution.py:140
  7.2 6.6 %collective-permute-start.2 = (bf16[2,32,1024]{2,1,0:T(8,128)(2,1)S(1)}, bf16[2,32,1024]{2,1,0:T(8,128)(2,1)S(1)}, u32[]{:S(2)}, u32[]{:S(2)}) collective-permute-start(bf16[2,32,1024]{2,1,0:T(8,128)(2,1)S(1)} %pad_maximum_fusion.refs_0_.refs_4_), channel_id=1, source_target_pairs={{0,17},{1,16},{2,19},{3,18},{4,21},{5,20},{6,23},{7,22},{8,25},{9,... | collective-permute-start | bytes 393224 | tf_op jit(solution)/shard_map/ppermute | solution.py:136
  9.7 5.9 %collective-permute-start.1 = (bf16[2,32,1024]{2,1,0:T(8,128)(2,1)S(1)}, bf16[2,32,1024]{2,1,0:T(8,128)(2,1)S(1)}, u32[]{:S(2)}, u32[]{:S(2)}) collective-permute-start(bf16[2,32,1024]{2,1,0:T(8,128)(2,1)S(1)} %pad_maximum_fusion.refs_0_.refs_4_), channel_id=1, source_target_pairs={{0,16},{1,17},{2,18},{3,19},{4,20},{5,21},{6,22},{7,23},{8,24},{9,... | collective-permute-start | bytes 393224 | tf_op jit(solution)/shard_map/ppermute | solution.py:136
  10.2 5.5 %collective-permute-start = (bf16[2,32,1024]{2,1,0:T(8,128)(2,1)S(1)}, bf16[2,32,1024]{2,1,0:T(8,128)(2,1)S(1)}, u32[]{:S(2)}, u32[]{:S(2)}) collective-permute-start(bf16[2,32,1024]{2,1,0:T(8,128)(2,1)S(1)} %pad_maximum_fusion.refs_0_.refs_4_), channel_id=1, source_target_pairs={{0,1},{1,0},{2,3},{3,2},{4,5},{5,4},{6,7},{7,6},{8,9},{9,8},{10,11... | collective-permute-start | bytes 393224 | tf_op jit(solution)/shard_map/ppermute | solution.py:136
  12.0 5.0 %collective-permute-start.5 = (bf16[2,32,1024]{2,1,0:T(8,128)(2,1)S(1)}, bf16[2,32,1024]{2,1,0:T(8,128)(2,1)S(1)}, u32[]{:S(2)}, u32[]{:S(2)}) collective-permute-start(bf16[2,32,1024]{2,1,0:T(8,128)(2,1)S(1)} %collective-permute-done.3.refs_5_), channel_id=1, source_target_pairs={{0,2},{1,3},{2,0},{3,1},{4,6},{5,7},{6,4},{7,5},{8,10},{9,11},{10,... | collective-permute-start | bytes 393224 | tf_op jit(solution)/shard_map/ppermute | solution.py:140
  12.7 4.5 %collective-permute-start.6 = (bf16[2,32,1024]{2,1,0:T(8,128)(2,1)S(1)}, bf16[2,32,1024]{2,1,0:T(8,128)(2,1)S(1)}, u32[]{:S(2)}, u32[]{:S(2)}) collective-permute-start(bf16[2,32,1024]{2,1,0:T(8,128)(2,1)S(1)} %pad_maximum_fusion.refs_0_.refs_4_), channel_id=1, source_target_pairs={{0,8},{8,0},{16,24},{24,16},{1,9},{9,1},{17,25},{25,17},{2,10},{10... | collective-permute-start | bytes 393224 | tf_op jit(solution)/shard_map/ppermute | solution.py:143
  13.8 3.4 %collective-permute-start.7 = (bf16[2,32,1024]{2,1,0:T(8,128)(2,1)S(1)}, bf16[2,32,1024]{2,1,0:T(8,128)(2,1)S(1)}, u32[]{:S(2)}, u32[]{:S(2)}) collective-permute-start(bf16[2,32,1024]{2,1,0:T(8,128)(2,1)S(1)} %collective-permute-done.3.refs_5_), channel_id=1, source_target_pairs={{0,8},{8,0},{16,24},{24,16},{1,9},{9,1},{17,25},{25,17},{2,10},{10... | collective-permute-start | bytes 393224 | tf_op jit(solution)/shard_map/ppermute | solution.py:143
  15.6 1.6 %collective-permute-start.8 = (bf16[2,32,1024]{2,1,0:T(8,128)(2,1)S(1)}, bf16[2,32,1024]{2,1,0:T(8,128)(2,1)S(1)}, u32[]{:S(2)}, u32[]{:S(2)}) collective-permute-start(bf16[2,32,1024]{2,1,0:T(8,128)(2,1)S(1)} %collective-permute-done.4.refs_6_), channel_id=1, source_target_pairs={{0,8},{8,0},{16,24},{24,16},{1,9},{9,1},{17,25},{25,17},{2,10},{10... | collective-permute-start | bytes 393224 | tf_op jit(solution)/shard_map/ppermute | solution.py:143
  17.0 1.3 %collective-permute-start.9 = (bf16[2,32,1024]{2,1,0:T(8,128)(2,1)S(1)}, bf16[2,32,1024]{2,1,0:T(8,128)(2,1)S(1)}, u32[]{:S(2)}, u32[]{:S(2)}) collective-permute-start(bf16[2,32,1024]{2,1,0:T(8,128)(2,1)S(1)} %collective-permute-done.5.refs_3_), channel_id=1, source_target_pairs={{0,8},{8,0},{16,24},{24,16},{1,9},{9,1},{17,25},{25,17},{2,10},{10... | collective-permute-start | bytes 393224 | tf_op jit(solution)/shard_map/ppermute | solution.py:143
  19.4 6.8 %collective-permute-start.12 = (f16[2,32,1024]{2,1,0:T(8,128)(2,1)S(1)}, f16[2,32,1024]{2,1,0:T(8,128)(2,1)S(1)}, u32[]{:S(2)}, u32[]{:S(2)}) collective-permute-start(f16[2,32,1024]{2,1,0:T(8,128)(2,1)S(1)} %convert_element_type.37), channel_id=1, source_target_pairs={{0,17},{1,16},{2,19},{3,18},{4,21},{5,20},{6,23},{7,22},{8,25},{9,... | collective-permute-start | bytes 393224 | tf_op jit(solution)/shard_map/ppermute | solution.py:169
  22.0 6.8 %collective-permute-start.11 = (f16[2,32,1024]{2,1,0:T(8,128)(2,1)S(1)}, f16[2,32,1024]{2,1,0:T(8,128)(2,1)S(1)}, u32[]{:S(2)}, u32[]{:S(2)}) collective-permute-start(f16[2,32,1024]{2,1,0:T(8,128)(2,1)S(1)} %convert_element_type.35), channel_id=1, source_target_pairs={{0,16},{1,17},{2,18},{3,19},{4,20},{5,21},{6,22},{7,23},{8,24},{9,... | collective-permute-start | bytes 393224 | tf_op jit(solution)/shard_map/ppermute | solution.py:169
  22.5 6.4 %collective-permute-start.10 = (f16[2,32,1024]{2,1,0:T(8,128)(2,1)S(1)}, f16[2,32,1024]{2,1,0:T(8,128)(2,1)S(1)}, u32[]{:S(2)}, u32[]{:S(2)}) collective-permute-start(f16[2,32,1024]{2,1,0:T(8,128)(2,1)S(1)} %convert_element_type.33), channel_id=1, source_target_pairs={{0,1},{1,0},{2,3},{3,2},{4,5},{5,4},{6,7},{7,6},{8,9},{9,8},{10,11... | collective-permute-start | bytes 393224 | tf_op jit(solution)/shard_map/ppermute | solution.py:169

commit v8 on v7

--- a/solution.py
+++ b/solution.py
@@ -135,14 +135,22 @@
 
     mine = [own] + [lax.ppermute(own, both, square_shift(n_row, n_col, j, k)) for j, k in square]
 
-    line = [own]
-    for which, perm in outer_moves(n_col):
-        line.append(lax.ppermute(line[which], "col", perm))
+    line, apart = [own], {0: [images, texts]}
+    for step, (which, perm) in enumerate(outer_moves(n_col), 1):
+        if which in apart and (which or step == 1):
+            apart[step] = [lax.ppermute(half, "col", perm) for half in apart[which]]
+            line.append(jnp.stack(apart[step]))
+        else:
+            line.append(lax.ppermute(line[which], "col", perm))
 
     def pair(block):
         return [lax.ppermute(block, "row", inner_shift(n_row, k)) for k in range(1, row_inner)]
 
-    early, copies = line[:-1], [copy for block in line[:-1] for copy in pair(block)]
+    early, copies = line[:-1], []
+    for i, block in enumerate(line[:-1]):
+        if i == 0 and square:
+            block, mine[-2] = lax.optimization_barrier((block, mine[-2]))
+        copies += pair(block)
     total = rows * len(line) * row_inner
     many = rows * len(mine)
     f32 = jnp.float32

time: 29.8 us -> 34.4 us (1.15)
  waiting for transfers between devices: 11.6 us -> 14.2 us
  starting transfers between devices: 13.6 us -> 15.5 us
    ppermute x0 -> x4, starting transfers between devices: none -> 5.76 us  [local(): apart[step] = [lax.ppermute(half, 'col', perm) for half in apart[which]]]
    ppermute x3 -> x1, starting transfers between devices: 6.29 us -> 1.9 us  [local(): line.append(lax.ppermute(line[which], 'col', perm))]
    ppermute x0 -> x4, waiting for transfers between devices: none -> 3.72 us  [local(): apart[step] = [lax.ppermute(half, 'col', perm) for half in apart[which]]]
    ppermute x3 -> x1, waiting for transfers between devices: 1.69 us -> 0.01 us  [local(): line.append(lax.ppermute(line[which], 'col', perm))]
    ppermute x3, waiting for transfers between devices: 2.93 us -> 3.43 us  [local(): lax.ppermute(own, both, square_shift(n_row, n_col, j, k))]
    ppermute x4, starting transfers between devices: 0.23 us -> 0.72 us  [pair(): lax.ppermute(block, 'row', inner_shift(n_row, k))]
  transfers between devices with their start and end apart: 13 -> 15, of which waited for: 9 -> 7; matrix products, arithmetic and copies ran while one was open for 1% -> 3% of each run, Pallas kernels for 3% -> 3%
where the time goes in v8:
time: 34.4 us; the launch traced here: 34.3 us
  starting transfers between devices  15.5 us (45%)
  waiting for transfers between devices  14.2 us (41%)
  Pallas kernels  1.88 us (5%)
  other arithmetic  1.76 us (5%)
  between operations  0.73 us (2%)
    ppermute x3, waiting for transfers between devices, local(): lax.ppermute(part.astype(jnp.float16), both, square_shift(n_row, n_col, -...  5.79 us
    ppermute x4, starting transfers between devices, local(): apart[step] = [lax.ppermute(half, 'col', perm) for half in apart[which]]  5.76 us
    ppermute x4, waiting for transfers between devices, local(): apart[step] = [lax.ppermute(half, 'col', perm) for half in apart[which]]  3.72 us
    ppermute x3, starting transfers between devices, local(): lax.ppermute(own, both, square_shift(n_row, n_col, j, k))  3.55 us
    ppermute x3, starting transfers between devices, local(): lax.ppermute(part.astype(jnp.float16), both, square_shift(n_row, n_col, -...  3.55 us
    ppermute x3, waiting for transfers between devices, local(): lax.ppermute(own, both, square_shift(n_row, n_col, j, k))  3.43 us
    ppermute x1, starting transfers between devices, local(): line.append(lax.ppermute(line[which], 'col', perm))  1.9 us
    pallas_call x2, Pallas kernels, call(): pl.pallas_call(kernel, out_shape=out_shape, in_specs=[vmem] * len(operand...  1.88 us
  transfers between devices with their start and end apart: 15, of which 7 were waited for; matrix products, arithmetic and copies ran while one was open for 3% of the time, Pallas kernels for 3%

profile of v8, /device:TPU:0, one launch (start us, length us, event | category | flops | bytes accessed | tf_op | source)
XLA Modules:
  0.0 34.3 jit_solution(16302690220166817645)
XLA Ops:
  0.6 4.1 %collective-permute-start.3 = (bf16[32,1024]{1,0:T(8,128)(2,1)}, bf16[32,1024]{1,0:T(8,128)(2,1)S(1)}, u32[]{:S(2)}, u32[]{:S(2)}) collective-permute-start(bf16[32,1024]{1,0:T(8,128)(2,1)} %param.3), channel_id=1, source_target_pairs={{0,4},{1,5},{2,6},{3,7},{4,0},{5,1},{6,2},{7,3},{8,12},{9,13},{10,... | collective-permute-start | bytes 196616 | tf_op jit(solution)/shard_map/ppermute | solution.py:141
  4.7 0.1 collective-permute-start.4
  4.8 0.0 copy-start
  4.8 0.9 %pad_maximum_fusion.refs_0_.refs_4_ = bf16[2,32,1024]{2,1,0:T(8,128)(2,1)S(1)} fusion(bf16[1,32,1024]{2,1,0:T(8,128)(2,1)} %bitcast.11, bf16[1,32,1024]{2,1,0:T(8,128)(2,1)} %bitcast.10), kind=kLoop, calls=%fused_computation | loop fusion | flops 65536 | bytes 262144 | tf_op jit(solution)/shard_map/stack | solution.py:134
  5.7 1.9 %collective-permute-start.5 = (bf16[2,32,1024]{2,1,0:T(8,128)(2,1)S(1)}, bf16[2,32,1024]{2,1,0:T(8,128)(2,1)S(1)}, u32[]{:S(2)}, u32[]{:S(2)}) collective-permute-start(bf16[2,32,1024]{2,1,0:T(8,128)(2,1)S(1)} %pad_maximum_fusion.refs_0_.refs_4_), channel_id=1, source_target_pairs={{0,2},{1,3},{2,0},{3,1},{4,6},{5,7},{6,4},{7,5},{8,10},{9,11},{10,... | collective-permute-start | bytes 393224 | tf_op jit(solution)/shard_map/ppermute | solution.py:144
  7.6 2.4 %collective-permute-start.2 = (bf16[2,32,1024]{2,1,0:T(8,128)(2,1)S(1)}, bf16[2,32,1024]{2,1,0:T(8,128)(2,1)S(1)}, u32[]{:S(2)}, u32[]{:S(2)}) collective-permute-start(bf16[2,32,1024]{2,1,0:T(8,128)(2,1)S(1)} %pad_maximum_fusion.refs_0_.refs_4_), channel_id=1, source_target_pairs={{0,17},{1,16},{2,19},{3,18},{4,21},{5,20},{6,23},{7,22},{8,25},{9,... | collective-permute-start | bytes 393224 | tf_op jit(solution)/shard_map/ppermute | solution.py:136
  10.1 0.5 %collective-permute-start.1 = (bf16[2,32,1024]{2,1,0:T(8,128)(2,1)S(1)}, bf16[2,32,1024]{2,1,0:T(8,128)(2,1)S(1)}, u32[]{:S(2)}, u32[]{:S(2)}) collective-permute-start(bf16[2,32,1024]{2,1,0:T(8,128)(2,1)S(1)} %pad_maximum_fusion.refs_0_.refs_4_), channel_id=1, source_target_pairs={{0,16},{1,17},{2,18},{3,19},{4,20},{5,21},{6,22},{7,23},{8,24},{9,... | collective-permute-start | bytes 393224 | tf_op jit(solution)/shard_map/ppermute | solution.py:136
  10.6 0.0 copy-done
  10.6 0.0 collective-permute-done.3
  10.6 0.6 %collective-permute-start = (bf16[2,32,1024]{2,1,0:T(8,128)(2,1)S(1)}, bf16[2,32,1024]{2,1,0:T(8,128)(2,1)S(1)}, u32[]{:S(2)}, u32[]{:S(2)}) collective-permute-start(bf16[2,32,1024]{2,1,0:T(8,128)(2,1)S(1)} %pad_maximum_fusion.refs_0_.refs_4_), channel_id=1, source_target_pairs={{0,1},{1,0},{2,3},{3,2},{4,5},{5,4},{6,7},{7,6},{8,9},{9,8},{10,11... | collective-permute-start | bytes 393224 | tf_op jit(solution)/shard_map/ppermute | solution.py:136
  11.2 0.0 collective-permute-done.4
  11.2 1.1 %collective-permute-start.6 = (bf16[32,1024]{1,0:T(8,128)(2,1)S(1)}, bf16[32,1024]{1,0:T(8,128)(2,1)S(1)}, u32[]{:S(2)}, u32[]{:S(2)}) collective-permute-start(bf16[32,1024]{1,0:T(8,128)(2,1)S(1)} %collective-permute-done.3), channel_id=1, source_target_pairs={{0,2},{1,3},{2,0},{3,1},{4,6},{5,7},{6,4},{7,5},{8,10},{9,11},{10,... | collective-permute-start | bytes 196616 | tf_op jit(solution)/shard_map/ppermute | solution.py:141
  12.3 3.4 %collective-permute-done.1.refs_2_ = bf16[2,32,1024]{2,1,0:T(8,128)(2,1)S(1)} collective-permute-done((bf16[2,32,1024]{2,1,0:T(8,128)(2,1)S(1)}, bf16[2,32,1024]{2,1,0:T(8,128)(2,1)S(1)}, u32[]{:S(2)}, u32[]{:S(2)}) %collective-permute-start.1) | collective-permute-done | bytes 131104 | tf_op jit(solution)/shard_map/ppermute | solution.py:136
  15.7 0.4 %collective-permute-start.7 = (bf16[32,1024]{1,0:T(8,128)(2,1)S(1)}, bf16[32,1024]{1,0:T(8,128)(2,1)S(1)}, u32[]{:S(2)}, u32[]{:S(2)}) collective-permute-start(bf16[32,1024]{1,0:T(8,128)(2,1)S(1)} %collective-permute-done.4), channel_id=1, source_target_pairs={{0,2},{1,3},{2,0},{3,1},{4,6},{5,7},{6,4},{7,5},{8,10},{9,11},{10,... | collective-permute-start | bytes 196616 | tf_op jit(solution)/shard_map/ppermute | solution.py:141
  16.2 0.0 collective-permute-done.6
  16.2 0.1 collective-permute-start.9
  16.3 3.7 %collective-permute-done.7 = bf16[32,1024]{1,0:T(8,128)(2,1)S(1)} collective-permute-done((bf16[32,1024]{1,0:T(8,128)(2,1)S(1)}, bf16[32,1024]{1,0:T(8,128)(2,1)S(1)}, u32[]{:S(2)}, u32[]{:S(2)}) %collective-permute-start.7) | collective-permute-done | bytes 65568 | tf_op jit(solution)/shard_map/ppermute | solution.py:141
  20.0 0.0 collective-permute-start.8
  20.0 0.0 collective-permute-done.5.refs_6_
  20.0 0.0 collective-permute-done.2.refs_3_
  20.0 0.0 collective-permute-done.refs_1_
  20.1 0.1 broadcast_in_dim.2.factors
  20.1 0.9 %shard_map.50 = (bf16[256,1024]{1,0:T(8,128)(2,1)S(1)}, f32[2,128,1024]{2,1,0:T(8,128)S(1)}, f32[128,128]{1,0:T(8,128)S(1)}, f32[32,128]{1,0:T(8,128)S(1)}) custom-call(f32[2,128]{1,0:T(2,128)S(1)} %broadcast_in_dim.2.factors, bf16[2,32,1024]{2,1,0:T(8,128)(2,1)S(1)} %pad_maximum_fusion.refs_0_.refs_4_, ...), custom_call_target="tpu_custom_call" | custom-call | flops 201326592 | bytes 2573312 | tf_op jit(solution)/shard_map/pallas_call | solution.py:116
  21.0 0.6 %collective-permute-start.10 = (bf16[2,32,1024]{2,1,0:T(8,128)(2,1)S(1)}, bf16[2,32,1024]{2,1,0:T(8,128)(2,1)S(1)}, u32[]{:S(2)}, u32[]{:S(2)}) collective-permute-start(bf16[2,32,1024]{2,1,0:T(8,128)(2,1)S(1)} %collective-permute-done.5.refs_6_), channel_id=1, source_target_pairs={{0,8},{8,0},{16,24},{24,16},{1,9},{9,1},{17,25},{25,17},{2,10},{10... | collective-permute-start | bytes 393224 | tf_op jit(solution)/shard_map/ppermute | solution.py:147
  21.6 0.1 collective-permute-start.11
  21.7 0.0 collective-permute-done.9.refs_1_
  21.7 0.9 %collective-permute-done.10.refs_2_ = bf16[2,32,1024]{2,1,0:T(8,128)(2,1)S(1)} collective-permute-done((bf16[2,32,1024]{2,1,0:T(8,128)(2,1)S(1)}, bf16[2,32,1024]{2,1,0:T(8,128)(2,1)S(1)}, u32[]{:S(2)}, u32[]{:S(2)}) %collective-permute-start.10) | collective-permute-done | bytes 131104 | tf_op jit(solution)/shard_map/ppermute | solution.py:147
  22.6 0.0 collective-permute-done.8.refs_0_
  22.6 0.4 %collective-permute-done.11.refs_4_ = bf16[2,32,1024]{2,1,0:T(8,128)(2,1)S(1)} collective-permute-done((bf16[2,32,1024]{2,1,0:T(8,128)(2,1)S(1)}, bf16[2,32,1024]{2,1,0:T(8,128)(2,1)S(1)}, u32[]{:S(2)}, u32[]{:S(2)}) %collective-permute-start.11) | collective-permute-done | bytes 131104 | tf_op jit(solution)/shard_map/ppermute | solution.py:147
  23.0 1.0 %shard_map.51 = (f32[2,32,1024]{2,1,0:T(8,128)S(1)}, f32[2,32,1024]{2,1,0:T(8,128)S(1)}, f32[2,32,1024]{2,1,0:T(8,128)S(1)}, f32[2,32,1024]{2,1,0:T(8,128)S(1)}) custom-call(f32[2,128]{1,0:T(2,128)S(1)} %broadcast_in_dim.2.factors, bf16[256,1024]{1,0:T(8,128)(2,1)S(1)} %get-tuple-element.15.own, f32[2,128,1024]{2,1,0:T(8,128)S(1)} %get-tuple-element.17.acc, ...), custom_call_target="tpu_custom_call" | custom-call | flops 335544320 | bytes 3343360 | tf_op jit(solution)/shard_map/pallas_call | solution.py:116
  24.0 1.8 %collective-permute-start.14 = (f16[2,32,1024]{2,1,0:T(8,128)(2,1)S(1)}, f16[2,32,1024]{2,1,0:T(8,128)(2,1)S(1)}, u32[]{:S(2)}, u32[]{:S(2)}) collective-permute-start(f16[2,32,1024]{2,1,0:T(8,128)(2,1)S(1)} %convert_element_type.37), channel_id=1, source_target_pairs={{0,17},{1,16},{2,19},{3,18},{4,21},{5,20},{6,23},{7,22},{8,25},{9,... | collective-permute-start | bytes 393224 | tf_op jit(solution)/shard_map/ppermute | solution.py:177
  25.8 1.2 %collective-permute-start.13 = (f16[2,32,1024]{2,1,0:T(8,128)(2,1)S(1)}, f16[2,32,1024]{2,1,0:T(8,128)(2,1)S(1)}, u32[]{:S(2)}, u32[]{:S(2)}) collective-permute-start(f16[2,32,1024]{2,1,0:T(8,128)(2,1)S(1)} %convert_element_type.35), channel_id=1, source_target_pairs={{0,16},{1,17},{2,18},{3,19},{4,20},{5,21},{6,22},{7,23},{8,24},{9,... | collective-permute-start | bytes 393224 | tf_op jit(solution)/shard_map/ppermute | solution.py:177
  27.0 0.5 %collective-permute-start.12 = (f16[2,32,1024]{2,1,0:T(8,128)(2,1)S(1)}, f16[2,32,1024]{2,1,0:T(8,128)(2,1)S(1)}, u32[]{:S(2)}, u32[]{:S(2)}) collective-permute-start(f16[2,32,1024]{2,1,0:T(8,128)(2,1)S(1)} %convert_element_type.33), channel_id=1, source_target_pairs={{0,1},{1,0},{2,3},{3,2},{4,5},{5,4},{6,7},{7,6},{8,9},{9,8},{10,11... | collective-permute-start | bytes 393224 | tf_op jit(solution)/shard_map/ppermute | solution.py:177
  27.6 0.1 slice_reduce_fusion
  27.7 3.6 %collective-permute-done.14 = f16[2,32,1024]{2,1,0:T(8,128)(2,1)S(1)} collective-permute-done((f16[2,32,1024]{2,1,0:T(8,128)(2,1)S(1)}, f16[2,32,1024]{2,1,0:T(8,128)(2,1)S(1)}, u32[]{:S(2)}, u32[]{:S(2)}) %collective-permute-start.14) | collective-permute-done | bytes 131104 | tf_op jit(solution)/shard_map/ppermute | solution.py:177
  31.3 2.1 %collective-permute-done.13 = f16[2,32,1024]{2,1,0:T(8,128)(2,1)S(1)} collective-permute-done((f16[2,32,1024]{2,1,0:T(8,128)(2,1)S(1)}, f16[2,32,1024]{2,1,0:T(8,128)(2,1)S(1)}, u32[]{:S(2)}, u32[]{:S(2)}) %collective-permute-start.13) | collective-permute-done | bytes 131104 | tf_op jit(solution)/shard_map/ppermute | solution.py:177
  33.4 0.1 collective-permute-done.12
  33.5 0.8 %bitcast_multiply_fusion = (f32[32,1024]{1,0:T(8,128)}, f32[32,1024]{1,0:T(8,128)}) fusion(f32[2,32,1024]{2,1,0:T(8,128)S(1)} %get-tuple-element.21, f16[2,32,1024]{2,1,0:T(8,128)(2,1)S(1)} %collective-permute-done.14, f16[2,32,1024]{2,1,0:T(8,128)(2,1)S(1)} %collective-permute-done.13, f16[2,32,1024]{2,1,0:T(8,128)(2,1)S(1)} %collective-permute-done.12, ...), kind=kLoop, calls=%fused_computation.3 | loop fusion | flops 458752 | bytes 917632 | tf_op jit(solution)/shard_map/mul | solution.py:185
  (6 shorter events, 0.1 us)
Async XLA Ops:
  0.6 9.9 %collective-permute-start.3 = (bf16[32,1024]{1,0:T(8,128)(2,1)}, bf16[32,1024]{1,0:T(8,128)(2,1)S(1)}, u32[]{:S(2)}, u32[]{:S(2)}) collective-permute-start(bf16[32,1024]{1,0:T(8,128)(2,1)} %param.3), channel_id=1, source_target_pairs={{0,4},{1,5},{2,6},{3,7},{4,0},{5,1},{6,2},{7,3},{8,12},{9,13},{10,... | collective-permute-start | bytes 196616 | tf_op jit(solution)/shard_map/ppermute | solution.py:141
  4.7 6.5 %collective-permute-start.4 = (bf16[32,1024]{1,0:T(8,128)(2,1)}, bf16[32,1024]{1,0:T(8,128)(2,1)S(1)}, u32[]{:S(2)}, u32[]{:S(2)}) collective-permute-start(bf16[32,1024]{1,0:T(8,128)(2,1)} %param.4), channel_id=1, source_target_pairs={{0,4},{1,5},{2,6},{3,7},{4,0},{5,1},{6,2},{7,3},{8,12},{9,13},{10,... | collective-permute-start | bytes 196616 | tf_op jit(solution)/shard_map/ppermute | solution.py:141
  4.8 5.8 %copy-start = (f32[2]{0:T(128)S(1)}, f32[2]{0:T(128)}, u32[]{:S(2)}) copy-start(f32[2]{0:T(128)} %param.5) | copy-start | bytes 28
  5.7 14.3 %collective-permute-start.5 = (bf16[2,32,1024]{2,1,0:T(8,128)(2,1)S(1)}, bf16[2,32,1024]{2,1,0:T(8,128)(2,1)S(1)}, u32[]{:S(2)}, u32[]{:S(2)}) collective-permute-start(bf16[2,32,1024]{2,1,0:T(8,128)(2,1)S(1)} %pad_maximum_fusion.refs_0_.refs_4_), channel_id=1, source_target_pairs={{0,2},{1,3},{2,0},{3,1},{4,6},{5,7},{6,4},{7,5},{8,10},{9,11},{10,... | collective-permute-start | bytes 393224 | tf_op jit(solution)/shard_map/ppermute | solution.py:144
  7.6 12.4 %collective-permute-start.2 = (bf16[2,32,1024]{2,1,0:T(8,128)(2,1)S(1)}, bf16[2,32,1024]{2,1,0:T(8,128)(2,1)S(1)}, u32[]{:S(2)}, u32[]{:S(2)}) collective-permute-start(bf16[2,32,1024]{2,1,0:T(8,128)(2,1)S(1)} %pad_maximum_fusion.refs_0_.refs_4_), channel_id=1, source_target_pairs={{0,17},{1,16},{2,19},{3,18},{4,21},{5,20},{6,23},{7,22},{8,25},{9,... | collective-permute-start | bytes 393224 | tf_op jit(solution)/shard_map/ppermute | solution.py:136
  10.1 5.7 %collective-permute-start.1 = (bf16[2,32,1024]{2,1,0:T(8,128)(2,1)S(1)}, bf16[2,32,1024]{2,1,0:T(8,128)(2,1)S(1)}, u32[]{:S(2)}, u32[]{:S(2)}) collective-permute-start(bf16[2,32,1024]{2,1,0:T(8,128)(2,1)S(1)} %pad_maximum_fusion.refs_0_.refs_4_), channel_id=1, source_target_pairs={{0,16},{1,17},{2,18},{3,19},{4,20},{5,21},{6,22},{7,23},{8,24},{9,... | collective-permute-start | bytes 393224 | tf_op jit(solution)/shard_map/ppermute | solution.py:136
  10.6 9.5 %collective-permute-start = (bf16[2,32,1024]{2,1,0:T(8,128)(2,1)S(1)}, bf16[2,32,1024]{2,1,0:T(8,128)(2,1)S(1)}, u32[]{:S(2)}, u32[]{:S(2)}) collective-permute-start(bf16[2,32,1024]{2,1,0:T(8,128)(2,1)S(1)} %pad_maximum_fusion.refs_0_.refs_4_), channel_id=1, source_target_pairs={{0,1},{1,0},{2,3},{3,2},{4,5},{5,4},{6,7},{7,6},{8,9},{9,8},{10,11... | collective-permute-start | bytes 393224 | tf_op jit(solution)/shard_map/ppermute | solution.py:136
  11.2 5.0 %collective-permute-start.6 = (bf16[32,1024]{1,0:T(8,128)(2,1)S(1)}, bf16[32,1024]{1,0:T(8,128)(2,1)S(1)}, u32[]{:S(2)}, u32[]{:S(2)}) collective-permute-start(bf16[32,1024]{1,0:T(8,128)(2,1)S(1)} %collective-permute-done.3), channel_id=1, source_target_pairs={{0,2},{1,3},{2,0},{3,1},{4,6},{5,7},{6,4},{7,5},{8,10},{9,11},{10,... | collective-permute-start | bytes 196616 | tf_op jit(solution)/shard_map/ppermute | solution.py:141
  15.7 4.3 %collective-permute-start.7 = (bf16[32,1024]{1,0:T(8,128)(2,1)S(1)}, bf16[32,1024]{1,0:T(8,128)(2,1)S(1)}, u32[]{:S(2)}, u32[]{:S(2)}) collective-permute-start(bf16[32,1024]{1,0:T(8,128)(2,1)S(1)} %collective-permute-done.4), channel_id=1, source_target_pairs={{0,2},{1,3},{2,0},{3,1},{4,6},{5,7},{6,4},{7,5},{8,10},{9,11},{10,... | collective-permute-start | bytes 196616 | tf_op jit(solution)/shard_map/ppermute | solution.py:141
  16.2 5.5 %collective-permute-start.9 = (bf16[2,32,1024]{2,1,0:T(8,128)(2,1)S(1)}, bf16[2,32,1024]{2,1,0:T(8,128)(2,1)S(1)}, u32[]{:S(2)}, u32[]{:S(2)}) collective-permute-start(bf16[2,32,1024]{2,1,0:T(8,128)(2,1)S(1)} %pad_maximum_fusion.1.refs_5_), channel_id=1, source_target_pairs={{0,8},{8,0},{16,24},{24,16},{1,9},{9,1},{17,25},{25,17},{2,10},{10... | collective-permute-start | bytes 393224 | tf_op jit(solution)/shard_map/ppermute | solution.py:147
  20.0 2.6 %collective-permute-start.8 = (bf16[2,32,1024]{2,1,0:T(8,128)(2,1)S(1)}, bf16[2,32,1024]{2,1,0:T(8,128)(2,1)S(1)}, u32[]{:S(2)}, u32[]{:S(2)}) collective-permute-start(bf16[2,32,1024]{2,1,0:T(8,128)(2,1)S(1)} %pad_maximum_fusion.refs_0_.refs_4_), channel_id=1, source_target_pairs={{0,8},{8,0},{16,24},{24,16},{1,9},{9,1},{17,25},{25,17},{2,10},{10... | collective-permute-start | bytes 393224 | tf_op jit(solution)/shard_map/ppermute | solution.py:147
  21.0 1.6 %collective-permute-start.10 = (bf16[2,32,1024]{2,1,0:T(8,128)(2,1)S(1)}, bf16[2,32,1024]{2,1,0:T(8,128)(2,1)S(1)}, u32[]{:S(2)}, u32[]{:S(2)}) collective-permute-start(bf16[2,32,1024]{2,1,0:T(8,128)(2,1)S(1)} %collective-permute-done.5.refs_6_), channel_id=1, source_target_pairs={{0,8},{8,0},{16,24},{24,16},{1,9},{9,1},{17,25},{25,17},{2,10},{10... | collective-permute-start | bytes 393224 | tf_op jit(solution)/shard_map/ppermute | solution.py:147
  21.6 1.3 %collective-permute-start.11 = (bf16[2,32,1024]{2,1,0:T(8,128)(2,1)S(1)}, bf16[2,32,1024]{2,1,0:T(8,128)(2,1)S(1)}, u32[]{:S(2)}, u32[]{:S(2)}) collective-permute-start(bf16[2,32,1024]{2,1,0:T(8,128)(2,1)S(1)} %pad_maximum_fusion.2.refs_3_), channel_id=1, source_target_pairs={{0,8},{8,0},{16,24},{24,16},{1,9},{9,1},{17,25},{25,17},{2,10},{10... | collective-permute-start | bytes 393224 | tf_op jit(solution)/shard_map/ppermute | solution.py:147
  24.0 7.3 %collective-permute-start.14 = (f16[2,32,1024]{2,1,0:T(8,128)(2,1)S(1)}, f16[2,32,1024]{2,1,0:T(8,128)(2,1)S(1)}, u32[]{:S(2)}, u32[]{:S(2)}) collective-permute-start(f16[2,32,1024]{2,1,0:T(8,128)(2,1)S(1)} %convert_element_type.37), channel_id=1, source_target_pairs={{0,17},{1,16},{2,19},{3,18},{4,21},{5,20},{6,23},{7,22},{8,25},{9,... | collective-permute-start | bytes 393224 | tf_op jit(solution)/shard_map/ppermute | solution.py:177
  25.8 7.5 %collective-permute-start.13 = (f16[2,32,1024]{2,1,0:T(8,128)(2,1)S(1)}, f16[2,32,1024]{2,1,0:T(8,128)(2,1)S(1)}, u32[]{:S(2)}, u32[]{:S(2)}) collective-permute-start(f16[2,32,1024]{2,1,0:T(8,128)(2,1)S(1)} %convert_element_type.35), channel_id=1, source_target_pairs={{0,16},{1,17},{2,18},{3,19},{4,20},{5,21},{6,22},{7,23},{8,24},{9,... | collective-permute-start | bytes 393224 | tf_op jit(solution)/shard_map/ppermute | solution.py:177
  27.0 6.4 %collective-permute-start.12 = (f16[2,32,1024]{2,1,0:T(8,128)(2,1)S(1)}, f16[2,32,1024]{2,1,0:T(8,128)(2,1)S(1)}, u32[]{:S(2)}, u32[]{:S(2)}) collective-permute-start(f16[2,32,1024]{2,1,0:T(8,128)(2,1)S(1)} %convert_element_type.33), channel_id=1, source_target_pairs={{0,1},{1,0},{2,3},{3,2},{4,5},{5,4},{6,7},{7,6},{8,9},{9,8},{10,11... | collective-permute-start | bytes 393224 | tf_op jit(solution)/shard_map/ppermute | solution.py:177

commit v9 on v7

--- a/solution.py
+++ b/solution.py
@@ -110,6 +110,25 @@
                 out[s, :, at] = grad[i * rows : (i + 1) * rows]
 
 
+def stack_kernel(images, texts, out, sems):
+    copies = [pltpu.make_async_copy(x, out.at[i], sems.at[i]) for i, x in enumerate((images, texts))]
+    for copy in copies:
+        copy.start()
+    for copy in copies:
+        copy.wait()
+
+
+def stack(images, texts):
+    return pl.pallas_call(
+        stack_kernel,
+        out_shape=jax.ShapeDtypeStruct((2, *images.shape), images.dtype),
+        in_specs=[pl.BlockSpec(memory_space=pltpu.HBM)] * 2,
+        out_specs=pl.BlockSpec(memory_space=pltpu.VMEM),
+        scratch_shapes=[pltpu.SemaphoreType.DMA((2,))],
+        compiler_params=pltpu.CompilerParams(vmem_limit_bytes=62 * 2**20),
+    )(images, texts)
+
+
 def call(kernel, operands, out_shape, flops):
     vmem = pl.BlockSpec(memory_space=pltpu.VMEM)
     moved = sum(x.size * x.dtype.itemsize for x in [*operands, *out_shape])
@@ -131,7 +150,7 @@
     factors = jnp.broadcast_to((loss_weights * (1.0 / math.sqrt(width * batch)))[:, None], (2, 128))
     both = ("row", "col")
     square = [(j, k) for j in range(halves(n_row)[0]) for k in range(halves(n_col)[1])][1:]
-    own = jnp.stack([images, texts])
+    own = stack(images, texts)
 
     mine = [own] + [lax.ppermute(own, both, square_shift(n_row, n_col, j, k)) for j, k in square]
 
@@ -167,7 +186,7 @@
     )
     back = [
         lax.ppermute(part.astype(jnp.float16), both, square_shift(n_row, n_col, -j, -k))
-        for part, (j, k) in zip(parts, square)
+        for part, (j, k) in reversed(list(zip(parts, square)))
     ]
     grads = []
     for s in range(2):

time: 29.8 us -> 31.8 us (1.067)
  Pallas kernels: 1.88 us -> 3.42 us
  local copies, waits for them, and re-layouts: 0.18 us -> 1.09 us
  other arithmetic: 1.73 us -> 0.84 us
  starting transfers between devices: 13.6 us -> 14 us
    pallas_call x0 -> x1, Pallas kernels: none -> 1.55 us  [stack(): pl.pallas_call(stack_kernel, out_shape=jax.ShapeDtypeStruct((2, *images.s...]
    unnamed x2 -> x4, local copies, waits for them, and re-layouts: 0.01 us -> 0.91 us
    another operation x1 -> x0, other arithmetic: 0.89 us -> none  [local(): own = jnp.stack([images, texts])]
    ppermute x3, waiting for transfers between devices: 5.8 us -> 6.17 us  [local(): lax.ppermute(part.astype(jnp.float16), both, square_shift(n_row, n_col, -...]
    ppermute x4, starting transfers between devices: 0.23 us -> 0.56 us  [pair(): lax.ppermute(block, 'row', inner_shift(n_row, k))]
  transfers between devices with their start and end apart: 13 -> 13, of which waited for: 9 -> 7; matrix products, arithmetic and copies ran while one was open for 1% -> 1% of each run, Pallas kernels for 3% -> 3%
where the time goes in v9:
time: 31.8 us; the launch traced here: 31.6 us
  starting transfers between devices  14 us (44%)
  waiting for transfers between devices  11.5 us (36%)
  Pallas kernels  3.42 us (11%)
  local copies, waits for them, and re-layouts  1.09 us (3%)
  other arithmetic  0.84 us (3%)
  between operations  0.72 us (2%)
    ppermute x3, starting transfers between devices, local(): line.append(lax.ppermute(line[which], 'col', perm))  6.4 us
    ppermute x3, waiting for transfers between devices, local(): lax.ppermute(part.astype(jnp.float16), both, square_shift(n_row, n_col, -...  6.17 us
    ppermute x3, starting transfers between devices, local(): lax.ppermute(part.astype(jnp.float16), both, square_shift(n_row, n_col, -...  3.57 us
    ppermute x3, starting transfers between devices, local(): lax.ppermute(own, both, square_shift(n_row, n_col, j, k))  3.49 us
    ppermute x3, waiting for transfers between devices, local(): lax.ppermute(own, both, square_shift(n_row, n_col, j, k))  2.82 us
    pallas_call x2, Pallas kernels, call(): pl.pallas_call(kernel, out_shape=out_shape, in_specs=[vmem] * len(operand...  1.87 us
    ppermute x3, waiting for transfers between devices, local(): line.append(lax.ppermute(line[which], 'col', perm))  1.56 us
    pallas_call x1, Pallas kernels, stack(): pl.pallas_call(stack_kernel, out_shape=jax.ShapeDtypeStruct((2, *images.s...  1.55 us
  transfers between devices with their start and end apart: 13, of which 7 were waited for; matrix products, arithmetic and copies ran while one was open for 1% of the time, Pallas kernels for 3%

profile of v9, /device:TPU:0, one launch (start us, length us, event | category | flops | bytes accessed | tf_op | source)
XLA Modules:
  0.0 31.6 jit_solution(1310979120128931989)
XLA Ops:
  0.6 0.0 copy-start.1
  0.6 1.5 %shard_map.50.refs_0_.refs_4_ = bf16[2,32,1024]{2,1,0:T(8,128)(2,1)} custom-call(bf16[32,1024]{1,0:T(8,128)(2,1)} %images.1, bf16[32,1024]{1,0:T(8,128)(2,1)} %texts.1), custom_call_target="tpu_custom_call" | custom-call | tf_op jit(solution)/shard_map/pallas_call | solution.py:122
  2.2 4.1 %collective-permute-start.3 = (bf16[2,32,1024]{2,1,0:T(8,128)(2,1)}, bf16[2,32,1024]{2,1,0:T(8,128)(2,1)S(1)}, u32[]{:S(2)}, u32[]{:S(2)}) collective-permute-start(bf16[2,32,1024]{2,1,0:T(8,128)(2,1)} %shard_map.50.refs_0_.refs_4_), channel_id=1, source_target_pairs={{0,4},{1,5},{2,6},{3,7},{4,0},{5,1},{6,2},{7,3},{8,12},{9,13},{10,... | collective-permute-start | bytes 393224 | tf_op jit(solution)/shard_map/ppermute | solution.py:159
  6.3 1.6 %collective-permute-start.4 = (bf16[2,32,1024]{2,1,0:T(8,128)(2,1)}, bf16[2,32,1024]{2,1,0:T(8,128)(2,1)S(1)}, u32[]{:S(2)}, u32[]{:S(2)}) collective-permute-start(bf16[2,32,1024]{2,1,0:T(8,128)(2,1)} %shard_map.50.refs_0_.refs_4_), channel_id=1, source_target_pairs={{0,2},{1,3},{2,0},{3,1},{4,6},{5,7},{6,4},{7,5},{8,10},{9,11},{10,... | collective-permute-start | bytes 393224 | tf_op jit(solution)/shard_map/ppermute | solution.py:159
  7.9 2.4 %collective-permute-start.2 = (bf16[2,32,1024]{2,1,0:T(8,128)(2,1)}, bf16[2,32,1024]{2,1,0:T(8,128)(2,1)S(1)}, u32[]{:S(2)}, u32[]{:S(2)}) collective-permute-start(bf16[2,32,1024]{2,1,0:T(8,128)(2,1)} %shard_map.50.refs_0_.refs_4_), channel_id=1, source_target_pairs={{0,17},{1,16},{2,19},{3,18},{4,21},{5,20},{6,23},{7,22},{8,25},{9,... | collective-permute-start | bytes 393224 | tf_op jit(solution)/shard_map/ppermute | solution.py:155
  10.3 0.5 %collective-permute-start.1 = (bf16[2,32,1024]{2,1,0:T(8,128)(2,1)}, bf16[2,32,1024]{2,1,0:T(8,128)(2,1)S(1)}, u32[]{:S(2)}, u32[]{:S(2)}) collective-permute-start(bf16[2,32,1024]{2,1,0:T(8,128)(2,1)} %shard_map.50.refs_0_.refs_4_), channel_id=1, source_target_pairs={{0,16},{1,17},{2,18},{3,19},{4,20},{5,21},{6,22},{7,23},{8,24},{9,... | collective-permute-start | bytes 393224 | tf_op jit(solution)/shard_map/ppermute | solution.py:155
  10.8 0.5 %collective-permute-start = (bf16[2,32,1024]{2,1,0:T(8,128)(2,1)}, bf16[2,32,1024]{2,1,0:T(8,128)(2,1)S(1)}, u32[]{:S(2)}, u32[]{:S(2)}) collective-permute-start(bf16[2,32,1024]{2,1,0:T(8,128)(2,1)} %shard_map.50.refs_0_.refs_4_), channel_id=1, source_target_pairs={{0,1},{1,0},{2,3},{3,2},{4,5},{5,4},{6,7},{7,6},{8,9},{9,8},{10,11... | collective-permute-start | bytes 393224 | tf_op jit(solution)/shard_map/ppermute | solution.py:155
  11.4 1.6 %collective-permute-done.3.refs_5_ = bf16[2,32,1024]{2,1,0:T(8,128)(2,1)S(1)} collective-permute-done((bf16[2,32,1024]{2,1,0:T(8,128)(2,1)}, bf16[2,32,1024]{2,1,0:T(8,128)(2,1)S(1)}, u32[]{:S(2)}, u32[]{:S(2)}) %collective-permute-start.3) | collective-permute-done | bytes 131104 | tf_op jit(solution)/shard_map/ppermute | solution.py:159
  12.9 0.7 %collective-permute-start.5 = (bf16[2,32,1024]{2,1,0:T(8,128)(2,1)S(1)}, bf16[2,32,1024]{2,1,0:T(8,128)(2,1)S(1)}, u32[]{:S(2)}, u32[]{:S(2)}) collective-permute-start(bf16[2,32,1024]{2,1,0:T(8,128)(2,1)S(1)} %collective-permute-done.3.refs_5_), channel_id=1, source_target_pairs={{0,2},{1,3},{2,0},{3,1},{4,6},{5,7},{6,4},{7,5},{8,10},{9,11},{10,... | collective-permute-start | bytes 393224 | tf_op jit(solution)/shard_map/ppermute | solution.py:159
  13.6 0.0 copy-done.1
  13.6 0.0 collective-permute-done.4.refs_6_
  13.7 0.1 collective-permute-start.6
  13.7 0.9 %collective-permute-done.2.refs_3_ = bf16[2,32,1024]{2,1,0:T(8,128)(2,1)S(1)} collective-permute-done((bf16[2,32,1024]{2,1,0:T(8,128)(2,1)}, bf16[2,32,1024]{2,1,0:T(8,128)(2,1)S(1)}, u32[]{:S(2)}, u32[]{:S(2)}) %collective-permute-start.2) | collective-permute-done | bytes 131104 | tf_op jit(solution)/shard_map/ppermute | solution.py:155
  14.6 0.0 collective-permute-start.7
  14.6 1.8 %collective-permute-done.1.refs_2_ = bf16[2,32,1024]{2,1,0:T(8,128)(2,1)S(1)} collective-permute-done((bf16[2,32,1024]{2,1,0:T(8,128)(2,1)}, bf16[2,32,1024]{2,1,0:T(8,128)(2,1)S(1)}, u32[]{:S(2)}, u32[]{:S(2)}) %collective-permute-start.1) | collective-permute-done | bytes 131104 | tf_op jit(solution)/shard_map/ppermute | solution.py:155
  16.5 0.0 collective-permute-start.8
  16.5 0.1 collective-permute-done.refs_1_
  16.6 0.1 broadcast_in_dim.2.factors
  16.6 0.0 copy-start
  16.6 0.9 %copy-done = bf16[2,32,1024]{2,1,0:T(8,128)(2,1)S(1)} copy-done((bf16[2,32,1024]{2,1,0:T(8,128)(2,1)S(1)}, bf16[2,32,1024]{2,1,0:T(8,128)(2,1)}, u32[]{:S(2)}) %copy-start) | copy-done | bytes 131096
  17.5 0.9 %shard_map.51 = (bf16[256,1024]{1,0:T(8,128)(2,1)S(1)}, f32[2,128,1024]{2,1,0:T(8,128)S(1)}, f32[128,128]{1,0:T(8,128)S(1)}, f32[32,128]{1,0:T(8,128)S(1)}) custom-call(f32[2,128]{1,0:T(2,128)S(1)} %broadcast_in_dim.2.factors, bf16[2,32,1024]{2,1,0:T(8,128)(2,1)S(1)} %copy-done, bf16[2,32,1024]{2,1,0:T(8,128)(2,1)S(1)} %collective-permute-done.refs_1_, ...), custom_call_target="tpu_custom_call" | custom-call | flops 201326592 | bytes 2573312 | tf_op jit(solution)/shard_map/pallas_call | solution.py:135
  18.5 0.0 collective-permute-done.5.refs_3_
  18.5 0.5 %collective-permute-start.9 = (bf16[2,32,1024]{2,1,0:T(8,128)(2,1)S(1)}, bf16[2,32,1024]{2,1,0:T(8,128)(2,1)S(1)}, u32[]{:S(2)}, u32[]{:S(2)}) collective-permute-start(bf16[2,32,1024]{2,1,0:T(8,128)(2,1)S(1)} %collective-permute-done.5.refs_3_), channel_id=1, source_target_pairs={{0,8},{8,0},{16,24},{24,16},{1,9},{9,1},{17,25},{25,17},{2,10},{10... | collective-permute-start | bytes 393224 | tf_op jit(solution)/shard_map/ppermute | solution.py:162
  18.9 0.0 collective-permute-done.6.refs_0_
  19.0 0.0 collective-permute-done.8.refs_2_
  19.0 0.0 collective-permute-done.7.refs_1_
  19.0 1.0 %collective-permute-done.9.refs_4_ = bf16[2,32,1024]{2,1,0:T(8,128)(2,1)S(1)} collective-permute-done((bf16[2,32,1024]{2,1,0:T(8,128)(2,1)S(1)}, bf16[2,32,1024]{2,1,0:T(8,128)(2,1)S(1)}, u32[]{:S(2)}, u32[]{:S(2)}) %collective-permute-start.9) | collective-permute-done | bytes 131104 | tf_op jit(solution)/shard_map/ppermute | solution.py:162
  19.9 1.0 %shard_map.52 = (f32[2,32,1024]{2,1,0:T(8,128)S(1)}, f32[2,32,1024]{2,1,0:T(8,128)S(1)}, f32[2,32,1024]{2,1,0:T(8,128)S(1)}, f32[2,32,1024]{2,1,0:T(8,128)S(1)}) custom-call(f32[2,128]{1,0:T(2,128)S(1)} %broadcast_in_dim.2.factors, bf16[256,1024]{1,0:T(8,128)(2,1)S(1)} %get-tuple-element.12.own, f32[2,128,1024]{2,1,0:T(8,128)S(1)} %get-tuple-element.14.acc, ...), custom_call_target="tpu_custom_call" | custom-call | flops 335544320 | bytes 3343360 | tf_op jit(solution)/shard_map/pallas_call | solution.py:135
  21.0 1.6 %collective-permute-start.12 = (f16[2,32,1024]{2,1,0:T(8,128)(2,1)S(1)}, f16[2,32,1024]{2,1,0:T(8,128)(2,1)S(1)}, u32[]{:S(2)}, u32[]{:S(2)}) collective-permute-start(f16[2,32,1024]{2,1,0:T(8,128)(2,1)S(1)} %convert_element_type.37), channel_id=1, source_target_pairs={{0,1},{1,0},{2,3},{3,2},{4,5},{5,4},{6,7},{7,6},{8,9},{9,8},{10,11... | collective-permute-start | bytes 393224 | tf_op jit(solution)/shard_map/ppermute | solution.py:188
  22.6 0.9 %collective-permute-start.11 = (f16[2,32,1024]{2,1,0:T(8,128)(2,1)S(1)}, f16[2,32,1024]{2,1,0:T(8,128)(2,1)S(1)}, u32[]{:S(2)}, u32[]{:S(2)}) collective-permute-start(f16[2,32,1024]{2,1,0:T(8,128)(2,1)S(1)} %convert_element_type.35), channel_id=1, source_target_pairs={{0,16},{1,17},{2,18},{3,19},{4,20},{5,21},{6,22},{7,23},{8,24},{9,... | collective-permute-start | bytes 393224 | tf_op jit(solution)/shard_map/ppermute | solution.py:188
  23.4 1.1 %collective-permute-start.10 = (f16[2,32,1024]{2,1,0:T(8,128)(2,1)S(1)}, f16[2,32,1024]{2,1,0:T(8,128)(2,1)S(1)}, u32[]{:S(2)}, u32[]{:S(2)}) collective-permute-start(f16[2,32,1024]{2,1,0:T(8,128)(2,1)S(1)} %convert_element_type.33), channel_id=1, source_target_pairs={{0,17},{1,16},{2,19},{3,18},{4,21},{5,20},{6,23},{7,22},{8,25},{9,... | collective-permute-start | bytes 393224 | tf_op jit(solution)/shard_map/ppermute | solution.py:188
  24.5 0.1 slice_reduce_fusion
  24.7 2.5 %collective-permute-done.12 = f16[2,32,1024]{2,1,0:T(8,128)(2,1)S(1)} collective-permute-done((f16[2,32,1024]{2,1,0:T(8,128)(2,1)S(1)}, f16[2,32,1024]{2,1,0:T(8,128)(2,1)S(1)}, u32[]{:S(2)}, u32[]{:S(2)}) %collective-permute-start.12) | collective-permute-done | bytes 131104 | tf_op jit(solution)/shard_map/ppermute | solution.py:188
  27.2 3.7 %collective-permute-done.11 = f16[2,32,1024]{2,1,0:T(8,128)(2,1)S(1)} collective-permute-done((f16[2,32,1024]{2,1,0:T(8,128)(2,1)S(1)}, f16[2,32,1024]{2,1,0:T(8,128)(2,1)S(1)}, u32[]{:S(2)}, u32[]{:S(2)}) %collective-permute-start.11) | collective-permute-done | bytes 131104 | tf_op jit(solution)/shard_map/ppermute | solution.py:188
  30.8 0.0 collective-permute-done.10
  30.8 0.8 %bitcast_multiply_fusion = (f32[32,1024]{1,0:T(8,128)}, f32[32,1024]{1,0:T(8,128)}) fusion(f32[2,32,1024]{2,1,0:T(8,128)S(1)} %get-tuple-element.17, f16[2,32,1024]{2,1,0:T(8,128)(2,1)S(1)} %collective-permute-done.12, f16[2,32,1024]{2,1,0:T(8,128)(2,1)S(1)} %collective-permute-done.11, f16[2,32,1024]{2,1,0:T(8,128)(2,1)S(1)} %collective-permute-done.10, ...), kind=kLoop, calls=%fused_computation | loop fusion | flops 458752 | bytes 917632 | tf_op jit(solution)/shard_map/mul | solution.py:196
  (4 shorter events, 0.1 us)
Async XLA Ops:
  0.6 13.0 %copy-start.1 = (f32[2]{0:T(128)S(1)}, f32[2]{0:T(128)}, u32[]{:S(2)}) copy-start(f32[2]{0:T(128)} %param.5) | copy-start | bytes 28
  2.2 10.7 %collective-permute-start.3 = (bf16[2,32,1024]{2,1,0:T(8,128)(2,1)}, bf16[2,32,1024]{2,1,0:T(8,128)(2,1)S(1)}, u32[]{:S(2)}, u32[]{:S(2)}) collective-permute-start(bf16[2,32,1024]{2,1,0:T(8,128)(2,1)} %shard_map.50.refs_0_.refs_4_), channel_id=1, source_target_pairs={{0,4},{1,5},{2,6},{3,7},{4,0},{5,1},{6,2},{7,3},{8,12},{9,13},{10,... | collective-permute-start | bytes 393224 | tf_op jit(solution)/shard_map/ppermute | solution.py:159
  6.3 7.4 %collective-permute-start.4 = (bf16[2,32,1024]{2,1,0:T(8,128)(2,1)}, bf16[2,32,1024]{2,1,0:T(8,128)(2,1)S(1)}, u32[]{:S(2)}, u32[]{:S(2)}) collective-permute-start(bf16[2,32,1024]{2,1,0:T(8,128)(2,1)} %shard_map.50.refs_0_.refs_4_), channel_id=1, source_target_pairs={{0,2},{1,3},{2,0},{3,1},{4,6},{5,7},{6,4},{7,5},{8,10},{9,11},{10,... | collective-permute-start | bytes 393224 | tf_op jit(solution)/shard_map/ppermute | solution.py:159
  7.9 6.8 %collective-permute-start.2 = (bf16[2,32,1024]{2,1,0:T(8,128)(2,1)}, bf16[2,32,1024]{2,1,0:T(8,128)(2,1)S(1)}, u32[]{:S(2)}, u32[]{:S(2)}) collective-permute-start(bf16[2,32,1024]{2,1,0:T(8,128)(2,1)} %shard_map.50.refs_0_.refs_4_), channel_id=1, source_target_pairs={{0,17},{1,16},{2,19},{3,18},{4,21},{5,20},{6,23},{7,22},{8,25},{9,... | collective-permute-start | bytes 393224 | tf_op jit(solution)/shard_map/ppermute | solution.py:155
  10.3 6.1 %collective-permute-start.1 = (bf16[2,32,1024]{2,1,0:T(8,128)(2,1)}, bf16[2,32,1024]{2,1,0:T(8,128)(2,1)S(1)}, u32[]{:S(2)}, u32[]{:S(2)}) collective-permute-start(bf16[2,32,1024]{2,1,0:T(8,128)(2,1)} %shard_map.50.refs_0_.refs_4_), channel_id=1, source_target_pairs={{0,16},{1,17},{2,18},{3,19},{4,20},{5,21},{6,22},{7,23},{8,24},{9,... | collective-permute-start | bytes 393224 | tf_op jit(solution)/shard_map/ppermute | solution.py:155
  10.8 5.7 %collective-permute-start = (bf16[2,32,1024]{2,1,0:T(8,128)(2,1)}, bf16[2,32,1024]{2,1,0:T(8,128)(2,1)S(1)}, u32[]{:S(2)}, u32[]{:S(2)}) collective-permute-start(bf16[2,32,1024]{2,1,0:T(8,128)(2,1)} %shard_map.50.refs_0_.refs_4_), channel_id=1, source_target_pairs={{0,1},{1,0},{2,3},{3,2},{4,5},{5,4},{6,7},{7,6},{8,9},{9,8},{10,11... | collective-permute-start | bytes 393224 | tf_op jit(solution)/shard_map/ppermute | solution.py:155
  12.9 5.5 %collective-permute-start.5 = (bf16[2,32,1024]{2,1,0:T(8,128)(2,1)S(1)}, bf16[2,32,1024]{2,1,0:T(8,128)(2,1)S(1)}, u32[]{:S(2)}, u32[]{:S(2)}) collective-permute-start(bf16[2,32,1024]{2,1,0:T(8,128)(2,1)S(1)} %collective-permute-done.3.refs_5_), channel_id=1, source_target_pairs={{0,2},{1,3},{2,0},{3,1},{4,6},{5,7},{6,4},{7,5},{8,10},{9,11},{10,... | collective-permute-start | bytes 393224 | tf_op jit(solution)/shard_map/ppermute | solution.py:159
  13.7 5.3 %collective-permute-start.6 = (bf16[2,32,1024]{2,1,0:T(8,128)(2,1)}, bf16[2,32,1024]{2,1,0:T(8,128)(2,1)S(1)}, u32[]{:S(2)}, u32[]{:S(2)}) collective-permute-start(bf16[2,32,1024]{2,1,0:T(8,128)(2,1)} %shard_map.50.refs_0_.refs_4_), channel_id=1, source_target_pairs={{0,8},{8,0},{16,24},{24,16},{1,9},{9,1},{17,25},{25,17},{2,10},{10... | collective-permute-start | bytes 393224 | tf_op jit(solution)/shard_map/ppermute | solution.py:162
  14.6 4.3 %collective-permute-start.7 = (bf16[2,32,1024]{2,1,0:T(8,128)(2,1)S(1)}, bf16[2,32,1024]{2,1,0:T(8,128)(2,1)S(1)}, u32[]{:S(2)}, u32[]{:S(2)}) collective-permute-start(bf16[2,32,1024]{2,1,0:T(8,128)(2,1)S(1)} %collective-permute-done.3.refs_5_), channel_id=1, source_target_pairs={{0,8},{8,0},{16,24},{24,16},{1,9},{9,1},{17,25},{25,17},{2,10},{10... | collective-permute-start | bytes 393224 | tf_op jit(solution)/shard_map/ppermute | solution.py:162
  16.5 2.5 %collective-permute-start.8 = (bf16[2,32,1024]{2,1,0:T(8,128)(2,1)S(1)}, bf16[2,32,1024]{2,1,0:T(8,128)(2,1)S(1)}, u32[]{:S(2)}, u32[]{:S(2)}) collective-permute-start(bf16[2,32,1024]{2,1,0:T(8,128)(2,1)S(1)} %collective-permute-done.4.refs_6_), channel_id=1, source_target_pairs={{0,8},{8,0},{16,24},{24,16},{1,9},{9,1},{17,25},{25,17},{2,10},{10... | collective-permute-start | bytes 393224 | tf_op jit(solution)/shard_map/ppermute | solution.py:162
  16.6 0.9 %copy-start = (bf16[2,32,1024]{2,1,0:T(8,128)(2,1)S(1)}, bf16[2,32,1024]{2,1,0:T(8,128)(2,1)}, u32[]{:S(2)}) copy-start(bf16[2,32,1024]{2,1,0:T(8,128)(2,1)} %shard_map.50.refs_0_.refs_4_) | copy-start | bytes 393220
  18.5 1.5 %collective-permute-start.9 = (bf16[2,32,1024]{2,1,0:T(8,128)(2,1)S(1)}, bf16[2,32,1024]{2,1,0:T(8,128)(2,1)S(1)}, u32[]{:S(2)}, u32[]{:S(2)}) collective-permute-start(bf16[2,32,1024]{2,1,0:T(8,128)(2,1)S(1)} %collective-permute-done.5.refs_3_), channel_id=1, source_target_pairs={{0,8},{8,0},{16,24},{24,16},{1,9},{9,1},{17,25},{25,17},{2,10},{10... | collective-permute-start | bytes 393224 | tf_op jit(solution)/shard_map/ppermute | solution.py:162
  21.0 6.2 %collective-permute-start.12 = (f16[2,32,1024]{2,1,0:T(8,128)(2,1)S(1)}, f16[2,32,1024]{2,1,0:T(8,128)(2,1)S(1)}, u32[]{:S(2)}, u32[]{:S(2)}) collective-permute-start(f16[2,32,1024]{2,1,0:T(8,128)(2,1)S(1)} %convert_element_type.37), channel_id=1, source_target_pairs={{0,1},{1,0},{2,3},{3,2},{4,5},{5,4},{6,7},{7,6},{8,9},{9,8},{10,11... | collective-permute-start | bytes 393224 | tf_op jit(solution)/shard_map/ppermute | solution.py:188
  22.6 8.3 %collective-permute-start.11 = (f16[2,32,1024]{2,1,0:T(8,128)(2,1)S(1)}, f16[2,32,1024]{2,1,0:T(8,128)(2,1)S(1)}, u32[]{:S(2)}, u32[]{:S(2)}) collective-permute-start(f16[2,32,1024]{2,1,0:T(8,128)(2,1)S(1)} %convert_element_type.35), channel_id=1, source_target_pairs={{0,16},{1,17},{2,18},{3,19},{4,20},{5,21},{6,22},{7,23},{8,24},{9,... | collective-permute-start | bytes 393224 | tf_op jit(solution)/shard_map/ppermute | solution.py:188
  23.4 7.4 %collective-permute-start.10 = (f16[2,32,1024]{2,1,0:T(8,128)(2,1)S(1)}, f16[2,32,1024]{2,1,0:T(8,128)(2,1)S(1)}, u32[]{:S(2)}, u32[]{:S(2)}) collective-permute-start(f16[2,32,1024]{2,1,0:T(8,128)(2,1)S(1)} %convert_element_type.33), channel_id=1, source_target_pairs={{0,17},{1,16},{2,19},{3,18},{4,21},{5,20},{6,23},{7,22},{8,25},{9,... | collective-permute-start | bytes 393224 | tf_op jit(solution)/shard_map/ppermute | solution.py:188

commit v10 on v7

--- a/solution.py
+++ b/solution.py
@@ -74,13 +74,10 @@
     return [slice(i, i + step) for i in range(0, width, step)]
 
 
-def tile_grads(p_mat, q_mat, keys, at):
-    m = keys.shape[0] // 2
-    img, txt = keys[:m, at], keys[m:, at]
-    nn = ((1,), (0,))
-    grad_img = dot(jnp.concatenate([q_mat, p_mat], axis=1), jnp.concatenate([img, txt]), nn)
-    grad_txt = dot(jnp.concatenate([-p_mat, -q_mat], axis=1), jnp.concatenate([img, txt]), nn)
-    return grad_img, grad_txt
+def spread(p_mat, q_mat):
+    return jnp.concatenate(
+        [jnp.concatenate([q_mat, p_mat], axis=1), jnp.concatenate([-p_mat, -q_mat], axis=1)], axis=0
+    )
 
 
 def early_kernel(total, n, factors, *refs):
@@ -88,26 +85,45 @@
     rows = join(refs[:n])
     own[...] = rows
     keys = join(refs[n:-4])
-    p_mat, q_mat = weigh(rows, keys, factors)
+    mix = spread(*weigh(rows, keys, factors))
     for at in tiles(keys.shape[1]):
-        acc[0, :, at], acc[1, :, at] = tile_grads(p_mat, q_mat, keys, at)
+        acc[:, at] = dot(mix, keys[:, at], ((1,), (0,)))
     size = jnp.sum(jnp.abs(rows.astype(jnp.float32)), axis=1, keepdims=True)
-    size = size[: size.shape[0] // 2] + size[size.shape[0] // 2 :]
+    half = size.shape[0] // 2
+    size = size[:half] + size[half:]
     most = size * ((factors[0:1, 0:1] + factors[1:2, 0:1]) * (1.02 * LIMIT * LIMIT * total)) + 1e-30
-    up[...] = jnp.broadcast_to(TOP / most, up.shape)
+    for s in range(2):
+        up[s * half : (s + 1) * half] = jnp.broadcast_to(TOP / most, (half, up.shape[1]))
     down[...] = jnp.broadcast_to((most / TOP)[: down.shape[0]], down.shape)
 
 
-def late_kernel(n, factors, own, acc, up, *refs):
-    outs = refs[-n:]
-    keys = join(refs[:-n])
-    p_mat, q_mat = weigh(own[...], keys, factors)
-    rows = outs[0].shape[1]
+def member(n_row, n_col, j=0, k=0):
+    (r_outer, r_inner), (_, c_inner) = halves(n_row), halves(n_col)
+    at_row, at_col = lax.axis_index("row") // r_inner, lax.axis_index("col") % c_inner
+    return (at_row + r_outer - j) % r_outer * c_inner + (at_col + c_inner - k) % c_inner
+
+
+def squares(n_row, n_col):
+    (r_outer, r_inner), (c_outer, c_inner) = halves(n_row), halves(n_col)
+    return [
+        [(j * r_inner + r) * n_col + c * c_inner + k for j in range(r_outer) for k in range(c_inner)]
+        for r in range(r_inner)
+        for c in range(c_outer)
+    ]
+
+
+def late_kernel(places, factors, own, acc, up, *refs):
+    out = refs[-1]
+    n = out.shape[0]
+    keys = join(refs[:-1])
+    slots = [place() for place in places]
+    mix = spread(*weigh(own[...], keys, factors))
+    rows = out.shape[2]
     for at in tiles(keys.shape[1]):
-        for s, grad in enumerate(tile_grads(p_mat, q_mat, keys, at)):
-            grad = (grad + acc[s, :, at]) * up[:, :1]
-            for i, out in enumerate(outs):
-                out[s, :, at] = grad[i * rows : (i + 1) * rows]
+        grad = (dot(mix, keys[:, at], ((1,), (0,))) + acc[:, at]) * up[:, :1]
+        for s in range(2):
+            for i, slot in enumerate(slots):
+                out[slot, s, :, at] = grad[(s * n + i) * rows : (s * n + i + 1) * rows]
 
 
 def call(kernel, operands, out_shape, flops):
@@ -154,26 +170,24 @@
         functools.partial(early_kernel, total, len(mine)),
         [factors] + mine + early,
         [jax.ShapeDtypeStruct((2 * many, width), images.dtype)]
-        + [jax.ShapeDtypeStruct(s, f32) for s in [(2, many, width), (many, 128), (rows, 128)]],
+        + [jax.ShapeDtypeStruct(s, f32) for s in [(2 * many, width), (2 * many, 128), (rows, 128)]],
         flops(early),
     )
     last, acc = lax.optimization_barrier((line[-1], acc))
     late = copies + [last] + pair(last)
-    first, *parts = call(
-        functools.partial(late_kernel, len(mine)),
+    places = [functools.partial(member, n_row, n_col, j, k) for j, k in [(0, 0), *square]]
+    (parts,) = call(
+        functools.partial(late_kernel, places),
         [factors, joined, acc, up] + late,
-        [jax.ShapeDtypeStruct((2, rows, width), f32)] * len(mine),
+        [jax.ShapeDtypeStruct((len(mine), 2, rows, width), f32)],
         flops(late),
     )
-    back = [
-        lax.ppermute(part.astype(jnp.float16), both, square_shift(n_row, n_col, -j, -k))
-        for part, (j, k) in zip(parts, square)
-    ]
+    back = lax.all_to_all(parts.astype(jnp.float16), both, 0, 0, axis_index_groups=squares(n_row, n_col))
     grads = []
     for s in range(2):
-        total = first[s]
-        for part in back:
-            total = total + part[s].astype(f32)
+        total = back[0, s].astype(f32)
+        for i in range(1, len(mine)):
+            total = total + back[i, s].astype(f32)
         grads.append(total * down[:, :1])
     return tuple(grads)
 

time: 29.8 us -> 33.4 us (1.12)
  waiting for transfers between devices: 11.6 us -> 14 us
  other arithmetic: 1.73 us -> 2.57 us
    all_to_all x0 -> x1, waiting for transfers between devices: none -> 8.22 us  [local(): lax.all_to_all(parts.astype(jnp.float16), both, 0, 0, axis_index_groups=s...]
    ppermute x3 -> x0, waiting for transfers between devices: 5.8 us -> none  [local(): lax.ppermute(part.astype(jnp.float16), both, square_shift(n_row, n_col, -...]
    all_to_all x0 -> x1, starting transfers between devices: none -> 3.76 us  [local(): lax.all_to_all(parts.astype(jnp.float16), both, 0, 0, axis_index_groups=s...]
    ppermute x3 -> x0, starting transfers between devices: 3.55 us -> none  [local(): lax.ppermute(part.astype(jnp.float16), both, square_shift(n_row, n_col, -...]
    convert_element_type x3 -> x1, other arithmetic: 0.05 us -> 0.88 us  [local(): parts.astype(jnp.float16)]
  transfers between devices with their start and end apart: 13 -> 11, of which waited for: 9 -> 7; matrix products, arithmetic and copies ran while one was open for 1% -> 1% of each run, Pallas kernels for 3% -> 3%
where the time goes in v10:
time: 33.4 us; the launch traced here: 33.2 us
  waiting for transfers between devices  14 us (42%)
  starting transfers between devices  13.8 us (41%)
  other arithmetic  2.57 us (8%)
  Pallas kernels  1.95 us (6%)
  between operations  0.68 us (2%)
    all_to_all x1, waiting for transfers between devices, local(): lax.all_to_all(parts.astype(jnp.float16), both, 0, 0, axis_index_groups=s...  8.22 us
    ppermute x3, starting transfers between devices, local(): line.append(lax.ppermute(line[which], 'col', perm))  6.29 us
    all_to_all x1, starting transfers between devices, local(): lax.all_to_all(parts.astype(jnp.float16), both, 0, 0, axis_index_groups=s...  3.76 us
    ppermute x3, starting transfers between devices, local(): lax.ppermute(own, both, square_shift(n_row, n_col, j, k))  3.49 us
    ppermute x3, waiting for transfers between devices, local(): lax.ppermute(own, both, square_shift(n_row, n_col, j, k))  2.93 us
    pallas_call x2, Pallas kernels, call(): pl.pallas_call(kernel, out_shape=out_shape, in_specs=[vmem] * len(operand...  1.95 us
    ppermute x3, waiting for transfers between devices, local(): line.append(lax.ppermute(line[which], 'col', perm))  1.69 us
    ppermute x4, waiting for transfers between devices, pair(): lax.ppermute(block, 'row', inner_shift(n_row, k))  1.19 us
  transfers between devices with their start and end apart: 11, of which 7 were waited for; matrix products, arithmetic and copies ran while one was open for 1% of the time, Pallas kernels for 3%

profile of v10, /device:TPU:0, one launch (start us, length us, event | category | flops | bytes accessed | tf_op | source)
XLA Modules:
  0.0 33.2 jit_solution(16748629359936825595)
XLA Ops:
  0.6 0.0 copy-start
  0.6 0.9 %pad_maximum_fusion.refs_0_.refs_4_ = bf16[2,32,1024]{2,1,0:T(8,128)(2,1)S(1)} fusion(bf16[1,32,1024]{2,1,0:T(8,128)(2,1)} %bitcast.6, bf16[1,32,1024]{2,1,0:T(8,128)(2,1)} %bitcast.7), kind=kLoop, calls=%fused_computation | loop fusion | flops 65536 | bytes 262144 | tf_op jit(solution)/shard_map/stack | solution.py:150
  1.5 4.1 %collective-permute-start.3 = (bf16[2,32,1024]{2,1,0:T(8,128)(2,1)S(1)}, bf16[2,32,1024]{2,1,0:T(8,128)(2,1)S(1)}, u32[]{:S(2)}, u32[]{:S(2)}) collective-permute-start(bf16[2,32,1024]{2,1,0:T(8,128)(2,1)S(1)} %pad_maximum_fusion.refs_0_.refs_4_), channel_id=1, source_target_pairs={{0,4},{1,5},{2,6},{3,7},{4,0},{5,1},{6,2},{7,3},{8,12},{9,13},{10,... | collective-permute-start | bytes 393224 | tf_op jit(solution)/shard_map/ppermute | solution.py:156
  5.6 1.6 %collective-permute-start.4 = (bf16[2,32,1024]{2,1,0:T(8,128)(2,1)S(1)}, bf16[2,32,1024]{2,1,0:T(8,128)(2,1)S(1)}, u32[]{:S(2)}, u32[]{:S(2)}) collective-permute-start(bf16[2,32,1024]{2,1,0:T(8,128)(2,1)S(1)} %pad_maximum_fusion.refs_0_.refs_4_), channel_id=1, source_target_pairs={{0,2},{1,3},{2,0},{3,1},{4,6},{5,7},{6,4},{7,5},{8,10},{9,11},{10,... | collective-permute-start | bytes 393224 | tf_op jit(solution)/shard_map/ppermute | solution.py:156
  7.2 2.4 %collective-permute-start.2 = (bf16[2,32,1024]{2,1,0:T(8,128)(2,1)S(1)}, bf16[2,32,1024]{2,1,0:T(8,128)(2,1)S(1)}, u32[]{:S(2)}, u32[]{:S(2)}) collective-permute-start(bf16[2,32,1024]{2,1,0:T(8,128)(2,1)S(1)} %pad_maximum_fusion.refs_0_.refs_4_), channel_id=1, source_target_pairs={{0,17},{1,16},{2,19},{3,18},{4,21},{5,20},{6,23},{7,22},{8,25},{9,... | collective-permute-start | bytes 393224 | tf_op jit(solution)/shard_map/ppermute | solution.py:152
  9.7 0.5 %collective-permute-start.1 = (bf16[2,32,1024]{2,1,0:T(8,128)(2,1)S(1)}, bf16[2,32,1024]{2,1,0:T(8,128)(2,1)S(1)}, u32[]{:S(2)}, u32[]{:S(2)}) collective-permute-start(bf16[2,32,1024]{2,1,0:T(8,128)(2,1)S(1)} %pad_maximum_fusion.refs_0_.refs_4_), channel_id=1, source_target_pairs={{0,16},{1,17},{2,18},{3,19},{4,20},{5,21},{6,22},{7,23},{8,24},{9,... | collective-permute-start | bytes 393224 | tf_op jit(solution)/shard_map/ppermute | solution.py:152
  10.2 0.5 %collective-permute-start = (bf16[2,32,1024]{2,1,0:T(8,128)(2,1)S(1)}, bf16[2,32,1024]{2,1,0:T(8,128)(2,1)S(1)}, u32[]{:S(2)}, u32[]{:S(2)}) collective-permute-start(bf16[2,32,1024]{2,1,0:T(8,128)(2,1)S(1)} %pad_maximum_fusion.refs_0_.refs_4_), channel_id=1, source_target_pairs={{0,1},{1,0},{2,3},{3,2},{4,5},{5,4},{6,7},{7,6},{8,9},{9,8},{10,11... | collective-permute-start | bytes 393224 | tf_op jit(solution)/shard_map/ppermute | solution.py:152
  10.7 1.3 %collective-permute-done.3.refs_5_ = bf16[2,32,1024]{2,1,0:T(8,128)(2,1)S(1)} collective-permute-done((bf16[2,32,1024]{2,1,0:T(8,128)(2,1)S(1)}, bf16[2,32,1024]{2,1,0:T(8,128)(2,1)S(1)}, u32[]{:S(2)}, u32[]{:S(2)}) %collective-permute-start.3) | collective-permute-done | bytes 131104 | tf_op jit(solution)/shard_map/ppermute | solution.py:156
  12.0 0.6 %collective-permute-start.5 = (bf16[2,32,1024]{2,1,0:T(8,128)(2,1)S(1)}, bf16[2,32,1024]{2,1,0:T(8,128)(2,1)S(1)}, u32[]{:S(2)}, u32[]{:S(2)}) collective-permute-start(bf16[2,32,1024]{2,1,0:T(8,128)(2,1)S(1)} %collective-permute-done.3.refs_5_), channel_id=1, source_target_pairs={{0,2},{1,3},{2,0},{3,1},{4,6},{5,7},{6,4},{7,5},{8,10},{9,11},{10,... | collective-permute-start | bytes 393224 | tf_op jit(solution)/shard_map/ppermute | solution.py:156
  12.7 0.0 copy-done
  12.7 0.0 collective-permute-done.4.refs_6_
  12.7 0.1 collective-permute-start.6
  12.8 1.0 %collective-permute-done.2.refs_3_ = bf16[2,32,1024]{2,1,0:T(8,128)(2,1)S(1)} collective-permute-done((bf16[2,32,1024]{2,1,0:T(8,128)(2,1)S(1)}, bf16[2,32,1024]{2,1,0:T(8,128)(2,1)S(1)}, u32[]{:S(2)}, u32[]{:S(2)}) %collective-permute-start.2) | collective-permute-done | bytes 131104 | tf_op jit(solution)/shard_map/ppermute | solution.py:152
  13.8 0.0 collective-permute-start.7
  13.8 1.8 %collective-permute-done.1.refs_2_ = bf16[2,32,1024]{2,1,0:T(8,128)(2,1)S(1)} collective-permute-done((bf16[2,32,1024]{2,1,0:T(8,128)(2,1)S(1)}, bf16[2,32,1024]{2,1,0:T(8,128)(2,1)S(1)}, u32[]{:S(2)}, u32[]{:S(2)}) %collective-permute-start.1) | collective-permute-done | bytes 131104 | tf_op jit(solution)/shard_map/ppermute | solution.py:152
  15.6 0.0 collective-permute-start.8
  15.6 0.1 collective-permute-done.refs_1_
  15.7 0.1 broadcast_in_dim.2.factors
  15.8 0.9 %shard_map.50 = (bf16[256,1024]{1,0:T(8,128)(2,1)S(1)}, f32[256,1024]{1,0:T(8,128)S(1)}, f32[256,128]{1,0:T(8,128)S(1)}, f32[32,128]{1,0:T(8,128)S(1)}) custom-call(f32[2,128]{1,0:T(2,128)S(1)} %broadcast_in_dim.2.factors, bf16[2,32,1024]{2,1,0:T(8,128)(2,1)S(1)} %pad_maximum_fusion.refs_0_.refs_4_, bf16[2,32,1024]{2,1,0:T(8,128)(2,1)S(1)} %collective-permute-done.refs_1_, ...), custom_call_target="tpu_custom_call" | custom-call | flops 201326592 | bytes 2638848 | tf_op jit(solution)/shard_map/pallas_call | solution.py:132
  16.7 0.3 %collective-permute-done.5.refs_3_ = bf16[2,32,1024]{2,1,0:T(8,128)(2,1)S(1)} collective-permute-done((bf16[2,32,1024]{2,1,0:T(8,128)(2,1)S(1)}, bf16[2,32,1024]{2,1,0:T(8,128)(2,1)S(1)}, u32[]{:S(2)}, u32[]{:S(2)}) %collective-permute-start.5) | collective-permute-done | bytes 131104 | tf_op jit(solution)/shard_map/ppermute | solution.py:156
  17.0 0.2 collective-permute-start.9
  17.2 0.0 collective-permute-done.6.refs_0_
  17.2 0.0 collective-permute-done.8.refs_2_
  17.2 0.0 collective-permute-done.7.refs_1_
  17.2 1.2 %collective-permute-done.9.refs_4_ = bf16[2,32,1024]{2,1,0:T(8,128)(2,1)S(1)} collective-permute-done((bf16[2,32,1024]{2,1,0:T(8,128)(2,1)S(1)}, bf16[2,32,1024]{2,1,0:T(8,128)(2,1)S(1)}, u32[]{:S(2)}, u32[]{:S(2)}) %collective-permute-start.9) | collective-permute-done | bytes 131104 | tf_op jit(solution)/shard_map/ppermute | solution.py:159
  18.4 1.0 %shard_map.51 = f32[4,2,32,1024]{3,2,1,0:T(8,128)S(1)} custom-call(f32[2,128]{1,0:T(2,128)S(1)} %broadcast_in_dim.2.factors, bf16[256,1024]{1,0:T(8,128)(2,1)S(1)} %get-tuple-element.8.own, f32[256,1024]{1,0:T(8,128)S(1)} %get-tuple-element.10.acc, f32[256,128]{1,0:T(8,128)S(1)} %get-tuple-element.11.up, ...), custom_call_target="tpu_custom_call" | custom-call | flops 335544320 | bytes 3408896 | tf_op jit(solution)/shard_map/pallas_call | solution.py:132
  19.4 0.9 %convert_element_type.35 = f16[4,2,32,1024]{3,2,1,0:T(8,128)(2,1)} convert(f32[4,2,32,1024]{3,2,1,0:T(8,128)S(1)} %shard_map.51) | non-fusion elementwise | flops 262144 | bytes 1572864 | tf_op jit(solution)/shard_map/convert_element_type | solution.py:185
  20.3 3.8 %all-to-all-start = ((f16[4,2,32,1024]{3,2,1,0:T(8,128)(2,1)}), f16[4,2,32,1024]{3,2,1,0:T(8,128)(2,1)S(1)}, u32[]{:S(2)}, u32[]{:S(2)}) async-start(f16[4,2,32,1024]{3,2,1,0:T(8,128)(2,1)} %convert_element_type.35), calls=%async_computation | async-start | bytes 1048576 | tf_op jit(solution)/shard_map/all_to_all | solution.py:185
  24.1 0.1 slice_reduce_fusion
  24.2 8.2 %all-to-all-done = f16[4,2,32,1024]{3,2,1,0:T(8,128)(2,1)S(1)} async-done(((f16[4,2,32,1024]{3,2,1,0:T(8,128)(2,1)}), f16[4,2,32,1024]{3,2,1,0:T(8,128)(2,1)S(1)}, u32[]{:S(2)}, u32[]{:S(2)}) %all-to-all-start) | async-done | bytes 524320 | tf_op jit(solution)/shard_map/all_to_all | solution.py:185
  32.4 0.8 %bitcast_multiply_fusion = (f32[32,1024]{1,0:T(8,128)}, f32[32,1024]{1,0:T(8,128)}) fusion(f16[4,2,32,1024]{3,2,1,0:T(8,128)(2,1)S(1)} %all-to-all-done, f32[32]{0:T(128)S(1)} %slice_reduce_fusion), kind=kLoop, calls=%fused_computation.1 | loop fusion | flops 524288 | bytes 786560 | tf_op jit(solution)/shard_map/mul | solution.py:191
  (1 shorter events, 0.0 us)
Async XLA Ops:
  0.6 12.0 %copy-start = (f32[2]{0:T(128)S(1)}, f32[2]{0:T(128)}, u32[]{:S(2)}) copy-start(f32[2]{0:T(128)} %param.5) | copy-start | bytes 28
  1.5 10.5 %collective-permute-start.3 = (bf16[2,32,1024]{2,1,0:T(8,128)(2,1)S(1)}, bf16[2,32,1024]{2,1,0:T(8,128)(2,1)S(1)}, u32[]{:S(2)}, u32[]{:S(2)}) collective-permute-start(bf16[2,32,1024]{2,1,0:T(8,128)(2,1)S(1)} %pad_maximum_fusion.refs_0_.refs_4_), channel_id=1, source_target_pairs={{0,4},{1,5},{2,6},{3,7},{4,0},{5,1},{6,2},{7,3},{8,12},{9,13},{10,... | collective-permute-start | bytes 393224 | tf_op jit(solution)/shard_map/ppermute | solution.py:156
  5.6 7.0 %collective-permute-start.4 = (bf16[2,32,1024]{2,1,0:T(8,128)(2,1)S(1)}, bf16[2,32,1024]{2,1,0:T(8,128)(2,1)S(1)}, u32[]{:S(2)}, u32[]{:S(2)}) collective-permute-start(bf16[2,32,1024]{2,1,0:T(8,128)(2,1)S(1)} %pad_maximum_fusion.refs_0_.refs_4_), channel_id=1, source_target_pairs={{0,2},{1,3},{2,0},{3,1},{4,6},{5,7},{6,4},{7,5},{8,10},{9,11},{10,... | collective-permute-start | bytes 393224 | tf_op jit(solution)/shard_map/ppermute | solution.py:156
  7.2 6.6 %collective-permute-start.2 = (bf16[2,32,1024]{2,1,0:T(8,128)(2,1)S(1)}, bf16[2,32,1024]{2,1,0:T(8,128)(2,1)S(1)}, u32[]{:S(2)}, u32[]{:S(2)}) collective-permute-start(bf16[2,32,1024]{2,1,0:T(8,128)(2,1)S(1)} %pad_maximum_fusion.refs_0_.refs_4_), channel_id=1, source_target_pairs={{0,17},{1,16},{2,19},{3,18},{4,21},{5,20},{6,23},{7,22},{8,25},{9,... | collective-permute-start | bytes 393224 | tf_op jit(solution)/shard_map/ppermute | solution.py:152
  9.7 5.9 %collective-permute-start.1 = (bf16[2,32,1024]{2,1,0:T(8,128)(2,1)S(1)}, bf16[2,32,1024]{2,1,0:T(8,128)(2,1)S(1)}, u32[]{:S(2)}, u32[]{:S(2)}) collective-permute-start(bf16[2,32,1024]{2,1,0:T(8,128)(2,1)S(1)} %pad_maximum_fusion.refs_0_.refs_4_), channel_id=1, source_target_pairs={{0,16},{1,17},{2,18},{3,19},{4,20},{5,21},{6,22},{7,23},{8,24},{9,... | collective-permute-start | bytes 393224 | tf_op jit(solution)/shard_map/ppermute | solution.py:152
  10.2 5.5 %collective-permute-start = (bf16[2,32,1024]{2,1,0:T(8,128)(2,1)S(1)}, bf16[2,32,1024]{2,1,0:T(8,128)(2,1)S(1)}, u32[]{:S(2)}, u32[]{:S(2)}) collective-permute-start(bf16[2,32,1024]{2,1,0:T(8,128)(2,1)S(1)} %pad_maximum_fusion.refs_0_.refs_4_), channel_id=1, source_target_pairs={{0,1},{1,0},{2,3},{3,2},{4,5},{5,4},{6,7},{7,6},{8,9},{9,8},{10,11... | collective-permute-start | bytes 393224 | tf_op jit(solution)/shard_map/ppermute | solution.py:152
  12.0 5.0 %collective-permute-start.5 = (bf16[2,32,1024]{2,1,0:T(8,128)(2,1)S(1)}, bf16[2,32,1024]{2,1,0:T(8,128)(2,1)S(1)}, u32[]{:S(2)}, u32[]{:S(2)}) collective-permute-start(bf16[2,32,1024]{2,1,0:T(8,128)(2,1)S(1)} %collective-permute-done.3.refs_5_), channel_id=1, source_target_pairs={{0,2},{1,3},{2,0},{3,1},{4,6},{5,7},{6,4},{7,5},{8,10},{9,11},{10,... | collective-permute-start | bytes 393224 | tf_op jit(solution)/shard_map/ppermute | solution.py:156
  12.7 4.5 %collective-permute-start.6 = (bf16[2,32,1024]{2,1,0:T(8,128)(2,1)S(1)}, bf16[2,32,1024]{2,1,0:T(8,128)(2,1)S(1)}, u32[]{:S(2)}, u32[]{:S(2)}) collective-permute-start(bf16[2,32,1024]{2,1,0:T(8,128)(2,1)S(1)} %pad_maximum_fusion.refs_0_.refs_4_), channel_id=1, source_target_pairs={{0,8},{8,0},{16,24},{24,16},{1,9},{9,1},{17,25},{25,17},{2,10},{10... | collective-permute-start | bytes 393224 | tf_op jit(solution)/shard_map/ppermute | solution.py:159
  13.8 3.4 %collective-permute-start.7 = (bf16[2,32,1024]{2,1,0:T(8,128)(2,1)S(1)}, bf16[2,32,1024]{2,1,0:T(8,128)(2,1)S(1)}, u32[]{:S(2)}, u32[]{:S(2)}) collective-permute-start(bf16[2,32,1024]{2,1,0:T(8,128)(2,1)S(1)} %collective-permute-done.3.refs_5_), channel_id=1, source_target_pairs={{0,8},{8,0},{16,24},{24,16},{1,9},{9,1},{17,25},{25,17},{2,10},{10... | collective-permute-start | bytes 393224 | tf_op jit(solution)/shard_map/ppermute | solution.py:159
  15.6 1.6 %collective-permute-start.8 = (bf16[2,32,1024]{2,1,0:T(8,128)(2,1)S(1)}, bf16[2,32,1024]{2,1,0:T(8,128)(2,1)S(1)}, u32[]{:S(2)}, u32[]{:S(2)}) collective-permute-start(bf16[2,32,1024]{2,1,0:T(8,128)(2,1)S(1)} %collective-permute-done.4.refs_6_), channel_id=1, source_target_pairs={{0,8},{8,0},{16,24},{24,16},{1,9},{9,1},{17,25},{25,17},{2,10},{10... | collective-permute-start | bytes 393224 | tf_op jit(solution)/shard_map/ppermute | solution.py:159
  17.0 1.3 %collective-permute-start.9 = (bf16[2,32,1024]{2,1,0:T(8,128)(2,1)S(1)}, bf16[2,32,1024]{2,1,0:T(8,128)(2,1)S(1)}, u32[]{:S(2)}, u32[]{:S(2)}) collective-permute-start(bf16[2,32,1024]{2,1,0:T(8,128)(2,1)S(1)} %collective-permute-done.5.refs_3_), channel_id=1, source_target_pairs={{0,8},{8,0},{16,24},{24,16},{1,9},{9,1},{17,25},{25,17},{2,10},{10... | collective-permute-start | bytes 393224 | tf_op jit(solution)/shard_map/ppermute | solution.py:159
  20.3 12.1 %all-to-all-start = ((f16[4,2,32,1024]{3,2,1,0:T(8,128)(2,1)}), f16[4,2,32,1024]{3,2,1,0:T(8,128)(2,1)S(1)}, u32[]{:S(2)}, u32[]{:S(2)}) async-start(f16[4,2,32,1024]{3,2,1,0:T(8,128)(2,1)} %convert_element_type.35), calls=%async_computation | async-start | bytes 1048576 | tf_op jit(solution)/shard_map/all_to_all | solution.py:185

commit v11 on v7

--- a/solution.py
+++ b/solution.py
@@ -98,14 +98,16 @@
     down[...] = jnp.broadcast_to((most / TOP)[: down.shape[0]], down.shape)
 
 
-def late_kernel(n, factors, own, acc, up, *refs):
-    outs = refs[-n:]
-    keys = join(refs[:-n])
-    p_mat, q_mat = weigh(own[...], keys, factors)
-    rows = outs[0].shape[1]
+def late_kernel(first, factors, own, acc, up, *refs, count):
+    outs = refs[-count:]
+    keys = join(refs[:-count])
+    rows, many = outs[0].shape[1], own.shape[0] // 2
+    low, size = first * rows, count * rows
+    mine = jnp.concatenate([own[low : low + size], own[many + low : many + low + size]], axis=0)
+    p_mat, q_mat = weigh(mine, keys, factors)
     for at in tiles(keys.shape[1]):
         for s, grad in enumerate(tile_grads(p_mat, q_mat, keys, at)):
-            grad = (grad + acc[s, :, at]) * up[:, :1]
+            grad = (grad + acc[s, low : low + size, at]) * up[low : low + size, :1]
             for i, out in enumerate(outs):
                 out[s, :, at] = grad[i * rows : (i + 1) * rows]
 
@@ -159,19 +161,24 @@
     )
     last, acc = lax.optimization_barrier((line[-1], acc))
     late = copies + [last] + pair(last)
-    first, *parts = call(
-        functools.partial(late_kernel, len(mine)),
-        [factors, joined, acc, up] + late,
-        [jax.ShapeDtypeStruct((2, rows, width), f32)] * len(mine),
-        flops(late),
-    )
+    def late_call(first, count):
+        return call(
+            functools.partial(late_kernel, first, count=count),
+            [factors, joined, acc, up] + late,
+            [jax.ShapeDtypeStruct((2, rows, width), f32)] * count,
+            flops(late) * count // len(mine),
+        )
+
+    parts = late_call(len(mine) - 1, 1)
+    if len(mine) > 1:
+        parts = late_call(0, len(mine) - 1) + parts
     back = [
         lax.ppermute(part.astype(jnp.float16), both, square_shift(n_row, n_col, -j, -k))
-        for part, (j, k) in zip(parts, square)
+        for part, (j, k) in zip(parts[1:], square)
     ]
     grads = []
     for s in range(2):
-        total = first[s]
+        total = parts[0][s]
         for part in back:
             total = total + part[s].astype(f32)
         grads.append(total * down[:, :1])

time: 29.8 us -> 30.4 us (1.020)
  waiting for transfers between devices: 11.6 us -> 10.5 us
  Pallas kernels: 1.88 us -> 2.76 us
  starting transfers between devices: 13.6 us -> 14.4 us
    ppermute x3, waiting for transfers between devices: 5.8 us -> 4.72 us  [local(): lax.ppermute(part.astype(jnp.float16), both, square_shift(n_row, n_col, -...]
    pallas_call x2 -> x3, Pallas kernels: 1.88 us -> 2.76 us  [call(): pl.pallas_call(kernel, out_shape=out_shape, in_specs=[vmem] * len(operand...]
    ppermute x4, starting transfers between devices: 0.23 us -> 0.97 us  [pair(): lax.ppermute(block, 'row', inner_shift(n_row, k))]
    ppermute x3, waiting for transfers between devices: 2.93 us -> 3.4 us  [local(): lax.ppermute(own, both, square_shift(n_row, n_col, j, k))]
    ppermute x3, waiting for transfers between devices: 1.69 us -> 1.35 us  [local(): line.append(lax.ppermute(line[which], 'col', perm))]
  transfers between devices with their start and end apart: 13 -> 13, of which waited for: 9 -> 7; matrix products, arithmetic and copies ran while one was open for 1% -> 1% of each run, Pallas kernels for 3% -> 6%
where the time goes in v11:
time: 30.4 us; the launch traced here: 30.3 us
  starting transfers between devices  14.4 us (47%)
  waiting for transfers between devices  10.5 us (35%)
  Pallas kernels  2.76 us (9%)
  other arithmetic  1.73 us (6%)
  between operations  0.71 us (2%)
    ppermute x3, starting transfers between devices, local(): line.append(lax.ppermute(line[which], 'col', perm))  6.29 us
    ppermute x3, waiting for transfers between devices, local(): lax.ppermute(part.astype(jnp.float16), both, square_shift(n_row, n_col, -...  4.72 us
    ppermute x3, starting transfers between devices, local(): lax.ppermute(part.astype(jnp.float16), both, square_shift(n_row, n_col, -...  3.69 us
    ppermute x3, starting transfers between devices, local(): lax.ppermute(own, both, square_shift(n_row, n_col, j, k))  3.49 us
    ppermute x3, waiting for transfers between devices, local(): lax.ppermute(own, both, square_shift(n_row, n_col, j, k))  3.4 us
    pallas_call x3, Pallas kernels, call(): pl.pallas_call(kernel, out_shape=out_shape, in_specs=[vmem] * len(operand...  2.76 us
    ppermute x3, waiting for transfers between devices, local(): line.append(lax.ppermute(line[which], 'col', perm))  1.35 us
    ppermute x4, waiting for transfers between devices, pair(): lax.ppermute(block, 'row', inner_shift(n_row, k))  0.98 us
  transfers between devices with their start and end apart: 13, of which 7 were waited for; matrix products, arithmetic and copies ran while one was open for 1% of the time, Pallas kernels for 6%

profile of v11, /device:TPU:0, one launch (start us, length us, event | category | flops | bytes accessed | tf_op | source)
XLA Modules:
  0.0 30.3 jit_solution(16694556230809323811)
XLA Ops:
  0.6 0.0 copy-start
  0.6 0.9 %pad_maximum_fusion.refs_0_.refs_4_ = bf16[2,32,1024]{2,1,0:T(8,128)(2,1)S(1)} fusion(bf16[1,32,1024]{2,1,0:T(8,128)(2,1)} %bitcast.6, bf16[1,32,1024]{2,1,0:T(8,128)(2,1)} %bitcast.7), kind=kLoop, calls=%fused_computation | loop fusion | flops 65536 | bytes 262144 | tf_op jit(solution)/shard_map/stack | solution.py:136
  1.5 4.1 %collective-permute-start.3 = (bf16[2,32,1024]{2,1,0:T(8,128)(2,1)S(1)}, bf16[2,32,1024]{2,1,0:T(8,128)(2,1)S(1)}, u32[]{:S(2)}, u32[]{:S(2)}) collective-permute-start(bf16[2,32,1024]{2,1,0:T(8,128)(2,1)S(1)} %pad_maximum_fusion.refs_0_.refs_4_), channel_id=1, source_target_pairs={{0,4},{1,5},{2,6},{3,7},{4,0},{5,1},{6,2},{7,3},{8,12},{9,13},{10,... | collective-permute-start | bytes 393224 | tf_op jit(solution)/shard_map/ppermute | solution.py:142
  5.6 1.6 %collective-permute-start.4 = (bf16[2,32,1024]{2,1,0:T(8,128)(2,1)S(1)}, bf16[2,32,1024]{2,1,0:T(8,128)(2,1)S(1)}, u32[]{:S(2)}, u32[]{:S(2)}) collective-permute-start(bf16[2,32,1024]{2,1,0:T(8,128)(2,1)S(1)} %pad_maximum_fusion.refs_0_.refs_4_), channel_id=1, source_target_pairs={{0,2},{1,3},{2,0},{3,1},{4,6},{5,7},{6,4},{7,5},{8,10},{9,11},{10,... | collective-permute-start | bytes 393224 | tf_op jit(solution)/shard_map/ppermute | solution.py:142
  7.2 1.5 %collective-permute-start = (bf16[2,32,1024]{2,1,0:T(8,128)(2,1)S(1)}, bf16[2,32,1024]{2,1,0:T(8,128)(2,1)S(1)}, u32[]{:S(2)}, u32[]{:S(2)}) collective-permute-start(bf16[2,32,1024]{2,1,0:T(8,128)(2,1)S(1)} %pad_maximum_fusion.refs_0_.refs_4_), channel_id=1, source_target_pairs={{0,1},{1,0},{2,3},{3,2},{4,5},{5,4},{6,7},{7,6},{8,9},{9,8},{10,11... | collective-permute-start | bytes 393224 | tf_op jit(solution)/shard_map/ppermute | solution.py:138
  8.7 1.5 %collective-permute-start.1 = (bf16[2,32,1024]{2,1,0:T(8,128)(2,1)S(1)}, bf16[2,32,1024]{2,1,0:T(8,128)(2,1)S(1)}, u32[]{:S(2)}, u32[]{:S(2)}) collective-permute-start(bf16[2,32,1024]{2,1,0:T(8,128)(2,1)S(1)} %pad_maximum_fusion.refs_0_.refs_4_), channel_id=1, source_target_pairs={{0,16},{1,17},{2,18},{3,19},{4,20},{5,21},{6,22},{7,23},{8,24},{9,... | collective-permute-start | bytes 393224 | tf_op jit(solution)/shard_map/ppermute | solution.py:138
  10.2 0.5 %collective-permute-start.2 = (bf16[2,32,1024]{2,1,0:T(8,128)(2,1)S(1)}, bf16[2,32,1024]{2,1,0:T(8,128)(2,1)S(1)}, u32[]{:S(2)}, u32[]{:S(2)}) collective-permute-start(bf16[2,32,1024]{2,1,0:T(8,128)(2,1)S(1)} %pad_maximum_fusion.refs_0_.refs_4_), channel_id=1, source_target_pairs={{0,17},{1,16},{2,19},{3,18},{4,21},{5,20},{6,23},{7,22},{8,25},{9,... | collective-permute-start | bytes 393224 | tf_op jit(solution)/shard_map/ppermute | solution.py:138
  10.7 1.3 %collective-permute-done.3.refs_5_ = bf16[2,32,1024]{2,1,0:T(8,128)(2,1)S(1)} collective-permute-done((bf16[2,32,1024]{2,1,0:T(8,128)(2,1)S(1)}, bf16[2,32,1024]{2,1,0:T(8,128)(2,1)S(1)}, u32[]{:S(2)}, u32[]{:S(2)}) %collective-permute-start.3) | collective-permute-done | bytes 131104 | tf_op jit(solution)/shard_map/ppermute | solution.py:142
  12.0 0.6 %collective-permute-start.5 = (bf16[2,32,1024]{2,1,0:T(8,128)(2,1)S(1)}, bf16[2,32,1024]{2,1,0:T(8,128)(2,1)S(1)}, u32[]{:S(2)}, u32[]{:S(2)}) collective-permute-start(bf16[2,32,1024]{2,1,0:T(8,128)(2,1)S(1)} %collective-permute-done.3.refs_5_), channel_id=1, source_target_pairs={{0,2},{1,3},{2,0},{3,1},{4,6},{5,7},{6,4},{7,5},{8,10},{9,11},{10,... | collective-permute-start | bytes 393224 | tf_op jit(solution)/shard_map/ppermute | solution.py:142
  12.7 0.0 copy-done
  12.7 0.0 collective-permute-done.4.refs_6_
  12.7 0.1 collective-permute-start.6
  12.8 0.2 collective-permute-done.refs_1_
  12.9 0.3 %collective-permute-start.7 = (bf16[2,32,1024]{2,1,0:T(8,128)(2,1)S(1)}, bf16[2,32,1024]{2,1,0:T(8,128)(2,1)S(1)}, u32[]{:S(2)}, u32[]{:S(2)}) collective-permute-start(bf16[2,32,1024]{2,1,0:T(8,128)(2,1)S(1)} %collective-permute-done.3.refs_5_), channel_id=1, source_target_pairs={{0,8},{8,0},{16,24},{24,16},{1,9},{9,1},{17,25},{25,17},{2,10},{10... | collective-permute-start | bytes 393224 | tf_op jit(solution)/shard_map/ppermute | solution.py:145
  13.3 3.2 %collective-permute-done.1.refs_2_ = bf16[2,32,1024]{2,1,0:T(8,128)(2,1)S(1)} collective-permute-done((bf16[2,32,1024]{2,1,0:T(8,128)(2,1)S(1)}, bf16[2,32,1024]{2,1,0:T(8,128)(2,1)S(1)}, u32[]{:S(2)}, u32[]{:S(2)}) %collective-permute-start.1) | collective-permute-done | bytes 131104 | tf_op jit(solution)/shard_map/ppermute | solution.py:138
  16.5 0.0 collective-permute-start.8
  16.5 0.0 collective-permute-done.2.refs_3_
  16.5 0.1 broadcast_in_dim.2.factors
  16.6 0.9 %shard_map.50 = (bf16[256,1024]{1,0:T(8,128)(2,1)S(1)}, f32[2,128,1024]{2,1,0:T(8,128)S(1)}, f32[128,128]{1,0:T(8,128)S(1)}, f32[32,128]{1,0:T(8,128)S(1)}) custom-call(f32[2,128]{1,0:T(2,128)S(1)} %broadcast_in_dim.2.factors, bf16[2,32,1024]{2,1,0:T(8,128)(2,1)S(1)} %pad_maximum_fusion.refs_0_.refs_4_, ...), custom_call_target="tpu_custom_call" | custom-call | flops 201326592 | bytes 2573312 | tf_op jit(solution)/shard_map/pallas_call | solution.py:118
  17.5 0.0 collective-permute-done.5.refs_3_
  17.5 0.6 %collective-permute-start.9 = (bf16[2,32,1024]{2,1,0:T(8,128)(2,1)S(1)}, bf16[2,32,1024]{2,1,0:T(8,128)(2,1)S(1)}, u32[]{:S(2)}, u32[]{:S(2)}) collective-permute-start(bf16[2,32,1024]{2,1,0:T(8,128)(2,1)S(1)} %collective-permute-done.5.refs_3_), channel_id=1, source_target_pairs={{0,8},{8,0},{16,24},{24,16},{1,9},{9,1},{17,25},{25,17},{2,10},{10... | collective-permute-start | bytes 393224 | tf_op jit(solution)/shard_map/ppermute | solution.py:145
  18.1 0.0 collective-permute-done.6.refs_0_
  18.1 0.0 collective-permute-done.7.refs_1_
  18.1 0.0 collective-permute-done.8.refs_2_
  18.1 1.0 %collective-permute-done.9.refs_4_ = bf16[2,32,1024]{2,1,0:T(8,128)(2,1)S(1)} collective-permute-done((bf16[2,32,1024]{2,1,0:T(8,128)(2,1)S(1)}, bf16[2,32,1024]{2,1,0:T(8,128)(2,1)S(1)}, u32[]{:S(2)}, u32[]{:S(2)}) %collective-permute-start.9) | collective-permute-done | bytes 131104 | tf_op jit(solution)/shard_map/ppermute | solution.py:145
  19.0 0.9 %shard_map.52 = f32[2,32,1024]{2,1,0:T(8,128)S(1)} custom-call(f32[2,128]{1,0:T(2,128)S(1)} %broadcast_in_dim.2.factors, bf16[256,1024]{1,0:T(8,128)(2,1)S(1)} %get-tuple-element.11.own, f32[2,128,1024]{2,1,0:T(8,128)S(1)} %get-tuple-element.13.acc, f32[128,128]{1,0:T(8,128)S(1)} %get-tuple-element.14.up, ...), custom_call_target="tpu_custom_call" | custom-call | flops 83886080 | bytes 2556928 | tf_op jit(solution)/shard_map/pallas_call | solution.py:118
  20.0 1.9 %collective-permute-start.12 = (f16[2,32,1024]{2,1,0:T(8,128)(2,1)S(1)}, f16[2,32,1024]{2,1,0:T(8,128)(2,1)S(1)}, u32[]{:S(2)}, u32[]{:S(2)}) collective-permute-start(f16[2,32,1024]{2,1,0:T(8,128)(2,1)S(1)} %convert_element_type.37), channel_id=1, source_target_pairs={{0,17},{1,16},{2,19},{3,18},{4,21},{5,20},{6,23},{7,22},{8,25},{9,... | collective-permute-start | bytes 393224 | tf_op jit(solution)/shard_map/ppermute | solution.py:176
  21.8 1.0 %shard_map.51 = (f32[2,32,1024]{2,1,0:T(8,128)S(1)}, f32[2,32,1024]{2,1,0:T(8,128)S(1)}, f32[2,32,1024]{2,1,0:T(8,128)S(1)}) custom-call(f32[2,128]{1,0:T(2,128)S(1)} %broadcast_in_dim.2.factors, bf16[256,1024]{1,0:T(8,128)(2,1)S(1)} %get-tuple-element.11.own, f32[2,128,1024]{2,1,0:T(8,128)S(1)} %get-tuple-element.13.acc, ...), custom_call_target="tpu_custom_call" | custom-call | flops 251658240 | bytes 3081216 | tf_op jit(solution)/shard_map/pallas_call | solution.py:118
  22.8 0.8 %collective-permute-start.10 = (f16[2,32,1024]{2,1,0:T(8,128)(2,1)S(1)}, f16[2,32,1024]{2,1,0:T(8,128)(2,1)S(1)}, u32[]{:S(2)}, u32[]{:S(2)}) collective-permute-start(f16[2,32,1024]{2,1,0:T(8,128)(2,1)S(1)} %convert_element_type.33), channel_id=1, source_target_pairs={{0,1},{1,0},{2,3},{3,2},{4,5},{5,4},{6,7},{7,6},{8,9},{9,8},{10,11... | collective-permute-start | bytes 393224 | tf_op jit(solution)/shard_map/ppermute | solution.py:176
  23.7 1.0 %collective-permute-start.11 = (f16[2,32,1024]{2,1,0:T(8,128)(2,1)S(1)}, f16[2,32,1024]{2,1,0:T(8,128)(2,1)S(1)}, u32[]{:S(2)}, u32[]{:S(2)}) collective-permute-start(f16[2,32,1024]{2,1,0:T(8,128)(2,1)S(1)} %convert_element_type.35), channel_id=1, source_target_pairs={{0,16},{1,17},{2,18},{3,19},{4,20},{5,21},{6,22},{7,23},{8,24},{9,... | collective-permute-start | bytes 393224 | tf_op jit(solution)/shard_map/ppermute | solution.py:176
  24.7 0.1 slice_reduce_fusion
  24.8 2.5 %collective-permute-done.12 = f16[2,32,1024]{2,1,0:T(8,128)(2,1)S(1)} collective-permute-done((f16[2,32,1024]{2,1,0:T(8,128)(2,1)S(1)}, f16[2,32,1024]{2,1,0:T(8,128)(2,1)S(1)}, u32[]{:S(2)}, u32[]{:S(2)}) %collective-permute-start.12) | collective-permute-done | bytes 131104 | tf_op jit(solution)/shard_map/ppermute | solution.py:176
  27.3 1.9 %collective-permute-done.10 = f16[2,32,1024]{2,1,0:T(8,128)(2,1)S(1)} collective-permute-done((f16[2,32,1024]{2,1,0:T(8,128)(2,1)S(1)}, f16[2,32,1024]{2,1,0:T(8,128)(2,1)S(1)}, u32[]{:S(2)}, u32[]{:S(2)}) %collective-permute-start.10) | collective-permute-done | bytes 131104 | tf_op jit(solution)/shard_map/ppermute | solution.py:176
  29.1 0.4 %collective-permute-done.11 = f16[2,32,1024]{2,1,0:T(8,128)(2,1)S(1)} collective-permute-done((f16[2,32,1024]{2,1,0:T(8,128)(2,1)S(1)}, f16[2,32,1024]{2,1,0:T(8,128)(2,1)S(1)}, u32[]{:S(2)}, u32[]{:S(2)}) %collective-permute-start.11) | collective-permute-done | bytes 131104 | tf_op jit(solution)/shard_map/ppermute | solution.py:176
  29.5 0.8 %bitcast_multiply_fusion = (f32[32,1024]{1,0:T(8,128)}, f32[32,1024]{1,0:T(8,128)}) fusion(f32[2,32,1024]{2,1,0:T(8,128)S(1)} %get-tuple-element.16, f16[2,32,1024]{2,1,0:T(8,128)(2,1)S(1)} %collective-permute-done.12, f16[2,32,1024]{2,1,0:T(8,128)(2,1)S(1)} %collective-permute-done.11, f16[2,32,1024]{2,1,0:T(8,128)(2,1)S(1)} %collective-permute-done.10, ...), kind=kLoop, calls=%fused_computation.1 | loop fusion | flops 458752 | bytes 917632 | tf_op jit(solution)/shard_map/mul | solution.py:184
  (4 shorter events, 0.1 us)
Async XLA Ops:
  0.6 12.0 %copy-start = (f32[2]{0:T(128)S(1)}, f32[2]{0:T(128)}, u32[]{:S(2)}) copy-start(f32[2]{0:T(128)} %param.5) | copy-start | bytes 28
  1.5 10.5 %collective-permute-start.3 = (bf16[2,32,1024]{2,1,0:T(8,128)(2,1)S(1)}, bf16[2,32,1024]{2,1,0:T(8,128)(2,1)S(1)}, u32[]{:S(2)}, u32[]{:S(2)}) collective-permute-start(bf16[2,32,1024]{2,1,0:T(8,128)(2,1)S(1)} %pad_maximum_fusion.refs_0_.refs_4_), channel_id=1, source_target_pairs={{0,4},{1,5},{2,6},{3,7},{4,0},{5,1},{6,2},{7,3},{8,12},{9,13},{10,... | collective-permute-start | bytes 393224 | tf_op jit(solution)/shard_map/ppermute | solution.py:142
  5.6 7.0 %collective-permute-start.4 = (bf16[2,32,1024]{2,1,0:T(8,128)(2,1)S(1)}, bf16[2,32,1024]{2,1,0:T(8,128)(2,1)S(1)}, u32[]{:S(2)}, u32[]{:S(2)}) collective-permute-start(bf16[2,32,1024]{2,1,0:T(8,128)(2,1)S(1)} %pad_maximum_fusion.refs_0_.refs_4_), channel_id=1, source_target_pairs={{0,2},{1,3},{2,0},{3,1},{4,6},{5,7},{6,4},{7,5},{8,10},{9,11},{10,... | collective-permute-start | bytes 393224 | tf_op jit(solution)/shard_map/ppermute | solution.py:142
  7.2 5.7 %collective-permute-start = (bf16[2,32,1024]{2,1,0:T(8,128)(2,1)S(1)}, bf16[2,32,1024]{2,1,0:T(8,128)(2,1)S(1)}, u32[]{:S(2)}, u32[]{:S(2)}) collective-permute-start(bf16[2,32,1024]{2,1,0:T(8,128)(2,1)S(1)} %pad_maximum_fusion.refs_0_.refs_4_), channel_id=1, source_target_pairs={{0,1},{1,0},{2,3},{3,2},{4,5},{5,4},{6,7},{7,6},{8,9},{9,8},{10,11... | collective-permute-start | bytes 393224 | tf_op jit(solution)/shard_map/ppermute | solution.py:138
  8.7 7.8 %collective-permute-start.1 = (bf16[2,32,1024]{2,1,0:T(8,128)(2,1)S(1)}, bf16[2,32,1024]{2,1,0:T(8,128)(2,1)S(1)}, u32[]{:S(2)}, u32[]{:S(2)}) collective-permute-start(bf16[2,32,1024]{2,1,0:T(8,128)(2,1)S(1)} %pad_maximum_fusion.refs_0_.refs_4_), channel_id=1, source_target_pairs={{0,16},{1,17},{2,18},{3,19},{4,20},{5,21},{6,22},{7,23},{8,24},{9,... | collective-permute-start | bytes 393224 | tf_op jit(solution)/shard_map/ppermute | solution.py:138
  10.2 6.3 %collective-permute-start.2 = (bf16[2,32,1024]{2,1,0:T(8,128)(2,1)S(1)}, bf16[2,32,1024]{2,1,0:T(8,128)(2,1)S(1)}, u32[]{:S(2)}, u32[]{:S(2)}) collective-permute-start(bf16[2,32,1024]{2,1,0:T(8,128)(2,1)S(1)} %pad_maximum_fusion.refs_0_.refs_4_), channel_id=1, source_target_pairs={{0,17},{1,16},{2,19},{3,18},{4,21},{5,20},{6,23},{7,22},{8,25},{9,... | collective-permute-start | bytes 393224 | tf_op jit(solution)/shard_map/ppermute | solution.py:138
  12.0 5.4 %collective-permute-start.5 = (bf16[2,32,1024]{2,1,0:T(8,128)(2,1)S(1)}, bf16[2,32,1024]{2,1,0:T(8,128)(2,1)S(1)}, u32[]{:S(2)}, u32[]{:S(2)}) collective-permute-start(bf16[2,32,1024]{2,1,0:T(8,128)(2,1)S(1)} %collective-permute-done.3.refs_5_), channel_id=1, source_target_pairs={{0,2},{1,3},{2,0},{3,1},{4,6},{5,7},{6,4},{7,5},{8,10},{9,11},{10,... | collective-permute-start | bytes 393224 | tf_op jit(solution)/shard_map/ppermute | solution.py:142
  12.7 5.4 %collective-permute-start.6 = (bf16[2,32,1024]{2,1,0:T(8,128)(2,1)S(1)}, bf16[2,32,1024]{2,1,0:T(8,128)(2,1)S(1)}, u32[]{:S(2)}, u32[]{:S(2)}) collective-permute-start(bf16[2,32,1024]{2,1,0:T(8,128)(2,1)S(1)} %pad_maximum_fusion.refs_0_.refs_4_), channel_id=1, source_target_pairs={{0,8},{8,0},{16,24},{24,16},{1,9},{9,1},{17,25},{25,17},{2,10},{10... | collective-permute-start | bytes 393224 | tf_op jit(solution)/shard_map/ppermute | solution.py:145
  12.9 5.1 %collective-permute-start.7 = (bf16[2,32,1024]{2,1,0:T(8,128)(2,1)S(1)}, bf16[2,32,1024]{2,1,0:T(8,128)(2,1)S(1)}, u32[]{:S(2)}, u32[]{:S(2)}) collective-permute-start(bf16[2,32,1024]{2,1,0:T(8,128)(2,1)S(1)} %collective-permute-done.3.refs_5_), channel_id=1, source_target_pairs={{0,8},{8,0},{16,24},{24,16},{1,9},{9,1},{17,25},{25,17},{2,10},{10... | collective-permute-start | bytes 393224 | tf_op jit(solution)/shard_map/ppermute | solution.py:145
  16.5 1.6 %collective-permute-start.8 = (bf16[2,32,1024]{2,1,0:T(8,128)(2,1)S(1)}, bf16[2,32,1024]{2,1,0:T(8,128)(2,1)S(1)}, u32[]{:S(2)}, u32[]{:S(2)}) collective-permute-start(bf16[2,32,1024]{2,1,0:T(8,128)(2,1)S(1)} %collective-permute-done.4.refs_6_), channel_id=1, source_target_pairs={{0,8},{8,0},{16,24},{24,16},{1,9},{9,1},{17,25},{25,17},{2,10},{10... | collective-permute-start | bytes 393224 | tf_op jit(solution)/shard_map/ppermute | solution.py:145
  17.5 1.6 %collective-permute-start.9 = (bf16[2,32,1024]{2,1,0:T(8,128)(2,1)S(1)}, bf16[2,32,1024]{2,1,0:T(8,128)(2,1)S(1)}, u32[]{:S(2)}, u32[]{:S(2)}) collective-permute-start(bf16[2,32,1024]{2,1,0:T(8,128)(2,1)S(1)} %collective-permute-done.5.refs_3_), channel_id=1, source_target_pairs={{0,8},{8,0},{16,24},{24,16},{1,9},{9,1},{17,25},{25,17},{2,10},{10... | collective-permute-start | bytes 393224 | tf_op jit(solution)/shard_map/ppermute | solution.py:145
  20.0 7.3 %collective-permute-start.12 = (f16[2,32,1024]{2,1,0:T(8,128)(2,1)S(1)}, f16[2,32,1024]{2,1,0:T(8,128)(2,1)S(1)}, u32[]{:S(2)}, u32[]{:S(2)}) collective-permute-start(f16[2,32,1024]{2,1,0:T(8,128)(2,1)S(1)} %convert_element_type.37), channel_id=1, source_target_pairs={{0,17},{1,16},{2,19},{3,18},{4,21},{5,20},{6,23},{7,22},{8,25},{9,... | collective-permute-start | bytes 393224 | tf_op jit(solution)/shard_map/ppermute | solution.py:176
  22.8 6.3 %collective-permute-start.10 = (f16[2,32,1024]{2,1,0:T(8,128)(2,1)S(1)}, f16[2,32,1024]{2,1,0:T(8,128)(2,1)S(1)}, u32[]{:S(2)}, u32[]{:S(2)}) collective-permute-start(f16[2,32,1024]{2,1,0:T(8,128)(2,1)S(1)} %convert_element_type.33), channel_id=1, source_target_pairs={{0,1},{1,0},{2,3},{3,2},{4,5},{5,4},{6,7},{7,6},{8,9},{9,8},{10,11... | collective-permute-start | bytes 393224 | tf_op jit(solution)/shard_map/ppermute | solution.py:176
  23.7 5.8 %collective-permute-start.11 = (f16[2,32,1024]{2,1,0:T(8,128)(2,1)S(1)}, f16[2,32,1024]{2,1,0:T(8,128)(2,1)S(1)}, u32[]{:S(2)}, u32[]{:S(2)}) collective-permute-start(f16[2,32,1024]{2,1,0:T(8,128)(2,1)S(1)} %convert_element_type.35), channel_id=1, source_target_pairs={{0,16},{1,17},{2,18},{3,19},{4,20},{5,21},{6,22},{7,23},{8,24},{9,... | collective-permute-start | bytes 393224 | tf_op jit(solution)/shard_map/ppermute | solution.py:176

commit v12 on v7

--- a/solution.py
+++ b/solution.py
@@ -55,62 +55,81 @@
     return lax.dot_general(a, b, (dims, ((), ())), preferred_element_type=jnp.float32)
 
 
-def join(refs):
-    return jnp.concatenate([ref[s] for s in range(2) for ref in refs], axis=0)
-
-
-def weigh(rows, keys, factors):
-    n, m = rows.shape[0] // 2, keys.shape[0] // 2
-    scores = dot(rows, keys, ((1,), (1,)))
-    cross = scores[:n, m:] - scores[n:, :m]
-    inmodal = scores[:n, :m] - scores[n:, m:]
+def joined(refs, parts, at):
+    return jnp.concatenate([ref[s, :, at] for s in parts for ref in refs], axis=0)
+
+
+def tiles(width, body):
+    step = 256 if width % 256 == 0 else width
+
+    @pl.loop(0, width // step)
+    def _(t):
+        body(pl.ds(pl.multiple_of(t * step, step), step))
+
+
+NT, NN = ((1,), (1,)), ((1,), (0,))
+
+
+def mixes(scores, mix, factors):
+    n = scores.shape[1] // 2
+    cross = scores[1, :n] - scores[0, n:]
+    inmodal = scores[0, :n] - scores[1, n:]
     p_mat = (cross * factors[0:1, 0:1]).astype(jnp.bfloat16)
     q_mat = (inmodal * factors[1:2, 0:1]).astype(jnp.bfloat16)
-    return p_mat, q_mat
-
-
-def tiles(width):
-    step = 256 if width % 256 == 0 else width
-    return [slice(i, i + step) for i in range(0, width, step)]
-
-
-def tile_grads(p_mat, q_mat, keys, at):
-    m = keys.shape[0] // 2
-    img, txt = keys[:m, at], keys[m:, at]
-    nn = ((1,), (0,))
-    grad_img = dot(jnp.concatenate([q_mat, p_mat], axis=1), jnp.concatenate([img, txt]), nn)
-    grad_txt = dot(jnp.concatenate([-p_mat, -q_mat], axis=1), jnp.concatenate([img, txt]), nn)
-    return grad_img, grad_txt
+    mix[0, :n], mix[0, n:] = q_mat, -p_mat
+    mix[1, :n], mix[1, n:] = p_mat, -q_mat
 
 
 def early_kernel(total, n, factors, *refs):
-    own, acc, up, down = refs[-4:]
-    rows = join(refs[:n])
-    own[...] = rows
-    keys = join(refs[n:-4])
-    p_mat, q_mat = weigh(rows, keys, factors)
-    for at in tiles(keys.shape[1]):
-        acc[0, :, at], acc[1, :, at] = tile_grads(p_mat, q_mat, keys, at)
-    size = jnp.sum(jnp.abs(rows.astype(jnp.float32)), axis=1, keepdims=True)
-    size = size[: size.shape[0] // 2] + size[size.shape[0] // 2 :]
-    most = size * ((factors[0:1, 0:1] + factors[1:2, 0:1]) * (1.02 * LIMIT * LIMIT * total)) + 1e-30
-    up[...] = jnp.broadcast_to(TOP / most, up.shape)
-    down[...] = jnp.broadcast_to((most / TOP)[: down.shape[0]], down.shape)
+    own, acc, up, down, scores, mix, size = refs[-7:]
+    blocks, keys = refs[:n], refs[n:-7]
+    scores[...] = jnp.zeros_like(scores)
+    size[...] = jnp.zeros_like(size)
+
+    def score(at):
+        rows = joined(blocks, (0, 1), at)
+        own[:, at] = rows
+        for s in range(2):
+            scores[s] += dot(rows, joined(keys, (s,), at), NT)
+        size[...] += jnp.sum(jnp.abs(rows.astype(jnp.float32)), axis=1, keepdims=True)
+
+    def grad(at):
+        acc[:, at] = sum(dot(mix[s], joined(keys, (s,), at), NN) for s in range(2))
+
+    tiles(own.shape[1], score)
+    mixes(scores, mix, factors)
+    tiles(own.shape[1], grad)
+    half = size.shape[0] // 2
+    both = size[:half] + size[half:]
+    most = both * ((factors[0:1, 0:1] + factors[1:2, 0:1]) * (1.02 * LIMIT * LIMIT * total)) + 1e-30
+    up[:half] = TOP / most
+    up[half:] = TOP / most
+    down[...] = (most / TOP)[: down.shape[0]]
 
 
 def late_kernel(n, factors, own, acc, up, *refs):
-    outs = refs[-n:]
-    keys = join(refs[:-n])
-    p_mat, q_mat = weigh(own[...], keys, factors)
+    keys, outs = refs[: -n - 2], refs[-n - 2 : -2]
+    scores, mix = refs[-2:]
     rows = outs[0].shape[1]
-    for at in tiles(keys.shape[1]):
-        for s, grad in enumerate(tile_grads(p_mat, q_mat, keys, at)):
-            grad = (grad + acc[s, :, at]) * up[:, :1]
+    scores[...] = jnp.zeros_like(scores)
+
+    def score(at):
+        for s in range(2):
+            scores[s] += dot(own[:, at], joined(keys, (s,), at), NT)
+
+    def grad(at):
+        total = acc[:, at] + sum(dot(mix[s], joined(keys, (s,), at), NN) for s in range(2))
+        total = total * up[:, :1]
+        for s in range(2):
             for i, out in enumerate(outs):
-                out[s, :, at] = grad[i * rows : (i + 1) * rows]
-
-
-def call(kernel, operands, out_shape, flops):
+                out[s, :, at] = total[(s * n + i) * rows : (s * n + i + 1) * rows]
+
+    tiles(own.shape[1], score)
+    mixes(scores, mix, factors)
+    tiles(own.shape[1], grad)
+
+
+def call(kernel, operands, out_shape, flops, scratch):
     vmem = pl.BlockSpec(memory_space=pltpu.VMEM)
     moved = sum(x.size * x.dtype.itemsize for x in [*operands, *out_shape])
     return pl.pallas_call(
@@ -118,6 +137,7 @@
         out_shape=out_shape,
         in_specs=[vmem] * len(operands),
         out_specs=[vmem] * len(out_shape),
+        scratch_shapes=scratch,
         compiler_params=pltpu.CompilerParams(vmem_limit_bytes=40 * 2**20),
         cost_estimate=pl.CostEstimate(flops=flops, bytes_accessed=moved, transcendentals=0),
     )(*operands)
@@ -150,20 +170,26 @@
     def flops(keys):
         return 16 * many * width * rows * len(keys)
 
-    joined, acc, up, down = call(
+    def scratch(keys):
+        shape = (2, 2 * many, rows * len(keys))
+        return [pltpu.VMEM(shape, f32), pltpu.VMEM(shape, images.dtype)]
+
+    mine_joined, acc, up, down = call(
         functools.partial(early_kernel, total, len(mine)),
         [factors] + mine + early,
         [jax.ShapeDtypeStruct((2 * many, width), images.dtype)]
-        + [jax.ShapeDtypeStruct(s, f32) for s in [(2, many, width), (many, 128), (rows, 128)]],
+        + [jax.ShapeDtypeStruct(s, f32) for s in [(2 * many, width), (2 * many, 128), (rows, 128)]],
         flops(early),
+        scratch(early) + [pltpu.VMEM((2 * many, 128), f32)],
     )
     last, acc = lax.optimization_barrier((line[-1], acc))
     late = copies + [last] + pair(last)
     first, *parts = call(
         functools.partial(late_kernel, len(mine)),
-        [factors, joined, acc, up] + late,
+        [factors, mine_joined, acc, up] + late,
         [jax.ShapeDtypeStruct((2, rows, width), f32)] * len(mine),
         flops(late),
+        scratch(late),
     )
     back = [
         lax.ppermute(part.astype(jnp.float16), both, square_shift(n_row, n_col, -j, -k))

time: 29.8 us -> 31.8 us (1.067)
  Pallas kernels: 1.88 us -> 3.88 us
  waiting for transfers between devices: 11.6 us -> 11.2 us
    pallas_call x2, Pallas kernels: 1.88 us -> 3.88 us  [call(): pl.pallas_call(kernel, out_shape=out_shape, in_specs=[vmem] * len(operand...]
    ppermute x3, waiting for transfers between devices: 1.69 us -> 1.35 us  [local(): line.append(lax.ppermute(line[which], 'col', perm))]
    ppermute x4, starting transfers between devices: 0.23 us -> 0.57 us  [pair(): lax.ppermute(block, 'row', inner_shift(n_row, k))]
  transfers between devices with their start and end apart: 13 -> 13, of which waited for: 9 -> 8; matrix products, arithmetic and copies ran while one was open for 1% -> 1% of each run, Pallas kernels for 3% -> 6%
where the time goes in v12:
time: 31.8 us; the launch traced here: 31.6 us
  starting transfers between devices  13.9 us (44%)
  waiting for transfers between devices  11.2 us (35%)
  Pallas kernels  3.88 us (12%)
  other arithmetic  1.73 us (5%)
  between operations  0.72 us (2%)
    ppermute x3, starting transfers between devices, local(): line.append(lax.ppermute(line[which], 'col', perm))  6.29 us
    ppermute x3, waiting for transfers between devices, local(): lax.ppermute(part.astype(jnp.float16), both, square_shift(n_row, n_col, -...  5.97 us
    pallas_call x2, Pallas kernels, call(): pl.pallas_call(kernel, out_shape=out_shape, in_specs=[vmem] * len(operand...  3.88 us
    ppermute x3, starting transfers between devices, local(): lax.ppermute(part.astype(jnp.float16), both, square_shift(n_row, n_col, -...  3.57 us
    ppermute x3, starting transfers between devices, local(): lax.ppermute(own, both, square_shift(n_row, n_col, j, k))  3.49 us
    ppermute x3, waiting for transfers between devices, local(): lax.ppermute(own, both, square_shift(n_row, n_col, j, k))  2.93 us
    ppermute x3, waiting for transfers between devices, local(): line.append(lax.ppermute(line[which], 'col', perm))  1.35 us
    ppermute x4, waiting for transfers between devices, pair(): lax.ppermute(block, 'row', inner_shift(n_row, k))  0.98 us
  transfers between devices with their start and end apart: 13, of which 8 were waited for; matrix products, arithmetic and copies ran while one was open for 1% of the time, Pallas kernels for 6%

profile of v12, /device:TPU:0, one launch (start us, length us, event | category | flops | bytes accessed | tf_op | source)
XLA Modules:
  0.0 31.6 jit_solution(13750121195382728305)
XLA Ops:
  0.6 0.0 copy-start
  0.6 0.9 %pad_maximum_fusion.refs_0_.refs_4_ = bf16[2,32,1024]{2,1,0:T(8,128)(2,1)S(1)} fusion(bf16[1,32,1024]{2,1,0:T(8,128)(2,1)} %bitcast.6, bf16[1,32,1024]{2,1,0:T(8,128)(2,1)} %bitcast.7), kind=kLoop, calls=%fused_computation | loop fusion | flops 65536 | bytes 262144 | tf_op jit(solution)/shard_map/stack | solution.py:154
  1.5 4.1 %collective-permute-start.3 = (bf16[2,32,1024]{2,1,0:T(8,128)(2,1)S(1)}, bf16[2,32,1024]{2,1,0:T(8,128)(2,1)S(1)}, u32[]{:S(2)}, u32[]{:S(2)}) collective-permute-start(bf16[2,32,1024]{2,1,0:T(8,128)(2,1)S(1)} %pad_maximum_fusion.refs_0_.refs_4_), channel_id=1, source_target_pairs={{0,4},{1,5},{2,6},{3,7},{4,0},{5,1},{6,2},{7,3},{8,12},{9,13},{10,... | collective-permute-start | bytes 393224 | tf_op jit(solution)/shard_map/ppermute | solution.py:160
  5.6 1.6 %collective-permute-start.4 = (bf16[2,32,1024]{2,1,0:T(8,128)(2,1)S(1)}, bf16[2,32,1024]{2,1,0:T(8,128)(2,1)S(1)}, u32[]{:S(2)}, u32[]{:S(2)}) collective-permute-start(bf16[2,32,1024]{2,1,0:T(8,128)(2,1)S(1)} %pad_maximum_fusion.refs_0_.refs_4_), channel_id=1, source_target_pairs={{0,2},{1,3},{2,0},{3,1},{4,6},{5,7},{6,4},{7,5},{8,10},{9,11},{10,... | collective-permute-start | bytes 393224 | tf_op jit(solution)/shard_map/ppermute | solution.py:160
  7.2 2.4 %collective-permute-start.2 = (bf16[2,32,1024]{2,1,0:T(8,128)(2,1)S(1)}, bf16[2,32,1024]{2,1,0:T(8,128)(2,1)S(1)}, u32[]{:S(2)}, u32[]{:S(2)}) collective-permute-start(bf16[2,32,1024]{2,1,0:T(8,128)(2,1)S(1)} %pad_maximum_fusion.refs_0_.refs_4_), channel_id=1, source_target_pairs={{0,17},{1,16},{2,19},{3,18},{4,21},{5,20},{6,23},{7,22},{8,25},{9,... | collective-permute-start | bytes 393224 | tf_op jit(solution)/shard_map/ppermute | solution.py:156
  9.7 0.5 %collective-permute-start.1 = (bf16[2,32,1024]{2,1,0:T(8,128)(2,1)S(1)}, bf16[2,32,1024]{2,1,0:T(8,128)(2,1)S(1)}, u32[]{:S(2)}, u32[]{:S(2)}) collective-permute-start(bf16[2,32,1024]{2,1,0:T(8,128)(2,1)S(1)} %pad_maximum_fusion.refs_0_.refs_4_), channel_id=1, source_target_pairs={{0,16},{1,17},{2,18},{3,19},{4,20},{5,21},{6,22},{7,23},{8,24},{9,... | collective-permute-start | bytes 393224 | tf_op jit(solution)/shard_map/ppermute | solution.py:156
  10.2 0.5 %collective-permute-start = (bf16[2,32,1024]{2,1,0:T(8,128)(2,1)S(1)}, bf16[2,32,1024]{2,1,0:T(8,128)(2,1)S(1)}, u32[]{:S(2)}, u32[]{:S(2)}) collective-permute-start(bf16[2,32,1024]{2,1,0:T(8,128)(2,1)S(1)} %pad_maximum_fusion.refs_0_.refs_4_), channel_id=1, source_target_pairs={{0,1},{1,0},{2,3},{3,2},{4,5},{5,4},{6,7},{7,6},{8,9},{9,8},{10,11... | collective-permute-start | bytes 393224 | tf_op jit(solution)/shard_map/ppermute | solution.py:156
  10.7 1.3 %collective-permute-done.3.refs_5_ = bf16[2,32,1024]{2,1,0:T(8,128)(2,1)S(1)} collective-permute-done((bf16[2,32,1024]{2,1,0:T(8,128)(2,1)S(1)}, bf16[2,32,1024]{2,1,0:T(8,128)(2,1)S(1)}, u32[]{:S(2)}, u32[]{:S(2)}) %collective-permute-start.3) | collective-permute-done | bytes 131104 | tf_op jit(solution)/shard_map/ppermute | solution.py:160
  12.0 0.6 %collective-permute-start.5 = (bf16[2,32,1024]{2,1,0:T(8,128)(2,1)S(1)}, bf16[2,32,1024]{2,1,0:T(8,128)(2,1)S(1)}, u32[]{:S(2)}, u32[]{:S(2)}) collective-permute-start(bf16[2,32,1024]{2,1,0:T(8,128)(2,1)S(1)} %collective-permute-done.3.refs_5_), channel_id=1, source_target_pairs={{0,2},{1,3},{2,0},{3,1},{4,6},{5,7},{6,4},{7,5},{8,10},{9,11},{10,... | collective-permute-start | bytes 393224 | tf_op jit(solution)/shard_map/ppermute | solution.py:160
  12.7 0.0 copy-done
  12.7 0.0 collective-permute-done.4.refs_6_
  12.7 0.1 collective-permute-start.6
  12.8 1.0 %collective-permute-done.2.refs_3_ = bf16[2,32,1024]{2,1,0:T(8,128)(2,1)S(1)} collective-permute-done((bf16[2,32,1024]{2,1,0:T(8,128)(2,1)S(1)}, bf16[2,32,1024]{2,1,0:T(8,128)(2,1)S(1)}, u32[]{:S(2)}, u32[]{:S(2)}) %collective-permute-start.2) | collective-permute-done | bytes 131104 | tf_op jit(solution)/shard_map/ppermute | solution.py:156
  13.8 0.0 collective-permute-start.7
  13.8 1.8 %collective-permute-done.1.refs_2_ = bf16[2,32,1024]{2,1,0:T(8,128)(2,1)S(1)} collective-permute-done((bf16[2,32,1024]{2,1,0:T(8,128)(2,1)S(1)}, bf16[2,32,1024]{2,1,0:T(8,128)(2,1)S(1)}, u32[]{:S(2)}, u32[]{:S(2)}) %collective-permute-start.1) | collective-permute-done | bytes 131104 | tf_op jit(solution)/shard_map/ppermute | solution.py:156
  15.6 0.0 collective-permute-start.8
  15.6 0.1 collective-permute-done.refs_1_
  15.7 0.1 broadcast_in_dim.2.factors
  15.8 1.9 %shard_map.50 = (bf16[256,1024]{1,0:T(8,128)(2,1)S(1)}, f32[256,1024]{1,0:T(8,128)S(1)}, f32[256,128]{1,0:T(8,128)S(1)}, f32[32,128]{1,0:T(8,128)S(1)}) custom-call(f32[2,128]{1,0:T(2,128)S(1)} %broadcast_in_dim.2.factors, bf16[2,32,1024]{2,1,0:T(8,128)(2,1)S(1)} %pad_maximum_fusion.refs_0_.refs_4_, bf16[2,32,1024]{2,1,0:T(8,128)(2,1)S(1)} %collective-permute-done.refs_1_, ...), custom_call_target="tpu_custom_call" | custom-call | flops 201326592 | bytes 2638848 | tf_op jit(solution)/shard_map/pallas_call | solution.py:135
  17.7 0.0 collective-permute-done.5.refs_3_
  17.7 0.5 %collective-permute-start.9 = (bf16[2,32,1024]{2,1,0:T(8,128)(2,1)S(1)}, bf16[2,32,1024]{2,1,0:T(8,128)(2,1)S(1)}, u32[]{:S(2)}, u32[]{:S(2)}) collective-permute-start(bf16[2,32,1024]{2,1,0:T(8,128)(2,1)S(1)} %collective-permute-done.5.refs_3_), channel_id=1, source_target_pairs={{0,8},{8,0},{16,24},{24,16},{1,9},{9,1},{17,25},{25,17},{2,10},{10... | collective-permute-start | bytes 393224 | tf_op jit(solution)/shard_map/ppermute | solution.py:163
  18.2 0.0 collective-permute-done.6.refs_0_
  18.2 0.0 collective-permute-done.8.refs_2_
  18.2 0.0 collective-permute-done.7.refs_1_
  18.2 1.0 %collective-permute-done.9.refs_4_ = bf16[2,32,1024]{2,1,0:T(8,128)(2,1)S(1)} collective-permute-done((bf16[2,32,1024]{2,1,0:T(8,128)(2,1)S(1)}, bf16[2,32,1024]{2,1,0:T(8,128)(2,1)S(1)}, u32[]{:S(2)}, u32[]{:S(2)}) %collective-permute-start.9) | collective-permute-done | bytes 131104 | tf_op jit(solution)/shard_map/ppermute | solution.py:163
  19.2 2.0 %shard_map.51 = (f32[2,32,1024]{2,1,0:T(8,128)S(1)}, f32[2,32,1024]{2,1,0:T(8,128)S(1)}, f32[2,32,1024]{2,1,0:T(8,128)S(1)}, f32[2,32,1024]{2,1,0:T(8,128)S(1)}) custom-call(f32[2,128]{1,0:T(2,128)S(1)} %broadcast_in_dim.2.factors, bf16[256,1024]{1,0:T(8,128)(2,1)S(1)} %get-tuple-element.12.own, f32[256,1024]{1,0:T(8,128)S(1)} %get-tuple-element.14.acc, ...), custom_call_target="tpu_custom_call" | custom-call | flops 335544320 | bytes 3408896 | tf_op jit(solution)/shard_map/pallas_call | solution.py:135
  21.2 1.8 %collective-permute-start.12 = (f16[2,32,1024]{2,1,0:T(8,128)(2,1)S(1)}, f16[2,32,1024]{2,1,0:T(8,128)(2,1)S(1)}, u32[]{:S(2)}, u32[]{:S(2)}) collective-permute-start(f16[2,32,1024]{2,1,0:T(8,128)(2,1)S(1)} %convert_element_type.37), channel_id=1, source_target_pairs={{0,17},{1,16},{2,19},{3,18},{4,21},{5,20},{6,23},{7,22},{8,25},{9,... | collective-permute-start | bytes 393224 | tf_op jit(solution)/shard_map/ppermute | solution.py:195
  23.0 1.2 %collective-permute-start.11 = (f16[2,32,1024]{2,1,0:T(8,128)(2,1)S(1)}, f16[2,32,1024]{2,1,0:T(8,128)(2,1)S(1)}, u32[]{:S(2)}, u32[]{:S(2)}) collective-permute-start(f16[2,32,1024]{2,1,0:T(8,128)(2,1)S(1)} %convert_element_type.35), channel_id=1, source_target_pairs={{0,16},{1,17},{2,18},{3,19},{4,20},{5,21},{6,22},{7,23},{8,24},{9,... | collective-permute-start | bytes 393224 | tf_op jit(solution)/shard_map/ppermute | solution.py:195
  24.2 0.5 %collective-permute-start.10 = (f16[2,32,1024]{2,1,0:T(8,128)(2,1)S(1)}, f16[2,32,1024]{2,1,0:T(8,128)(2,1)S(1)}, u32[]{:S(2)}, u32[]{:S(2)}) collective-permute-start(f16[2,32,1024]{2,1,0:T(8,128)(2,1)S(1)} %convert_element_type.33), channel_id=1, source_target_pairs={{0,1},{1,0},{2,3},{3,2},{4,5},{5,4},{6,7},{7,6},{8,9},{9,8},{10,11... | collective-permute-start | bytes 393224 | tf_op jit(solution)/shard_map/ppermute | solution.py:195
  24.8 0.1 slice_reduce_fusion
  24.9 3.6 %collective-permute-done.12 = f16[2,32,1024]{2,1,0:T(8,128)(2,1)S(1)} collective-permute-done((f16[2,32,1024]{2,1,0:T(8,128)(2,1)S(1)}, f16[2,32,1024]{2,1,0:T(8,128)(2,1)S(1)}, u32[]{:S(2)}, u32[]{:S(2)}) %collective-permute-start.12) | collective-permute-done | bytes 131104 | tf_op jit(solution)/shard_map/ppermute | solution.py:195
  28.5 2.2 %collective-permute-done.11 = f16[2,32,1024]{2,1,0:T(8,128)(2,1)S(1)} collective-permute-done((f16[2,32,1024]{2,1,0:T(8,128)(2,1)S(1)}, f16[2,32,1024]{2,1,0:T(8,128)(2,1)S(1)}, u32[]{:S(2)}, u32[]{:S(2)}) %collective-permute-start.11) | collective-permute-done | bytes 131104 | tf_op jit(solution)/shard_map/ppermute | solution.py:195
  30.8 0.1 collective-permute-done.10
  30.9 0.8 %bitcast_multiply_fusion = (f32[32,1024]{1,0:T(8,128)}, f32[32,1024]{1,0:T(8,128)}) fusion(f32[2,32,1024]{2,1,0:T(8,128)S(1)} %get-tuple-element.17, f16[2,32,1024]{2,1,0:T(8,128)(2,1)S(1)} %collective-permute-done.12, f16[2,32,1024]{2,1,0:T(8,128)(2,1)S(1)} %collective-permute-done.11, f16[2,32,1024]{2,1,0:T(8,128)(2,1)S(1)} %collective-permute-done.10, ...), kind=kLoop, calls=%fused_computation.1 | loop fusion | flops 458752 | bytes 917632 | tf_op jit(solution)/shard_map/mul | solution.py:203
  (4 shorter events, 0.1 us)
Async XLA Ops:
  0.6 12.0 %copy-start = (f32[2]{0:T(128)S(1)}, f32[2]{0:T(128)}, u32[]{:S(2)}) copy-start(f32[2]{0:T(128)} %param.5) | copy-start | bytes 28
  1.5 10.5 %collective-permute-start.3 = (bf16[2,32,1024]{2,1,0:T(8,128)(2,1)S(1)}, bf16[2,32,1024]{2,1,0:T(8,128)(2,1)S(1)}, u32[]{:S(2)}, u32[]{:S(2)}) collective-permute-start(bf16[2,32,1024]{2,1,0:T(8,128)(2,1)S(1)} %pad_maximum_fusion.refs_0_.refs_4_), channel_id=1, source_target_pairs={{0,4},{1,5},{2,6},{3,7},{4,0},{5,1},{6,2},{7,3},{8,12},{9,13},{10,... | collective-permute-start | bytes 393224 | tf_op jit(solution)/shard_map/ppermute | solution.py:160
  5.6 7.0 %collective-permute-start.4 = (bf16[2,32,1024]{2,1,0:T(8,128)(2,1)S(1)}, bf16[2,32,1024]{2,1,0:T(8,128)(2,1)S(1)}, u32[]{:S(2)}, u32[]{:S(2)}) collective-permute-start(bf16[2,32,1024]{2,1,0:T(8,128)(2,1)S(1)} %pad_maximum_fusion.refs_0_.refs_4_), channel_id=1, source_target_pairs={{0,2},{1,3},{2,0},{3,1},{4,6},{5,7},{6,4},{7,5},{8,10},{9,11},{10,... | collective-permute-start | bytes 393224 | tf_op jit(solution)/shard_map/ppermute | solution.py:160
  7.2 6.6 %collective-permute-start.2 = (bf16[2,32,1024]{2,1,0:T(8,128)(2,1)S(1)}, bf16[2,32,1024]{2,1,0:T(8,128)(2,1)S(1)}, u32[]{:S(2)}, u32[]{:S(2)}) collective-permute-start(bf16[2,32,1024]{2,1,0:T(8,128)(2,1)S(1)} %pad_maximum_fusion.refs_0_.refs_4_), channel_id=1, source_target_pairs={{0,17},{1,16},{2,19},{3,18},{4,21},{5,20},{6,23},{7,22},{8,25},{9,... | collective-permute-start | bytes 393224 | tf_op jit(solution)/shard_map/ppermute | solution.py:156
  9.7 5.9 %collective-permute-start.1 = (bf16[2,32,1024]{2,1,0:T(8,128)(2,1)S(1)}, bf16[2,32,1024]{2,1,0:T(8,128)(2,1)S(1)}, u32[]{:S(2)}, u32[]{:S(2)}) collective-permute-start(bf16[2,32,1024]{2,1,0:T(8,128)(2,1)S(1)} %pad_maximum_fusion.refs_0_.refs_4_), channel_id=1, source_target_pairs={{0,16},{1,17},{2,18},{3,19},{4,20},{5,21},{6,22},{7,23},{8,24},{9,... | collective-permute-start | bytes 393224 | tf_op jit(solution)/shard_map/ppermute | solution.py:156
  10.2 5.5 %collective-permute-start = (bf16[2,32,1024]{2,1,0:T(8,128)(2,1)S(1)}, bf16[2,32,1024]{2,1,0:T(8,128)(2,1)S(1)}, u32[]{:S(2)}, u32[]{:S(2)}) collective-permute-start(bf16[2,32,1024]{2,1,0:T(8,128)(2,1)S(1)} %pad_maximum_fusion.refs_0_.refs_4_), channel_id=1, source_target_pairs={{0,1},{1,0},{2,3},{3,2},{4,5},{5,4},{6,7},{7,6},{8,9},{9,8},{10,11... | collective-permute-start | bytes 393224 | tf_op jit(solution)/shard_map/ppermute | solution.py:156
  12.0 5.6 %collective-permute-start.5 = (bf16[2,32,1024]{2,1,0:T(8,128)(2,1)S(1)}, bf16[2,32,1024]{2,1,0:T(8,128)(2,1)S(1)}, u32[]{:S(2)}, u32[]{:S(2)}) collective-permute-start(bf16[2,32,1024]{2,1,0:T(8,128)(2,1)S(1)} %collective-permute-done.3.refs_5_), channel_id=1, source_target_pairs={{0,2},{1,3},{2,0},{3,1},{4,6},{5,7},{6,4},{7,5},{8,10},{9,11},{10,... | collective-permute-start | bytes 393224 | tf_op jit(solution)/shard_map/ppermute | solution.py:160
  12.7 5.5 %collective-permute-start.6 = (bf16[2,32,1024]{2,1,0:T(8,128)(2,1)S(1)}, bf16[2,32,1024]{2,1,0:T(8,128)(2,1)S(1)}, u32[]{:S(2)}, u32[]{:S(2)}) collective-permute-start(bf16[2,32,1024]{2,1,0:T(8,128)(2,1)S(1)} %pad_maximum_fusion.refs_0_.refs_4_), channel_id=1, source_target_pairs={{0,8},{8,0},{16,24},{24,16},{1,9},{9,1},{17,25},{25,17},{2,10},{10... | collective-permute-start | bytes 393224 | tf_op jit(solution)/shard_map/ppermute | solution.py:163
  13.8 4.4 %collective-permute-start.7 = (bf16[2,32,1024]{2,1,0:T(8,128)(2,1)S(1)}, bf16[2,32,1024]{2,1,0:T(8,128)(2,1)S(1)}, u32[]{:S(2)}, u32[]{:S(2)}) collective-permute-start(bf16[2,32,1024]{2,1,0:T(8,128)(2,1)S(1)} %collective-permute-done.3.refs_5_), channel_id=1, source_target_pairs={{0,8},{8,0},{16,24},{24,16},{1,9},{9,1},{17,25},{25,17},{2,10},{10... | collective-permute-start | bytes 393224 | tf_op jit(solution)/shard_map/ppermute | solution.py:163
  15.6 2.6 %collective-permute-start.8 = (bf16[2,32,1024]{2,1,0:T(8,128)(2,1)S(1)}, bf16[2,32,1024]{2,1,0:T(8,128)(2,1)S(1)}, u32[]{:S(2)}, u32[]{:S(2)}) collective-permute-start(bf16[2,32,1024]{2,1,0:T(8,128)(2,1)S(1)} %collective-permute-done.4.refs_6_), channel_id=1, source_target_pairs={{0,8},{8,0},{16,24},{24,16},{1,9},{9,1},{17,25},{25,17},{2,10},{10... | collective-permute-start | bytes 393224 | tf_op jit(solution)/shard_map/ppermute | solution.py:163
  17.7 1.5 %collective-permute-start.9 = (bf16[2,32,1024]{2,1,0:T(8,128)(2,1)S(1)}, bf16[2,32,1024]{2,1,0:T(8,128)(2,1)S(1)}, u32[]{:S(2)}, u32[]{:S(2)}) collective-permute-start(bf16[2,32,1024]{2,1,0:T(8,128)(2,1)S(1)} %collective-permute-done.5.refs_3_), channel_id=1, source_target_pairs={{0,8},{8,0},{16,24},{24,16},{1,9},{9,1},{17,25},{25,17},{2,10},{10... | collective-permute-start | bytes 393224 | tf_op jit(solution)/shard_map/ppermute | solution.py:163
  21.2 7.3 %collective-permute-start.12 = (f16[2,32,1024]{2,1,0:T(8,128)(2,1)S(1)}, f16[2,32,1024]{2,1,0:T(8,128)(2,1)S(1)}, u32[]{:S(2)}, u32[]{:S(2)}) collective-permute-start(f16[2,32,1024]{2,1,0:T(8,128)(2,1)S(1)} %convert_element_type.37), channel_id=1, source_target_pairs={{0,17},{1,16},{2,19},{3,18},{4,21},{5,20},{6,23},{7,22},{8,25},{9,... | collective-permute-start | bytes 393224 | tf_op jit(solution)/shard_map/ppermute | solution.py:195
  23.0 7.7 %collective-permute-start.11 = (f16[2,32,1024]{2,1,0:T(8,128)(2,1)S(1)}, f16[2,32,1024]{2,1,0:T(8,128)(2,1)S(1)}, u32[]{:S(2)}, u32[]{:S(2)}) collective-permute-start(f16[2,32,1024]{2,1,0:T(8,128)(2,1)S(1)} %convert_element_type.35), channel_id=1, source_target_pairs={{0,16},{1,17},{2,18},{3,19},{4,20},{5,21},{6,22},{7,23},{8,24},{9,... | collective-permute-start | bytes 393224 | tf_op jit(solution)/shard_map/ppermute | solution.py:195
  24.2 6.6 %collective-permute-start.10 = (f16[2,32,1024]{2,1,0:T(8,128)(2,1)S(1)}, f16[2,32,1024]{2,1,0:T(8,128)(2,1)S(1)}, u32[]{:S(2)}, u32[]{:S(2)}) collective-permute-start(f16[2,32,1024]{2,1,0:T(8,128)(2,1)S(1)} %convert_element_type.33), channel_id=1, source_target_pairs={{0,1},{1,0},{2,3},{3,2},{4,5},{5,4},{6,7},{7,6},{8,9},{9,8},{10,11... | collective-permute-start | bytes 393224 | tf_op jit(solution)/shard_map/ppermute | solution.py:195

commit v13 on v8

--- a/solution.py
+++ b/solution.py
@@ -83,6 +83,12 @@
     return grad_img, grad_txt
 
 
+def bounds(rows, factors, total):
+    size = jnp.sum(jnp.abs(rows.astype(jnp.float32)), axis=1, keepdims=True)
+    size = size[: size.shape[0] // 2] + size[size.shape[0] // 2 :]
+    return size * ((factors[0:1, 0:1] + factors[1:2, 0:1]) * (1.02 * LIMIT * LIMIT * total)) + 1e-30
+
+
 def early_kernel(total, n, factors, *refs):
     own, acc, up, down = refs[-4:]
     rows = join(refs[:n])
@@ -91,23 +97,26 @@
     p_mat, q_mat = weigh(rows, keys, factors)
     for at in tiles(keys.shape[1]):
         acc[0, :, at], acc[1, :, at] = tile_grads(p_mat, q_mat, keys, at)
-    size = jnp.sum(jnp.abs(rows.astype(jnp.float32)), axis=1, keepdims=True)
-    size = size[: size.shape[0] // 2] + size[size.shape[0] // 2 :]
-    most = size * ((factors[0:1, 0:1] + factors[1:2, 0:1]) * (1.02 * LIMIT * LIMIT * total)) + 1e-30
+    most = bounds(rows, factors, total)
     up[...] = jnp.broadcast_to(TOP / most, up.shape)
     down[...] = jnp.broadcast_to((most / TOP)[: down.shape[0]], down.shape)
 
 
-def late_kernel(n, factors, own, acc, up, *refs):
-    outs = refs[-n:]
-    keys = join(refs[:-n])
+def late_kernel(total, n, m, factors, own, acc, up, *refs):
+    last, early, late, outs = refs[0], refs[1 : m + 1], refs[m + 1 : -n - 1], refs[-n - 1 :]
+    rows = last.shape[1]
+    keys, every = join(late), join(early + late)
     p_mat, q_mat = weigh(own[...], keys, factors)
-    rows = outs[0].shape[1]
+    rest = join([last])
+    p_rest, q_rest = weigh(rest, every, factors)
+    factor = TOP / bounds(rest, factors, total)
     for at in tiles(keys.shape[1]):
         for s, grad in enumerate(tile_grads(p_mat, q_mat, keys, at)):
             grad = (grad + acc[s, :, at]) * up[:, :1]
-            for i, out in enumerate(outs):
-                out[s, :, at] = grad[i * rows : (i + 1) * rows]
+            for i in range(n):
+                outs[i][s, :, at] = grad[i * rows : (i + 1) * rows]
+        for s, grad in enumerate(tile_grads(p_rest, q_rest, every, at)):
+            outs[n][s, :, at] = grad * factor
 
 
 def call(kernel, operands, out_shape, flops):
@@ -130,7 +139,8 @@
     batch = rows * n_row * n_col
     factors = jnp.broadcast_to((loss_weights * (1.0 / math.sqrt(width * batch)))[:, None], (2, 128))
     both = ("row", "col")
-    square = [(j, k) for j in range(halves(n_row)[0]) for k in range(halves(n_col)[1])][1:]
+    square = [(j, k) for j in range(halves(n_row)[0]) for k in range(halves(n_col)[1])]
+    square = square[2:] + square[1:2]
     own = jnp.stack([images, texts])
 
     mine = [own] + [lax.ppermute(own, both, square_shift(n_row, n_col, j, k)) for j, k in square]
@@ -147,39 +157,39 @@
         return [lax.ppermute(block, "row", inner_shift(n_row, k)) for k in range(1, row_inner)]
 
     early, copies = line[:-1], []
-    for i, block in enumerate(line[:-1]):
-        if i == 0 and square:
-            block, mine[-2] = lax.optimization_barrier((block, mine[-2]))
+    for block in early:
+        if block is own and len(mine) > 1:
+            block, mine[1] = lax.optimization_barrier((block, mine[1]))
         copies += pair(block)
     total = rows * len(line) * row_inner
-    many = rows * len(mine)
     f32 = jnp.float32
-
-    def flops(keys):
-        return 16 * many * width * rows * len(keys)
-
-    joined, acc, up, down = call(
-        functools.partial(early_kernel, total, len(mine)),
-        [factors] + mine + early,
+    *first, last = mine
+    many = rows * len(first)
+
+    def flops(blocks, keys):
+        return 16 * rows * width * rows * blocks * keys
+
+    mine_joined, acc, up, down = call(
+        functools.partial(early_kernel, total, len(first)),
+        [factors] + first + early,
         [jax.ShapeDtypeStruct((2 * many, width), images.dtype)]
         + [jax.ShapeDtypeStruct(s, f32) for s in [(2, many, width), (many, 128), (rows, 128)]],
-        flops(early),
+        flops(len(first), len(early)),
     )
-    last, acc = lax.optimization_barrier((line[-1], acc))
-    late = copies + [last] + pair(last)
-    first, *parts = call(
-        functools.partial(late_kernel, len(mine)),
-        [factors, joined, acc, up] + late,
+    late = copies + [line[-1]] + pair(line[-1])
+    parts = call(
+        functools.partial(late_kernel, total, len(first), len(early)),
+        [factors, mine_joined, acc, up, last] + early + late,
         [jax.ShapeDtypeStruct((2, rows, width), f32)] * len(mine),
-        flops(late),
+        flops(len(first), len(late)) + flops(1, len(early + late)),
     )
+    far = sorted(zip(square, parts[1:]), key=lambda item: sum(item[0]))
     back = [
-        lax.ppermute(part.astype(jnp.float16), both, square_shift(n_row, n_col, -j, -k))
-        for part, (j, k) in zip(parts, square)
+        lax.ppermute(part.astype(jnp.float16), both, square_shift(n_row, n_col, -j, -k)) for (j, k), part in far
     ]
     grads = []
     for s in range(2):
-        total = first[s]
+        total = parts[0][s]
         for part in back:
             total = total + part[s].astype(f32)
         grads.append(total * down[:, :1])

time: 34.4 us -> 29.5 us (0.86)
  waiting for transfers between devices: 14.2 us -> 8.66 us
  starting transfers between devices: 15.5 us -> 15.9 us
    ppermute x3, waiting for transfers between devices: 3.43 us -> 0.31 us  [local(): lax.ppermute(own, both, square_shift(n_row, n_col, j, k))]
    ppermute x4, waiting for transfers between devices: 1.27 us -> 0.09 us  [pair(): lax.ppermute(block, 'row', inner_shift(n_row, k))]
    ppermute x4, waiting for transfers between devices: 3.72 us -> 2.57 us  [local(): apart[step] = [lax.ppermute(half, 'col', perm) for half in apart[which]]]
    ppermute x3, starting transfers between devices: 3.55 us -> 4.36 us  [local(): lax.ppermute(own, both, square_shift(n_row, n_col, j, k))]
  transfers between devices with their start and end apart: 15 -> 15, of which waited for: 7 -> 8; matrix products, arithmetic and copies ran while one was open for 3% -> 4% of each run, Pallas kernels for 3% -> 3%
where the time goes in v13:
time: 29.5 us; the launch traced here: 29.3 us
  starting transfers between devices  15.9 us (54%)
  waiting for transfers between devices  8.66 us (29%)
  Pallas kernels  2.13 us (7%)
  other arithmetic  1.75 us (6%)
  between operations  0.71 us (2%)
    ppermute x4, starting transfers between devices, local(): apart[step] = [lax.ppermute(half, 'col', perm) for half in apart[which]]  5.71 us
    ppermute x3, waiting for transfers between devices, local(): lax.ppermute(part.astype(jnp.float16), both, square_shift(n_row, n_col, -...  5.69 us
    ppermute x3, starting transfers between devices, local(): lax.ppermute(own, both, square_shift(n_row, n_col, j, k))  4.36 us
    ppermute x3, starting transfers between devices, local(): lax.ppermute(part.astype(jnp.float16), both, square_shift(n_row, n_col, -...  3.55 us
    ppermute x4, waiting for transfers between devices, local(): apart[step] = [lax.ppermute(half, 'col', perm) for half in apart[which]]  2.57 us
    pallas_call x2, Pallas kernels, call(): pl.pallas_call(kernel, out_shape=out_shape, in_specs=[vmem] * len(operand...  2.13 us
    ppermute x1, starting transfers between devices, local(): line.append(lax.ppermute(line[which], 'col', perm))  1.58 us
    another operation x1, other arithmetic, local(): own = jnp.stack([images, texts])  0.89 us
  transfers between devices with their start and end apart: 15, of which 8 were waited for; matrix products, arithmetic and copies ran while one was open for 4% of the time, Pallas kernels for 3%

profile of v13, /device:TPU:0, one launch (start us, length us, event | category | flops | bytes accessed | tf_op | source)
XLA Modules:
  0.0 29.3 jit_solution(13500265923920094316)
XLA Ops:
  0.6 4.1 %collective-permute-start.2 = (bf16[32,1024]{1,0:T(8,128)(2,1)}, bf16[32,1024]{1,0:T(8,128)(2,1)S(1)}, u32[]{:S(2)}, u32[]{:S(2)}) collective-permute-start(bf16[32,1024]{1,0:T(8,128)(2,1)} %param.3), channel_id=1, source_target_pairs={{0,4},{1,5},{2,6},{3,7},{4,0},{5,1},{6,2},{7,3},{8,12},{9,13},{10,... | collective-permute-start | bytes 196616 | tf_op jit(solution)/shard_map/ppermute | solution.py:151
  4.7 0.1 collective-permute-start.3
  4.8 0.9 %pad_maximum_fusion.refs_0_.refs_3_.refs_1_ = bf16[2,32,1024]{2,1,0:T(8,128)(2,1)S(1)} fusion(bf16[1,32,1024]{2,1,0:T(8,128)(2,1)} %bitcast.11, bf16[1,32,1024]{2,1,0:T(8,128)(2,1)} %bitcast.10), kind=kLoop, calls=%fused_computation | loop fusion | flops 65536 | bytes 262144 | tf_op jit(solution)/shard_map/stack | solution.py:144
  5.7 1.8 %collective-permute-start = (bf16[2,32,1024]{2,1,0:T(8,128)(2,1)S(1)}, bf16[2,32,1024]{2,1,0:T(8,128)(2,1)S(1)}, u32[]{:S(2)}, u32[]{:S(2)}) collective-permute-start(bf16[2,32,1024]{2,1,0:T(8,128)(2,1)S(1)} %pad_maximum_fusion.refs_0_.refs_3_.refs_1_), channel_id=1, source_target_pairs={{0,16},{1,17},{2,18},{3,19},{4,20},{5,21},{6,22},{7,23},{8,24},{9,... | collective-permute-start | bytes 393224 | tf_op jit(solution)/shard_map/ppermute | solution.py:146
  7.5 1.6 %collective-permute-start.4 = (bf16[2,32,1024]{2,1,0:T(8,128)(2,1)S(1)}, bf16[2,32,1024]{2,1,0:T(8,128)(2,1)S(1)}, u32[]{:S(2)}, u32[]{:S(2)}) collective-permute-start(bf16[2,32,1024]{2,1,0:T(8,128)(2,1)S(1)} %pad_maximum_fusion.refs_0_.refs_3_.refs_1_), channel_id=1, source_target_pairs={{0,2},{1,3},{2,0},{3,1},{4,6},{5,7},{6,4},{7,5},{8,10},{9,11},{10,... | collective-permute-start | bytes 393224 | tf_op jit(solution)/shard_map/ppermute | solution.py:154
  9.1 1.4 %collective-permute-start.1 = (bf16[2,32,1024]{2,1,0:T(8,128)(2,1)S(1)}, bf16[2,32,1024]{2,1,0:T(8,128)(2,1)S(1)}, u32[]{:S(2)}, u32[]{:S(2)}) collective-permute-start(bf16[2,32,1024]{2,1,0:T(8,128)(2,1)S(1)} %pad_maximum_fusion.refs_0_.refs_3_.refs_1_), channel_id=1, source_target_pairs={{0,17},{1,16},{2,19},{3,18},{4,21},{5,20},{6,23},{7,22},{8,25},{9,... | collective-permute-start | bytes 393224 | tf_op jit(solution)/shard_map/ppermute | solution.py:146
  10.6 0.0 collective-permute-done.2
  10.6 0.5 %collective-permute-start.9 = (bf16[32,1024]{1,0:T(8,128)(2,1)S(1)}, bf16[32,1024]{1,0:T(8,128)(2,1)S(1)}, u32[]{:S(2)}, u32[]{:S(2)}) collective-permute-start(bf16[32,1024]{1,0:T(8,128)(2,1)S(1)} %collective-permute-done.2), channel_id=1, source_target_pairs={{0,2},{1,3},{2,0},{3,1},{4,6},{5,7},{6,4},{7,5},{8,10},{9,11},{10,... | collective-permute-start | bytes 196616 | tf_op jit(solution)/shard_map/ppermute | solution.py:151
  11.0 0.5 %collective-permute-done.3 = bf16[32,1024]{1,0:T(8,128)(2,1)S(1)} collective-permute-done((bf16[32,1024]{1,0:T(8,128)(2,1)}, bf16[32,1024]{1,0:T(8,128)(2,1)S(1)}, u32[]{:S(2)}, u32[]{:S(2)}) %collective-permute-start.3) | collective-permute-done | bytes 65568 | tf_op jit(solution)/shard_map/ppermute | solution.py:151
  11.5 1.1 %collective-permute-start.10 = (bf16[32,1024]{1,0:T(8,128)(2,1)S(1)}, bf16[32,1024]{1,0:T(8,128)(2,1)S(1)}, u32[]{:S(2)}, u32[]{:S(2)}) collective-permute-start(bf16[32,1024]{1,0:T(8,128)(2,1)S(1)} %collective-permute-done.3), channel_id=1, source_target_pairs={{0,2},{1,3},{2,0},{3,1},{4,6},{5,7},{6,4},{7,5},{8,10},{9,11},{10,... | collective-permute-start | bytes 196616 | tf_op jit(solution)/shard_map/ppermute | solution.py:151
  12.6 0.0 collective-permute-done.refs_1_
  12.6 1.1 %collective-permute-start.5 = (bf16[2,32,1024]{2,1,0:T(8,128)(2,1)S(1)}, bf16[2,32,1024]{2,1,0:T(8,128)(2,1)S(1)}, u32[]{:S(2)}, u32[]{:S(2)}) collective-permute-start(bf16[2,32,1024]{2,1,0:T(8,128)(2,1)S(1)} %pad_maximum_fusion.refs_0_.refs_3_.refs_1_), channel_id=1, source_target_pairs={{0,1},{1,0},{2,3},{3,2},{4,5},{5,4},{6,7},{7,6},{8,9},{9,8},{10,11... | collective-permute-start | bytes 393224 | tf_op jit(solution)/shard_map/ppermute | solution.py:146
  13.7 1.3 %collective-permute-done.9 = bf16[32,1024]{1,0:T(8,128)(2,1)S(1)} collective-permute-done((bf16[32,1024]{1,0:T(8,128)(2,1)S(1)}, bf16[32,1024]{1,0:T(8,128)(2,1)S(1)}, u32[]{:S(2)}, u32[]{:S(2)}) %collective-permute-start.9) | collective-permute-done | bytes 65568 | tf_op jit(solution)/shard_map/ppermute | solution.py:151
  15.0 0.0 collective-permute-start.7
  15.0 0.8 %collective-permute-done.10 = bf16[32,1024]{1,0:T(8,128)(2,1)S(1)} collective-permute-done((bf16[32,1024]{1,0:T(8,128)(2,1)S(1)}, bf16[32,1024]{1,0:T(8,128)(2,1)S(1)}, u32[]{:S(2)}, u32[]{:S(2)}) %collective-permute-start.10) | collective-permute-done | bytes 65568 | tf_op jit(solution)/shard_map/ppermute | solution.py:151
  15.8 0.0 collective-permute-start.6
  15.8 0.0 copy-start
  15.8 0.0 collective-permute-done.4.refs_5_.refs_3_
  15.8 0.6 %collective-permute-start.11 = (bf16[2,32,1024]{2,1,0:T(8,128)(2,1)S(1)}, bf16[2,32,1024]{2,1,0:T(8,128)(2,1)S(1)}, u32[]{:S(2)}, u32[]{:S(2)}) collective-permute-start(bf16[2,32,1024]{2,1,0:T(8,128)(2,1)S(1)} %pad_maximum_fusion.2.refs_7_), channel_id=1, source_target_pairs={{0,8},{8,0},{16,24},{24,16},{1,9},{9,1},{17,25},{25,17},{2,10},{10... | collective-permute-start | bytes 393224 | tf_op jit(solution)/shard_map/ppermute | solution.py:157
  16.4 0.0 collective-permute-done.1.refs_2_
  16.4 0.1 collective-permute-start.8
  16.5 0.0 copy-done
  16.5 0.1 broadcast_in_dim.2.factors
  16.5 0.8 %shard_map.50 = (bf16[192,1024]{1,0:T(8,128)(2,1)S(1)}, f32[2,96,1024]{2,1,0:T(8,128)S(1)}, f32[96,128]{1,0:T(8,128)S(1)}, f32[32,128]{1,0:T(8,128)S(1)}) custom-call(f32[2,128]{1,0:T(2,128)S(1)} %broadcast_in_dim.2.factors, bf16[2,32,1024]{2,1,0:T(8,128)(2,1)S(1)} %pad_maximum_fusion.refs_0_.refs_3_.refs_1_, ...), custom_call_target="tpu_custom_call" | custom-call | flops 150994944 | bytes 2032640 | tf_op jit(solution)/shard_map/pallas_call | solution.py:125
  17.3 0.3 %collective-permute-done.5.refs_0_ = bf16[2,32,1024]{2,1,0:T(8,128)(2,1)S(1)} collective-permute-done((bf16[2,32,1024]{2,1,0:T(8,128)(2,1)S(1)}, bf16[2,32,1024]{2,1,0:T(8,128)(2,1)S(1)}, u32[]{:S(2)}, u32[]{:S(2)}) %collective-permute-start.5) | collective-permute-done | bytes 131104 | tf_op jit(solution)/shard_map/ppermute | solution.py:146
  17.6 0.0 collective-permute-done.7.refs_5_
  17.7 0.1 collective-permute-done.8.refs_6_
  17.7 0.0 collective-permute-done.6.refs_4_
  17.7 0.0 collective-permute-done.11.refs_8_
  17.7 1.3 %shard_map.51 = (f32[2,32,1024]{2,1,0:T(8,128)S(1)}, f32[2,32,1024]{2,1,0:T(8,128)S(1)}, f32[2,32,1024]{2,1,0:T(8,128)S(1)}, f32[2,32,1024]{2,1,0:T(8,128)S(1)}) custom-call(f32[2,128]{1,0:T(2,128)S(1)} %broadcast_in_dim.2.factors, bf16[192,1024]{1,0:T(8,128)(2,1)S(1)} %get-tuple-element.13.own, f32[2,96,1024]{2,1,0:T(8,128)S(1)} %get-tuple-element.14.acc, ...), custom_call_target="tpu_custom_call" | custom-call | flops 385875968 | bytes 3458048 | tf_op jit(solution)/shard_map/pallas_call | solution.py:125
  19.2 2.4 %collective-permute-start.14 = (f16[2,32,1024]{2,1,0:T(8,128)(2,1)S(1)}, f16[2,32,1024]{2,1,0:T(8,128)(2,1)S(1)}, u32[]{:S(2)}, u32[]{:S(2)}) collective-permute-start(f16[2,32,1024]{2,1,0:T(8,128)(2,1)S(1)} %convert_element_type.37), channel_id=1, source_target_pairs={{0,17},{1,16},{2,19},{3,18},{4,21},{5,20},{6,23},{7,22},{8,25},{9,... | collective-permute-start | bytes 393224 | tf_op jit(solution)/shard_map/ppermute | solution.py:188
  21.5 0.6 %collective-permute-start.13 = (f16[2,32,1024]{2,1,0:T(8,128)(2,1)S(1)}, f16[2,32,1024]{2,1,0:T(8,128)(2,1)S(1)}, u32[]{:S(2)}, u32[]{:S(2)}) collective-permute-start(f16[2,32,1024]{2,1,0:T(8,128)(2,1)S(1)} %convert_element_type.35), channel_id=1, source_target_pairs={{0,1},{1,0},{2,3},{3,2},{4,5},{5,4},{6,7},{7,6},{8,9},{9,8},{10,11... | collective-permute-start | bytes 393224 | tf_op jit(solution)/shard_map/ppermute | solution.py:188
  22.1 0.6 %collective-permute-start.12 = (f16[2,32,1024]{2,1,0:T(8,128)(2,1)S(1)}, f16[2,32,1024]{2,1,0:T(8,128)(2,1)S(1)}, u32[]{:S(2)}, u32[]{:S(2)}) collective-permute-start(f16[2,32,1024]{2,1,0:T(8,128)(2,1)S(1)} %convert_element_type.33), channel_id=1, source_target_pairs={{0,16},{1,17},{2,18},{3,19},{4,20},{5,21},{6,22},{7,23},{8,24},{9,... | collective-permute-start | bytes 393224 | tf_op jit(solution)/shard_map/ppermute | solution.py:188
  22.7 0.1 slice_reduce_fusion
  22.8 3.6 %collective-permute-done.14 = f16[2,32,1024]{2,1,0:T(8,128)(2,1)S(1)} collective-permute-done((f16[2,32,1024]{2,1,0:T(8,128)(2,1)S(1)}, f16[2,32,1024]{2,1,0:T(8,128)(2,1)S(1)}, u32[]{:S(2)}, u32[]{:S(2)}) %collective-permute-start.14) | collective-permute-done | bytes 131104 | tf_op jit(solution)/shard_map/ppermute | solution.py:188
  26.5 2.0 %collective-permute-done.13 = f16[2,32,1024]{2,1,0:T(8,128)(2,1)S(1)} collective-permute-done((f16[2,32,1024]{2,1,0:T(8,128)(2,1)S(1)}, f16[2,32,1024]{2,1,0:T(8,128)(2,1)S(1)}, u32[]{:S(2)}, u32[]{:S(2)}) %collective-permute-start.13) | collective-permute-done | bytes 131104 | tf_op jit(solution)/shard_map/ppermute | solution.py:188
  28.5 0.1 collective-permute-done.12
  28.5 0.8 %bitcast_multiply_fusion = (f32[32,1024]{1,0:T(8,128)}, f32[32,1024]{1,0:T(8,128)}) fusion(f32[2,32,1024]{2,1,0:T(8,128)S(1)} %get-tuple-element.17, f16[2,32,1024]{2,1,0:T(8,128)(2,1)S(1)} %collective-permute-done.14, f16[2,32,1024]{2,1,0:T(8,128)(2,1)S(1)} %collective-permute-done.13, f16[2,32,1024]{2,1,0:T(8,128)(2,1)S(1)} %collective-permute-done.12, ...), kind=kLoop, calls=%fused_computation.3 | loop fusion | flops 458752 | bytes 917632 | tf_op jit(solution)/shard_map/mul | solution.py:195
  (6 shorter events, 0.1 us)
Async XLA Ops:
  0.6 9.9 %collective-permute-start.2 = (bf16[32,1024]{1,0:T(8,128)(2,1)}, bf16[32,1024]{1,0:T(8,128)(2,1)S(1)}, u32[]{:S(2)}, u32[]{:S(2)}) collective-permute-start(bf16[32,1024]{1,0:T(8,128)(2,1)} %param.3), channel_id=1, source_target_pairs={{0,4},{1,5},{2,6},{3,7},{4,0},{5,1},{6,2},{7,3},{8,12},{9,13},{10,... | collective-permute-start | bytes 196616 | tf_op jit(solution)/shard_map/ppermute | solution.py:151
  4.7 6.8 %collective-permute-start.3 = (bf16[32,1024]{1,0:T(8,128)(2,1)}, bf16[32,1024]{1,0:T(8,128)(2,1)S(1)}, u32[]{:S(2)}, u32[]{:S(2)}) collective-permute-start(bf16[32,1024]{1,0:T(8,128)(2,1)} %param.4), channel_id=1, source_target_pairs={{0,4},{1,5},{2,6},{3,7},{4,0},{5,1},{6,2},{7,3},{8,12},{9,13},{10,... | collective-permute-start | bytes 196616 | tf_op jit(solution)/shard_map/ppermute | solution.py:151
  5.7 6.9 %collective-permute-start = (bf16[2,32,1024]{2,1,0:T(8,128)(2,1)S(1)}, bf16[2,32,1024]{2,1,0:T(8,128)(2,1)S(1)}, u32[]{:S(2)}, u32[]{:S(2)}) collective-permute-start(bf16[2,32,1024]{2,1,0:T(8,128)(2,1)S(1)} %pad_maximum_fusion.refs_0_.refs_3_.refs_1_), channel_id=1, source_target_pairs={{0,16},{1,17},{2,18},{3,19},{4,20},{5,21},{6,22},{7,23},{8,24},{9,... | collective-permute-start | bytes 393224 | tf_op jit(solution)/shard_map/ppermute | solution.py:146
  7.5 8.3 %collective-permute-start.4 = (bf16[2,32,1024]{2,1,0:T(8,128)(2,1)S(1)}, bf16[2,32,1024]{2,1,0:T(8,128)(2,1)S(1)}, u32[]{:S(2)}, u32[]{:S(2)}) collective-permute-start(bf16[2,32,1024]{2,1,0:T(8,128)(2,1)S(1)} %pad_maximum_fusion.refs_0_.refs_3_.refs_1_), channel_id=1, source_target_pairs={{0,2},{1,3},{2,0},{3,1},{4,6},{5,7},{6,4},{7,5},{8,10},{9,11},{10,... | collective-permute-start | bytes 393224 | tf_op jit(solution)/shard_map/ppermute | solution.py:154
  9.1 7.3 %collective-permute-start.1 = (bf16[2,32,1024]{2,1,0:T(8,128)(2,1)S(1)}, bf16[2,32,1024]{2,1,0:T(8,128)(2,1)S(1)}, u32[]{:S(2)}, u32[]{:S(2)}) collective-permute-start(bf16[2,32,1024]{2,1,0:T(8,128)(2,1)S(1)} %pad_maximum_fusion.refs_0_.refs_3_.refs_1_), channel_id=1, source_target_pairs={{0,17},{1,16},{2,19},{3,18},{4,21},{5,20},{6,23},{7,22},{8,25},{9,... | collective-permute-start | bytes 393224 | tf_op jit(solution)/shard_map/ppermute | solution.py:146
  10.6 4.4 %collective-permute-start.9 = (bf16[32,1024]{1,0:T(8,128)(2,1)S(1)}, bf16[32,1024]{1,0:T(8,128)(2,1)S(1)}, u32[]{:S(2)}, u32[]{:S(2)}) collective-permute-start(bf16[32,1024]{1,0:T(8,128)(2,1)S(1)} %collective-permute-done.2), channel_id=1, source_target_pairs={{0,2},{1,3},{2,0},{3,1},{4,6},{5,7},{6,4},{7,5},{8,10},{9,11},{10,... | collective-permute-start | bytes 196616 | tf_op jit(solution)/shard_map/ppermute | solution.py:151
  11.5 4.3 %collective-permute-start.10 = (bf16[32,1024]{1,0:T(8,128)(2,1)S(1)}, bf16[32,1024]{1,0:T(8,128)(2,1)S(1)}, u32[]{:S(2)}, u32[]{:S(2)}) collective-permute-start(bf16[32,1024]{1,0:T(8,128)(2,1)S(1)} %collective-permute-done.3), channel_id=1, source_target_pairs={{0,2},{1,3},{2,0},{3,1},{4,6},{5,7},{6,4},{7,5},{8,10},{9,11},{10,... | collective-permute-start | bytes 196616 | tf_op jit(solution)/shard_map/ppermute | solution.py:151
  12.6 5.0 %collective-permute-start.5 = (bf16[2,32,1024]{2,1,0:T(8,128)(2,1)S(1)}, bf16[2,32,1024]{2,1,0:T(8,128)(2,1)S(1)}, u32[]{:S(2)}, u32[]{:S(2)}) collective-permute-start(bf16[2,32,1024]{2,1,0:T(8,128)(2,1)S(1)} %pad_maximum_fusion.refs_0_.refs_3_.refs_1_), channel_id=1, source_target_pairs={{0,1},{1,0},{2,3},{3,2},{4,5},{5,4},{6,7},{7,6},{8,9},{9,8},{10,11... | collective-permute-start | bytes 393224 | tf_op jit(solution)/shard_map/ppermute | solution.py:146
  15.0 2.7 %collective-permute-start.7 = (bf16[2,32,1024]{2,1,0:T(8,128)(2,1)S(1)}, bf16[2,32,1024]{2,1,0:T(8,128)(2,1)S(1)}, u32[]{:S(2)}, u32[]{:S(2)}) collective-permute-start(bf16[2,32,1024]{2,1,0:T(8,128)(2,1)S(1)} %pad_maximum_fusion.1.refs_4_.refs_2_), channel_id=1, source_target_pairs={{0,8},{8,0},{16,24},{24,16},{1,9},{9,1},{17,25},{25,17},{2,10},{10... | collective-permute-start | bytes 393224 | tf_op jit(solution)/shard_map/ppermute | solution.py:157
  15.8 2.0 %collective-permute-start.6 = (bf16[2,32,1024]{2,1,0:T(8,128)(2,1)S(1)}, bf16[2,32,1024]{2,1,0:T(8,128)(2,1)S(1)}, u32[]{:S(2)}, u32[]{:S(2)}) collective-permute-start(bf16[2,32,1024]{2,1,0:T(8,128)(2,1)S(1)} %pad_maximum_fusion.refs_0_.refs_3_.refs_1_), channel_id=1, source_target_pairs={{0,8},{8,0},{16,24},{24,16},{1,9},{9,1},{17,25},{25,17},{2,10},{10... | collective-permute-start | bytes 393224 | tf_op jit(solution)/shard_map/ppermute | solution.py:157
  15.8 0.7 %copy-start = (f32[2]{0:T(128)S(1)}, f32[2]{0:T(128)}, u32[]{:S(2)}) copy-start(f32[2]{0:T(128)} %param.5) | copy-start | bytes 28
  15.8 1.9 %collective-permute-start.11 = (bf16[2,32,1024]{2,1,0:T(8,128)(2,1)S(1)}, bf16[2,32,1024]{2,1,0:T(8,128)(2,1)S(1)}, u32[]{:S(2)}, u32[]{:S(2)}) collective-permute-start(bf16[2,32,1024]{2,1,0:T(8,128)(2,1)S(1)} %pad_maximum_fusion.2.refs_7_), channel_id=1, source_target_pairs={{0,8},{8,0},{16,24},{24,16},{1,9},{9,1},{17,25},{25,17},{2,10},{10... | collective-permute-start | bytes 393224 | tf_op jit(solution)/shard_map/ppermute | solution.py:157
  16.4 1.3 %collective-permute-start.8 = (bf16[2,32,1024]{2,1,0:T(8,128)(2,1)S(1)}, bf16[2,32,1024]{2,1,0:T(8,128)(2,1)S(1)}, u32[]{:S(2)}, u32[]{:S(2)}) collective-permute-start(bf16[2,32,1024]{2,1,0:T(8,128)(2,1)S(1)} %collective-permute-done.4.refs_5_.refs_3_), channel_id=1, source_target_pairs={{0,8},{8,0},{16,24},{24,16},{1,9},{9,1},{17,25},{25,17},{2,10},{10... | collective-permute-start | bytes 393224 | tf_op jit(solution)/shard_map/ppermute | solution.py:157
  19.2 7.3 %collective-permute-start.14 = (f16[2,32,1024]{2,1,0:T(8,128)(2,1)S(1)}, f16[2,32,1024]{2,1,0:T(8,128)(2,1)S(1)}, u32[]{:S(2)}, u32[]{:S(2)}) collective-permute-start(f16[2,32,1024]{2,1,0:T(8,128)(2,1)S(1)} %convert_element_type.37), channel_id=1, source_target_pairs={{0,17},{1,16},{2,19},{3,18},{4,21},{5,20},{6,23},{7,22},{8,25},{9,... | collective-permute-start | bytes 393224 | tf_op jit(solution)/shard_map/ppermute | solution.py:188
  21.5 6.9 %collective-permute-start.13 = (f16[2,32,1024]{2,1,0:T(8,128)(2,1)S(1)}, f16[2,32,1024]{2,1,0:T(8,128)(2,1)S(1)}, u32[]{:S(2)}, u32[]{:S(2)}) collective-permute-start(f16[2,32,1024]{2,1,0:T(8,128)(2,1)S(1)} %convert_element_type.35), channel_id=1, source_target_pairs={{0,1},{1,0},{2,3},{3,2},{4,5},{5,4},{6,7},{7,6},{8,9},{9,8},{10,11... | collective-permute-start | bytes 393224 | tf_op jit(solution)/shard_map/ppermute | solution.py:188
  22.1 6.4 %collective-permute-start.12 = (f16[2,32,1024]{2,1,0:T(8,128)(2,1)S(1)}, f16[2,32,1024]{2,1,0:T(8,128)(2,1)S(1)}, u32[]{:S(2)}, u32[]{:S(2)}) collective-permute-start(f16[2,32,1024]{2,1,0:T(8,128)(2,1)S(1)} %convert_element_type.33), channel_id=1, source_target_pairs={{0,16},{1,17},{2,18},{3,19},{4,20},{5,21},{6,22},{7,23},{8,24},{9,... | collective-permute-start | bytes 393224 | tf_op jit(solution)/shard_map/ppermute | solution.py:188

commit v14 on v13

--- a/solution.py
+++ b/solution.py
@@ -157,9 +157,11 @@
         return [lax.ppermute(block, "row", inner_shift(n_row, k)) for k in range(1, row_inner)]
 
     early, copies = line[:-1], []
-    for block in early:
-        if block is own and len(mine) > 1:
+    for i, block in enumerate(line[:-1]):
+        if i == 0 and len(mine) > 1:
             block, mine[1] = lax.optimization_barrier((block, mine[1]))
+        if i == 1 and len(early) > 2:
+            block, early[2] = lax.optimization_barrier((block, early[2]))
         copies += pair(block)
     total = rows * len(line) * row_inner
     f32 = jnp.float32

time: 29.5 us -> 29.4 us (level)
  waiting for transfers between devices: 8.66 us -> 6.85 us
  starting transfers between devices: 15.9 us -> 17.6 us
    ppermute x4, waiting for transfers between devices: 2.57 us -> 0.05 us  [local(): apart[step] = [lax.ppermute(half, 'col', perm) for half in apart[which]]]
    ppermute x3, waiting for transfers between devices: 0.31 us -> 1.03 us  [local(): lax.ppermute(own, both, square_shift(n_row, n_col, j, k))]
    ppermute x3, starting transfers between devices: 4.36 us -> 4.84 us  [local(): lax.ppermute(own, both, square_shift(n_row, n_col, j, k))]
    ppermute x4, starting transfers between devices: 5.71 us -> 6.17 us  [local(): apart[step] = [lax.ppermute(half, 'col', perm) for half in apart[which]]]
    ppermute x4, starting transfers between devices: 0.66 us -> 1.09 us  [pair(): lax.ppermute(block, 'row', inner_shift(n_row, k))]
    ppermute x1, starting transfers between devices: 1.58 us -> 1.9 us  [local(): line.append(lax.ppermute(line[which], 'col', perm))]
  transfers between devices with their start and end apart: 15 -> 15, of which waited for: 8 -> 6; matrix products, arithmetic and copies ran while one was open for 4% -> 4% of each run, Pallas kernels for 3% -> 3%
where the time goes in v14:
time: 29.4 us; the launch traced here: 29.2 us
  starting transfers between devices  17.6 us (60%)
  waiting for transfers between devices  6.85 us (23%)
  Pallas kernels  2.13 us (7%)
  other arithmetic  1.75 us (6%)
  between operations  0.7 us (2%)
    ppermute x4, starting transfers between devices, local(): apart[step] = [lax.ppermute(half, 'col', perm) for half in apart[which]]  6.17 us
    ppermute x3, waiting for transfers between devices, local(): lax.ppermute(part.astype(jnp.float16), both, square_shift(n_row, n_col, -...  5.67 us
    ppermute x3, starting transfers between devices, local(): lax.ppermute(own, both, square_shift(n_row, n_col, j, k))  4.84 us
    ppermute x3, starting transfers between devices, local(): lax.ppermute(part.astype(jnp.float16), both, square_shift(n_row, n_col, -...  3.56 us
    pallas_call x2, Pallas kernels, call(): pl.pallas_call(kernel, out_shape=out_shape, in_specs=[vmem] * len(operand...  2.13 us
    ppermute x1, starting transfers between devices, local(): line.append(lax.ppermute(line[which], 'col', perm))  1.9 us
    ppermute x4, starting transfers between devices, pair(): lax.ppermute(block, 'row', inner_shift(n_row, k))  1.09 us
    ppermute x3, waiting for transfers between devices, local(): lax.ppermute(own, both, square_shift(n_row, n_col, j, k))  1.03 us
  transfers between devices with their start and end apart: 15, of which 6 were waited for; matrix products, arithmetic and copies ran while one was open for 4% of the time, Pallas kernels for 3%

profile of v14, /device:TPU:0, one launch (start us, length us, event | category | flops | bytes accessed | tf_op | source)
XLA Modules:
  0.0 29.2 jit_solution(675813437878671366)
XLA Ops:
  0.6 4.1 %collective-permute-start.2 = (bf16[32,1024]{1,0:T(8,128)(2,1)}, bf16[32,1024]{1,0:T(8,128)(2,1)S(1)}, u32[]{:S(2)}, u32[]{:S(2)}) collective-permute-start(bf16[32,1024]{1,0:T(8,128)(2,1)} %param.3), channel_id=1, source_target_pairs={{0,4},{1,5},{2,6},{3,7},{4,0},{5,1},{6,2},{7,3},{8,12},{9,13},{10,... | collective-permute-start | bytes 196616 | tf_op jit(solution)/shard_map/ppermute | solution.py:151
  4.7 0.1 collective-permute-start.3
  4.8 0.9 %pad_maximum_fusion.refs_0_.refs_3_.refs_1_ = bf16[2,32,1024]{2,1,0:T(8,128)(2,1)S(1)} fusion(bf16[1,32,1024]{2,1,0:T(8,128)(2,1)} %bitcast.11, bf16[1,32,1024]{2,1,0:T(8,128)(2,1)} %bitcast.10), kind=kLoop, calls=%fused_computation | loop fusion | flops 65536 | bytes 262144 | tf_op jit(solution)/shard_map/stack | solution.py:144
  5.7 1.9 %collective-permute-start.4 = (bf16[2,32,1024]{2,1,0:T(8,128)(2,1)S(1)}, bf16[2,32,1024]{2,1,0:T(8,128)(2,1)S(1)}, u32[]{:S(2)}, u32[]{:S(2)}) collective-permute-start(bf16[2,32,1024]{2,1,0:T(8,128)(2,1)S(1)} %pad_maximum_fusion.refs_0_.refs_3_.refs_1_), channel_id=1, source_target_pairs={{0,2},{1,3},{2,0},{3,1},{4,6},{5,7},{6,4},{7,5},{8,10},{9,11},{10,... | collective-permute-start | bytes 393224 | tf_op jit(solution)/shard_map/ppermute | solution.py:154
  7.6 1.5 %collective-permute-start = (bf16[2,32,1024]{2,1,0:T(8,128)(2,1)S(1)}, bf16[2,32,1024]{2,1,0:T(8,128)(2,1)S(1)}, u32[]{:S(2)}, u32[]{:S(2)}) collective-permute-start(bf16[2,32,1024]{2,1,0:T(8,128)(2,1)S(1)} %pad_maximum_fusion.refs_0_.refs_3_.refs_1_), channel_id=1, source_target_pairs={{0,16},{1,17},{2,18},{3,19},{4,20},{5,21},{6,22},{7,23},{8,24},{9,... | collective-permute-start | bytes 393224 | tf_op jit(solution)/shard_map/ppermute | solution.py:146
  9.1 1.4 %collective-permute-start.1 = (bf16[2,32,1024]{2,1,0:T(8,128)(2,1)S(1)}, bf16[2,32,1024]{2,1,0:T(8,128)(2,1)S(1)}, u32[]{:S(2)}, u32[]{:S(2)}) collective-permute-start(bf16[2,32,1024]{2,1,0:T(8,128)(2,1)S(1)} %pad_maximum_fusion.refs_0_.refs_3_.refs_1_), channel_id=1, source_target_pairs={{0,17},{1,16},{2,19},{3,18},{4,21},{5,20},{6,23},{7,22},{8,25},{9,... | collective-permute-start | bytes 393224 | tf_op jit(solution)/shard_map/ppermute | solution.py:146
  10.6 0.0 collective-permute-done.2
  10.6 0.5 %collective-permute-start.9 = (bf16[32,1024]{1,0:T(8,128)(2,1)S(1)}, bf16[32,1024]{1,0:T(8,128)(2,1)S(1)}, u32[]{:S(2)}, u32[]{:S(2)}) collective-permute-start(bf16[32,1024]{1,0:T(8,128)(2,1)S(1)} %collective-permute-done.2), channel_id=1, source_target_pairs={{0,2},{1,3},{2,0},{3,1},{4,6},{5,7},{6,4},{7,5},{8,10},{9,11},{10,... | collective-permute-start | bytes 196616 | tf_op jit(solution)/shard_map/ppermute | solution.py:151
  11.0 0.0 collective-permute-done.3
  11.0 1.5 %collective-permute-start.10 = (bf16[32,1024]{1,0:T(8,128)(2,1)S(1)}, bf16[32,1024]{1,0:T(8,128)(2,1)S(1)}, u32[]{:S(2)}, u32[]{:S(2)}) collective-permute-start(bf16[32,1024]{1,0:T(8,128)(2,1)S(1)} %collective-permute-done.3), channel_id=1, source_target_pairs={{0,2},{1,3},{2,0},{3,1},{4,6},{5,7},{6,4},{7,5},{8,10},{9,11},{10,... | collective-permute-start | bytes 196616 | tf_op jit(solution)/shard_map/ppermute | solution.py:151
  12.6 0.1 collective-permute-done.4.refs_5_.refs_3_
  12.7 1.9 %collective-permute-start.5 = (bf16[2,32,1024]{2,1,0:T(8,128)(2,1)S(1)}, bf16[2,32,1024]{2,1,0:T(8,128)(2,1)S(1)}, u32[]{:S(2)}, u32[]{:S(2)}) collective-permute-start(bf16[2,32,1024]{2,1,0:T(8,128)(2,1)S(1)} %pad_maximum_fusion.refs_0_.refs_3_.refs_1_), channel_id=1, source_target_pairs={{0,1},{1,0},{2,3},{3,2},{4,5},{5,4},{6,7},{7,6},{8,9},{9,8},{10,11... | collective-permute-start | bytes 393224 | tf_op jit(solution)/shard_map/ppermute | solution.py:146
  14.6 0.8 %collective-permute-done.refs_1_ = bf16[2,32,1024]{2,1,0:T(8,128)(2,1)S(1)} collective-permute-done((bf16[2,32,1024]{2,1,0:T(8,128)(2,1)S(1)}, bf16[2,32,1024]{2,1,0:T(8,128)(2,1)S(1)}, u32[]{:S(2)}, u32[]{:S(2)}) %collective-permute-start) | collective-permute-done | bytes 131104 | tf_op jit(solution)/shard_map/ppermute | solution.py:146
  15.4 0.0 collective-permute-start.7
  15.4 0.0 collective-permute-done.9
  15.4 0.5 %collective-permute-start.6 = (bf16[2,32,1024]{2,1,0:T(8,128)(2,1)S(1)}, bf16[2,32,1024]{2,1,0:T(8,128)(2,1)S(1)}, u32[]{:S(2)}, u32[]{:S(2)}) collective-permute-start(bf16[2,32,1024]{2,1,0:T(8,128)(2,1)S(1)} %pad_maximum_fusion.refs_0_.refs_3_.refs_1_), channel_id=1, source_target_pairs={{0,8},{8,0},{16,24},{24,16},{1,9},{9,1},{17,25},{25,17},{2,10},{10... | collective-permute-start | bytes 393224 | tf_op jit(solution)/shard_map/ppermute | solution.py:157
  15.9 0.0 collective-permute-done.10
  15.9 0.0 copy-start
  15.9 0.1 collective-permute-start.11
  16.0 0.0 collective-permute-done.1.refs_2_
  16.0 0.5 %collective-permute-start.8 = (bf16[2,32,1024]{2,1,0:T(8,128)(2,1)S(1)}, bf16[2,32,1024]{2,1,0:T(8,128)(2,1)S(1)}, u32[]{:S(2)}, u32[]{:S(2)}) collective-permute-start(bf16[2,32,1024]{2,1,0:T(8,128)(2,1)S(1)} %collective-permute-done.4.refs_5_.refs_3_), channel_id=1, source_target_pairs={{0,8},{8,0},{16,24},{24,16},{1,9},{9,1},{17,25},{25,17},{2,10},{10... | collective-permute-start | bytes 393224 | tf_op jit(solution)/shard_map/ppermute | solution.py:157
  16.5 0.1 copy-done
  16.6 0.1 broadcast_in_dim.2.factors
  16.6 0.8 %shard_map.50 = (bf16[192,1024]{1,0:T(8,128)(2,1)S(1)}, f32[2,96,1024]{2,1,0:T(8,128)S(1)}, f32[96,128]{1,0:T(8,128)S(1)}, f32[32,128]{1,0:T(8,128)S(1)}) custom-call(f32[2,128]{1,0:T(2,128)S(1)} %broadcast_in_dim.2.factors, bf16[2,32,1024]{2,1,0:T(8,128)(2,1)S(1)} %pad_maximum_fusion.refs_0_.refs_3_.refs_1_, ...), custom_call_target="tpu_custom_call" | custom-call | flops 150994944 | bytes 2032640 | tf_op jit(solution)/shard_map/pallas_call | solution.py:125
  17.4 0.2 collective-permute-done.5.refs_0_
  17.7 0.0 collective-permute-done.7.refs_5_
  17.7 0.0 collective-permute-done.8.refs_6_
  17.7 0.0 collective-permute-done.6.refs_4_
  17.7 0.0 collective-permute-done.11.refs_8_
  17.7 1.3 %shard_map.51 = (f32[2,32,1024]{2,1,0:T(8,128)S(1)}, f32[2,32,1024]{2,1,0:T(8,128)S(1)}, f32[2,32,1024]{2,1,0:T(8,128)S(1)}, f32[2,32,1024]{2,1,0:T(8,128)S(1)}) custom-call(f32[2,128]{1,0:T(2,128)S(1)} %broadcast_in_dim.2.factors, bf16[192,1024]{1,0:T(8,128)(2,1)S(1)} %get-tuple-element.16.own, f32[2,96,1024]{2,1,0:T(8,128)S(1)} %get-tuple-element.17.acc, ...), custom_call_target="tpu_custom_call" | custom-call | flops 385875968 | bytes 3458048 | tf_op jit(solution)/shard_map/pallas_call | solution.py:125
  19.1 2.9 %collective-permute-start.14 = (f16[2,32,1024]{2,1,0:T(8,128)(2,1)S(1)}, f16[2,32,1024]{2,1,0:T(8,128)(2,1)S(1)}, u32[]{:S(2)}, u32[]{:S(2)}) collective-permute-start(f16[2,32,1024]{2,1,0:T(8,128)(2,1)S(1)} %convert_element_type.37), channel_id=1, source_target_pairs={{0,17},{1,16},{2,19},{3,18},{4,21},{5,20},{6,23},{7,22},{8,25},{9,... | collective-permute-start | bytes 393224 | tf_op jit(solution)/shard_map/ppermute | solution.py:190
  22.0 0.5 %collective-permute-start.13 = (f16[2,32,1024]{2,1,0:T(8,128)(2,1)S(1)}, f16[2,32,1024]{2,1,0:T(8,128)(2,1)S(1)}, u32[]{:S(2)}, u32[]{:S(2)}) collective-permute-start(f16[2,32,1024]{2,1,0:T(8,128)(2,1)S(1)} %convert_element_type.35), channel_id=1, source_target_pairs={{0,1},{1,0},{2,3},{3,2},{4,5},{5,4},{6,7},{7,6},{8,9},{9,8},{10,11... | collective-permute-start | bytes 393224 | tf_op jit(solution)/shard_map/ppermute | solution.py:190
  22.6 0.1 collective-permute-start.12
  22.7 0.1 slice_reduce_fusion
  22.8 3.6 %collective-permute-done.14 = f16[2,32,1024]{2,1,0:T(8,128)(2,1)S(1)} collective-permute-done((f16[2,32,1024]{2,1,0:T(8,128)(2,1)S(1)}, f16[2,32,1024]{2,1,0:T(8,128)(2,1)S(1)}, u32[]{:S(2)}, u32[]{:S(2)}) %collective-permute-start.14) | collective-permute-done | bytes 131104 | tf_op jit(solution)/shard_map/ppermute | solution.py:190
  26.4 1.9 %collective-permute-done.13 = f16[2,32,1024]{2,1,0:T(8,128)(2,1)S(1)} collective-permute-done((f16[2,32,1024]{2,1,0:T(8,128)(2,1)S(1)}, f16[2,32,1024]{2,1,0:T(8,128)(2,1)S(1)}, u32[]{:S(2)}, u32[]{:S(2)}) %collective-permute-start.13) | collective-permute-done | bytes 131104 | tf_op jit(solution)/shard_map/ppermute | solution.py:190
  28.3 0.1 collective-permute-done.12
  28.4 0.8 %bitcast_multiply_fusion = (f32[32,1024]{1,0:T(8,128)}, f32[32,1024]{1,0:T(8,128)}) fusion(f32[2,32,1024]{2,1,0:T(8,128)S(1)} %get-tuple-element.21, f16[2,32,1024]{2,1,0:T(8,128)(2,1)S(1)} %collective-permute-done.14, f16[2,32,1024]{2,1,0:T(8,128)(2,1)S(1)} %collective-permute-done.13, f16[2,32,1024]{2,1,0:T(8,128)(2,1)S(1)} %collective-permute-done.12, ...), kind=kLoop, calls=%fused_computation.3 | loop fusion | flops 458752 | bytes 917632 | tf_op jit(solution)/shard_map/mul | solution.py:197
  (6 shorter events, 0.1 us)
Async XLA Ops:
  0.6 9.9 %collective-permute-start.2 = (bf16[32,1024]{1,0:T(8,128)(2,1)}, bf16[32,1024]{1,0:T(8,128)(2,1)S(1)}, u32[]{:S(2)}, u32[]{:S(2)}) collective-permute-start(bf16[32,1024]{1,0:T(8,128)(2,1)} %param.3), channel_id=1, source_target_pairs={{0,4},{1,5},{2,6},{3,7},{4,0},{5,1},{6,2},{7,3},{8,12},{9,13},{10,... | collective-permute-start | bytes 196616 | tf_op jit(solution)/shard_map/ppermute | solution.py:151
  4.7 6.3 %collective-permute-start.3 = (bf16[32,1024]{1,0:T(8,128)(2,1)}, bf16[32,1024]{1,0:T(8,128)(2,1)S(1)}, u32[]{:S(2)}, u32[]{:S(2)}) collective-permute-start(bf16[32,1024]{1,0:T(8,128)(2,1)} %param.4), channel_id=1, source_target_pairs={{0,4},{1,5},{2,6},{3,7},{4,0},{5,1},{6,2},{7,3},{8,12},{9,13},{10,... | collective-permute-start | bytes 196616 | tf_op jit(solution)/shard_map/ppermute | solution.py:151
  5.7 7.0 %collective-permute-start.4 = (bf16[2,32,1024]{2,1,0:T(8,128)(2,1)S(1)}, bf16[2,32,1024]{2,1,0:T(8,128)(2,1)S(1)}, u32[]{:S(2)}, u32[]{:S(2)}) collective-permute-start(bf16[2,32,1024]{2,1,0:T(8,128)(2,1)S(1)} %pad_maximum_fusion.refs_0_.refs_3_.refs_1_), channel_id=1, source_target_pairs={{0,2},{1,3},{2,0},{3,1},{4,6},{5,7},{6,4},{7,5},{8,10},{9,11},{10,... | collective-permute-start | bytes 393224 | tf_op jit(solution)/shard_map/ppermute | solution.py:154
  7.6 7.8 %collective-permute-start = (bf16[2,32,1024]{2,1,0:T(8,128)(2,1)S(1)}, bf16[2,32,1024]{2,1,0:T(8,128)(2,1)S(1)}, u32[]{:S(2)}, u32[]{:S(2)}) collective-permute-start(bf16[2,32,1024]{2,1,0:T(8,128)(2,1)S(1)} %pad_maximum_fusion.refs_0_.refs_3_.refs_1_), channel_id=1, source_target_pairs={{0,16},{1,17},{2,18},{3,19},{4,20},{5,21},{6,22},{7,23},{8,24},{9,... | collective-permute-start | bytes 393224 | tf_op jit(solution)/shard_map/ppermute | solution.py:146
  9.1 6.9 %collective-permute-start.1 = (bf16[2,32,1024]{2,1,0:T(8,128)(2,1)S(1)}, bf16[2,32,1024]{2,1,0:T(8,128)(2,1)S(1)}, u32[]{:S(2)}, u32[]{:S(2)}) collective-permute-start(bf16[2,32,1024]{2,1,0:T(8,128)(2,1)S(1)} %pad_maximum_fusion.refs_0_.refs_3_.refs_1_), channel_id=1, source_target_pairs={{0,17},{1,16},{2,19},{3,18},{4,21},{5,20},{6,23},{7,22},{8,25},{9,... | collective-permute-start | bytes 393224 | tf_op jit(solution)/shard_map/ppermute | solution.py:146
  10.6 4.8 %collective-permute-start.9 = (bf16[32,1024]{1,0:T(8,128)(2,1)S(1)}, bf16[32,1024]{1,0:T(8,128)(2,1)S(1)}, u32[]{:S(2)}, u32[]{:S(2)}) collective-permute-start(bf16[32,1024]{1,0:T(8,128)(2,1)S(1)} %collective-permute-done.2), channel_id=1, source_target_pairs={{0,2},{1,3},{2,0},{3,1},{4,6},{5,7},{6,4},{7,5},{8,10},{9,11},{10,... | collective-permute-start | bytes 196616 | tf_op jit(solution)/shard_map/ppermute | solution.py:151
  11.0 4.8 %collective-permute-start.10 = (bf16[32,1024]{1,0:T(8,128)(2,1)S(1)}, bf16[32,1024]{1,0:T(8,128)(2,1)S(1)}, u32[]{:S(2)}, u32[]{:S(2)}) collective-permute-start(bf16[32,1024]{1,0:T(8,128)(2,1)S(1)} %collective-permute-done.3), channel_id=1, source_target_pairs={{0,2},{1,3},{2,0},{3,1},{4,6},{5,7},{6,4},{7,5},{8,10},{9,11},{10,... | collective-permute-start | bytes 196616 | tf_op jit(solution)/shard_map/ppermute | solution.py:151
  12.7 5.0 %collective-permute-start.5 = (bf16[2,32,1024]{2,1,0:T(8,128)(2,1)S(1)}, bf16[2,32,1024]{2,1,0:T(8,128)(2,1)S(1)}, u32[]{:S(2)}, u32[]{:S(2)}) collective-permute-start(bf16[2,32,1024]{2,1,0:T(8,128)(2,1)S(1)} %pad_maximum_fusion.refs_0_.refs_3_.refs_1_), channel_id=1, source_target_pairs={{0,1},{1,0},{2,3},{3,2},{4,5},{5,4},{6,7},{7,6},{8,9},{9,8},{10,11... | collective-permute-start | bytes 393224 | tf_op jit(solution)/shard_map/ppermute | solution.py:146
  15.4 2.3 %collective-permute-start.7 = (bf16[2,32,1024]{2,1,0:T(8,128)(2,1)S(1)}, bf16[2,32,1024]{2,1,0:T(8,128)(2,1)S(1)}, u32[]{:S(2)}, u32[]{:S(2)}) collective-permute-start(bf16[2,32,1024]{2,1,0:T(8,128)(2,1)S(1)} %pad_maximum_fusion.1.refs_4_.refs_2_), channel_id=1, source_target_pairs={{0,8},{8,0},{16,24},{24,16},{1,9},{9,1},{17,25},{25,17},{2,10},{10... | collective-permute-start | bytes 393224 | tf_op jit(solution)/shard_map/ppermute | solution.py:157
  15.4 2.3 %collective-permute-start.6 = (bf16[2,32,1024]{2,1,0:T(8,128)(2,1)S(1)}, bf16[2,32,1024]{2,1,0:T(8,128)(2,1)S(1)}, u32[]{:S(2)}, u32[]{:S(2)}) collective-permute-start(bf16[2,32,1024]{2,1,0:T(8,128)(2,1)S(1)} %pad_maximum_fusion.refs_0_.refs_3_.refs_1_), channel_id=1, source_target_pairs={{0,8},{8,0},{16,24},{24,16},{1,9},{9,1},{17,25},{25,17},{2,10},{10... | collective-permute-start | bytes 393224 | tf_op jit(solution)/shard_map/ppermute | solution.py:157
  15.9 0.7 %copy-start = (f32[2]{0:T(128)S(1)}, f32[2]{0:T(128)}, u32[]{:S(2)}) copy-start(f32[2]{0:T(128)} %param.5) | copy-start | bytes 28
  15.9 1.8 %collective-permute-start.11 = (bf16[2,32,1024]{2,1,0:T(8,128)(2,1)S(1)}, bf16[2,32,1024]{2,1,0:T(8,128)(2,1)S(1)}, u32[]{:S(2)}, u32[]{:S(2)}) collective-permute-start(bf16[2,32,1024]{2,1,0:T(8,128)(2,1)S(1)} %pad_maximum_fusion.2.refs_7_), channel_id=1, source_target_pairs={{0,8},{8,0},{16,24},{24,16},{1,9},{9,1},{17,25},{25,17},{2,10},{10... | collective-permute-start | bytes 393224 | tf_op jit(solution)/shard_map/ppermute | solution.py:157
  16.0 1.7 %collective-permute-start.8 = (bf16[2,32,1024]{2,1,0:T(8,128)(2,1)S(1)}, bf16[2,32,1024]{2,1,0:T(8,128)(2,1)S(1)}, u32[]{:S(2)}, u32[]{:S(2)}) collective-permute-start(bf16[2,32,1024]{2,1,0:T(8,128)(2,1)S(1)} %collective-permute-done.4.refs_5_.refs_3_), channel_id=1, source_target_pairs={{0,8},{8,0},{16,24},{24,16},{1,9},{9,1},{17,25},{25,17},{2,10},{10... | collective-permute-start | bytes 393224 | tf_op jit(solution)/shard_map/ppermute | solution.py:157
  19.1 7.3 %collective-permute-start.14 = (f16[2,32,1024]{2,1,0:T(8,128)(2,1)S(1)}, f16[2,32,1024]{2,1,0:T(8,128)(2,1)S(1)}, u32[]{:S(2)}, u32[]{:S(2)}) collective-permute-start(f16[2,32,1024]{2,1,0:T(8,128)(2,1)S(1)} %convert_element_type.37), channel_id=1, source_target_pairs={{0,17},{1,16},{2,19},{3,18},{4,21},{5,20},{6,23},{7,22},{8,25},{9,... | collective-permute-start | bytes 393224 | tf_op jit(solution)/shard_map/ppermute | solution.py:190
  22.0 6.3 %collective-permute-start.13 = (f16[2,32,1024]{2,1,0:T(8,128)(2,1)S(1)}, f16[2,32,1024]{2,1,0:T(8,128)(2,1)S(1)}, u32[]{:S(2)}, u32[]{:S(2)}) collective-permute-start(f16[2,32,1024]{2,1,0:T(8,128)(2,1)S(1)} %convert_element_type.35), channel_id=1, source_target_pairs={{0,1},{1,0},{2,3},{3,2},{4,5},{5,4},{6,7},{7,6},{8,9},{9,8},{10,11... | collective-permute-start | bytes 393224 | tf_op jit(solution)/shard_map/ppermute | solution.py:190
  22.6 5.9 %collective-permute-start.12 = (f16[2,32,1024]{2,1,0:T(8,128)(2,1)S(1)}, f16[2,32,1024]{2,1,0:T(8,128)(2,1)S(1)}, u32[]{:S(2)}, u32[]{:S(2)}) collective-permute-start(f16[2,32,1024]{2,1,0:T(8,128)(2,1)S(1)} %convert_element_type.33), channel_id=1, source_target_pairs={{0,16},{1,17},{2,18},{3,19},{4,20},{5,21},{6,22},{7,23},{8,24},{9,... | collective-permute-start | bytes 393224 | tf_op jit(solution)/shard_map/ppermute | solution.py:190

commit v15 on v14

--- a/solution.py
+++ b/solution.py
@@ -74,13 +74,10 @@
     return [slice(i, i + step) for i in range(0, width, step)]
 
 
-def tile_grads(p_mat, q_mat, keys, at):
-    m = keys.shape[0] // 2
-    img, txt = keys[:m, at], keys[m:, at]
-    nn = ((1,), (0,))
-    grad_img = dot(jnp.concatenate([q_mat, p_mat], axis=1), jnp.concatenate([img, txt]), nn)
-    grad_txt = dot(jnp.concatenate([-p_mat, -q_mat], axis=1), jnp.concatenate([img, txt]), nn)
-    return grad_img, grad_txt
+def spread(p_mat, q_mat):
+    return jnp.concatenate(
+        [jnp.concatenate([q_mat, p_mat], axis=1), jnp.concatenate([-p_mat, -q_mat], axis=1)], axis=0
+    )
 
 
 def bounds(rows, factors, total):
@@ -94,29 +91,37 @@
     rows = join(refs[:n])
     own[...] = rows
     keys = join(refs[n:-4])
-    p_mat, q_mat = weigh(rows, keys, factors)
+    mix = spread(*weigh(rows, keys, factors))
     for at in tiles(keys.shape[1]):
-        acc[0, :, at], acc[1, :, at] = tile_grads(p_mat, q_mat, keys, at)
+        acc[:, at] = dot(mix, keys[:, at], ((1,), (0,)))
     most = bounds(rows, factors, total)
-    up[...] = jnp.broadcast_to(TOP / most, up.shape)
+    half = most.shape[0]
+    for s in range(2):
+        up[s * half : (s + 1) * half] = jnp.broadcast_to(TOP / most, (half, up.shape[1]))
     down[...] = jnp.broadcast_to((most / TOP)[: down.shape[0]], down.shape)
 
 
 def late_kernel(total, n, m, factors, own, acc, up, *refs):
-    last, early, late, outs = refs[0], refs[1 : m + 1], refs[m + 1 : -n - 1], refs[-n - 1 :]
+    last, outs = refs[0], refs[-n - 1 :]
+    early, late = join(refs[1 : m + 1]), join(refs[m + 1 : -n - 1])
     rows = last.shape[1]
-    keys, every = join(late), join(early + late)
-    p_mat, q_mat = weigh(own[...], keys, factors)
+    half = n * rows
     rest = join([last])
-    p_rest, q_rest = weigh(rest, every, factors)
+    every = jnp.concatenate([own[:half], last[0], own[half:], last[1]], axis=0)
+    mix = spread(*weigh(every, late, factors))
+    mix_rest = spread(*weigh(rest, early, factors))
     factor = TOP / bounds(rest, factors, total)
-    for at in tiles(keys.shape[1]):
-        for s, grad in enumerate(tile_grads(p_mat, q_mat, keys, at)):
-            grad = (grad + acc[s, :, at]) * up[:, :1]
+    for at in tiles(late.shape[1]):
+        grad = dot(mix, late[:, at], ((1,), (0,)))
+        grad_rest = dot(mix_rest, early[:, at], ((1,), (0,)))
+        for s in range(2):
+            low = s * (half + rows)
+            mine = slice(s * half, (s + 1) * half)
+            ready = (grad[low : low + half] + acc[mine, at]) * up[mine, :1]
             for i in range(n):
-                outs[i][s, :, at] = grad[i * rows : (i + 1) * rows]
-        for s, grad in enumerate(tile_grads(p_rest, q_rest, every, at)):
-            outs[n][s, :, at] = grad * factor
+                outs[i][s, :, at] = ready[i * rows : (i + 1) * rows]
+            both = grad[low + half : low + half + rows] + grad_rest[s * rows : (s + 1) * rows]
+            outs[n][s, :, at] = both * factor
 
 
 def call(kernel, operands, out_shape, flops):
@@ -175,7 +180,7 @@
         functools.partial(early_kernel, total, len(first)),
         [factors] + first + early,
         [jax.ShapeDtypeStruct((2 * many, width), images.dtype)]
-        + [jax.ShapeDtypeStruct(s, f32) for s in [(2, many, width), (many, 128), (rows, 128)]],
+        + [jax.ShapeDtypeStruct(s, f32) for s in [(2 * many, width), (2 * many, 128), (rows, 128)]],
         flops(len(first), len(early)),
     )
     late = copies + [line[-1]] + pair(line[-1])
@@ -189,12 +194,9 @@
     back = [
         lax.ppermute(part.astype(jnp.float16), both, square_shift(n_row, n_col, -j, -k)) for (j, k), part in far
     ]
-    grads = []
-    for s in range(2):
-        total = parts[0][s]
-        for part in back:
-            total = total + part[s].astype(f32)
-        grads.append(total * down[:, :1])
+    ready = [sum((part[s].astype(f32) for part in back[1:]), parts[0][s]) for s in range(2)]
+    ready = lax.optimization_barrier(ready)
+    grads = [(ready[s] + back[0][s].astype(f32)) * down[:, :1] for s in range(2)]
     return tuple(grads)
 
 

time: 29.4 us -> 29.2 us (level)
  no operation moved by 1% of the time
where the time goes in v15:
time: 29.2 us; the launch traced here: 29 us
  starting transfers between devices  17.6 us (60%)
  waiting for transfers between devices  6.71 us (23%)
  Pallas kernels  1.92 us (7%)
  other arithmetic  1.8 us (6%)
  between operations  0.7 us (2%)
    ppermute x4, starting transfers between devices, local(): apart[step] = [lax.ppermute(half, 'col', perm) for half in apart[which]]  6.17 us
    ppermute x3, waiting for transfers between devices, local(): lax.ppermute(part.astype(jnp.float16), both, square_shift(n_row, n_col, -...  5.53 us
    ppermute x3, starting transfers between devices, local(): lax.ppermute(own, both, square_shift(n_row, n_col, j, k))  4.84 us
    ppermute x3, starting transfers between devices, local(): lax.ppermute(part.astype(jnp.float16), both, square_shift(n_row, n_col, -...  3.62 us
    pallas_call x2, Pallas kernels, call(): pl.pallas_call(kernel, out_shape=out_shape, in_specs=[vmem] * len(operand...  1.92 us
    ppermute x1, starting transfers between devices, local(): line.append(lax.ppermute(line[which], 'col', perm))  1.9 us
    ppermute x4, starting transfers between devices, pair(): lax.ppermute(block, 'row', inner_shift(n_row, k))  1.09 us
    ppermute x3, waiting for transfers between devices, local(): lax.ppermute(own, both, square_shift(n_row, n_col, j, k))  1.03 us
  transfers between devices with their start and end apart: 15, of which 6 were waited for; matrix products, arithmetic and copies ran while one was open for 4% of the time, Pallas kernels for 3%

profile of v15, /device:TPU:0, one launch (start us, length us, event | category | flops | bytes accessed | tf_op | source)
XLA Modules:
  0.0 29.0 jit_solution(5787957158493478751)
XLA Ops:
  0.6 4.1 %collective-permute-start.2 = (bf16[32,1024]{1,0:T(8,128)(2,1)}, bf16[32,1024]{1,0:T(8,128)(2,1)S(1)}, u32[]{:S(2)}, u32[]{:S(2)}) collective-permute-start(bf16[32,1024]{1,0:T(8,128)(2,1)} %param.3), channel_id=1, source_target_pairs={{0,4},{1,5},{2,6},{3,7},{4,0},{5,1},{6,2},{7,3},{8,12},{9,13},{10,... | collective-permute-start | bytes 196616 | tf_op jit(solution)/shard_map/ppermute | solution.py:156
  4.7 0.1 collective-permute-start.3
  4.8 0.9 %pad_maximum_fusion.refs_0_.refs_3_.refs_1_ = bf16[2,32,1024]{2,1,0:T(8,128)(2,1)S(1)} fusion(bf16[1,32,1024]{2,1,0:T(8,128)(2,1)} %bitcast.21, bf16[1,32,1024]{2,1,0:T(8,128)(2,1)} %bitcast.20), kind=kLoop, calls=%fused_computation | loop fusion | flops 65536 | bytes 262144 | tf_op jit(solution)/shard_map/stack | solution.py:149
  5.7 1.9 %collective-permute-start.4 = (bf16[2,32,1024]{2,1,0:T(8,128)(2,1)S(1)}, bf16[2,32,1024]{2,1,0:T(8,128)(2,1)S(1)}, u32[]{:S(2)}, u32[]{:S(2)}) collective-permute-start(bf16[2,32,1024]{2,1,0:T(8,128)(2,1)S(1)} %pad_maximum_fusion.refs_0_.refs_3_.refs_1_), channel_id=1, source_target_pairs={{0,2},{1,3},{2,0},{3,1},{4,6},{5,7},{6,4},{7,5},{8,10},{9,11},{10,... | collective-permute-start | bytes 393224 | tf_op jit(solution)/shard_map/ppermute | solution.py:159
  7.6 1.5 %collective-permute-start = (bf16[2,32,1024]{2,1,0:T(8,128)(2,1)S(1)}, bf16[2,32,1024]{2,1,0:T(8,128)(2,1)S(1)}, u32[]{:S(2)}, u32[]{:S(2)}) collective-permute-start(bf16[2,32,1024]{2,1,0:T(8,128)(2,1)S(1)} %pad_maximum_fusion.refs_0_.refs_3_.refs_1_), channel_id=1, source_target_pairs={{0,16},{1,17},{2,18},{3,19},{4,20},{5,21},{6,22},{7,23},{8,24},{9,... | collective-permute-start | bytes 393224 | tf_op jit(solution)/shard_map/ppermute | solution.py:151
  9.1 1.4 %collective-permute-start.1 = (bf16[2,32,1024]{2,1,0:T(8,128)(2,1)S(1)}, bf16[2,32,1024]{2,1,0:T(8,128)(2,1)S(1)}, u32[]{:S(2)}, u32[]{:S(2)}) collective-permute-start(bf16[2,32,1024]{2,1,0:T(8,128)(2,1)S(1)} %pad_maximum_fusion.refs_0_.refs_3_.refs_1_), channel_id=1, source_target_pairs={{0,17},{1,16},{2,19},{3,18},{4,21},{5,20},{6,23},{7,22},{8,25},{9,... | collective-permute-start | bytes 393224 | tf_op jit(solution)/shard_map/ppermute | solution.py:151
  10.6 0.0 collective-permute-done.2
  10.6 0.5 %collective-permute-start.9 = (bf16[32,1024]{1,0:T(8,128)(2,1)S(1)}, bf16[32,1024]{1,0:T(8,128)(2,1)S(1)}, u32[]{:S(2)}, u32[]{:S(2)}) collective-permute-start(bf16[32,1024]{1,0:T(8,128)(2,1)S(1)} %collective-permute-done.2), channel_id=1, source_target_pairs={{0,2},{1,3},{2,0},{3,1},{4,6},{5,7},{6,4},{7,5},{8,10},{9,11},{10,... | collective-permute-start | bytes 196616 | tf_op jit(solution)/shard_map/ppermute | solution.py:156
  11.0 0.0 collective-permute-done.3
  11.0 1.5 %collective-permute-start.10 = (bf16[32,1024]{1,0:T(8,128)(2,1)S(1)}, bf16[32,1024]{1,0:T(8,128)(2,1)S(1)}, u32[]{:S(2)}, u32[]{:S(2)}) collective-permute-start(bf16[32,1024]{1,0:T(8,128)(2,1)S(1)} %collective-permute-done.3), channel_id=1, source_target_pairs={{0,2},{1,3},{2,0},{3,1},{4,6},{5,7},{6,4},{7,5},{8,10},{9,11},{10,... | collective-permute-start | bytes 196616 | tf_op jit(solution)/shard_map/ppermute | solution.py:156
  12.6 0.1 collective-permute-done.4.refs_5_.refs_3_
  12.7 1.9 %collective-permute-start.5 = (bf16[2,32,1024]{2,1,0:T(8,128)(2,1)S(1)}, bf16[2,32,1024]{2,1,0:T(8,128)(2,1)S(1)}, u32[]{:S(2)}, u32[]{:S(2)}) collective-permute-start(bf16[2,32,1024]{2,1,0:T(8,128)(2,1)S(1)} %pad_maximum_fusion.refs_0_.refs_3_.refs_1_), channel_id=1, source_target_pairs={{0,1},{1,0},{2,3},{3,2},{4,5},{5,4},{6,7},{7,6},{8,9},{9,8},{10,11... | collective-permute-start | bytes 393224 | tf_op jit(solution)/shard_map/ppermute | solution.py:151
  14.6 0.8 %collective-permute-done.refs_1_ = bf16[2,32,1024]{2,1,0:T(8,128)(2,1)S(1)} collective-permute-done((bf16[2,32,1024]{2,1,0:T(8,128)(2,1)S(1)}, bf16[2,32,1024]{2,1,0:T(8,128)(2,1)S(1)}, u32[]{:S(2)}, u32[]{:S(2)}) %collective-permute-start) | collective-permute-done | bytes 131104 | tf_op jit(solution)/shard_map/ppermute | solution.py:151
  15.4 0.0 collective-permute-start.7
  15.4 0.0 collective-permute-done.9
  15.4 0.5 %collective-permute-start.6 = (bf16[2,32,1024]{2,1,0:T(8,128)(2,1)S(1)}, bf16[2,32,1024]{2,1,0:T(8,128)(2,1)S(1)}, u32[]{:S(2)}, u32[]{:S(2)}) collective-permute-start(bf16[2,32,1024]{2,1,0:T(8,128)(2,1)S(1)} %pad_maximum_fusion.refs_0_.refs_3_.refs_1_), channel_id=1, source_target_pairs={{0,8},{8,0},{16,24},{24,16},{1,9},{9,1},{17,25},{25,17},{2,10},{10... | collective-permute-start | bytes 393224 | tf_op jit(solution)/shard_map/ppermute | solution.py:162
  15.9 0.0 collective-permute-done.10
  15.9 0.0 copy-start
  15.9 0.1 collective-permute-start.11
  16.0 0.0 collective-permute-done.1.refs_2_
  16.0 0.5 %collective-permute-start.8 = (bf16[2,32,1024]{2,1,0:T(8,128)(2,1)S(1)}, bf16[2,32,1024]{2,1,0:T(8,128)(2,1)S(1)}, u32[]{:S(2)}, u32[]{:S(2)}) collective-permute-start(bf16[2,32,1024]{2,1,0:T(8,128)(2,1)S(1)} %collective-permute-done.4.refs_5_.refs_3_), channel_id=1, source_target_pairs={{0,8},{8,0},{16,24},{24,16},{1,9},{9,1},{17,25},{25,17},{2,10},{10... | collective-permute-start | bytes 393224 | tf_op jit(solution)/shard_map/ppermute | solution.py:162
  16.5 0.1 copy-done
  16.6 0.1 broadcast_in_dim.2.factors
  16.6 0.8 %shard_map.50 = (bf16[192,1024]{1,0:T(8,128)(2,1)S(1)}, f32[192,1024]{1,0:T(8,128)S(1)}, f32[192,128]{1,0:T(8,128)S(1)}, f32[32,128]{1,0:T(8,128)S(1)}) custom-call(f32[2,128]{1,0:T(2,128)S(1)} %broadcast_in_dim.2.factors, bf16[2,32,1024]{2,1,0:T(8,128)(2,1)S(1)} %pad_maximum_fusion.refs_0_.refs_3_.refs_1_, ...), custom_call_target="tpu_custom_call" | custom-call | flops 150994944 | bytes 2081792 | tf_op jit(solution)/shard_map/pallas_call | solution.py:130
  17.4 0.2 collective-permute-done.5.refs_0_
  17.7 0.0 collective-permute-done.7.refs_5_
  17.7 0.0 collective-permute-done.8.refs_6_
  17.7 0.0 collective-permute-done.6.refs_4_
  17.7 0.0 collective-permute-done.11.refs_8_
  17.7 1.1 %shard_map.51 = (f32[2,32,1024]{2,1,0:T(8,128)S(1)}, f32[2,32,1024]{2,1,0:T(8,128)S(1)}, f32[2,32,1024]{2,1,0:T(8,128)S(1)}, f32[2,32,1024]{2,1,0:T(8,128)S(1)}) custom-call(f32[2,128]{1,0:T(2,128)S(1)} %broadcast_in_dim.2.factors, bf16[192,1024]{1,0:T(8,128)(2,1)S(1)} %get-tuple-element.18.own, f32[192,1024]{1,0:T(8,128)S(1)} %get-tuple-element.19.acc, ...), custom_call_target="tpu_custom_call" | custom-call | flops 385875968 | bytes 3507200 | tf_op jit(solution)/shard_map/pallas_call | solution.py:130
  18.9 2.9 %collective-permute-start.13 = (f16[2,32,1024]{2,1,0:T(8,128)(2,1)S(1)}, f16[2,32,1024]{2,1,0:T(8,128)(2,1)S(1)}, u32[]{:S(2)}, u32[]{:S(2)}) collective-permute-start(f16[2,32,1024]{2,1,0:T(8,128)(2,1)S(1)} %convert_element_type.39), channel_id=1, source_target_pairs={{0,17},{1,16},{2,19},{3,18},{4,21},{5,20},{6,23},{7,22},{8,25},{9,... | collective-permute-start | bytes 393224 | tf_op jit(solution)/shard_map/ppermute | solution.py:195
  21.8 0.5 %collective-permute-start.12 = (f16[2,32,1024]{2,1,0:T(8,128)(2,1)S(1)}, f16[2,32,1024]{2,1,0:T(8,128)(2,1)S(1)}, u32[]{:S(2)}, u32[]{:S(2)}) collective-permute-start(f16[2,32,1024]{2,1,0:T(8,128)(2,1)S(1)} %convert_element_type.37), channel_id=1, source_target_pairs={{0,1},{1,0},{2,3},{3,2},{4,5},{5,4},{6,7},{7,6},{8,9},{9,8},{10,11... | collective-permute-start | bytes 393224 | tf_op jit(solution)/shard_map/ppermute | solution.py:195
  22.3 0.1 slice_reduce_fusion
  22.5 0.2 collective-permute-start.14
  22.6 3.6 %collective-permute-done.13 = f16[2,32,1024]{2,1,0:T(8,128)(2,1)S(1)} collective-permute-done((f16[2,32,1024]{2,1,0:T(8,128)(2,1)S(1)}, f16[2,32,1024]{2,1,0:T(8,128)(2,1)S(1)}, u32[]{:S(2)}, u32[]{:S(2)}) %collective-permute-start.13) | collective-permute-done | bytes 131104 | tf_op jit(solution)/shard_map/ppermute | solution.py:195
  26.2 1.9 %collective-permute-done.12 = f16[2,32,1024]{2,1,0:T(8,128)(2,1)S(1)} collective-permute-done((f16[2,32,1024]{2,1,0:T(8,128)(2,1)S(1)}, f16[2,32,1024]{2,1,0:T(8,128)(2,1)S(1)}, u32[]{:S(2)}, u32[]{:S(2)}) %collective-permute-start.12) | collective-permute-done | bytes 131104 | tf_op jit(solution)/shard_map/ppermute | solution.py:195
  28.1 0.1 collective-permute-done.14
  28.2 0.8 %fusion = (f32[32,1024]{1,0:T(8,128)}, f32[32,1024]{1,0:T(8,128)}) fusion(f32[32,1024]{1,0:T(8,128)S(1)} %get-tuple-element.29, f16[2,32,1024]{2,1,0:T(8,128)(2,1)S(1)} %collective-permute-done.14, f32[32]{0:T(128)S(1)} %slice_reduce_fusion, f32[32,1024]{1,0:T(8,128)S(1)} %get-tuple-element.26), kind=kLoop, calls=%fused_computation.4 | loop fusion | flops 196608 | bytes 655488 | tf_op jit(solution)/shard_map/mul | solution.py:199
  (7 shorter events, 0.1 us)
Async XLA Ops:
  0.6 9.9 %collective-permute-start.2 = (bf16[32,1024]{1,0:T(8,128)(2,1)}, bf16[32,1024]{1,0:T(8,128)(2,1)S(1)}, u32[]{:S(2)}, u32[]{:S(2)}) collective-permute-start(bf16[32,1024]{1,0:T(8,128)(2,1)} %param.3), channel_id=1, source_target_pairs={{0,4},{1,5},{2,6},{3,7},{4,0},{5,1},{6,2},{7,3},{8,12},{9,13},{10,... | collective-permute-start | bytes 196616 | tf_op jit(solution)/shard_map/ppermute | solution.py:156
  4.7 6.3 %collective-permute-start.3 = (bf16[32,1024]{1,0:T(8,128)(2,1)}, bf16[32,1024]{1,0:T(8,128)(2,1)S(1)}, u32[]{:S(2)}, u32[]{:S(2)}) collective-permute-start(bf16[32,1024]{1,0:T(8,128)(2,1)} %param.4), channel_id=1, source_target_pairs={{0,4},{1,5},{2,6},{3,7},{4,0},{5,1},{6,2},{7,3},{8,12},{9,13},{10,... | collective-permute-start | bytes 196616 | tf_op jit(solution)/shard_map/ppermute | solution.py:156
  5.7 7.0 %collective-permute-start.4 = (bf16[2,32,1024]{2,1,0:T(8,128)(2,1)S(1)}, bf16[2,32,1024]{2,1,0:T(8,128)(2,1)S(1)}, u32[]{:S(2)}, u32[]{:S(2)}) collective-permute-start(bf16[2,32,1024]{2,1,0:T(8,128)(2,1)S(1)} %pad_maximum_fusion.refs_0_.refs_3_.refs_1_), channel_id=1, source_target_pairs={{0,2},{1,3},{2,0},{3,1},{4,6},{5,7},{6,4},{7,5},{8,10},{9,11},{10,... | collective-permute-start | bytes 393224 | tf_op jit(solution)/shard_map/ppermute | solution.py:159
  7.6 7.8 %collective-permute-start = (bf16[2,32,1024]{2,1,0:T(8,128)(2,1)S(1)}, bf16[2,32,1024]{2,1,0:T(8,128)(2,1)S(1)}, u32[]{:S(2)}, u32[]{:S(2)}) collective-permute-start(bf16[2,32,1024]{2,1,0:T(8,128)(2,1)S(1)} %pad_maximum_fusion.refs_0_.refs_3_.refs_1_), channel_id=1, source_target_pairs={{0,16},{1,17},{2,18},{3,19},{4,20},{5,21},{6,22},{7,23},{8,24},{9,... | collective-permute-start | bytes 393224 | tf_op jit(solution)/shard_map/ppermute | solution.py:151
  9.1 6.9 %collective-permute-start.1 = (bf16[2,32,1024]{2,1,0:T(8,128)(2,1)S(1)}, bf16[2,32,1024]{2,1,0:T(8,128)(2,1)S(1)}, u32[]{:S(2)}, u32[]{:S(2)}) collective-permute-start(bf16[2,32,1024]{2,1,0:T(8,128)(2,1)S(1)} %pad_maximum_fusion.refs_0_.refs_3_.refs_1_), channel_id=1, source_target_pairs={{0,17},{1,16},{2,19},{3,18},{4,21},{5,20},{6,23},{7,22},{8,25},{9,... | collective-permute-start | bytes 393224 | tf_op jit(solution)/shard_map/ppermute | solution.py:151
  10.6 4.8 %collective-permute-start.9 = (bf16[32,1024]{1,0:T(8,128)(2,1)S(1)}, bf16[32,1024]{1,0:T(8,128)(2,1)S(1)}, u32[]{:S(2)}, u32[]{:S(2)}) collective-permute-start(bf16[32,1024]{1,0:T(8,128)(2,1)S(1)} %collective-permute-done.2), channel_id=1, source_target_pairs={{0,2},{1,3},{2,0},{3,1},{4,6},{5,7},{6,4},{7,5},{8,10},{9,11},{10,... | collective-permute-start | bytes 196616 | tf_op jit(solution)/shard_map/ppermute | solution.py:156
  11.0 4.8 %collective-permute-start.10 = (bf16[32,1024]{1,0:T(8,128)(2,1)S(1)}, bf16[32,1024]{1,0:T(8,128)(2,1)S(1)}, u32[]{:S(2)}, u32[]{:S(2)}) collective-permute-start(bf16[32,1024]{1,0:T(8,128)(2,1)S(1)} %collective-permute-done.3), channel_id=1, source_target_pairs={{0,2},{1,3},{2,0},{3,1},{4,6},{5,7},{6,4},{7,5},{8,10},{9,11},{10,... | collective-permute-start | bytes 196616 | tf_op jit(solution)/shard_map/ppermute | solution.py:156
  12.7 5.0 %collective-permute-start.5 = (bf16[2,32,1024]{2,1,0:T(8,128)(2,1)S(1)}, bf16[2,32,1024]{2,1,0:T(8,128)(2,1)S(1)}, u32[]{:S(2)}, u32[]{:S(2)}) collective-permute-start(bf16[2,32,1024]{2,1,0:T(8,128)(2,1)S(1)} %pad_maximum_fusion.refs_0_.refs_3_.refs_1_), channel_id=1, source_target_pairs={{0,1},{1,0},{2,3},{3,2},{4,5},{5,4},{6,7},{7,6},{8,9},{9,8},{10,11... | collective-permute-start | bytes 393224 | tf_op jit(solution)/shard_map/ppermute | solution.py:151
  15.4 2.3 %collective-permute-start.7 = (bf16[2,32,1024]{2,1,0:T(8,128)(2,1)S(1)}, bf16[2,32,1024]{2,1,0:T(8,128)(2,1)S(1)}, u32[]{:S(2)}, u32[]{:S(2)}) collective-permute-start(bf16[2,32,1024]{2,1,0:T(8,128)(2,1)S(1)} %pad_maximum_fusion.1.refs_4_.refs_2_), channel_id=1, source_target_pairs={{0,8},{8,0},{16,24},{24,16},{1,9},{9,1},{17,25},{25,17},{2,10},{10... | collective-permute-start | bytes 393224 | tf_op jit(solution)/shard_map/ppermute | solution.py:162
  15.4 2.3 %collective-permute-start.6 = (bf16[2,32,1024]{2,1,0:T(8,128)(2,1)S(1)}, bf16[2,32,1024]{2,1,0:T(8,128)(2,1)S(1)}, u32[]{:S(2)}, u32[]{:S(2)}) collective-permute-start(bf16[2,32,1024]{2,1,0:T(8,128)(2,1)S(1)} %pad_maximum_fusion.refs_0_.refs_3_.refs_1_), channel_id=1, source_target_pairs={{0,8},{8,0},{16,24},{24,16},{1,9},{9,1},{17,25},{25,17},{2,10},{10... | collective-permute-start | bytes 393224 | tf_op jit(solution)/shard_map/ppermute | solution.py:162
  15.9 0.7 %copy-start = (f32[2]{0:T(128)S(1)}, f32[2]{0:T(128)}, u32[]{:S(2)}) copy-start(f32[2]{0:T(128)} %param.5) | copy-start | bytes 28
  15.9 1.8 %collective-permute-start.11 = (bf16[2,32,1024]{2,1,0:T(8,128)(2,1)S(1)}, bf16[2,32,1024]{2,1,0:T(8,128)(2,1)S(1)}, u32[]{:S(2)}, u32[]{:S(2)}) collective-permute-start(bf16[2,32,1024]{2,1,0:T(8,128)(2,1)S(1)} %pad_maximum_fusion.2.refs_7_), channel_id=1, source_target_pairs={{0,8},{8,0},{16,24},{24,16},{1,9},{9,1},{17,25},{25,17},{2,10},{10... | collective-permute-start | bytes 393224 | tf_op jit(solution)/shard_map/ppermute | solution.py:162
  16.0 1.7 %collective-permute-start.8 = (bf16[2,32,1024]{2,1,0:T(8,128)(2,1)S(1)}, bf16[2,32,1024]{2,1,0:T(8,128)(2,1)S(1)}, u32[]{:S(2)}, u32[]{:S(2)}) collective-permute-start(bf16[2,32,1024]{2,1,0:T(8,128)(2,1)S(1)} %collective-permute-done.4.refs_5_.refs_3_), channel_id=1, source_target_pairs={{0,8},{8,0},{16,24},{24,16},{1,9},{9,1},{17,25},{25,17},{2,10},{10... | collective-permute-start | bytes 393224 | tf_op jit(solution)/shard_map/ppermute | solution.py:162
  18.9 7.3 %collective-permute-start.13 = (f16[2,32,1024]{2,1,0:T(8,128)(2,1)S(1)}, f16[2,32,1024]{2,1,0:T(8,128)(2,1)S(1)}, u32[]{:S(2)}, u32[]{:S(2)}) collective-permute-start(f16[2,32,1024]{2,1,0:T(8,128)(2,1)S(1)} %convert_element_type.39), channel_id=1, source_target_pairs={{0,17},{1,16},{2,19},{3,18},{4,21},{5,20},{6,23},{7,22},{8,25},{9,... | collective-permute-start | bytes 393224 | tf_op jit(solution)/shard_map/ppermute | solution.py:195
  21.8 6.3 %collective-permute-start.12 = (f16[2,32,1024]{2,1,0:T(8,128)(2,1)S(1)}, f16[2,32,1024]{2,1,0:T(8,128)(2,1)S(1)}, u32[]{:S(2)}, u32[]{:S(2)}) collective-permute-start(f16[2,32,1024]{2,1,0:T(8,128)(2,1)S(1)} %convert_element_type.37), channel_id=1, source_target_pairs={{0,1},{1,0},{2,3},{3,2},{4,5},{5,4},{6,7},{7,6},{8,9},{9,8},{10,11... | collective-permute-start | bytes 393224 | tf_op jit(solution)/shard_map/ppermute | solution.py:195
  22.5 5.8 %collective-permute-start.14 = (f16[2,32,1024]{2,1,0:T(8,128)(2,1)S(1)}, f16[2,32,1024]{2,1,0:T(8,128)(2,1)S(1)}, u32[]{:S(2)}, u32[]{:S(2)}) collective-permute-start(f16[2,32,1024]{2,1,0:T(8,128)(2,1)S(1)} %convert_element_type.43), channel_id=1, source_target_pairs={{0,16},{1,17},{2,18},{3,19},{4,20},{5,21},{6,22},{7,23},{8,24},{9,... | collective-permute-start | bytes 393224 | tf_op jit(solution)/shard_map/ppermute | solution.py:195

commit v16 on v15

--- a/solution.py
+++ b/solution.py
@@ -144,8 +144,8 @@
     batch = rows * n_row * n_col
     factors = jnp.broadcast_to((loss_weights * (1.0 / math.sqrt(width * batch)))[:, None], (2, 128))
     both = ("row", "col")
-    square = [(j, k) for j in range(halves(n_row)[0]) for k in range(halves(n_col)[1])]
-    square = square[2:] + square[1:2]
+    square = [(j, k) for j in range(halves(n_row)[0]) for k in range(halves(n_col)[1])][1:]
+    square.sort(key=lambda place: (sum(map(bool, place)), -place[0]))
     own = jnp.stack([images, texts])
 
     mine = [own] + [lax.ppermute(own, both, square_shift(n_row, n_col, j, k)) for j, k in square]
@@ -163,10 +163,8 @@
 
     early, copies = line[:-1], []
     for i, block in enumerate(line[:-1]):
-        if i == 0 and len(mine) > 1:
-            block, mine[1] = lax.optimization_barrier((block, mine[1]))
-        if i == 1 and len(early) > 2:
-            block, early[2] = lax.optimization_barrier((block, early[2]))
+        if i < 2 and i + 2 < len(mine):
+            block, mine[i + 1] = lax.optimization_barrier((block, mine[i + 1]))
         copies += pair(block)
     total = rows * len(line) * row_inner
     f32 = jnp.float32

time: 29.2 us -> 29.6 us (1.014)
  waiting for transfers between devices: 6.71 us -> 7.63 us
  starting transfers between devices: 17.6 us -> 17.1 us
    ppermute x4, waiting for transfers between devices: 0.05 us -> 1.82 us  [local(): apart[step] = [lax.ppermute(half, 'col', perm) for half in apart[which]]]
    ppermute x3, starting transfers between devices: 4.84 us -> 5.58 us  [local(): lax.ppermute(own, both, square_shift(n_row, n_col, j, k))]
    ppermute x4, starting transfers between devices: 1.09 us -> 0.57 us  [pair(): lax.ppermute(block, 'row', inner_shift(n_row, k))]
    ppermute x3, waiting for transfers between devices: 5.53 us -> 5.03 us  [local(): lax.ppermute(part.astype(jnp.float16), both, square_shift(n_row, n_col, -...]
    ppermute x4, starting transfers between devices: 6.17 us -> 5.77 us  [local(): apart[step] = [lax.ppermute(half, 'col', perm) for half in apart[which]]]
    ppermute x1, starting transfers between devices: 1.9 us -> 1.58 us  [local(): line.append(lax.ppermute(line[which], 'col', perm))]
  transfers between devices with their start and end apart: 15 -> 15, of which waited for: 6 -> 7; matrix products, arithmetic and copies ran while one was open for 4% -> 4% of each run, Pallas kernels for 3% -> 3%
where the time goes in v16:
time: 29.6 us; the launch traced here: 29.4 us
  starting transfers between devices  17.1 us (58%)
  waiting for transfers between devices  7.63 us (26%)
  Pallas kernels  1.92 us (6%)
  other arithmetic  1.8 us (6%)
  between operations  0.72 us (2%)
    ppermute x4, starting transfers between devices, local(): apart[step] = [lax.ppermute(half, 'col', perm) for half in apart[which]]  5.77 us
    ppermute x3, starting transfers between devices, local(): lax.ppermute(own, both, square_shift(n_row, n_col, j, k))  5.58 us
    ppermute x3, waiting for transfers between devices, local(): lax.ppermute(part.astype(jnp.float16), both, square_shift(n_row, n_col, -...  5.03 us
    ppermute x3, starting transfers between devices, local(): lax.ppermute(part.astype(jnp.float16), both, square_shift(n_row, n_col, -...  3.62 us
    pallas_call x2, Pallas kernels, call(): pl.pallas_call(kernel, out_shape=out_shape, in_specs=[vmem] * len(operand...  1.92 us
    ppermute x4, waiting for transfers between devices, local(): apart[step] = [lax.ppermute(half, 'col', perm) for half in apart[which]]  1.82 us
    ppermute x1, starting transfers between devices, local(): line.append(lax.ppermute(line[which], 'col', perm))  1.58 us
    another operation x1, other arithmetic, local(): own = jnp.stack([images, texts])  0.89 us
  transfers between devices with their start and end apart: 15, of which 7 were waited for; matrix products, arithmetic and copies ran while one was open for 4% of the time, Pallas kernels for 3%

profile of v16, /device:TPU:0, one launch (start us, length us, event | category | flops | bytes accessed | tf_op | source)
XLA Modules:
  0.0 29.4 jit_solution(3611149369866726704)
XLA Ops:
  0.6 4.1 %collective-permute-start.1 = (bf16[32,1024]{1,0:T(8,128)(2,1)}, bf16[32,1024]{1,0:T(8,128)(2,1)S(1)}, u32[]{:S(2)}, u32[]{:S(2)}) collective-permute-start(bf16[32,1024]{1,0:T(8,128)(2,1)} %param.3), channel_id=1, source_target_pairs={{0,4},{1,5},{2,6},{3,7},{4,0},{5,1},{6,2},{7,3},{8,12},{9,13},{10,... | collective-permute-start | bytes 196616 | tf_op jit(solution)/shard_map/ppermute | solution.py:156
  4.7 0.1 collective-permute-start.2
  4.8 0.9 %pad_maximum_fusion.refs_0_.refs_3_.refs_1_ = bf16[2,32,1024]{2,1,0:T(8,128)(2,1)S(1)} fusion(bf16[1,32,1024]{2,1,0:T(8,128)(2,1)} %bitcast.21, bf16[1,32,1024]{2,1,0:T(8,128)(2,1)} %bitcast.20), kind=kLoop, calls=%fused_computation | loop fusion | flops 65536 | bytes 262144 | tf_op jit(solution)/shard_map/stack | solution.py:149
  5.7 1.8 %collective-permute-start.3 = (bf16[2,32,1024]{2,1,0:T(8,128)(2,1)S(1)}, bf16[2,32,1024]{2,1,0:T(8,128)(2,1)S(1)}, u32[]{:S(2)}, u32[]{:S(2)}) collective-permute-start(bf16[2,32,1024]{2,1,0:T(8,128)(2,1)S(1)} %pad_maximum_fusion.refs_0_.refs_3_.refs_1_), channel_id=1, source_target_pairs={{0,1},{1,0},{2,3},{3,2},{4,5},{5,4},{6,7},{7,6},{8,9},{9,8},{10,11... | collective-permute-start | bytes 393224 | tf_op jit(solution)/shard_map/ppermute | solution.py:151
  7.5 1.5 %collective-permute-start = (bf16[2,32,1024]{2,1,0:T(8,128)(2,1)S(1)}, bf16[2,32,1024]{2,1,0:T(8,128)(2,1)S(1)}, u32[]{:S(2)}, u32[]{:S(2)}) collective-permute-start(bf16[2,32,1024]{2,1,0:T(8,128)(2,1)S(1)} %pad_maximum_fusion.refs_0_.refs_3_.refs_1_), channel_id=1, source_target_pairs={{0,16},{1,17},{2,18},{3,19},{4,20},{5,21},{6,22},{7,23},{8,24},{9,... | collective-permute-start | bytes 393224 | tf_op jit(solution)/shard_map/ppermute | solution.py:151
  9.0 1.6 %collective-permute-start.4 = (bf16[2,32,1024]{2,1,0:T(8,128)(2,1)S(1)}, bf16[2,32,1024]{2,1,0:T(8,128)(2,1)S(1)}, u32[]{:S(2)}, u32[]{:S(2)}) collective-permute-start(bf16[2,32,1024]{2,1,0:T(8,128)(2,1)S(1)} %pad_maximum_fusion.refs_0_.refs_3_.refs_1_), channel_id=1, source_target_pairs={{0,2},{1,3},{2,0},{3,1},{4,6},{5,7},{6,4},{7,5},{8,10},{9,11},{10,... | collective-permute-start | bytes 393224 | tf_op jit(solution)/shard_map/ppermute | solution.py:159
  10.6 0.0 collective-permute-done.1
  10.6 0.5 %collective-permute-start.9 = (bf16[32,1024]{1,0:T(8,128)(2,1)S(1)}, bf16[32,1024]{1,0:T(8,128)(2,1)S(1)}, u32[]{:S(2)}, u32[]{:S(2)}) collective-permute-start(bf16[32,1024]{1,0:T(8,128)(2,1)S(1)} %collective-permute-done.1), channel_id=1, source_target_pairs={{0,2},{1,3},{2,0},{3,1},{4,6},{5,7},{6,4},{7,5},{8,10},{9,11},{10,... | collective-permute-start | bytes 196616 | tf_op jit(solution)/shard_map/ppermute | solution.py:156
  11.1 0.4 %collective-permute-done.2 = bf16[32,1024]{1,0:T(8,128)(2,1)S(1)} collective-permute-done((bf16[32,1024]{1,0:T(8,128)(2,1)}, bf16[32,1024]{1,0:T(8,128)(2,1)S(1)}, u32[]{:S(2)}, u32[]{:S(2)}) %collective-permute-start.2) | collective-permute-done | bytes 65568 | tf_op jit(solution)/shard_map/ppermute | solution.py:156
  11.5 1.1 %collective-permute-start.10 = (bf16[32,1024]{1,0:T(8,128)(2,1)S(1)}, bf16[32,1024]{1,0:T(8,128)(2,1)S(1)}, u32[]{:S(2)}, u32[]{:S(2)}) collective-permute-start(bf16[32,1024]{1,0:T(8,128)(2,1)S(1)} %collective-permute-done.2), channel_id=1, source_target_pairs={{0,2},{1,3},{2,0},{3,1},{4,6},{5,7},{6,4},{7,5},{8,10},{9,11},{10,... | collective-permute-start | bytes 196616 | tf_op jit(solution)/shard_map/ppermute | solution.py:156
  12.7 0.0 collective-permute-done.3.refs_2_
  12.7 2.3 %collective-permute-start.5 = (bf16[2,32,1024]{2,1,0:T(8,128)(2,1)S(1)}, bf16[2,32,1024]{2,1,0:T(8,128)(2,1)S(1)}, u32[]{:S(2)}, u32[]{:S(2)}) collective-permute-start(bf16[2,32,1024]{2,1,0:T(8,128)(2,1)S(1)} %pad_maximum_fusion.refs_0_.refs_3_.refs_1_), channel_id=1, source_target_pairs={{0,17},{1,16},{2,19},{3,18},{4,21},{5,20},{6,23},{7,22},{8,25},{9,... | collective-permute-start | bytes 393224 | tf_op jit(solution)/shard_map/ppermute | solution.py:151
  14.9 0.0 collective-permute-done.refs_1_
  14.9 0.0 collective-permute-start.7
  14.9 0.7 %collective-permute-done.9 = bf16[32,1024]{1,0:T(8,128)(2,1)S(1)} collective-permute-done((bf16[32,1024]{1,0:T(8,128)(2,1)S(1)}, bf16[32,1024]{1,0:T(8,128)(2,1)S(1)}, u32[]{:S(2)}, u32[]{:S(2)}) %collective-permute-start.9) | collective-permute-done | bytes 65568 | tf_op jit(solution)/shard_map/ppermute | solution.py:156
  15.6 0.0 collective-permute-start.6
  15.6 0.7 %collective-permute-done.10 = bf16[32,1024]{1,0:T(8,128)(2,1)S(1)} collective-permute-done((bf16[32,1024]{1,0:T(8,128)(2,1)S(1)}, bf16[32,1024]{1,0:T(8,128)(2,1)S(1)}, u32[]{:S(2)}, u32[]{:S(2)}) %collective-permute-start.10) | collective-permute-done | bytes 65568 | tf_op jit(solution)/shard_map/ppermute | solution.py:156
  16.3 0.0 copy-start
  16.3 0.1 collective-permute-start.11
  16.4 0.0 collective-permute-done.4.refs_5_.refs_3_
  16.4 0.5 %collective-permute-start.8 = (bf16[2,32,1024]{2,1,0:T(8,128)(2,1)S(1)}, bf16[2,32,1024]{2,1,0:T(8,128)(2,1)S(1)}, u32[]{:S(2)}, u32[]{:S(2)}) collective-permute-start(bf16[2,32,1024]{2,1,0:T(8,128)(2,1)S(1)} %collective-permute-done.4.refs_5_.refs_3_), channel_id=1, source_target_pairs={{0,8},{8,0},{16,24},{24,16},{1,9},{9,1},{17,25},{25,17},{2,10},{10... | collective-permute-start | bytes 393224 | tf_op jit(solution)/shard_map/ppermute | solution.py:162
  16.9 0.1 copy-done
  17.0 0.1 broadcast_in_dim.2.factors
  17.0 0.8 %shard_map.50 = (bf16[192,1024]{1,0:T(8,128)(2,1)S(1)}, f32[192,1024]{1,0:T(8,128)S(1)}, f32[192,128]{1,0:T(8,128)S(1)}, f32[32,128]{1,0:T(8,128)S(1)}) custom-call(f32[2,128]{1,0:T(2,128)S(1)} %broadcast_in_dim.2.factors, bf16[2,32,1024]{2,1,0:T(8,128)(2,1)S(1)} %pad_maximum_fusion.refs_0_.refs_3_.refs_1_, ...), custom_call_target="tpu_custom_call" | custom-call | flops 150994944 | bytes 2081792 | tf_op jit(solution)/shard_map/pallas_call | solution.py:130
  17.8 0.8 %collective-permute-done.5.refs_0_ = bf16[2,32,1024]{2,1,0:T(8,128)(2,1)S(1)} collective-permute-done((bf16[2,32,1024]{2,1,0:T(8,128)(2,1)S(1)}, bf16[2,32,1024]{2,1,0:T(8,128)(2,1)S(1)}, u32[]{:S(2)}, u32[]{:S(2)}) %collective-permute-start.5) | collective-permute-done | bytes 131104 | tf_op jit(solution)/shard_map/ppermute | solution.py:151
  18.6 0.0 collective-permute-done.8.refs_6_
  18.6 0.0 collective-permute-done.7.refs_5_
  18.6 0.0 collective-permute-done.6.refs_4_
  18.6 0.0 collective-permute-done.11.refs_8_
  18.6 1.1 %shard_map.51 = (f32[2,32,1024]{2,1,0:T(8,128)S(1)}, f32[2,32,1024]{2,1,0:T(8,128)S(1)}, f32[2,32,1024]{2,1,0:T(8,128)S(1)}, f32[2,32,1024]{2,1,0:T(8,128)S(1)}) custom-call(f32[2,128]{1,0:T(2,128)S(1)} %broadcast_in_dim.2.factors, bf16[192,1024]{1,0:T(8,128)(2,1)S(1)} %get-tuple-element.18.own, f32[192,1024]{1,0:T(8,128)S(1)} %get-tuple-element.19.acc, ...), custom_call_target="tpu_custom_call" | custom-call | flops 385875968 | bytes 3507200 | tf_op jit(solution)/shard_map/pallas_call | solution.py:130
  19.8 2.2 %collective-permute-start.13 = (f16[2,32,1024]{2,1,0:T(8,128)(2,1)S(1)}, f16[2,32,1024]{2,1,0:T(8,128)(2,1)S(1)}, u32[]{:S(2)}, u32[]{:S(2)}) collective-permute-start(f16[2,32,1024]{2,1,0:T(8,128)(2,1)S(1)} %convert_element_type.39), channel_id=1, source_target_pairs={{0,17},{1,16},{2,19},{3,18},{4,21},{5,20},{6,23},{7,22},{8,25},{9,... | collective-permute-start | bytes 393224 | tf_op jit(solution)/shard_map/ppermute | solution.py:193
  22.1 0.4 %collective-permute-start.12 = (f16[2,32,1024]{2,1,0:T(8,128)(2,1)S(1)}, f16[2,32,1024]{2,1,0:T(8,128)(2,1)S(1)}, u32[]{:S(2)}, u32[]{:S(2)}) collective-permute-start(f16[2,32,1024]{2,1,0:T(8,128)(2,1)S(1)} %convert_element_type.37), channel_id=1, source_target_pairs={{0,1},{1,0},{2,3},{3,2},{4,5},{5,4},{6,7},{7,6},{8,9},{9,8},{10,11... | collective-permute-start | bytes 393224 | tf_op jit(solution)/shard_map/ppermute | solution.py:193
  22.5 0.1 slice_reduce_fusion
  22.6 0.9 %collective-permute-start.14 = (f16[2,32,1024]{2,1,0:T(8,128)(2,1)S(1)}, f16[2,32,1024]{2,1,0:T(8,128)(2,1)S(1)}, u32[]{:S(2)}, u32[]{:S(2)}) collective-permute-start(f16[2,32,1024]{2,1,0:T(8,128)(2,1)S(1)} %convert_element_type.43), channel_id=1, source_target_pairs={{0,16},{1,17},{2,18},{3,19},{4,20},{5,21},{6,22},{7,23},{8,24},{9,... | collective-permute-start | bytes 393224 | tf_op jit(solution)/shard_map/ppermute | solution.py:193
  23.6 3.6 %collective-permute-done.13 = f16[2,32,1024]{2,1,0:T(8,128)(2,1)S(1)} collective-permute-done((f16[2,32,1024]{2,1,0:T(8,128)(2,1)S(1)}, f16[2,32,1024]{2,1,0:T(8,128)(2,1)S(1)}, u32[]{:S(2)}, u32[]{:S(2)}) %collective-permute-start.13) | collective-permute-done | bytes 131104 | tf_op jit(solution)/shard_map/ppermute | solution.py:193
  27.2 1.3 %collective-permute-done.12 = f16[2,32,1024]{2,1,0:T(8,128)(2,1)S(1)} collective-permute-done((f16[2,32,1024]{2,1,0:T(8,128)(2,1)S(1)}, f16[2,32,1024]{2,1,0:T(8,128)(2,1)S(1)}, u32[]{:S(2)}, u32[]{:S(2)}) %collective-permute-start.12) | collective-permute-done | bytes 131104 | tf_op jit(solution)/shard_map/ppermute | solution.py:193
  28.5 0.2 collective-permute-done.14
  28.6 0.8 %fusion = (f32[32,1024]{1,0:T(8,128)}, f32[32,1024]{1,0:T(8,128)}) fusion(f32[32,1024]{1,0:T(8,128)S(1)} %get-tuple-element.29, f16[2,32,1024]{2,1,0:T(8,128)(2,1)S(1)} %collective-permute-done.14, f32[32]{0:T(128)S(1)} %slice_reduce_fusion, f32[32,1024]{1,0:T(8,128)S(1)} %get-tuple-element.26), kind=kLoop, calls=%fused_computation.4 | loop fusion | flops 196608 | bytes 655488 | tf_op jit(solution)/shard_map/mul | solution.py:197
  (7 shorter events, 0.1 us)
Async XLA Ops:
  0.6 10.0 %collective-permute-start.1 = (bf16[32,1024]{1,0:T(8,128)(2,1)}, bf16[32,1024]{1,0:T(8,128)(2,1)S(1)}, u32[]{:S(2)}, u32[]{:S(2)}) collective-permute-start(bf16[32,1024]{1,0:T(8,128)(2,1)} %param.3), channel_id=1, source_target_pairs={{0,4},{1,5},{2,6},{3,7},{4,0},{5,1},{6,2},{7,3},{8,12},{9,13},{10,... | collective-permute-start | bytes 196616 | tf_op jit(solution)/shard_map/ppermute | solution.py:156
  4.7 6.8 %collective-permute-start.2 = (bf16[32,1024]{1,0:T(8,128)(2,1)}, bf16[32,1024]{1,0:T(8,128)(2,1)S(1)}, u32[]{:S(2)}, u32[]{:S(2)}) collective-permute-start(bf16[32,1024]{1,0:T(8,128)(2,1)} %param.4), channel_id=1, source_target_pairs={{0,4},{1,5},{2,6},{3,7},{4,0},{5,1},{6,2},{7,3},{8,12},{9,13},{10,... | collective-permute-start | bytes 196616 | tf_op jit(solution)/shard_map/ppermute | solution.py:156
  5.7 7.0 %collective-permute-start.3 = (bf16[2,32,1024]{2,1,0:T(8,128)(2,1)S(1)}, bf16[2,32,1024]{2,1,0:T(8,128)(2,1)S(1)}, u32[]{:S(2)}, u32[]{:S(2)}) collective-permute-start(bf16[2,32,1024]{2,1,0:T(8,128)(2,1)S(1)} %pad_maximum_fusion.refs_0_.refs_3_.refs_1_), channel_id=1, source_target_pairs={{0,1},{1,0},{2,3},{3,2},{4,5},{5,4},{6,7},{7,6},{8,9},{9,8},{10,11... | collective-permute-start | bytes 393224 | tf_op jit(solution)/shard_map/ppermute | solution.py:151
  7.5 7.4 %collective-permute-start = (bf16[2,32,1024]{2,1,0:T(8,128)(2,1)S(1)}, bf16[2,32,1024]{2,1,0:T(8,128)(2,1)S(1)}, u32[]{:S(2)}, u32[]{:S(2)}) collective-permute-start(bf16[2,32,1024]{2,1,0:T(8,128)(2,1)S(1)} %pad_maximum_fusion.refs_0_.refs_3_.refs_1_), channel_id=1, source_target_pairs={{0,16},{1,17},{2,18},{3,19},{4,20},{5,21},{6,22},{7,23},{8,24},{9,... | collective-permute-start | bytes 393224 | tf_op jit(solution)/shard_map/ppermute | solution.py:151
  9.0 7.4 %collective-permute-start.4 = (bf16[2,32,1024]{2,1,0:T(8,128)(2,1)S(1)}, bf16[2,32,1024]{2,1,0:T(8,128)(2,1)S(1)}, u32[]{:S(2)}, u32[]{:S(2)}) collective-permute-start(bf16[2,32,1024]{2,1,0:T(8,128)(2,1)S(1)} %pad_maximum_fusion.refs_0_.refs_3_.refs_1_), channel_id=1, source_target_pairs={{0,2},{1,3},{2,0},{3,1},{4,6},{5,7},{6,4},{7,5},{8,10},{9,11},{10,... | collective-permute-start | bytes 393224 | tf_op jit(solution)/shard_map/ppermute | solution.py:159
  10.6 5.0 %collective-permute-start.9 = (bf16[32,1024]{1,0:T(8,128)(2,1)S(1)}, bf16[32,1024]{1,0:T(8,128)(2,1)S(1)}, u32[]{:S(2)}, u32[]{:S(2)}) collective-permute-start(bf16[32,1024]{1,0:T(8,128)(2,1)S(1)} %collective-permute-done.1), channel_id=1, source_target_pairs={{0,2},{1,3},{2,0},{3,1},{4,6},{5,7},{6,4},{7,5},{8,10},{9,11},{10,... | collective-permute-start | bytes 196616 | tf_op jit(solution)/shard_map/ppermute | solution.py:156
  11.5 4.8 %collective-permute-start.10 = (bf16[32,1024]{1,0:T(8,128)(2,1)S(1)}, bf16[32,1024]{1,0:T(8,128)(2,1)S(1)}, u32[]{:S(2)}, u32[]{:S(2)}) collective-permute-start(bf16[32,1024]{1,0:T(8,128)(2,1)S(1)} %collective-permute-done.2), channel_id=1, source_target_pairs={{0,2},{1,3},{2,0},{3,1},{4,6},{5,7},{6,4},{7,5},{8,10},{9,11},{10,... | collective-permute-start | bytes 196616 | tf_op jit(solution)/shard_map/ppermute | solution.py:156
  12.7 5.9 %collective-permute-start.5 = (bf16[2,32,1024]{2,1,0:T(8,128)(2,1)S(1)}, bf16[2,32,1024]{2,1,0:T(8,128)(2,1)S(1)}, u32[]{:S(2)}, u32[]{:S(2)}) collective-permute-start(bf16[2,32,1024]{2,1,0:T(8,128)(2,1)S(1)} %pad_maximum_fusion.refs_0_.refs_3_.refs_1_), channel_id=1, source_target_pairs={{0,17},{1,16},{2,19},{3,18},{4,21},{5,20},{6,23},{7,22},{8,25},{9,... | collective-permute-start | bytes 393224 | tf_op jit(solution)/shard_map/ppermute | solution.py:151
  14.9 3.7 %collective-permute-start.7 = (bf16[2,32,1024]{2,1,0:T(8,128)(2,1)S(1)}, bf16[2,32,1024]{2,1,0:T(8,128)(2,1)S(1)}, u32[]{:S(2)}, u32[]{:S(2)}) collective-permute-start(bf16[2,32,1024]{2,1,0:T(8,128)(2,1)S(1)} %pad_maximum_fusion.1.refs_4_.refs_2_), channel_id=1, source_target_pairs={{0,8},{8,0},{16,24},{24,16},{1,9},{9,1},{17,25},{25,17},{2,10},{10... | collective-permute-start | bytes 393224 | tf_op jit(solution)/shard_map/ppermute | solution.py:162
  15.6 3.0 %collective-permute-start.6 = (bf16[2,32,1024]{2,1,0:T(8,128)(2,1)S(1)}, bf16[2,32,1024]{2,1,0:T(8,128)(2,1)S(1)}, u32[]{:S(2)}, u32[]{:S(2)}) collective-permute-start(bf16[2,32,1024]{2,1,0:T(8,128)(2,1)S(1)} %pad_maximum_fusion.refs_0_.refs_3_.refs_1_), channel_id=1, source_target_pairs={{0,8},{8,0},{16,24},{24,16},{1,9},{9,1},{17,25},{25,17},{2,10},{10... | collective-permute-start | bytes 393224 | tf_op jit(solution)/shard_map/ppermute | solution.py:162
  16.3 0.7 %copy-start = (f32[2]{0:T(128)S(1)}, f32[2]{0:T(128)}, u32[]{:S(2)}) copy-start(f32[2]{0:T(128)} %param.5) | copy-start | bytes 28
  16.3 2.3 %collective-permute-start.11 = (bf16[2,32,1024]{2,1,0:T(8,128)(2,1)S(1)}, bf16[2,32,1024]{2,1,0:T(8,128)(2,1)S(1)}, u32[]{:S(2)}, u32[]{:S(2)}) collective-permute-start(bf16[2,32,1024]{2,1,0:T(8,128)(2,1)S(1)} %pad_maximum_fusion.2.refs_7_), channel_id=1, source_target_pairs={{0,8},{8,0},{16,24},{24,16},{1,9},{9,1},{17,25},{25,17},{2,10},{10... | collective-permute-start | bytes 393224 | tf_op jit(solution)/shard_map/ppermute | solution.py:162
  16.4 2.2 %collective-permute-start.8 = (bf16[2,32,1024]{2,1,0:T(8,128)(2,1)S(1)}, bf16[2,32,1024]{2,1,0:T(8,128)(2,1)S(1)}, u32[]{:S(2)}, u32[]{:S(2)}) collective-permute-start(bf16[2,32,1024]{2,1,0:T(8,128)(2,1)S(1)} %collective-permute-done.4.refs_5_.refs_3_), channel_id=1, source_target_pairs={{0,8},{8,0},{16,24},{24,16},{1,9},{9,1},{17,25},{25,17},{2,10},{10... | collective-permute-start | bytes 393224 | tf_op jit(solution)/shard_map/ppermute | solution.py:162
  19.8 7.4 %collective-permute-start.13 = (f16[2,32,1024]{2,1,0:T(8,128)(2,1)S(1)}, f16[2,32,1024]{2,1,0:T(8,128)(2,1)S(1)}, u32[]{:S(2)}, u32[]{:S(2)}) collective-permute-start(f16[2,32,1024]{2,1,0:T(8,128)(2,1)S(1)} %convert_element_type.39), channel_id=1, source_target_pairs={{0,17},{1,16},{2,19},{3,18},{4,21},{5,20},{6,23},{7,22},{8,25},{9,... | collective-permute-start | bytes 393224 | tf_op jit(solution)/shard_map/ppermute | solution.py:193
  22.1 6.4 %collective-permute-start.12 = (f16[2,32,1024]{2,1,0:T(8,128)(2,1)S(1)}, f16[2,32,1024]{2,1,0:T(8,128)(2,1)S(1)}, u32[]{:S(2)}, u32[]{:S(2)}) collective-permute-start(f16[2,32,1024]{2,1,0:T(8,128)(2,1)S(1)} %convert_element_type.37), channel_id=1, source_target_pairs={{0,1},{1,0},{2,3},{3,2},{4,5},{5,4},{6,7},{7,6},{8,9},{9,8},{10,11... | collective-permute-start | bytes 393224 | tf_op jit(solution)/shard_map/ppermute | solution.py:193
  22.6 6.0 %collective-permute-start.14 = (f16[2,32,1024]{2,1,0:T(8,128)(2,1)S(1)}, f16[2,32,1024]{2,1,0:T(8,128)(2,1)S(1)}, u32[]{:S(2)}, u32[]{:S(2)}) collective-permute-start(f16[2,32,1024]{2,1,0:T(8,128)(2,1)S(1)} %convert_element_type.43), channel_id=1, source_target_pairs={{0,16},{1,17},{2,18},{3,19},{4,20},{5,21},{6,22},{7,23},{8,24},{9,... | collective-permute-start | bytes 393224 | tf_op jit(solution)/shard_map/ppermute | solution.py:193

commit v17 on v15

--- a/solution.py
+++ b/solution.py
@@ -8,8 +8,8 @@
 from jax.experimental.pallas import tpu as pltpu
 from jax.sharding import PartitionSpec as P
 
-LIMIT = 6.0
 TOP = 32768.0
+LEAST = 2.0**-40
 
 
 def halves(count):
@@ -83,14 +83,18 @@
 def bounds(rows, factors, total):
     size = jnp.sum(jnp.abs(rows.astype(jnp.float32)), axis=1, keepdims=True)
     size = size[: size.shape[0] // 2] + size[size.shape[0] // 2 :]
-    return size * ((factors[0:1, 0:1] + factors[1:2, 0:1]) * (1.02 * LIMIT * LIMIT * total)) + 1e-30
+    return size * ((factors[0:1, 0:1] + factors[1:2, 0:1]) * (1.02 * total)) + 1e-25
+
+
+def largest(keys):
+    return jnp.max(jnp.max(jnp.abs(keys.astype(jnp.float32)), axis=0, keepdims=True), axis=1, keepdims=True)
 
 
 def early_kernel(total, n, factors, *refs):
-    own, acc, up, down = refs[-4:]
+    own, acc, up, down, most_key = refs[-5:]
     rows = join(refs[:n])
     own[...] = rows
-    keys = join(refs[n:-4])
+    keys = join(refs[n:-5])
     mix = spread(*weigh(rows, keys, factors))
     for at in tiles(keys.shape[1]):
         acc[:, at] = dot(mix, keys[:, at], ((1,), (0,)))
@@ -99,29 +103,60 @@
     for s in range(2):
         up[s * half : (s + 1) * half] = jnp.broadcast_to(TOP / most, (half, up.shape[1]))
     down[...] = jnp.broadcast_to((most / TOP)[: down.shape[0]], down.shape)
-
-
-def late_kernel(total, n, m, factors, own, acc, up, *refs):
+    most_key[...] = jnp.broadcast_to(largest(keys), most_key.shape)
+
+
+def late_kernel(total, n, m, factors, own, acc, up, most_key, *refs):
     last, outs = refs[0], refs[-n - 1 :]
     early, late = join(refs[1 : m + 1]), join(refs[m + 1 : -n - 1])
-    rows = last.shape[1]
+    rows, width = last.shape[1:]
     half = n * rows
     rest = join([last])
     every = jnp.concatenate([own[:half], last[0], own[half:], last[1]], axis=0)
     mix = spread(*weigh(every, late, factors))
     mix_rest = spread(*weigh(rest, early, factors))
+    magnitude = jnp.maximum(jnp.maximum(largest(late), most_key[0:1, 0:1]), LEAST)
+    exponent = jnp.ceil(jnp.log2(magnitude))
+    shrink = jnp.exp2(-2.0 * exponent)
     factor = TOP / bounds(rest, factors, total)
-    for at in tiles(late.shape[1]):
+
+    def send(out, s, at, values):
+        across = width // 128
+        for r in range(0, rows, 8):
+            for c in range(0, values.shape[1], 128):
+                tile = (s * rows + r) // 8 * across + (at.start + c) // 128
+                out[tile] = values[r : r + 8, c : c + 128]
+
+    for out in outs[1:]:
+        out[out.shape[0] - 1] = jnp.broadcast_to(exponent, (8, 128))
+    for at in tiles(width):
         grad = dot(mix, late[:, at], ((1,), (0,)))
         grad_rest = dot(mix_rest, early[:, at], ((1,), (0,)))
         for s in range(2):
             low = s * (half + rows)
             mine = slice(s * half, (s + 1) * half)
-            ready = (grad[low : low + half] + acc[mine, at]) * up[mine, :1]
-            for i in range(n):
-                outs[i][s, :, at] = ready[i * rows : (i + 1) * rows]
+            ready = grad[low : low + half] + acc[mine, at]
+            outs[0][s, :, at] = ready[:rows]
+            ready = ready * up[mine, :1] * shrink
+            for i in range(1, n):
+                send(outs[i], s, at, ready[i * rows : (i + 1) * rows])
             both = grad[low + half : low + half + rows] + grad_rest[s * rows : (s + 1) * rows]
-            outs[n][s, :, at] = both * factor
+            send(outs[n], s, at, both * factor * shrink)
+
+
+def sum_kernel(own, down, *refs):
+    *parts, images, texts = refs
+    rows, width = images.shape
+    across = width // 128
+    grow = [jnp.exp2(2.0 * part[part.shape[0] - 1]) for part in parts]
+    for s, out in enumerate((images, texts)):
+        for r in range(0, rows, 8):
+            scales = [down[r : r + 8] * g for g in grow]
+            for c in range(across):
+                total = own[s, r : r + 8, c * 128 : (c + 1) * 128]
+                for part, scale in zip(parts, scales):
+                    total = total + part[(s * rows + r) // 8 * across + c] * scale
+                out[r : r + 8, c * 128 : (c + 1) * 128] = total
 
 
 def call(kernel, operands, out_shape, flops):
@@ -176,28 +211,33 @@
     def flops(blocks, keys):
         return 16 * rows * width * rows * blocks * keys
 
-    mine_joined, acc, up, down = call(
+    mine_joined, acc, up, down, most_key = call(
         functools.partial(early_kernel, total, len(first)),
         [factors] + first + early,
         [jax.ShapeDtypeStruct((2 * many, width), images.dtype)]
-        + [jax.ShapeDtypeStruct(s, f32) for s in [(2 * many, width), (2 * many, 128), (rows, 128)]],
+        + [jax.ShapeDtypeStruct(s, f32) for s in [(2 * many, width), (2 * many, 128), (rows, 128), (8, 128)]],
         flops(len(first), len(early)),
     )
     late = copies + [line[-1]] + pair(line[-1])
     parts = call(
         functools.partial(late_kernel, total, len(first), len(early)),
-        [factors, mine_joined, acc, up, last] + early + late,
-        [jax.ShapeDtypeStruct((2, rows, width), f32)] * len(mine),
+        [factors, mine_joined, acc, up, most_key, last] + early + late,
+        [jax.ShapeDtypeStruct((2, rows, width), f32)]
+        + [jax.ShapeDtypeStruct((2 * rows * width // 1024 + 1, 8, 128), f32)] * len(square),
         flops(len(first), len(late)) + flops(1, len(early + late)),
     )
     far = sorted(zip(square, parts[1:]), key=lambda item: sum(item[0]))
     back = [
         lax.ppermute(part.astype(jnp.float16), both, square_shift(n_row, n_col, -j, -k)) for (j, k), part in far
     ]
-    ready = [sum((part[s].astype(f32) for part in back[1:]), parts[0][s]) for s in range(2)]
-    ready = lax.optimization_barrier(ready)
-    grads = [(ready[s] + back[0][s].astype(f32)) * down[:, :1] for s in range(2)]
-    return tuple(grads)
+    return tuple(
+        call(
+            sum_kernel,
+            [parts[0], down] + [part.astype(f32) for part in back],
+            [jax.ShapeDtypeStruct((rows, width), f32)] * 2,
+            4 * rows * width * len(mine),
+        )
+    )
 
 
 def solution(mesh):

time: 29.2 us -> 29.3 us (level)
  Pallas kernels: 1.92 us -> 2.74 us
  other arithmetic: 1.8 us -> 1.04 us
    pallas_call x2 -> x3, Pallas kernels: 1.92 us -> 2.74 us  [call(): pl.pallas_call(kernel, out_shape=out_shape, in_specs=[vmem] * len(operand...]
    mul x1 -> x0, other arithmetic: 0.78 us -> none  [local(): (ready[s] + back[0][s].astype(f32)) * down[:, :1]]
where the time goes in v17:
time: 29.3 us; the launch traced here: 29.1 us
  starting transfers between devices  17.6 us (60%)
  waiting for transfers between devices  6.89 us (24%)
  Pallas kernels  2.74 us (9%)
  other arithmetic  1.04 us (4%)
  between operations  0.71 us (2%)
    ppermute x4, starting transfers between devices, local(): apart[step] = [lax.ppermute(half, 'col', perm) for half in apart[which]]  6.17 us
    ppermute x3, waiting for transfers between devices, local(): lax.ppermute(part.astype(jnp.float16), both, square_shift(n_row, n_col, -...  5.73 us
    ppermute x3, starting transfers between devices, local(): lax.ppermute(own, both, square_shift(n_row, n_col, j, k))  4.84 us
    ppermute x3, starting transfers between devices, local(): lax.ppermute(part.astype(jnp.float16), both, square_shift(n_row, n_col, -...  3.62 us
    pallas_call x3, Pallas kernels, call(): pl.pallas_call(kernel, out_shape=out_shape, in_specs=[vmem] * len(operand...  2.74 us
    ppermute x1, starting transfers between devices, local(): line.append(lax.ppermute(line[which], 'col', perm))  1.9 us
    ppermute x4, starting transfers between devices, pair(): lax.ppermute(block, 'row', inner_shift(n_row, k))  1.09 us
    ppermute x3, waiting for transfers between devices, local(): lax.ppermute(own, both, square_shift(n_row, n_col, j, k))  1.01 us
  transfers between devices with their start and end apart: 15, of which 6 were waited for; matrix products, arithmetic and copies ran while one was open for 4% of the time, Pallas kernels for 3%

profile of v17, /device:TPU:0, one launch (start us, length us, event | category | flops | bytes accessed | tf_op | source)
XLA Modules:
  0.0 29.1 jit_solution(3022192388881500034)
XLA Ops:
  0.6 4.1 %collective-permute-start.2 = (bf16[32,1024]{1,0:T(8,128)(2,1)}, bf16[32,1024]{1,0:T(8,128)(2,1)S(1)}, u32[]{:S(2)}, u32[]{:S(2)}) collective-permute-start(bf16[32,1024]{1,0:T(8,128)(2,1)} %param.3), channel_id=1, source_target_pairs={{0,4},{1,5},{2,6},{3,7},{4,0},{5,1},{6,2},{7,3},{8,12},{9,13},{10,... | collective-permute-start | bytes 196616 | tf_op jit(solution)/shard_map/ppermute | solution.py:191
  4.7 0.1 collective-permute-start.3
  4.8 0.9 %pad_maximum_fusion.refs_0_.refs_3_.refs_1_ = bf16[2,32,1024]{2,1,0:T(8,128)(2,1)S(1)} fusion(bf16[1,32,1024]{2,1,0:T(8,128)(2,1)} %bitcast.7, bf16[1,32,1024]{2,1,0:T(8,128)(2,1)} %bitcast.6), kind=kLoop, calls=%fused_computation | loop fusion | flops 65536 | bytes 262144 | tf_op jit(solution)/shard_map/stack | solution.py:184
  5.7 1.9 %collective-permute-start.4 = (bf16[2,32,1024]{2,1,0:T(8,128)(2,1)S(1)}, bf16[2,32,1024]{2,1,0:T(8,128)(2,1)S(1)}, u32[]{:S(2)}, u32[]{:S(2)}) collective-permute-start(bf16[2,32,1024]{2,1,0:T(8,128)(2,1)S(1)} %pad_maximum_fusion.refs_0_.refs_3_.refs_1_), channel_id=1, source_target_pairs={{0,2},{1,3},{2,0},{3,1},{4,6},{5,7},{6,4},{7,5},{8,10},{9,11},{10,... | collective-permute-start | bytes 393224 | tf_op jit(solution)/shard_map/ppermute | solution.py:194
  7.6 1.5 %collective-permute-start = (bf16[2,32,1024]{2,1,0:T(8,128)(2,1)S(1)}, bf16[2,32,1024]{2,1,0:T(8,128)(2,1)S(1)}, u32[]{:S(2)}, u32[]{:S(2)}) collective-permute-start(bf16[2,32,1024]{2,1,0:T(8,128)(2,1)S(1)} %pad_maximum_fusion.refs_0_.refs_3_.refs_1_), channel_id=1, source_target_pairs={{0,16},{1,17},{2,18},{3,19},{4,20},{5,21},{6,22},{7,23},{8,24},{9,... | collective-permute-start | bytes 393224 | tf_op jit(solution)/shard_map/ppermute | solution.py:186
  9.1 1.4 %collective-permute-start.1 = (bf16[2,32,1024]{2,1,0:T(8,128)(2,1)S(1)}, bf16[2,32,1024]{2,1,0:T(8,128)(2,1)S(1)}, u32[]{:S(2)}, u32[]{:S(2)}) collective-permute-start(bf16[2,32,1024]{2,1,0:T(8,128)(2,1)S(1)} %pad_maximum_fusion.refs_0_.refs_3_.refs_1_), channel_id=1, source_target_pairs={{0,17},{1,16},{2,19},{3,18},{4,21},{5,20},{6,23},{7,22},{8,25},{9,... | collective-permute-start | bytes 393224 | tf_op jit(solution)/shard_map/ppermute | solution.py:186
  10.6 0.0 collective-permute-done.2
  10.6 0.5 %collective-permute-start.9 = (bf16[32,1024]{1,0:T(8,128)(2,1)S(1)}, bf16[32,1024]{1,0:T(8,128)(2,1)S(1)}, u32[]{:S(2)}, u32[]{:S(2)}) collective-permute-start(bf16[32,1024]{1,0:T(8,128)(2,1)S(1)} %collective-permute-done.2), channel_id=1, source_target_pairs={{0,2},{1,3},{2,0},{3,1},{4,6},{5,7},{6,4},{7,5},{8,10},{9,11},{10,... | collective-permute-start | bytes 196616 | tf_op jit(solution)/shard_map/ppermute | solution.py:191
  11.0 0.0 collective-permute-done.3
  11.0 1.5 %collective-permute-start.10 = (bf16[32,1024]{1,0:T(8,128)(2,1)S(1)}, bf16[32,1024]{1,0:T(8,128)(2,1)S(1)}, u32[]{:S(2)}, u32[]{:S(2)}) collective-permute-start(bf16[32,1024]{1,0:T(8,128)(2,1)S(1)} %collective-permute-done.3), channel_id=1, source_target_pairs={{0,2},{1,3},{2,0},{3,1},{4,6},{5,7},{6,4},{7,5},{8,10},{9,11},{10,... | collective-permute-start | bytes 196616 | tf_op jit(solution)/shard_map/ppermute | solution.py:191
  12.6 0.1 collective-permute-done.4.refs_5_.refs_3_
  12.7 1.9 %collective-permute-start.5 = (bf16[2,32,1024]{2,1,0:T(8,128)(2,1)S(1)}, bf16[2,32,1024]{2,1,0:T(8,128)(2,1)S(1)}, u32[]{:S(2)}, u32[]{:S(2)}) collective-permute-start(bf16[2,32,1024]{2,1,0:T(8,128)(2,1)S(1)} %pad_maximum_fusion.refs_0_.refs_3_.refs_1_), channel_id=1, source_target_pairs={{0,1},{1,0},{2,3},{3,2},{4,5},{5,4},{6,7},{7,6},{8,9},{9,8},{10,11... | collective-permute-start | bytes 393224 | tf_op jit(solution)/shard_map/ppermute | solution.py:186
  14.6 0.8 %collective-permute-done.refs_1_ = bf16[2,32,1024]{2,1,0:T(8,128)(2,1)S(1)} collective-permute-done((bf16[2,32,1024]{2,1,0:T(8,128)(2,1)S(1)}, bf16[2,32,1024]{2,1,0:T(8,128)(2,1)S(1)}, u32[]{:S(2)}, u32[]{:S(2)}) %collective-permute-start) | collective-permute-done | bytes 131104 | tf_op jit(solution)/shard_map/ppermute | solution.py:186
  15.4 0.0 collective-permute-start.7
  15.4 0.0 collective-permute-done.9
  15.4 0.5 %collective-permute-start.6 = (bf16[2,32,1024]{2,1,0:T(8,128)(2,1)S(1)}, bf16[2,32,1024]{2,1,0:T(8,128)(2,1)S(1)}, u32[]{:S(2)}, u32[]{:S(2)}) collective-permute-start(bf16[2,32,1024]{2,1,0:T(8,128)(2,1)S(1)} %pad_maximum_fusion.refs_0_.refs_3_.refs_1_), channel_id=1, source_target_pairs={{0,8},{8,0},{16,24},{24,16},{1,9},{9,1},{17,25},{25,17},{2,10},{10... | collective-permute-start | bytes 393224 | tf_op jit(solution)/shard_map/ppermute | solution.py:197
  15.9 0.0 collective-permute-done.10
  15.9 0.0 copy-start
  15.9 0.1 collective-permute-start.11
  16.0 0.0 collective-permute-done.1.refs_2_
  16.0 0.5 %collective-permute-start.8 = (bf16[2,32,1024]{2,1,0:T(8,128)(2,1)S(1)}, bf16[2,32,1024]{2,1,0:T(8,128)(2,1)S(1)}, u32[]{:S(2)}, u32[]{:S(2)}) collective-permute-start(bf16[2,32,1024]{2,1,0:T(8,128)(2,1)S(1)} %collective-permute-done.4.refs_5_.refs_3_), channel_id=1, source_target_pairs={{0,8},{8,0},{16,24},{24,16},{1,9},{9,1},{17,25},{25,17},{2,10},{10... | collective-permute-start | bytes 393224 | tf_op jit(solution)/shard_map/ppermute | solution.py:197
  16.5 0.1 copy-done
  16.6 0.1 broadcast_in_dim.2.factors
  16.6 0.8 %shard_map.50 = (bf16[192,1024]{1,0:T(8,128)(2,1)S(1)}, f32[192,1024]{1,0:T(8,128)S(1)}, f32[192,128]{1,0:T(8,128)S(1)}, f32[32,128]{1,0:T(8,128)S(1)}, f32[8,128]{1,0:T(8,128)S(1)}) custom-call(f32[2,128]{1,0:T(2,128)S(1)} %broadcast_in_dim.2.factors, bf16[2,32,1024]{2,1,0:T(8,128)(2,1)S(1)} %pad_maximum_fusion.refs_0_.refs_3_.refs_1_, ...), custom_call_target="tpu_custom_call" | custom-call | flops 150994944 | bytes 2085888 | tf_op jit(solution)/shard_map/pallas_call | solution.py:165
  17.4 0.2 collective-permute-done.5.refs_0_
  17.7 0.0 collective-permute-done.7.refs_5_
  17.7 0.0 collective-permute-done.8.refs_6_
  17.7 0.0 collective-permute-done.6.refs_4_
  17.7 0.0 collective-permute-done.11.refs_8_
  17.7 1.2 %shard_map.51 = (f32[2,32,1024]{2,1,0:T(8,128)S(1)}, f32[65,8,128]{2,1,0:T(8,128)S(1)}, f32[65,8,128]{2,1,0:T(8,128)S(1)}, f32[65,8,128]{2,1,0:T(8,128)S(1)}) custom-call(f32[2,128]{1,0:T(2,128)S(1)} %broadcast_in_dim.2.factors, bf16[192,1024]{1,0:T(8,128)(2,1)S(1)} %get-tuple-element.17.own, f32[192,1024]{1,0:T(8,128)S(1)} %get-tuple-element.18.acc, ...), custom_call_target="tpu_custom_call" | custom-call | flops 385875968 | bytes 3523584 | tf_op jit(solution)/shard_map/pallas_call | solution.py:165
  18.9 2.9 %collective-permute-start.14 = (f16[65,8,128]{2,1,0:T(8,128)(2,1)S(1)}, f16[65,8,128]{2,1,0:T(8,128)(2,1)S(1)}, u32[]{:S(2)}, u32[]{:S(2)}) collective-permute-start(f16[65,8,128]{2,1,0:T(8,128)(2,1)S(1)} %convert_element_type.22), channel_id=1, source_target_pairs={{0,17},{1,16},{2,19},{3,18},{4,21},{5,20},{6,23},{7,22},{8,25},{9,... | collective-permute-start | bytes 399368 | tf_op jit(solution)/shard_map/ppermute | solution.py:231
  21.8 0.5 %collective-permute-start.13 = (f16[65,8,128]{2,1,0:T(8,128)(2,1)S(1)}, f16[65,8,128]{2,1,0:T(8,128)(2,1)S(1)}, u32[]{:S(2)}, u32[]{:S(2)}) collective-permute-start(f16[65,8,128]{2,1,0:T(8,128)(2,1)S(1)} %convert_element_type.20), channel_id=1, source_target_pairs={{0,1},{1,0},{2,3},{3,2},{4,5},{5,4},{6,7},{7,6},{8,9},{9,8},{10,11... | collective-permute-start | bytes 399368 | tf_op jit(solution)/shard_map/ppermute | solution.py:231
  22.4 0.2 collective-permute-start.12
  22.6 3.7 %collective-permute-done.14 = f16[65,8,128]{2,1,0:T(8,128)(2,1)S(1)} collective-permute-done((f16[65,8,128]{2,1,0:T(8,128)(2,1)S(1)}, f16[65,8,128]{2,1,0:T(8,128)(2,1)S(1)}, u32[]{:S(2)}, u32[]{:S(2)}) %collective-permute-start.14) | collective-permute-done | bytes 133152 | tf_op jit(solution)/shard_map/ppermute | solution.py:231
  26.3 1.9 %collective-permute-done.13 = f16[65,8,128]{2,1,0:T(8,128)(2,1)S(1)} collective-permute-done((f16[65,8,128]{2,1,0:T(8,128)(2,1)S(1)}, f16[65,8,128]{2,1,0:T(8,128)(2,1)S(1)}, u32[]{:S(2)}, u32[]{:S(2)}) %collective-permute-start.13) | collective-permute-done | bytes 133152 | tf_op jit(solution)/shard_map/ppermute | solution.py:231
  28.2 0.1 collective-permute-done.12
  28.4 0.8 %shard_map.52 = (f32[32,1024]{1,0:T(8,128)}, f32[32,1024]{1,0:T(8,128)}) custom-call(f32[2,32,1024]{2,1,0:T(8,128)S(1)} %get-tuple-element.23.own, f32[32,128]{1,0:T(8,128)S(1)} %get-tuple-element.24.down, f32[65,8,128]{2,1,0:T(8,128)S(1)} %convert_element_type.19.refs_0_, f32[65,8,128]{2,1,0:T(8,128)S(1)} %convert_element_type.21.refs_1_, ...), custom_call_target="tpu_custom_call" | custom-call | flops 524288 | bytes 1339392 | tf_op jit(solution)/shard_map/pallas_call | solution.py:165
  (9 shorter events, 0.2 us)
Async XLA Ops:
  0.6 9.9 %collective-permute-start.2 = (bf16[32,1024]{1,0:T(8,128)(2,1)}, bf16[32,1024]{1,0:T(8,128)(2,1)S(1)}, u32[]{:S(2)}, u32[]{:S(2)}) collective-permute-start(bf16[32,1024]{1,0:T(8,128)(2,1)} %param.3), channel_id=1, source_target_pairs={{0,4},{1,5},{2,6},{3,7},{4,0},{5,1},{6,2},{7,3},{8,12},{9,13},{10,... | collective-permute-start | bytes 196616 | tf_op jit(solution)/shard_map/ppermute | solution.py:191
  4.7 6.3 %collective-permute-start.3 = (bf16[32,1024]{1,0:T(8,128)(2,1)}, bf16[32,1024]{1,0:T(8,128)(2,1)S(1)}, u32[]{:S(2)}, u32[]{:S(2)}) collective-permute-start(bf16[32,1024]{1,0:T(8,128)(2,1)} %param.4), channel_id=1, source_target_pairs={{0,4},{1,5},{2,6},{3,7},{4,0},{5,1},{6,2},{7,3},{8,12},{9,13},{10,... | collective-permute-start | bytes 196616 | tf_op jit(solution)/shard_map/ppermute | solution.py:191
  5.7 7.0 %collective-permute-start.4 = (bf16[2,32,1024]{2,1,0:T(8,128)(2,1)S(1)}, bf16[2,32,1024]{2,1,0:T(8,128)(2,1)S(1)}, u32[]{:S(2)}, u32[]{:S(2)}) collective-permute-start(bf16[2,32,1024]{2,1,0:T(8,128)(2,1)S(1)} %pad_maximum_fusion.refs_0_.refs_3_.refs_1_), channel_id=1, source_target_pairs={{0,2},{1,3},{2,0},{3,1},{4,6},{5,7},{6,4},{7,5},{8,10},{9,11},{10,... | collective-permute-start | bytes 393224 | tf_op jit(solution)/shard_map/ppermute | solution.py:194
  7.6 7.8 %collective-permute-start = (bf16[2,32,1024]{2,1,0:T(8,128)(2,1)S(1)}, bf16[2,32,1024]{2,1,0:T(8,128)(2,1)S(1)}, u32[]{:S(2)}, u32[]{:S(2)}) collective-permute-start(bf16[2,32,1024]{2,1,0:T(8,128)(2,1)S(1)} %pad_maximum_fusion.refs_0_.refs_3_.refs_1_), channel_id=1, source_target_pairs={{0,16},{1,17},{2,18},{3,19},{4,20},{5,21},{6,22},{7,23},{8,24},{9,... | collective-permute-start | bytes 393224 | tf_op jit(solution)/shard_map/ppermute | solution.py:186
  9.1 6.9 %collective-permute-start.1 = (bf16[2,32,1024]{2,1,0:T(8,128)(2,1)S(1)}, bf16[2,32,1024]{2,1,0:T(8,128)(2,1)S(1)}, u32[]{:S(2)}, u32[]{:S(2)}) collective-permute-start(bf16[2,32,1024]{2,1,0:T(8,128)(2,1)S(1)} %pad_maximum_fusion.refs_0_.refs_3_.refs_1_), channel_id=1, source_target_pairs={{0,17},{1,16},{2,19},{3,18},{4,21},{5,20},{6,23},{7,22},{8,25},{9,... | collective-permute-start | bytes 393224 | tf_op jit(solution)/shard_map/ppermute | solution.py:186
  10.6 4.8 %collective-permute-start.9 = (bf16[32,1024]{1,0:T(8,128)(2,1)S(1)}, bf16[32,1024]{1,0:T(8,128)(2,1)S(1)}, u32[]{:S(2)}, u32[]{:S(2)}) collective-permute-start(bf16[32,1024]{1,0:T(8,128)(2,1)S(1)} %collective-permute-done.2), channel_id=1, source_target_pairs={{0,2},{1,3},{2,0},{3,1},{4,6},{5,7},{6,4},{7,5},{8,10},{9,11},{10,... | collective-permute-start | bytes 196616 | tf_op jit(solution)/shard_map/ppermute | solution.py:191
  11.0 4.8 %collective-permute-start.10 = (bf16[32,1024]{1,0:T(8,128)(2,1)S(1)}, bf16[32,1024]{1,0:T(8,128)(2,1)S(1)}, u32[]{:S(2)}, u32[]{:S(2)}) collective-permute-start(bf16[32,1024]{1,0:T(8,128)(2,1)S(1)} %collective-permute-done.3), channel_id=1, source_target_pairs={{0,2},{1,3},{2,0},{3,1},{4,6},{5,7},{6,4},{7,5},{8,10},{9,11},{10,... | collective-permute-start | bytes 196616 | tf_op jit(solution)/shard_map/ppermute | solution.py:191
  12.7 5.0 %collective-permute-start.5 = (bf16[2,32,1024]{2,1,0:T(8,128)(2,1)S(1)}, bf16[2,32,1024]{2,1,0:T(8,128)(2,1)S(1)}, u32[]{:S(2)}, u32[]{:S(2)}) collective-permute-start(bf16[2,32,1024]{2,1,0:T(8,128)(2,1)S(1)} %pad_maximum_fusion.refs_0_.refs_3_.refs_1_), channel_id=1, source_target_pairs={{0,1},{1,0},{2,3},{3,2},{4,5},{5,4},{6,7},{7,6},{8,9},{9,8},{10,11... | collective-permute-start | bytes 393224 | tf_op jit(solution)/shard_map/ppermute | solution.py:186
  15.4 2.3 %collective-permute-start.7 = (bf16[2,32,1024]{2,1,0:T(8,128)(2,1)S(1)}, bf16[2,32,1024]{2,1,0:T(8,128)(2,1)S(1)}, u32[]{:S(2)}, u32[]{:S(2)}) collective-permute-start(bf16[2,32,1024]{2,1,0:T(8,128)(2,1)S(1)} %pad_maximum_fusion.1.refs_4_.refs_2_), channel_id=1, source_target_pairs={{0,8},{8,0},{16,24},{24,16},{1,9},{9,1},{17,25},{25,17},{2,10},{10... | collective-permute-start | bytes 393224 | tf_op jit(solution)/shard_map/ppermute | solution.py:197
  15.4 2.3 %collective-permute-start.6 = (bf16[2,32,1024]{2,1,0:T(8,128)(2,1)S(1)}, bf16[2,32,1024]{2,1,0:T(8,128)(2,1)S(1)}, u32[]{:S(2)}, u32[]{:S(2)}) collective-permute-start(bf16[2,32,1024]{2,1,0:T(8,128)(2,1)S(1)} %pad_maximum_fusion.refs_0_.refs_3_.refs_1_), channel_id=1, source_target_pairs={{0,8},{8,0},{16,24},{24,16},{1,9},{9,1},{17,25},{25,17},{2,10},{10... | collective-permute-start | bytes 393224 | tf_op jit(solution)/shard_map/ppermute | solution.py:197
  15.9 0.7 %copy-start = (f32[2]{0:T(128)S(1)}, f32[2]{0:T(128)}, u32[]{:S(2)}) copy-start(f32[2]{0:T(128)} %param.5) | copy-start | bytes 28
  15.9 1.8 %collective-permute-start.11 = (bf16[2,32,1024]{2,1,0:T(8,128)(2,1)S(1)}, bf16[2,32,1024]{2,1,0:T(8,128)(2,1)S(1)}, u32[]{:S(2)}, u32[]{:S(2)}) collective-permute-start(bf16[2,32,1024]{2,1,0:T(8,128)(2,1)S(1)} %pad_maximum_fusion.2.refs_7_), channel_id=1, source_target_pairs={{0,8},{8,0},{16,24},{24,16},{1,9},{9,1},{17,25},{25,17},{2,10},{10... | collective-permute-start | bytes 393224 | tf_op jit(solution)/shard_map/ppermute | solution.py:197
  16.0 1.7 %collective-permute-start.8 = (bf16[2,32,1024]{2,1,0:T(8,128)(2,1)S(1)}, bf16[2,32,1024]{2,1,0:T(8,128)(2,1)S(1)}, u32[]{:S(2)}, u32[]{:S(2)}) collective-permute-start(bf16[2,32,1024]{2,1,0:T(8,128)(2,1)S(1)} %collective-permute-done.4.refs_5_.refs_3_), channel_id=1, source_target_pairs={{0,8},{8,0},{16,24},{24,16},{1,9},{9,1},{17,25},{25,17},{2,10},{10... | collective-permute-start | bytes 393224 | tf_op jit(solution)/shard_map/ppermute | solution.py:197
  18.9 7.3 %collective-permute-start.14 = (f16[65,8,128]{2,1,0:T(8,128)(2,1)S(1)}, f16[65,8,128]{2,1,0:T(8,128)(2,1)S(1)}, u32[]{:S(2)}, u32[]{:S(2)}) collective-permute-start(f16[65,8,128]{2,1,0:T(8,128)(2,1)S(1)} %convert_element_type.22), channel_id=1, source_target_pairs={{0,17},{1,16},{2,19},{3,18},{4,21},{5,20},{6,23},{7,22},{8,25},{9,... | collective-permute-start | bytes 399368 | tf_op jit(solution)/shard_map/ppermute | solution.py:231
  21.8 6.4 %collective-permute-start.13 = (f16[65,8,128]{2,1,0:T(8,128)(2,1)S(1)}, f16[65,8,128]{2,1,0:T(8,128)(2,1)S(1)}, u32[]{:S(2)}, u32[]{:S(2)}) collective-permute-start(f16[65,8,128]{2,1,0:T(8,128)(2,1)S(1)} %convert_element_type.20), channel_id=1, source_target_pairs={{0,1},{1,0},{2,3},{3,2},{4,5},{5,4},{6,7},{7,6},{8,9},{9,8},{10,11... | collective-permute-start | bytes 399368 | tf_op jit(solution)/shard_map/ppermute | solution.py:231
  22.4 6.0 %collective-permute-start.12 = (f16[65,8,128]{2,1,0:T(8,128)(2,1)S(1)}, f16[65,8,128]{2,1,0:T(8,128)(2,1)S(1)}, u32[]{:S(2)}, u32[]{:S(2)}) collective-permute-start(f16[65,8,128]{2,1,0:T(8,128)(2,1)S(1)} %convert_element_type.18), channel_id=1, source_target_pairs={{0,16},{1,17},{2,18},{3,19},{4,20},{5,21},{6,22},{7,23},{8,24},{9,... | collective-permute-start | bytes 399368 | tf_op jit(solution)/shard_map/ppermute | solution.py:231

commit v18 on v17

--- a/solution.py
+++ b/solution.py
@@ -102,7 +102,12 @@
     half = most.shape[0]
     for s in range(2):
         up[s * half : (s + 1) * half] = jnp.broadcast_to(TOP / most, (half, up.shape[1]))
-    down[...] = jnp.broadcast_to((most / TOP)[: down.shape[0]], down.shape)
+    rows, across = refs[0].shape[1], keys.shape[1] // 128
+    for r in range(0, rows, 8):
+        tile = jnp.broadcast_to(most[r : r + 8] / TOP, (8, 128))
+        for s in range(2):
+            for c in range(across):
+                down[(s * rows + r) // 8 * across + c] = tile
     most_key[...] = jnp.broadcast_to(largest(keys), most_key.shape)
 
 
@@ -136,7 +141,7 @@
             low = s * (half + rows)
             mine = slice(s * half, (s + 1) * half)
             ready = grad[low : low + half] + acc[mine, at]
-            outs[0][s, :, at] = ready[:rows]
+            send(outs[0], s, at, ready[:rows])
             ready = ready * up[mine, :1] * shrink
             for i in range(1, n):
                 send(outs[i], s, at, ready[i * rows : (i + 1) * rows])
@@ -144,19 +149,19 @@
             send(outs[n], s, at, both * factor * shrink)
 
 
-def sum_kernel(own, down, *refs):
-    *parts, images, texts = refs
-    rows, width = images.shape
+def sum_kernel(ready, down, last, images, texts, total, sems):
+    _, rows, width = total.shape
     across = width // 128
-    grow = [jnp.exp2(2.0 * part[part.shape[0] - 1]) for part in parts]
-    for s, out in enumerate((images, texts)):
+    grow = jnp.exp2(2.0 * last[last.shape[0] - 1])
+    copies = [pltpu.make_async_copy(total.at[s], out, sems.at[s]) for s, out in enumerate((images, texts))]
+    for s, copy in enumerate(copies):
         for r in range(0, rows, 8):
-            scales = [down[r : r + 8] * g for g in grow]
             for c in range(across):
-                total = own[s, r : r + 8, c * 128 : (c + 1) * 128]
-                for part, scale in zip(parts, scales):
-                    total = total + part[(s * rows + r) // 8 * across + c] * scale
-                out[r : r + 8, c * 128 : (c + 1) * 128] = total
+                tile = (s * rows + r) // 8 * across + c
+                total[s, r : r + 8, c * 128 : (c + 1) * 128] = ready[tile] + last[tile] * (down[tile] * grow)
+        copy.start()
+    for copy in copies:
+        copy.wait()
 
 
 def call(kernel, operands, out_shape, flops):
@@ -204,7 +209,7 @@
             block, early[2] = lax.optimization_barrier((block, early[2]))
         copies += pair(block)
     total = rows * len(line) * row_inner
-    f32 = jnp.float32
+    f32, count = jnp.float32, 2 * rows * width // 1024
     *first, last = mine
     many = rows * len(first)
 
@@ -215,28 +220,35 @@
         functools.partial(early_kernel, total, len(first)),
         [factors] + first + early,
         [jax.ShapeDtypeStruct((2 * many, width), images.dtype)]
-        + [jax.ShapeDtypeStruct(s, f32) for s in [(2 * many, width), (2 * many, 128), (rows, 128), (8, 128)]],
+        + [jax.ShapeDtypeStruct(s, f32) for s in [(2 * many, width), (2 * many, 128), (count, 8, 128), (8, 128)]],
         flops(len(first), len(early)),
     )
     late = copies + [line[-1]] + pair(line[-1])
     parts = call(
         functools.partial(late_kernel, total, len(first), len(early)),
         [factors, mine_joined, acc, up, most_key, last] + early + late,
-        [jax.ShapeDtypeStruct((2, rows, width), f32)]
-        + [jax.ShapeDtypeStruct((2 * rows * width // 1024 + 1, 8, 128), f32)] * len(square),
+        [jax.ShapeDtypeStruct((count, 8, 128), f32)]
+        + [jax.ShapeDtypeStruct((count + 1, 8, 128), f32)] * len(square),
         flops(len(first), len(late)) + flops(1, len(early + late)),
     )
     far = sorted(zip(square, parts[1:]), key=lambda item: sum(item[0]))
     back = [
         lax.ppermute(part.astype(jnp.float16), both, square_shift(n_row, n_col, -j, -k)) for (j, k), part in far
     ]
+    last, *back = [part.astype(f32) for part in back]
+    grow = [down * jnp.exp2(2.0 * part[-1, 0, 0]) for part in back]
+    ready = parts[0] + sum(part[:-1] * scale for part, scale in zip(back, grow))
+    ready = lax.optimization_barrier(ready)
+    vmem, hbm = pl.BlockSpec(memory_space=pltpu.VMEM), pl.BlockSpec(memory_space=pltpu.HBM)
     return tuple(
-        call(
+        pl.pallas_call(
             sum_kernel,
-            [parts[0], down] + [part.astype(f32) for part in back],
-            [jax.ShapeDtypeStruct((rows, width), f32)] * 2,
-            4 * rows * width * len(mine),
-        )
+            out_shape=[jax.ShapeDtypeStruct((rows, width), f32)] * 2,
+            in_specs=[vmem] * 3,
+            out_specs=[hbm] * 2,
+            scratch_shapes=[pltpu.VMEM((2, rows, width), f32), pltpu.SemaphoreType.DMA((2,))],
+            compiler_params=pltpu.CompilerParams(vmem_limit_bytes=40 * 2**20),
+        )(ready, down, last)
     )
 
 

time: 29.3 us -> 30.5 us (1.041)
  between operations: 0.71 us -> 2.1 us
  waiting for transfers between devices: 6.89 us -> 5.52 us
  local copies, waits for them, and re-layouts: 0.13 us -> 1.16 us
    ppermute x3, waiting for transfers between devices: 5.73 us -> 4.36 us  [local(): lax.ppermute(part.astype(jnp.float16), both, square_shift(n_row, n_col, -...]
    slice x0 -> x2, local copies, waits for them, and re-layouts: none -> 1.03 us  [local(): grow = [down * jnp.exp2(2.0 * part[-1, 0, 0]) for part in back]]
    pallas_call x3 -> x2, Pallas kernels: 2.74 us -> 1.96 us  [call(): pl.pallas_call(kernel, out_shape=out_shape, in_specs=[vmem] * len(operand...]
    pallas_call x0 -> x1, Pallas kernels: none -> 0.74 us  [local(): pl.pallas_call(sum_kernel, out_shape=[jax.ShapeDtypeStruct((rows, width),...]
  transfers between devices with their start and end apart: 15 -> 15, of which waited for: 6 -> 5; matrix products, arithmetic and copies ran while one was open for 4% -> 7% of each run, Pallas kernels for 3% -> 3%
where the time goes in v18:
time: 30.5 us; the launch traced here: 30.3 us
  starting transfers between devices  17.7 us (58%)
  waiting for transfers between devices  5.52 us (18%)
  Pallas kernels  2.7 us (9%)
  between operations  2.1 us (7%)
  local copies, waits for them, and re-layouts  1.16 us (4%)
  other arithmetic  1.14 us (4%)
    ppermute x4, starting transfers between devices, local(): apart[step] = [lax.ppermute(half, 'col', perm) for half in apart[which]]  6.17 us
    ppermute x3, starting transfers between devices, local(): lax.ppermute(own, both, square_shift(n_row, n_col, j, k))  4.84 us
    ppermute x3, waiting for transfers between devices, local(): lax.ppermute(part.astype(jnp.float16), both, square_shift(n_row, n_col, -...  4.36 us
    ppermute x3, starting transfers between devices, local(): lax.ppermute(part.astype(jnp.float16), both, square_shift(n_row, n_col, -...  3.68 us
    pallas_call x2, Pallas kernels, call(): pl.pallas_call(kernel, out_shape=out_shape, in_specs=[vmem] * len(operand...  1.96 us
    ppermute x1, starting transfers between devices, local(): line.append(lax.ppermute(line[which], 'col', perm))  1.9 us
    ppermute x4, starting transfers between devices, pair(): lax.ppermute(block, 'row', inner_shift(n_row, k))  1.09 us
    slice x2, local copies, waits for them, and re-layouts, local(): grow = [down * jnp.exp2(2.0 * part[-1, 0, 0]) for part in back]  1.03 us
  transfers between devices with their start and end apart: 15, of which 5 were waited for; matrix products, arithmetic and copies ran while one was open for 7% of the time, Pallas kernels for 3%

profile of v18, /device:TPU:0, one launch (start us, length us, event | category | flops | bytes accessed | tf_op | source)
XLA Modules:
  0.0 30.3 jit_solution(165190132543634380)
XLA Ops:
  0.6 4.1 %collective-permute-start.2 = (bf16[32,1024]{1,0:T(8,128)(2,1)}, bf16[32,1024]{1,0:T(8,128)(2,1)S(1)}, u32[]{:S(2)}, u32[]{:S(2)}) collective-permute-start(bf16[32,1024]{1,0:T(8,128)(2,1)} %param.3), channel_id=1, source_target_pairs={{0,4},{1,5},{2,6},{3,7},{4,0},{5,1},{6,2},{7,3},{8,12},{9,13},{10,... | collective-permute-start | bytes 196616 | tf_op jit(solution)/shard_map/ppermute | solution.py:196
  4.7 0.1 collective-permute-start.3
  4.8 0.9 %pad_maximum_fusion.refs_0_.refs_3_.refs_1_ = bf16[2,32,1024]{2,1,0:T(8,128)(2,1)S(1)} fusion(bf16[1,32,1024]{2,1,0:T(8,128)(2,1)} %bitcast.9, bf16[1,32,1024]{2,1,0:T(8,128)(2,1)} %bitcast.8), kind=kLoop, calls=%fused_computation.4 | loop fusion | flops 65536 | bytes 262144 | tf_op jit(solution)/shard_map/stack | solution.py:189
  5.7 1.9 %collective-permute-start.4 = (bf16[2,32,1024]{2,1,0:T(8,128)(2,1)S(1)}, bf16[2,32,1024]{2,1,0:T(8,128)(2,1)S(1)}, u32[]{:S(2)}, u32[]{:S(2)}) collective-permute-start(bf16[2,32,1024]{2,1,0:T(8,128)(2,1)S(1)} %pad_maximum_fusion.refs_0_.refs_3_.refs_1_), channel_id=1, source_target_pairs={{0,2},{1,3},{2,0},{3,1},{4,6},{5,7},{6,4},{7,5},{8,10},{9,11},{10,... | collective-permute-start | bytes 393224 | tf_op jit(solution)/shard_map/ppermute | solution.py:199
  7.6 1.5 %collective-permute-start = (bf16[2,32,1024]{2,1,0:T(8,128)(2,1)S(1)}, bf16[2,32,1024]{2,1,0:T(8,128)(2,1)S(1)}, u32[]{:S(2)}, u32[]{:S(2)}) collective-permute-start(bf16[2,32,1024]{2,1,0:T(8,128)(2,1)S(1)} %pad_maximum_fusion.refs_0_.refs_3_.refs_1_), channel_id=1, source_target_pairs={{0,16},{1,17},{2,18},{3,19},{4,20},{5,21},{6,22},{7,23},{8,24},{9,... | collective-permute-start | bytes 393224 | tf_op jit(solution)/shard_map/ppermute | solution.py:191
  9.1 1.4 %collective-permute-start.1 = (bf16[2,32,1024]{2,1,0:T(8,128)(2,1)S(1)}, bf16[2,32,1024]{2,1,0:T(8,128)(2,1)S(1)}, u32[]{:S(2)}, u32[]{:S(2)}) collective-permute-start(bf16[2,32,1024]{2,1,0:T(8,128)(2,1)S(1)} %pad_maximum_fusion.refs_0_.refs_3_.refs_1_), channel_id=1, source_target_pairs={{0,17},{1,16},{2,19},{3,18},{4,21},{5,20},{6,23},{7,22},{8,25},{9,... | collective-permute-start | bytes 393224 | tf_op jit(solution)/shard_map/ppermute | solution.py:191
  10.6 0.0 collective-permute-done.2
  10.6 0.5 %collective-permute-start.9 = (bf16[32,1024]{1,0:T(8,128)(2,1)S(1)}, bf16[32,1024]{1,0:T(8,128)(2,1)S(1)}, u32[]{:S(2)}, u32[]{:S(2)}) collective-permute-start(bf16[32,1024]{1,0:T(8,128)(2,1)S(1)} %collective-permute-done.2), channel_id=1, source_target_pairs={{0,2},{1,3},{2,0},{3,1},{4,6},{5,7},{6,4},{7,5},{8,10},{9,11},{10,... | collective-permute-start | bytes 196616 | tf_op jit(solution)/shard_map/ppermute | solution.py:196
  11.0 0.0 collective-permute-done.3
  11.0 1.5 %collective-permute-start.10 = (bf16[32,1024]{1,0:T(8,128)(2,1)S(1)}, bf16[32,1024]{1,0:T(8,128)(2,1)S(1)}, u32[]{:S(2)}, u32[]{:S(2)}) collective-permute-start(bf16[32,1024]{1,0:T(8,128)(2,1)S(1)} %collective-permute-done.3), channel_id=1, source_target_pairs={{0,2},{1,3},{2,0},{3,1},{4,6},{5,7},{6,4},{7,5},{8,10},{9,11},{10,... | collective-permute-start | bytes 196616 | tf_op jit(solution)/shard_map/ppermute | solution.py:196
  12.6 0.1 collective-permute-done.4.refs_5_.refs_3_
  12.7 1.9 %collective-permute-start.5 = (bf16[2,32,1024]{2,1,0:T(8,128)(2,1)S(1)}, bf16[2,32,1024]{2,1,0:T(8,128)(2,1)S(1)}, u32[]{:S(2)}, u32[]{:S(2)}) collective-permute-start(bf16[2,32,1024]{2,1,0:T(8,128)(2,1)S(1)} %pad_maximum_fusion.refs_0_.refs_3_.refs_1_), channel_id=1, source_target_pairs={{0,1},{1,0},{2,3},{3,2},{4,5},{5,4},{6,7},{7,6},{8,9},{9,8},{10,11... | collective-permute-start | bytes 393224 | tf_op jit(solution)/shard_map/ppermute | solution.py:191
  14.6 0.8 %collective-permute-done.refs_1_ = bf16[2,32,1024]{2,1,0:T(8,128)(2,1)S(1)} collective-permute-done((bf16[2,32,1024]{2,1,0:T(8,128)(2,1)S(1)}, bf16[2,32,1024]{2,1,0:T(8,128)(2,1)S(1)}, u32[]{:S(2)}, u32[]{:S(2)}) %collective-permute-start) | collective-permute-done | bytes 131104 | tf_op jit(solution)/shard_map/ppermute | solution.py:191
  15.4 0.0 collective-permute-start.7
  15.4 0.0 collective-permute-done.9
  15.4 0.5 %collective-permute-start.6 = (bf16[2,32,1024]{2,1,0:T(8,128)(2,1)S(1)}, bf16[2,32,1024]{2,1,0:T(8,128)(2,1)S(1)}, u32[]{:S(2)}, u32[]{:S(2)}) collective-permute-start(bf16[2,32,1024]{2,1,0:T(8,128)(2,1)S(1)} %pad_maximum_fusion.refs_0_.refs_3_.refs_1_), channel_id=1, source_target_pairs={{0,8},{8,0},{16,24},{24,16},{1,9},{9,1},{17,25},{25,17},{2,10},{10... | collective-permute-start | bytes 393224 | tf_op jit(solution)/shard_map/ppermute | solution.py:202
  15.9 0.0 collective-permute-done.10
  15.9 0.0 copy-start
  15.9 0.1 collective-permute-start.11
  16.0 0.0 collective-permute-done.1.refs_2_
  16.0 0.5 %collective-permute-start.8 = (bf16[2,32,1024]{2,1,0:T(8,128)(2,1)S(1)}, bf16[2,32,1024]{2,1,0:T(8,128)(2,1)S(1)}, u32[]{:S(2)}, u32[]{:S(2)}) collective-permute-start(bf16[2,32,1024]{2,1,0:T(8,128)(2,1)S(1)} %collective-permute-done.4.refs_5_.refs_3_), channel_id=1, source_target_pairs={{0,8},{8,0},{16,24},{24,16},{1,9},{9,1},{17,25},{25,17},{2,10},{10... | collective-permute-start | bytes 393224 | tf_op jit(solution)/shard_map/ppermute | solution.py:202
  16.5 0.1 copy-done
  16.6 0.1 broadcast_in_dim.2.factors
  16.6 0.8 %shard_map.50 = (bf16[192,1024]{1,0:T(8,128)(2,1)S(1)}, f32[192,1024]{1,0:T(8,128)S(1)}, f32[192,128]{1,0:T(8,128)S(1)}, f32[64,8,128]{2,1,0:T(8,128)S(1)}, f32[8,128]{1,0:T(8,128)S(1)}) custom-call(f32[2,128]{1,0:T(2,128)S(1)} %broadcast_in_dim.2.factors, bf16[2,32,1024]{2,1,0:T(8,128)(2,1)S(1)} %pad_maximum_fusion.refs_0_.refs_3_.refs_1_, ...), custom_call_target="tpu_custom_call" | custom-call | flops 150994944 | bytes 2331648 | tf_op jit(solution)/shard_map/pallas_call | solution.py:170
  17.4 0.2 collective-permute-done.5.refs_0_
  17.7 0.0 collective-permute-done.7.refs_5_
  17.7 0.0 collective-permute-done.8.refs_6_
  17.7 0.0 collective-permute-done.6.refs_4_
  17.7 0.0 collective-permute-done.11.refs_8_
  17.7 1.2 %shard_map.51 = (f32[64,8,128]{2,1,0:T(8,128)S(1)}, f32[65,8,128]{2,1,0:T(8,128)S(1)}, f32[65,8,128]{2,1,0:T(8,128)S(1)}, f32[65,8,128]{2,1,0:T(8,128)S(1)}) custom-call(f32[2,128]{1,0:T(2,128)S(1)} %broadcast_in_dim.2.factors, bf16[192,1024]{1,0:T(8,128)(2,1)S(1)} %get-tuple-element.17.own, f32[192,1024]{1,0:T(8,128)S(1)} %get-tuple-element.18.acc, ...), custom_call_target="tpu_custom_call" | custom-call | flops 385875968 | bytes 3523584 | tf_op jit(solution)/shard_map/pallas_call | solution.py:170
  18.9 2.9 %collective-permute-start.13 = (f16[65,8,128]{2,1,0:T(8,128)(2,1)S(1)}, f16[65,8,128]{2,1,0:T(8,128)(2,1)S(1)}, u32[]{:S(2)}, u32[]{:S(2)}) collective-permute-start(f16[65,8,128]{2,1,0:T(8,128)(2,1)S(1)} %convert_element_type.20), channel_id=1, source_target_pairs={{0,17},{1,16},{2,19},{3,18},{4,21},{5,20},{6,23},{7,22},{8,25},{9,... | collective-permute-start | bytes 399368 | tf_op jit(solution)/shard_map/ppermute | solution.py:236
  21.8 0.6 %collective-permute-start.12 = (f16[65,8,128]{2,1,0:T(8,128)(2,1)S(1)}, f16[65,8,128]{2,1,0:T(8,128)(2,1)S(1)}, u32[]{:S(2)}, u32[]{:S(2)}) collective-permute-start(f16[65,8,128]{2,1,0:T(8,128)(2,1)S(1)} %convert_element_type.18), channel_id=1, source_target_pairs={{0,1},{1,0},{2,3},{3,2},{4,5},{5,4},{6,7},{7,6},{8,9},{9,8},{10,11... | collective-permute-start | bytes 399368 | tf_op jit(solution)/shard_map/ppermute | solution.py:236
  22.4 0.2 collective-permute-start.14
  22.6 3.6 %collective-permute-done.13 = f16[65,8,128]{2,1,0:T(8,128)(2,1)S(1)} collective-permute-done((f16[65,8,128]{2,1,0:T(8,128)(2,1)S(1)}, f16[65,8,128]{2,1,0:T(8,128)(2,1)S(1)}, u32[]{:S(2)}, u32[]{:S(2)}) %collective-permute-start.13) | collective-permute-done | bytes 133152 | tf_op jit(solution)/shard_map/ppermute | solution.py:236
  26.3 0.5 %slice.19 = f32[1,1,1]{2,1,0:T(1,128)} slice(f32[65,8,128]{2,1,0:T(8,128)S(1)} %convert_element_type.21), slice={[64:65], [0:1], [0:1]} | slice | bytes 8 | tf_op jit(solution)/shard_map/slice | solution.py:239
  27.5 0.7 %collective-permute-done.12 = f16[65,8,128]{2,1,0:T(8,128)(2,1)S(1)} collective-permute-done((f16[65,8,128]{2,1,0:T(8,128)(2,1)S(1)}, f16[65,8,128]{2,1,0:T(8,128)(2,1)S(1)}, u32[]{:S(2)}, u32[]{:S(2)}) %collective-permute-start.12) | collective-permute-done | bytes 133152 | tf_op jit(solution)/shard_map/ppermute | solution.py:236
  28.2 0.5 %slice.17 = f32[1,1,1]{2,1,0:T(1,128)} slice(f32[65,8,128]{2,1,0:T(8,128)S(1)} %convert_element_type.19), slice={[64:65], [0:1], [0:1]} | slice | bytes 8 | tf_op jit(solution)/shard_map/slice | solution.py:239
  29.4 0.1 fusion.1.ready
  29.5 0.0 collective-permute-done.14
  29.6 0.7 %shard_map.52 = (f32[32,1024]{1,0:T(8,128)}, f32[32,1024]{1,0:T(8,128)}) custom-call(f32[64,8,128]{2,1,0:T(8,128)S(1)} %fusion.1.ready, f32[64,8,128]{2,1,0:T(8,128)S(1)} %get-tuple-element.25.down, f32[65,8,128]{2,1,0:T(8,128)S(1)} %convert_element_type.23.last), custom_call_target="tpu_custom_call" | custom-call | tf_op jit(solution)/shard_map/pallas_call | solution.py:244
  (9 shorter events, 0.2 us)
Async XLA Ops:
  0.6 9.9 %collective-permute-start.2 = (bf16[32,1024]{1,0:T(8,128)(2,1)}, bf16[32,1024]{1,0:T(8,128)(2,1)S(1)}, u32[]{:S(2)}, u32[]{:S(2)}) collective-permute-start(bf16[32,1024]{1,0:T(8,128)(2,1)} %param.3), channel_id=1, source_target_pairs={{0,4},{1,5},{2,6},{3,7},{4,0},{5,1},{6,2},{7,3},{8,12},{9,13},{10,... | collective-permute-start | bytes 196616 | tf_op jit(solution)/shard_map/ppermute | solution.py:196
  4.7 6.3 %collective-permute-start.3 = (bf16[32,1024]{1,0:T(8,128)(2,1)}, bf16[32,1024]{1,0:T(8,128)(2,1)S(1)}, u32[]{:S(2)}, u32[]{:S(2)}) collective-permute-start(bf16[32,1024]{1,0:T(8,128)(2,1)} %param.4), channel_id=1, source_target_pairs={{0,4},{1,5},{2,6},{3,7},{4,0},{5,1},{6,2},{7,3},{8,12},{9,13},{10,... | collective-permute-start | bytes 196616 | tf_op jit(solution)/shard_map/ppermute | solution.py:196
  5.7 7.0 %collective-permute-start.4 = (bf16[2,32,1024]{2,1,0:T(8,128)(2,1)S(1)}, bf16[2,32,1024]{2,1,0:T(8,128)(2,1)S(1)}, u32[]{:S(2)}, u32[]{:S(2)}) collective-permute-start(bf16[2,32,1024]{2,1,0:T(8,128)(2,1)S(1)} %pad_maximum_fusion.refs_0_.refs_3_.refs_1_), channel_id=1, source_target_pairs={{0,2},{1,3},{2,0},{3,1},{4,6},{5,7},{6,4},{7,5},{8,10},{9,11},{10,... | collective-permute-start | bytes 393224 | tf_op jit(solution)/shard_map/ppermute | solution.py:199
  7.6 7.8 %collective-permute-start = (bf16[2,32,1024]{2,1,0:T(8,128)(2,1)S(1)}, bf16[2,32,1024]{2,1,0:T(8,128)(2,1)S(1)}, u32[]{:S(2)}, u32[]{:S(2)}) collective-permute-start(bf16[2,32,1024]{2,1,0:T(8,128)(2,1)S(1)} %pad_maximum_fusion.refs_0_.refs_3_.refs_1_), channel_id=1, source_target_pairs={{0,16},{1,17},{2,18},{3,19},{4,20},{5,21},{6,22},{7,23},{8,24},{9,... | collective-permute-start | bytes 393224 | tf_op jit(solution)/shard_map/ppermute | solution.py:191
  9.1 6.9 %collective-permute-start.1 = (bf16[2,32,1024]{2,1,0:T(8,128)(2,1)S(1)}, bf16[2,32,1024]{2,1,0:T(8,128)(2,1)S(1)}, u32[]{:S(2)}, u32[]{:S(2)}) collective-permute-start(bf16[2,32,1024]{2,1,0:T(8,128)(2,1)S(1)} %pad_maximum_fusion.refs_0_.refs_3_.refs_1_), channel_id=1, source_target_pairs={{0,17},{1,16},{2,19},{3,18},{4,21},{5,20},{6,23},{7,22},{8,25},{9,... | collective-permute-start | bytes 393224 | tf_op jit(solution)/shard_map/ppermute | solution.py:191
  10.6 4.8 %collective-permute-start.9 = (bf16[32,1024]{1,0:T(8,128)(2,1)S(1)}, bf16[32,1024]{1,0:T(8,128)(2,1)S(1)}, u32[]{:S(2)}, u32[]{:S(2)}) collective-permute-start(bf16[32,1024]{1,0:T(8,128)(2,1)S(1)} %collective-permute-done.2), channel_id=1, source_target_pairs={{0,2},{1,3},{2,0},{3,1},{4,6},{5,7},{6,4},{7,5},{8,10},{9,11},{10,... | collective-permute-start | bytes 196616 | tf_op jit(solution)/shard_map/ppermute | solution.py:196
  11.0 4.8 %collective-permute-start.10 = (bf16[32,1024]{1,0:T(8,128)(2,1)S(1)}, bf16[32,1024]{1,0:T(8,128)(2,1)S(1)}, u32[]{:S(2)}, u32[]{:S(2)}) collective-permute-start(bf16[32,1024]{1,0:T(8,128)(2,1)S(1)} %collective-permute-done.3), channel_id=1, source_target_pairs={{0,2},{1,3},{2,0},{3,1},{4,6},{5,7},{6,4},{7,5},{8,10},{9,11},{10,... | collective-permute-start | bytes 196616 | tf_op jit(solution)/shard_map/ppermute | solution.py:196
  12.7 5.0 %collective-permute-start.5 = (bf16[2,32,1024]{2,1,0:T(8,128)(2,1)S(1)}, bf16[2,32,1024]{2,1,0:T(8,128)(2,1)S(1)}, u32[]{:S(2)}, u32[]{:S(2)}) collective-permute-start(bf16[2,32,1024]{2,1,0:T(8,128)(2,1)S(1)} %pad_maximum_fusion.refs_0_.refs_3_.refs_1_), channel_id=1, source_target_pairs={{0,1},{1,0},{2,3},{3,2},{4,5},{5,4},{6,7},{7,6},{8,9},{9,8},{10,11... | collective-permute-start | bytes 393224 | tf_op jit(solution)/shard_map/ppermute | solution.py:191
  15.4 2.3 %collective-permute-start.7 = (bf16[2,32,1024]{2,1,0:T(8,128)(2,1)S(1)}, bf16[2,32,1024]{2,1,0:T(8,128)(2,1)S(1)}, u32[]{:S(2)}, u32[]{:S(2)}) collective-permute-start(bf16[2,32,1024]{2,1,0:T(8,128)(2,1)S(1)} %pad_maximum_fusion.1.refs_4_.refs_2_), channel_id=1, source_target_pairs={{0,8},{8,0},{16,24},{24,16},{1,9},{9,1},{17,25},{25,17},{2,10},{10... | collective-permute-start | bytes 393224 | tf_op jit(solution)/shard_map/ppermute | solution.py:202
  15.4 2.3 %collective-permute-start.6 = (bf16[2,32,1024]{2,1,0:T(8,128)(2,1)S(1)}, bf16[2,32,1024]{2,1,0:T(8,128)(2,1)S(1)}, u32[]{:S(2)}, u32[]{:S(2)}) collective-permute-start(bf16[2,32,1024]{2,1,0:T(8,128)(2,1)S(1)} %pad_maximum_fusion.refs_0_.refs_3_.refs_1_), channel_id=1, source_target_pairs={{0,8},{8,0},{16,24},{24,16},{1,9},{9,1},{17,25},{25,17},{2,10},{10... | collective-permute-start | bytes 393224 | tf_op jit(solution)/shard_map/ppermute | solution.py:202
  15.9 0.7 %copy-start = (f32[2]{0:T(128)S(1)}, f32[2]{0:T(128)}, u32[]{:S(2)}) copy-start(f32[2]{0:T(128)} %param.5) | copy-start | bytes 28
  15.9 1.8 %collective-permute-start.11 = (bf16[2,32,1024]{2,1,0:T(8,128)(2,1)S(1)}, bf16[2,32,1024]{2,1,0:T(8,128)(2,1)S(1)}, u32[]{:S(2)}, u32[]{:S(2)}) collective-permute-start(bf16[2,32,1024]{2,1,0:T(8,128)(2,1)S(1)} %pad_maximum_fusion.2.refs_7_), channel_id=1, source_target_pairs={{0,8},{8,0},{16,24},{24,16},{1,9},{9,1},{17,25},{25,17},{2,10},{10... | collective-permute-start | bytes 393224 | tf_op jit(solution)/shard_map/ppermute | solution.py:202
  16.0 1.7 %collective-permute-start.8 = (bf16[2,32,1024]{2,1,0:T(8,128)(2,1)S(1)}, bf16[2,32,1024]{2,1,0:T(8,128)(2,1)S(1)}, u32[]{:S(2)}, u32[]{:S(2)}) collective-permute-start(bf16[2,32,1024]{2,1,0:T(8,128)(2,1)S(1)} %collective-permute-done.4.refs_5_.refs_3_), channel_id=1, source_target_pairs={{0,8},{8,0},{16,24},{24,16},{1,9},{9,1},{17,25},{25,17},{2,10},{10... | collective-permute-start | bytes 393224 | tf_op jit(solution)/shard_map/ppermute | solution.py:202
  18.9 7.3 %collective-permute-start.13 = (f16[65,8,128]{2,1,0:T(8,128)(2,1)S(1)}, f16[65,8,128]{2,1,0:T(8,128)(2,1)S(1)}, u32[]{:S(2)}, u32[]{:S(2)}) collective-permute-start(f16[65,8,128]{2,1,0:T(8,128)(2,1)S(1)} %convert_element_type.20), channel_id=1, source_target_pairs={{0,17},{1,16},{2,19},{3,18},{4,21},{5,20},{6,23},{7,22},{8,25},{9,... | collective-permute-start | bytes 399368 | tf_op jit(solution)/shard_map/ppermute | solution.py:236
  21.8 6.4 %collective-permute-start.12 = (f16[65,8,128]{2,1,0:T(8,128)(2,1)S(1)}, f16[65,8,128]{2,1,0:T(8,128)(2,1)S(1)}, u32[]{:S(2)}, u32[]{:S(2)}) collective-permute-start(f16[65,8,128]{2,1,0:T(8,128)(2,1)S(1)} %convert_element_type.18), channel_id=1, source_target_pairs={{0,1},{1,0},{2,3},{3,2},{4,5},{5,4},{6,7},{7,6},{8,9},{9,8},{10,11... | collective-permute-start | bytes 399368 | tf_op jit(solution)/shard_map/ppermute | solution.py:236
  22.4 7.1 %collective-permute-start.14 = (f16[65,8,128]{2,1,0:T(8,128)(2,1)S(1)}, f16[65,8,128]{2,1,0:T(8,128)(2,1)S(1)}, u32[]{:S(2)}, u32[]{:S(2)}) collective-permute-start(f16[65,8,128]{2,1,0:T(8,128)(2,1)S(1)} %convert_element_type.22), channel_id=1, source_target_pairs={{0,16},{1,17},{2,18},{3,19},{4,20},{5,21},{6,22},{7,23},{8,24},{9,... | collective-permute-start | bytes 399368 | tf_op jit(solution)/shard_map/ppermute | solution.py:236

commit v19 on v17

--- a/solution.py
+++ b/solution.py
@@ -226,7 +226,7 @@
         + [jax.ShapeDtypeStruct((2 * rows * width // 1024 + 1, 8, 128), f32)] * len(square),
         flops(len(first), len(late)) + flops(1, len(early + late)),
     )
-    far = sorted(zip(square, parts[1:]), key=lambda item: sum(item[0]))
+    far = sorted(zip(square, parts[1:]), key=lambda item: (sum(item[0]), item[0][0]))
     back = [
         lax.ppermute(part.astype(jnp.float16), both, square_shift(n_row, n_col, -j, -k)) for (j, k), part in far
     ]

time: 29.3 us -> 29.3 us (level)
  transfers between devices with their start and end apart: 15 -> 15, of which waited for: 6 -> 5; matrix products, arithmetic and copies ran while one was open for 4% -> 4% of each run, Pallas kernels for 3% -> 3%
where the time goes in v19:
time: 29.3 us; the launch traced here: 29.2 us
  starting transfers between devices  17.6 us (60%)
  waiting for transfers between devices  6.92 us (24%)
  Pallas kernels  2.74 us (9%)
  other arithmetic  1.04 us (4%)
  between operations  0.72 us (2%)
    ppermute x4, starting transfers between devices, local(): apart[step] = [lax.ppermute(half, 'col', perm) for half in apart[which]]  6.17 us
    ppermute x3, waiting for transfers between devices, local(): lax.ppermute(part.astype(jnp.float16), both, square_shift(n_row, n_col, -...  5.76 us
    ppermute x3, starting transfers between devices, local(): lax.ppermute(own, both, square_shift(n_row, n_col, j, k))  4.84 us
    ppermute x3, starting transfers between devices, local(): lax.ppermute(part.astype(jnp.float16), both, square_shift(n_row, n_col, -...  3.62 us
    pallas_call x3, Pallas kernels, call(): pl.pallas_call(kernel, out_shape=out_shape, in_specs=[vmem] * len(operand...  2.74 us
    ppermute x1, starting transfers between devices, local(): line.append(lax.ppermute(line[which], 'col', perm))  1.9 us
    ppermute x4, starting transfers between devices, pair(): lax.ppermute(block, 'row', inner_shift(n_row, k))  1.09 us
    ppermute x3, waiting for transfers between devices, local(): lax.ppermute(own, both, square_shift(n_row, n_col, j, k))  1.01 us
  transfers between devices with their start and end apart: 15, of which 5 were waited for; matrix products, arithmetic and copies ran while one was open for 4% of the time, Pallas kernels for 3%

profile of v19, /device:TPU:0, one launch (start us, length us, event | category | flops | bytes accessed | tf_op | source)
XLA Modules:
  0.0 29.2 jit_solution(13013081596841686105)
XLA Ops:
  0.6 4.1 %collective-permute-start.2 = (bf16[32,1024]{1,0:T(8,128)(2,1)}, bf16[32,1024]{1,0:T(8,128)(2,1)S(1)}, u32[]{:S(2)}, u32[]{:S(2)}) collective-permute-start(bf16[32,1024]{1,0:T(8,128)(2,1)} %param.3), channel_id=1, source_target_pairs={{0,4},{1,5},{2,6},{3,7},{4,0},{5,1},{6,2},{7,3},{8,12},{9,13},{10,... | collective-permute-start | bytes 196616 | tf_op jit(solution)/shard_map/ppermute | solution.py:191
  4.7 0.1 collective-permute-start.3
  4.8 0.9 %pad_maximum_fusion.refs_0_.refs_3_.refs_1_ = bf16[2,32,1024]{2,1,0:T(8,128)(2,1)S(1)} fusion(bf16[1,32,1024]{2,1,0:T(8,128)(2,1)} %bitcast.7, bf16[1,32,1024]{2,1,0:T(8,128)(2,1)} %bitcast.6), kind=kLoop, calls=%fused_computation | loop fusion | flops 65536 | bytes 262144 | tf_op jit(solution)/shard_map/stack | solution.py:184
  5.7 1.9 %collective-permute-start.4 = (bf16[2,32,1024]{2,1,0:T(8,128)(2,1)S(1)}, bf16[2,32,1024]{2,1,0:T(8,128)(2,1)S(1)}, u32[]{:S(2)}, u32[]{:S(2)}) collective-permute-start(bf16[2,32,1024]{2,1,0:T(8,128)(2,1)S(1)} %pad_maximum_fusion.refs_0_.refs_3_.refs_1_), channel_id=1, source_target_pairs={{0,2},{1,3},{2,0},{3,1},{4,6},{5,7},{6,4},{7,5},{8,10},{9,11},{10,... | collective-permute-start | bytes 393224 | tf_op jit(solution)/shard_map/ppermute | solution.py:194
  7.6 1.5 %collective-permute-start = (bf16[2,32,1024]{2,1,0:T(8,128)(2,1)S(1)}, bf16[2,32,1024]{2,1,0:T(8,128)(2,1)S(1)}, u32[]{:S(2)}, u32[]{:S(2)}) collective-permute-start(bf16[2,32,1024]{2,1,0:T(8,128)(2,1)S(1)} %pad_maximum_fusion.refs_0_.refs_3_.refs_1_), channel_id=1, source_target_pairs={{0,16},{1,17},{2,18},{3,19},{4,20},{5,21},{6,22},{7,23},{8,24},{9,... | collective-permute-start | bytes 393224 | tf_op jit(solution)/shard_map/ppermute | solution.py:186
  9.1 1.4 %collective-permute-start.1 = (bf16[2,32,1024]{2,1,0:T(8,128)(2,1)S(1)}, bf16[2,32,1024]{2,1,0:T(8,128)(2,1)S(1)}, u32[]{:S(2)}, u32[]{:S(2)}) collective-permute-start(bf16[2,32,1024]{2,1,0:T(8,128)(2,1)S(1)} %pad_maximum_fusion.refs_0_.refs_3_.refs_1_), channel_id=1, source_target_pairs={{0,17},{1,16},{2,19},{3,18},{4,21},{5,20},{6,23},{7,22},{8,25},{9,... | collective-permute-start | bytes 393224 | tf_op jit(solution)/shard_map/ppermute | solution.py:186
  10.6 0.0 collective-permute-done.2
  10.6 0.5 %collective-permute-start.9 = (bf16[32,1024]{1,0:T(8,128)(2,1)S(1)}, bf16[32,1024]{1,0:T(8,128)(2,1)S(1)}, u32[]{:S(2)}, u32[]{:S(2)}) collective-permute-start(bf16[32,1024]{1,0:T(8,128)(2,1)S(1)} %collective-permute-done.2), channel_id=1, source_target_pairs={{0,2},{1,3},{2,0},{3,1},{4,6},{5,7},{6,4},{7,5},{8,10},{9,11},{10,... | collective-permute-start | bytes 196616 | tf_op jit(solution)/shard_map/ppermute | solution.py:191
  11.0 0.0 collective-permute-done.3
  11.0 1.5 %collective-permute-start.10 = (bf16[32,1024]{1,0:T(8,128)(2,1)S(1)}, bf16[32,1024]{1,0:T(8,128)(2,1)S(1)}, u32[]{:S(2)}, u32[]{:S(2)}) collective-permute-start(bf16[32,1024]{1,0:T(8,128)(2,1)S(1)} %collective-permute-done.3), channel_id=1, source_target_pairs={{0,2},{1,3},{2,0},{3,1},{4,6},{5,7},{6,4},{7,5},{8,10},{9,11},{10,... | collective-permute-start | bytes 196616 | tf_op jit(solution)/shard_map/ppermute | solution.py:191
  12.6 0.1 collective-permute-done.4.refs_5_.refs_3_
  12.7 1.9 %collective-permute-start.5 = (bf16[2,32,1024]{2,1,0:T(8,128)(2,1)S(1)}, bf16[2,32,1024]{2,1,0:T(8,128)(2,1)S(1)}, u32[]{:S(2)}, u32[]{:S(2)}) collective-permute-start(bf16[2,32,1024]{2,1,0:T(8,128)(2,1)S(1)} %pad_maximum_fusion.refs_0_.refs_3_.refs_1_), channel_id=1, source_target_pairs={{0,1},{1,0},{2,3},{3,2},{4,5},{5,4},{6,7},{7,6},{8,9},{9,8},{10,11... | collective-permute-start | bytes 393224 | tf_op jit(solution)/shard_map/ppermute | solution.py:186
  14.6 0.8 %collective-permute-done.refs_1_ = bf16[2,32,1024]{2,1,0:T(8,128)(2,1)S(1)} collective-permute-done((bf16[2,32,1024]{2,1,0:T(8,128)(2,1)S(1)}, bf16[2,32,1024]{2,1,0:T(8,128)(2,1)S(1)}, u32[]{:S(2)}, u32[]{:S(2)}) %collective-permute-start) | collective-permute-done | bytes 131104 | tf_op jit(solution)/shard_map/ppermute | solution.py:186
  15.4 0.0 collective-permute-start.7
  15.4 0.0 collective-permute-done.9
  15.4 0.5 %collective-permute-start.6 = (bf16[2,32,1024]{2,1,0:T(8,128)(2,1)S(1)}, bf16[2,32,1024]{2,1,0:T(8,128)(2,1)S(1)}, u32[]{:S(2)}, u32[]{:S(2)}) collective-permute-start(bf16[2,32,1024]{2,1,0:T(8,128)(2,1)S(1)} %pad_maximum_fusion.refs_0_.refs_3_.refs_1_), channel_id=1, source_target_pairs={{0,8},{8,0},{16,24},{24,16},{1,9},{9,1},{17,25},{25,17},{2,10},{10... | collective-permute-start | bytes 393224 | tf_op jit(solution)/shard_map/ppermute | solution.py:197
  15.9 0.0 collective-permute-done.10
  15.9 0.0 copy-start
  15.9 0.1 collective-permute-start.11
  16.0 0.0 collective-permute-done.1.refs_2_
  16.0 0.5 %collective-permute-start.8 = (bf16[2,32,1024]{2,1,0:T(8,128)(2,1)S(1)}, bf16[2,32,1024]{2,1,0:T(8,128)(2,1)S(1)}, u32[]{:S(2)}, u32[]{:S(2)}) collective-permute-start(bf16[2,32,1024]{2,1,0:T(8,128)(2,1)S(1)} %collective-permute-done.4.refs_5_.refs_3_), channel_id=1, source_target_pairs={{0,8},{8,0},{16,24},{24,16},{1,9},{9,1},{17,25},{25,17},{2,10},{10... | collective-permute-start | bytes 393224 | tf_op jit(solution)/shard_map/ppermute | solution.py:197
  16.5 0.1 copy-done
  16.6 0.1 broadcast_in_dim.2.factors
  16.6 0.8 %shard_map.50 = (bf16[192,1024]{1,0:T(8,128)(2,1)S(1)}, f32[192,1024]{1,0:T(8,128)S(1)}, f32[192,128]{1,0:T(8,128)S(1)}, f32[32,128]{1,0:T(8,128)S(1)}, f32[8,128]{1,0:T(8,128)S(1)}) custom-call(f32[2,128]{1,0:T(2,128)S(1)} %broadcast_in_dim.2.factors, bf16[2,32,1024]{2,1,0:T(8,128)(2,1)S(1)} %pad_maximum_fusion.refs_0_.refs_3_.refs_1_, ...), custom_call_target="tpu_custom_call" | custom-call | flops 150994944 | bytes 2085888 | tf_op jit(solution)/shard_map/pallas_call | solution.py:165
  17.4 0.2 collective-permute-done.5.refs_0_
  17.7 0.0 collective-permute-done.7.refs_5_
  17.7 0.0 collective-permute-done.8.refs_6_
  17.7 0.0 collective-permute-done.6.refs_4_
  17.7 0.0 collective-permute-done.11.refs_8_
  17.7 1.2 %shard_map.51 = (f32[2,32,1024]{2,1,0:T(8,128)S(1)}, f32[65,8,128]{2,1,0:T(8,128)S(1)}, f32[65,8,128]{2,1,0:T(8,128)S(1)}, f32[65,8,128]{2,1,0:T(8,128)S(1)}) custom-call(f32[2,128]{1,0:T(2,128)S(1)} %broadcast_in_dim.2.factors, bf16[192,1024]{1,0:T(8,128)(2,1)S(1)} %get-tuple-element.17.own, f32[192,1024]{1,0:T(8,128)S(1)} %get-tuple-element.18.acc, ...), custom_call_target="tpu_custom_call" | custom-call | flops 385875968 | bytes 3523584 | tf_op jit(solution)/shard_map/pallas_call | solution.py:165
  18.9 2.9 %collective-permute-start.14 = (f16[65,8,128]{2,1,0:T(8,128)(2,1)S(1)}, f16[65,8,128]{2,1,0:T(8,128)(2,1)S(1)}, u32[]{:S(2)}, u32[]{:S(2)}) collective-permute-start(f16[65,8,128]{2,1,0:T(8,128)(2,1)S(1)} %convert_element_type.22), channel_id=1, source_target_pairs={{0,17},{1,16},{2,19},{3,18},{4,21},{5,20},{6,23},{7,22},{8,25},{9,... | collective-permute-start | bytes 399368 | tf_op jit(solution)/shard_map/ppermute | solution.py:231
  21.8 0.5 %collective-permute-start.13 = (f16[65,8,128]{2,1,0:T(8,128)(2,1)S(1)}, f16[65,8,128]{2,1,0:T(8,128)(2,1)S(1)}, u32[]{:S(2)}, u32[]{:S(2)}) collective-permute-start(f16[65,8,128]{2,1,0:T(8,128)(2,1)S(1)} %convert_element_type.20), channel_id=1, source_target_pairs={{0,16},{1,17},{2,18},{3,19},{4,20},{5,21},{6,22},{7,23},{8,24},{9,... | collective-permute-start | bytes 399368 | tf_op jit(solution)/shard_map/ppermute | solution.py:231
  22.4 0.2 collective-permute-start.12
  22.6 3.3 %collective-permute-done.14 = f16[65,8,128]{2,1,0:T(8,128)(2,1)S(1)} collective-permute-done((f16[65,8,128]{2,1,0:T(8,128)(2,1)S(1)}, f16[65,8,128]{2,1,0:T(8,128)(2,1)S(1)}, u32[]{:S(2)}, u32[]{:S(2)}) %collective-permute-start.14) | collective-permute-done | bytes 133152 | tf_op jit(solution)/shard_map/ppermute | solution.py:231
  25.9 2.4 %collective-permute-done.13 = f16[65,8,128]{2,1,0:T(8,128)(2,1)S(1)} collective-permute-done((f16[65,8,128]{2,1,0:T(8,128)(2,1)S(1)}, f16[65,8,128]{2,1,0:T(8,128)(2,1)S(1)}, u32[]{:S(2)}, u32[]{:S(2)}) %collective-permute-start.13) | collective-permute-done | bytes 133152 | tf_op jit(solution)/shard_map/ppermute | solution.py:231
  28.4 0.0 collective-permute-done.12
  28.4 0.8 %shard_map.52 = (f32[32,1024]{1,0:T(8,128)}, f32[32,1024]{1,0:T(8,128)}) custom-call(f32[2,32,1024]{2,1,0:T(8,128)S(1)} %get-tuple-element.23.own, f32[32,128]{1,0:T(8,128)S(1)} %get-tuple-element.24.down, f32[65,8,128]{2,1,0:T(8,128)S(1)} %convert_element_type.19.refs_0_, f32[65,8,128]{2,1,0:T(8,128)S(1)} %convert_element_type.21.refs_1_, ...), custom_call_target="tpu_custom_call" | custom-call | flops 524288 | bytes 1339392 | tf_op jit(solution)/shard_map/pallas_call | solution.py:165
  (9 shorter events, 0.2 us)
Async XLA Ops:
  0.6 9.9 %collective-permute-start.2 = (bf16[32,1024]{1,0:T(8,128)(2,1)}, bf16[32,1024]{1,0:T(8,128)(2,1)S(1)}, u32[]{:S(2)}, u32[]{:S(2)}) collective-permute-start(bf16[32,1024]{1,0:T(8,128)(2,1)} %param.3), channel_id=1, source_target_pairs={{0,4},{1,5},{2,6},{3,7},{4,0},{5,1},{6,2},{7,3},{8,12},{9,13},{10,... | collective-permute-start | bytes 196616 | tf_op jit(solution)/shard_map/ppermute | solution.py:191
  4.7 6.3 %collective-permute-start.3 = (bf16[32,1024]{1,0:T(8,128)(2,1)}, bf16[32,1024]{1,0:T(8,128)(2,1)S(1)}, u32[]{:S(2)}, u32[]{:S(2)}) collective-permute-start(bf16[32,1024]{1,0:T(8,128)(2,1)} %param.4), channel_id=1, source_target_pairs={{0,4},{1,5},{2,6},{3,7},{4,0},{5,1},{6,2},{7,3},{8,12},{9,13},{10,... | collective-permute-start | bytes 196616 | tf_op jit(solution)/shard_map/ppermute | solution.py:191
  5.7 7.0 %collective-permute-start.4 = (bf16[2,32,1024]{2,1,0:T(8,128)(2,1)S(1)}, bf16[2,32,1024]{2,1,0:T(8,128)(2,1)S(1)}, u32[]{:S(2)}, u32[]{:S(2)}) collective-permute-start(bf16[2,32,1024]{2,1,0:T(8,128)(2,1)S(1)} %pad_maximum_fusion.refs_0_.refs_3_.refs_1_), channel_id=1, source_target_pairs={{0,2},{1,3},{2,0},{3,1},{4,6},{5,7},{6,4},{7,5},{8,10},{9,11},{10,... | collective-permute-start | bytes 393224 | tf_op jit(solution)/shard_map/ppermute | solution.py:194
  7.6 7.8 %collective-permute-start = (bf16[2,32,1024]{2,1,0:T(8,128)(2,1)S(1)}, bf16[2,32,1024]{2,1,0:T(8,128)(2,1)S(1)}, u32[]{:S(2)}, u32[]{:S(2)}) collective-permute-start(bf16[2,32,1024]{2,1,0:T(8,128)(2,1)S(1)} %pad_maximum_fusion.refs_0_.refs_3_.refs_1_), channel_id=1, source_target_pairs={{0,16},{1,17},{2,18},{3,19},{4,20},{5,21},{6,22},{7,23},{8,24},{9,... | collective-permute-start | bytes 393224 | tf_op jit(solution)/shard_map/ppermute | solution.py:186
  9.1 6.9 %collective-permute-start.1 = (bf16[2,32,1024]{2,1,0:T(8,128)(2,1)S(1)}, bf16[2,32,1024]{2,1,0:T(8,128)(2,1)S(1)}, u32[]{:S(2)}, u32[]{:S(2)}) collective-permute-start(bf16[2,32,1024]{2,1,0:T(8,128)(2,1)S(1)} %pad_maximum_fusion.refs_0_.refs_3_.refs_1_), channel_id=1, source_target_pairs={{0,17},{1,16},{2,19},{3,18},{4,21},{5,20},{6,23},{7,22},{8,25},{9,... | collective-permute-start | bytes 393224 | tf_op jit(solution)/shard_map/ppermute | solution.py:186
  10.6 4.8 %collective-permute-start.9 = (bf16[32,1024]{1,0:T(8,128)(2,1)S(1)}, bf16[32,1024]{1,0:T(8,128)(2,1)S(1)}, u32[]{:S(2)}, u32[]{:S(2)}) collective-permute-start(bf16[32,1024]{1,0:T(8,128)(2,1)S(1)} %collective-permute-done.2), channel_id=1, source_target_pairs={{0,2},{1,3},{2,0},{3,1},{4,6},{5,7},{6,4},{7,5},{8,10},{9,11},{10,... | collective-permute-start | bytes 196616 | tf_op jit(solution)/shard_map/ppermute | solution.py:191
  11.0 4.8 %collective-permute-start.10 = (bf16[32,1024]{1,0:T(8,128)(2,1)S(1)}, bf16[32,1024]{1,0:T(8,128)(2,1)S(1)}, u32[]{:S(2)}, u32[]{:S(2)}) collective-permute-start(bf16[32,1024]{1,0:T(8,128)(2,1)S(1)} %collective-permute-done.3), channel_id=1, source_target_pairs={{0,2},{1,3},{2,0},{3,1},{4,6},{5,7},{6,4},{7,5},{8,10},{9,11},{10,... | collective-permute-start | bytes 196616 | tf_op jit(solution)/shard_map/ppermute | solution.py:191
  12.7 5.0 %collective-permute-start.5 = (bf16[2,32,1024]{2,1,0:T(8,128)(2,1)S(1)}, bf16[2,32,1024]{2,1,0:T(8,128)(2,1)S(1)}, u32[]{:S(2)}, u32[]{:S(2)}) collective-permute-start(bf16[2,32,1024]{2,1,0:T(8,128)(2,1)S(1)} %pad_maximum_fusion.refs_0_.refs_3_.refs_1_), channel_id=1, source_target_pairs={{0,1},{1,0},{2,3},{3,2},{4,5},{5,4},{6,7},{7,6},{8,9},{9,8},{10,11... | collective-permute-start | bytes 393224 | tf_op jit(solution)/shard_map/ppermute | solution.py:186
  15.4 2.3 %collective-permute-start.7 = (bf16[2,32,1024]{2,1,0:T(8,128)(2,1)S(1)}, bf16[2,32,1024]{2,1,0:T(8,128)(2,1)S(1)}, u32[]{:S(2)}, u32[]{:S(2)}) collective-permute-start(bf16[2,32,1024]{2,1,0:T(8,128)(2,1)S(1)} %pad_maximum_fusion.1.refs_4_.refs_2_), channel_id=1, source_target_pairs={{0,8},{8,0},{16,24},{24,16},{1,9},{9,1},{17,25},{25,17},{2,10},{10... | collective-permute-start | bytes 393224 | tf_op jit(solution)/shard_map/ppermute | solution.py:197
  15.4 2.3 %collective-permute-start.6 = (bf16[2,32,1024]{2,1,0:T(8,128)(2,1)S(1)}, bf16[2,32,1024]{2,1,0:T(8,128)(2,1)S(1)}, u32[]{:S(2)}, u32[]{:S(2)}) collective-permute-start(bf16[2,32,1024]{2,1,0:T(8,128)(2,1)S(1)} %pad_maximum_fusion.refs_0_.refs_3_.refs_1_), channel_id=1, source_target_pairs={{0,8},{8,0},{16,24},{24,16},{1,9},{9,1},{17,25},{25,17},{2,10},{10... | collective-permute-start | bytes 393224 | tf_op jit(solution)/shard_map/ppermute | solution.py:197
  15.9 0.7 %copy-start = (f32[2]{0:T(128)S(1)}, f32[2]{0:T(128)}, u32[]{:S(2)}) copy-start(f32[2]{0:T(128)} %param.5) | copy-start | bytes 28
  15.9 1.8 %collective-permute-start.11 = (bf16[2,32,1024]{2,1,0:T(8,128)(2,1)S(1)}, bf16[2,32,1024]{2,1,0:T(8,128)(2,1)S(1)}, u32[]{:S(2)}, u32[]{:S(2)}) collective-permute-start(bf16[2,32,1024]{2,1,0:T(8,128)(2,1)S(1)} %pad_maximum_fusion.2.refs_7_), channel_id=1, source_target_pairs={{0,8},{8,0},{16,24},{24,16},{1,9},{9,1},{17,25},{25,17},{2,10},{10... | collective-permute-start | bytes 393224 | tf_op jit(solution)/shard_map/ppermute | solution.py:197
  16.0 1.7 %collective-permute-start.8 = (bf16[2,32,1024]{2,1,0:T(8,128)(2,1)S(1)}, bf16[2,32,1024]{2,1,0:T(8,128)(2,1)S(1)}, u32[]{:S(2)}, u32[]{:S(2)}) collective-permute-start(bf16[2,32,1024]{2,1,0:T(8,128)(2,1)S(1)} %collective-permute-done.4.refs_5_.refs_3_), channel_id=1, source_target_pairs={{0,8},{8,0},{16,24},{24,16},{1,9},{9,1},{17,25},{25,17},{2,10},{10... | collective-permute-start | bytes 393224 | tf_op jit(solution)/shard_map/ppermute | solution.py:197
  18.9 7.0 %collective-permute-start.14 = (f16[65,8,128]{2,1,0:T(8,128)(2,1)S(1)}, f16[65,8,128]{2,1,0:T(8,128)(2,1)S(1)}, u32[]{:S(2)}, u32[]{:S(2)}) collective-permute-start(f16[65,8,128]{2,1,0:T(8,128)(2,1)S(1)} %convert_element_type.22), channel_id=1, source_target_pairs={{0,17},{1,16},{2,19},{3,18},{4,21},{5,20},{6,23},{7,22},{8,25},{9,... | collective-permute-start | bytes 399368 | tf_op jit(solution)/shard_map/ppermute | solution.py:231
  21.8 6.5 %collective-permute-start.13 = (f16[65,8,128]{2,1,0:T(8,128)(2,1)S(1)}, f16[65,8,128]{2,1,0:T(8,128)(2,1)S(1)}, u32[]{:S(2)}, u32[]{:S(2)}) collective-permute-start(f16[65,8,128]{2,1,0:T(8,128)(2,1)S(1)} %convert_element_type.20), channel_id=1, source_target_pairs={{0,16},{1,17},{2,18},{3,19},{4,20},{5,21},{6,22},{7,23},{8,24},{9,... | collective-permute-start | bytes 399368 | tf_op jit(solution)/shard_map/ppermute | solution.py:231
  22.4 6.0 %collective-permute-start.12 = (f16[65,8,128]{2,1,0:T(8,128)(2,1)S(1)}, f16[65,8,128]{2,1,0:T(8,128)(2,1)S(1)}, u32[]{:S(2)}, u32[]{:S(2)}) collective-permute-start(f16[65,8,128]{2,1,0:T(8,128)(2,1)S(1)} %convert_element_type.18), channel_id=1, source_target_pairs={{0,1},{1,0},{2,3},{3,2},{4,5},{5,4},{6,7},{7,6},{8,9},{9,8},{10,11... | collective-permute-start | bytes 399368 | tf_op jit(solution)/shard_map/ppermute | solution.py:231

commit v20 on v17

--- a/solution.py
+++ b/solution.py
@@ -56,7 +56,7 @@
 
 
 def join(refs):
-    return jnp.concatenate([ref[s] for s in range(2) for ref in refs], axis=0)
+    return jnp.concatenate([ref[i] for s in range(2) for ref in refs for i in range(s, ref.shape[0], 2)], axis=0)
 
 
 def weigh(rows, keys, factors):
@@ -70,7 +70,7 @@
 
 
 def tiles(width):
-    step = 256 if width % 256 == 0 else width
+    step = 512 if width % 512 == 0 else width
     return [slice(i, i + step) for i in range(0, width, step)]
 
 

time: 29.3 us -> 29.3 us (level)
  no operation moved by 1% of the time
where the time goes in v20:
time: 29.3 us; the launch traced here: 29.1 us
  starting transfers between devices  17.6 us (60%)
  waiting for transfers between devices  6.89 us (24%)
  Pallas kernels  2.72 us (9%)
  other arithmetic  1.04 us (4%)
  between operations  0.71 us (2%)
    ppermute x4, starting transfers between devices, local(): apart[step] = [lax.ppermute(half, 'col', perm) for half in apart[which]]  6.17 us
    ppermute x3, waiting for transfers between devices, local(): lax.ppermute(part.astype(jnp.float16), both, square_shift(n_row, n_col, -...  5.73 us
    ppermute x3, starting transfers between devices, local(): lax.ppermute(own, both, square_shift(n_row, n_col, j, k))  4.84 us
    ppermute x3, starting transfers between devices, local(): lax.ppermute(part.astype(jnp.float16), both, square_shift(n_row, n_col, -...  3.62 us
    pallas_call x3, Pallas kernels, call(): pl.pallas_call(kernel, out_shape=out_shape, in_specs=[vmem] * len(operand...  2.72 us
    ppermute x1, starting transfers between devices, local(): line.append(lax.ppermute(line[which], 'col', perm))  1.9 us
    ppermute x4, starting transfers between devices, pair(): lax.ppermute(block, 'row', inner_shift(n_row, k))  1.09 us
    ppermute x3, waiting for transfers between devices, local(): lax.ppermute(own, both, square_shift(n_row, n_col, j, k))  1.01 us
  transfers between devices with their start and end apart: 15, of which 6 were waited for; matrix products, arithmetic and copies ran while one was open for 4% of the time, Pallas kernels for 3%

profile of v20, /device:TPU:0, one launch (start us, length us, event | category | flops | bytes accessed | tf_op | source)
XLA Modules:
  0.0 29.1 jit_solution(2827997045774720055)
XLA Ops:
  0.6 4.1 %collective-permute-start.2 = (bf16[32,1024]{1,0:T(8,128)(2,1)}, bf16[32,1024]{1,0:T(8,128)(2,1)S(1)}, u32[]{:S(2)}, u32[]{:S(2)}) collective-permute-start(bf16[32,1024]{1,0:T(8,128)(2,1)} %param.3), channel_id=1, source_target_pairs={{0,4},{1,5},{2,6},{3,7},{4,0},{5,1},{6,2},{7,3},{8,12},{9,13},{10,... | collective-permute-start | bytes 196616 | tf_op jit(solution)/shard_map/ppermute | solution.py:191
  4.7 0.1 collective-permute-start.3
  4.8 0.9 %pad_maximum_fusion.refs_0_.refs_3_.refs_1_ = bf16[2,32,1024]{2,1,0:T(8,128)(2,1)S(1)} fusion(bf16[1,32,1024]{2,1,0:T(8,128)(2,1)} %bitcast.7, bf16[1,32,1024]{2,1,0:T(8,128)(2,1)} %bitcast.6), kind=kLoop, calls=%fused_computation | loop fusion | flops 65536 | bytes 262144 | tf_op jit(solution)/shard_map/stack | solution.py:184
  5.7 1.9 %collective-permute-start.4 = (bf16[2,32,1024]{2,1,0:T(8,128)(2,1)S(1)}, bf16[2,32,1024]{2,1,0:T(8,128)(2,1)S(1)}, u32[]{:S(2)}, u32[]{:S(2)}) collective-permute-start(bf16[2,32,1024]{2,1,0:T(8,128)(2,1)S(1)} %pad_maximum_fusion.refs_0_.refs_3_.refs_1_), channel_id=1, source_target_pairs={{0,2},{1,3},{2,0},{3,1},{4,6},{5,7},{6,4},{7,5},{8,10},{9,11},{10,... | collective-permute-start | bytes 393224 | tf_op jit(solution)/shard_map/ppermute | solution.py:194
  7.6 1.5 %collective-permute-start = (bf16[2,32,1024]{2,1,0:T(8,128)(2,1)S(1)}, bf16[2,32,1024]{2,1,0:T(8,128)(2,1)S(1)}, u32[]{:S(2)}, u32[]{:S(2)}) collective-permute-start(bf16[2,32,1024]{2,1,0:T(8,128)(2,1)S(1)} %pad_maximum_fusion.refs_0_.refs_3_.refs_1_), channel_id=1, source_target_pairs={{0,16},{1,17},{2,18},{3,19},{4,20},{5,21},{6,22},{7,23},{8,24},{9,... | collective-permute-start | bytes 393224 | tf_op jit(solution)/shard_map/ppermute | solution.py:186
  9.1 1.4 %collective-permute-start.1 = (bf16[2,32,1024]{2,1,0:T(8,128)(2,1)S(1)}, bf16[2,32,1024]{2,1,0:T(8,128)(2,1)S(1)}, u32[]{:S(2)}, u32[]{:S(2)}) collective-permute-start(bf16[2,32,1024]{2,1,0:T(8,128)(2,1)S(1)} %pad_maximum_fusion.refs_0_.refs_3_.refs_1_), channel_id=1, source_target_pairs={{0,17},{1,16},{2,19},{3,18},{4,21},{5,20},{6,23},{7,22},{8,25},{9,... | collective-permute-start | bytes 393224 | tf_op jit(solution)/shard_map/ppermute | solution.py:186
  10.6 0.0 collective-permute-done.2
  10.6 0.5 %collective-permute-start.9 = (bf16[32,1024]{1,0:T(8,128)(2,1)S(1)}, bf16[32,1024]{1,0:T(8,128)(2,1)S(1)}, u32[]{:S(2)}, u32[]{:S(2)}) collective-permute-start(bf16[32,1024]{1,0:T(8,128)(2,1)S(1)} %collective-permute-done.2), channel_id=1, source_target_pairs={{0,2},{1,3},{2,0},{3,1},{4,6},{5,7},{6,4},{7,5},{8,10},{9,11},{10,... | collective-permute-start | bytes 196616 | tf_op jit(solution)/shard_map/ppermute | solution.py:191
  11.0 0.0 collective-permute-done.3
  11.0 1.5 %collective-permute-start.10 = (bf16[32,1024]{1,0:T(8,128)(2,1)S(1)}, bf16[32,1024]{1,0:T(8,128)(2,1)S(1)}, u32[]{:S(2)}, u32[]{:S(2)}) collective-permute-start(bf16[32,1024]{1,0:T(8,128)(2,1)S(1)} %collective-permute-done.3), channel_id=1, source_target_pairs={{0,2},{1,3},{2,0},{3,1},{4,6},{5,7},{6,4},{7,5},{8,10},{9,11},{10,... | collective-permute-start | bytes 196616 | tf_op jit(solution)/shard_map/ppermute | solution.py:191
  12.6 0.1 collective-permute-done.4.refs_5_.refs_3_
  12.7 1.9 %collective-permute-start.5 = (bf16[2,32,1024]{2,1,0:T(8,128)(2,1)S(1)}, bf16[2,32,1024]{2,1,0:T(8,128)(2,1)S(1)}, u32[]{:S(2)}, u32[]{:S(2)}) collective-permute-start(bf16[2,32,1024]{2,1,0:T(8,128)(2,1)S(1)} %pad_maximum_fusion.refs_0_.refs_3_.refs_1_), channel_id=1, source_target_pairs={{0,1},{1,0},{2,3},{3,2},{4,5},{5,4},{6,7},{7,6},{8,9},{9,8},{10,11... | collective-permute-start | bytes 393224 | tf_op jit(solution)/shard_map/ppermute | solution.py:186
  14.6 0.8 %collective-permute-done.refs_1_ = bf16[2,32,1024]{2,1,0:T(8,128)(2,1)S(1)} collective-permute-done((bf16[2,32,1024]{2,1,0:T(8,128)(2,1)S(1)}, bf16[2,32,1024]{2,1,0:T(8,128)(2,1)S(1)}, u32[]{:S(2)}, u32[]{:S(2)}) %collective-permute-start) | collective-permute-done | bytes 131104 | tf_op jit(solution)/shard_map/ppermute | solution.py:186
  15.4 0.0 collective-permute-start.7
  15.4 0.0 collective-permute-done.9
  15.4 0.5 %collective-permute-start.6 = (bf16[2,32,1024]{2,1,0:T(8,128)(2,1)S(1)}, bf16[2,32,1024]{2,1,0:T(8,128)(2,1)S(1)}, u32[]{:S(2)}, u32[]{:S(2)}) collective-permute-start(bf16[2,32,1024]{2,1,0:T(8,128)(2,1)S(1)} %pad_maximum_fusion.refs_0_.refs_3_.refs_1_), channel_id=1, source_target_pairs={{0,8},{8,0},{16,24},{24,16},{1,9},{9,1},{17,25},{25,17},{2,10},{10... | collective-permute-start | bytes 393224 | tf_op jit(solution)/shard_map/ppermute | solution.py:197
  15.9 0.0 collective-permute-done.10
  15.9 0.0 copy-start
  15.9 0.1 collective-permute-start.11
  16.0 0.0 collective-permute-done.1.refs_2_
  16.0 0.5 %collective-permute-start.8 = (bf16[2,32,1024]{2,1,0:T(8,128)(2,1)S(1)}, bf16[2,32,1024]{2,1,0:T(8,128)(2,1)S(1)}, u32[]{:S(2)}, u32[]{:S(2)}) collective-permute-start(bf16[2,32,1024]{2,1,0:T(8,128)(2,1)S(1)} %collective-permute-done.4.refs_5_.refs_3_), channel_id=1, source_target_pairs={{0,8},{8,0},{16,24},{24,16},{1,9},{9,1},{17,25},{25,17},{2,10},{10... | collective-permute-start | bytes 393224 | tf_op jit(solution)/shard_map/ppermute | solution.py:197
  16.5 0.1 copy-done
  16.6 0.1 broadcast_in_dim.2.factors
  16.6 0.8 %shard_map.50 = (bf16[192,1024]{1,0:T(8,128)(2,1)S(1)}, f32[192,1024]{1,0:T(8,128)S(1)}, f32[192,128]{1,0:T(8,128)S(1)}, f32[32,128]{1,0:T(8,128)S(1)}, f32[8,128]{1,0:T(8,128)S(1)}) custom-call(f32[2,128]{1,0:T(2,128)S(1)} %broadcast_in_dim.2.factors, bf16[2,32,1024]{2,1,0:T(8,128)(2,1)S(1)} %pad_maximum_fusion.refs_0_.refs_3_.refs_1_, ...), custom_call_target="tpu_custom_call" | custom-call | flops 150994944 | bytes 2085888 | tf_op jit(solution)/shard_map/pallas_call | solution.py:165
  17.4 0.2 collective-permute-done.5.refs_0_
  17.7 0.0 collective-permute-done.7.refs_5_
  17.7 0.0 collective-permute-done.8.refs_6_
  17.7 0.0 collective-permute-done.6.refs_4_
  17.7 0.0 collective-permute-done.11.refs_8_
  17.7 1.1 %shard_map.51 = (f32[2,32,1024]{2,1,0:T(8,128)S(1)}, f32[65,8,128]{2,1,0:T(8,128)S(1)}, f32[65,8,128]{2,1,0:T(8,128)S(1)}, f32[65,8,128]{2,1,0:T(8,128)S(1)}) custom-call(f32[2,128]{1,0:T(2,128)S(1)} %broadcast_in_dim.2.factors, bf16[192,1024]{1,0:T(8,128)(2,1)S(1)} %get-tuple-element.17.own, f32[192,1024]{1,0:T(8,128)S(1)} %get-tuple-element.18.acc, ...), custom_call_target="tpu_custom_call" | custom-call | flops 385875968 | bytes 3523584 | tf_op jit(solution)/shard_map/pallas_call | solution.py:165
  18.9 2.9 %collective-permute-start.14 = (f16[65,8,128]{2,1,0:T(8,128)(2,1)S(1)}, f16[65,8,128]{2,1,0:T(8,128)(2,1)S(1)}, u32[]{:S(2)}, u32[]{:S(2)}) collective-permute-start(f16[65,8,128]{2,1,0:T(8,128)(2,1)S(1)} %convert_element_type.22), channel_id=1, source_target_pairs={{0,17},{1,16},{2,19},{3,18},{4,21},{5,20},{6,23},{7,22},{8,25},{9,... | collective-permute-start | bytes 399368 | tf_op jit(solution)/shard_map/ppermute | solution.py:231
  21.8 0.5 %collective-permute-start.13 = (f16[65,8,128]{2,1,0:T(8,128)(2,1)S(1)}, f16[65,8,128]{2,1,0:T(8,128)(2,1)S(1)}, u32[]{:S(2)}, u32[]{:S(2)}) collective-permute-start(f16[65,8,128]{2,1,0:T(8,128)(2,1)S(1)} %convert_element_type.20), channel_id=1, source_target_pairs={{0,1},{1,0},{2,3},{3,2},{4,5},{5,4},{6,7},{7,6},{8,9},{9,8},{10,11... | collective-permute-start | bytes 399368 | tf_op jit(solution)/shard_map/ppermute | solution.py:231
  22.4 0.2 collective-permute-start.12
  22.5 3.7 %collective-permute-done.14 = f16[65,8,128]{2,1,0:T(8,128)(2,1)S(1)} collective-permute-done((f16[65,8,128]{2,1,0:T(8,128)(2,1)S(1)}, f16[65,8,128]{2,1,0:T(8,128)(2,1)S(1)}, u32[]{:S(2)}, u32[]{:S(2)}) %collective-permute-start.14) | collective-permute-done | bytes 133152 | tf_op jit(solution)/shard_map/ppermute | solution.py:231
  26.3 1.9 %collective-permute-done.13 = f16[65,8,128]{2,1,0:T(8,128)(2,1)S(1)} collective-permute-done((f16[65,8,128]{2,1,0:T(8,128)(2,1)S(1)}, f16[65,8,128]{2,1,0:T(8,128)(2,1)S(1)}, u32[]{:S(2)}, u32[]{:S(2)}) %collective-permute-start.13) | collective-permute-done | bytes 133152 | tf_op jit(solution)/shard_map/ppermute | solution.py:231
  28.2 0.1 collective-permute-done.12
  28.3 0.8 %shard_map.52 = (f32[32,1024]{1,0:T(8,128)}, f32[32,1024]{1,0:T(8,128)}) custom-call(f32[2,32,1024]{2,1,0:T(8,128)S(1)} %get-tuple-element.23.own, f32[32,128]{1,0:T(8,128)S(1)} %get-tuple-element.24.down, f32[65,8,128]{2,1,0:T(8,128)S(1)} %convert_element_type.19.refs_0_, f32[65,8,128]{2,1,0:T(8,128)S(1)} %convert_element_type.21.refs_1_, ...), custom_call_target="tpu_custom_call" | custom-call | flops 524288 | bytes 1339392 | tf_op jit(solution)/shard_map/pallas_call | solution.py:165
  (9 shorter events, 0.2 us)
Async XLA Ops:
  0.6 9.9 %collective-permute-start.2 = (bf16[32,1024]{1,0:T(8,128)(2,1)}, bf16[32,1024]{1,0:T(8,128)(2,1)S(1)}, u32[]{:S(2)}, u32[]{:S(2)}) collective-permute-start(bf16[32,1024]{1,0:T(8,128)(2,1)} %param.3), channel_id=1, source_target_pairs={{0,4},{1,5},{2,6},{3,7},{4,0},{5,1},{6,2},{7,3},{8,12},{9,13},{10,... | collective-permute-start | bytes 196616 | tf_op jit(solution)/shard_map/ppermute | solution.py:191
  4.7 6.3 %collective-permute-start.3 = (bf16[32,1024]{1,0:T(8,128)(2,1)}, bf16[32,1024]{1,0:T(8,128)(2,1)S(1)}, u32[]{:S(2)}, u32[]{:S(2)}) collective-permute-start(bf16[32,1024]{1,0:T(8,128)(2,1)} %param.4), channel_id=1, source_target_pairs={{0,4},{1,5},{2,6},{3,7},{4,0},{5,1},{6,2},{7,3},{8,12},{9,13},{10,... | collective-permute-start | bytes 196616 | tf_op jit(solution)/shard_map/ppermute | solution.py:191
  5.7 7.0 %collective-permute-start.4 = (bf16[2,32,1024]{2,1,0:T(8,128)(2,1)S(1)}, bf16[2,32,1024]{2,1,0:T(8,128)(2,1)S(1)}, u32[]{:S(2)}, u32[]{:S(2)}) collective-permute-start(bf16[2,32,1024]{2,1,0:T(8,128)(2,1)S(1)} %pad_maximum_fusion.refs_0_.refs_3_.refs_1_), channel_id=1, source_target_pairs={{0,2},{1,3},{2,0},{3,1},{4,6},{5,7},{6,4},{7,5},{8,10},{9,11},{10,... | collective-permute-start | bytes 393224 | tf_op jit(solution)/shard_map/ppermute | solution.py:194
  7.6 7.8 %collective-permute-start = (bf16[2,32,1024]{2,1,0:T(8,128)(2,1)S(1)}, bf16[2,32,1024]{2,1,0:T(8,128)(2,1)S(1)}, u32[]{:S(2)}, u32[]{:S(2)}) collective-permute-start(bf16[2,32,1024]{2,1,0:T(8,128)(2,1)S(1)} %pad_maximum_fusion.refs_0_.refs_3_.refs_1_), channel_id=1, source_target_pairs={{0,16},{1,17},{2,18},{3,19},{4,20},{5,21},{6,22},{7,23},{8,24},{9,... | collective-permute-start | bytes 393224 | tf_op jit(solution)/shard_map/ppermute | solution.py:186
  9.1 6.9 %collective-permute-start.1 = (bf16[2,32,1024]{2,1,0:T(8,128)(2,1)S(1)}, bf16[2,32,1024]{2,1,0:T(8,128)(2,1)S(1)}, u32[]{:S(2)}, u32[]{:S(2)}) collective-permute-start(bf16[2,32,1024]{2,1,0:T(8,128)(2,1)S(1)} %pad_maximum_fusion.refs_0_.refs_3_.refs_1_), channel_id=1, source_target_pairs={{0,17},{1,16},{2,19},{3,18},{4,21},{5,20},{6,23},{7,22},{8,25},{9,... | collective-permute-start | bytes 393224 | tf_op jit(solution)/shard_map/ppermute | solution.py:186
  10.6 4.8 %collective-permute-start.9 = (bf16[32,1024]{1,0:T(8,128)(2,1)S(1)}, bf16[32,1024]{1,0:T(8,128)(2,1)S(1)}, u32[]{:S(2)}, u32[]{:S(2)}) collective-permute-start(bf16[32,1024]{1,0:T(8,128)(2,1)S(1)} %collective-permute-done.2), channel_id=1, source_target_pairs={{0,2},{1,3},{2,0},{3,1},{4,6},{5,7},{6,4},{7,5},{8,10},{9,11},{10,... | collective-permute-start | bytes 196616 | tf_op jit(solution)/shard_map/ppermute | solution.py:191
  11.0 4.8 %collective-permute-start.10 = (bf16[32,1024]{1,0:T(8,128)(2,1)S(1)}, bf16[32,1024]{1,0:T(8,128)(2,1)S(1)}, u32[]{:S(2)}, u32[]{:S(2)}) collective-permute-start(bf16[32,1024]{1,0:T(8,128)(2,1)S(1)} %collective-permute-done.3), channel_id=1, source_target_pairs={{0,2},{1,3},{2,0},{3,1},{4,6},{5,7},{6,4},{7,5},{8,10},{9,11},{10,... | collective-permute-start | bytes 196616 | tf_op jit(solution)/shard_map/ppermute | solution.py:191
  12.7 5.0 %collective-permute-start.5 = (bf16[2,32,1024]{2,1,0:T(8,128)(2,1)S(1)}, bf16[2,32,1024]{2,1,0:T(8,128)(2,1)S(1)}, u32[]{:S(2)}, u32[]{:S(2)}) collective-permute-start(bf16[2,32,1024]{2,1,0:T(8,128)(2,1)S(1)} %pad_maximum_fusion.refs_0_.refs_3_.refs_1_), channel_id=1, source_target_pairs={{0,1},{1,0},{2,3},{3,2},{4,5},{5,4},{6,7},{7,6},{8,9},{9,8},{10,11... | collective-permute-start | bytes 393224 | tf_op jit(solution)/shard_map/ppermute | solution.py:186
  15.4 2.3 %collective-permute-start.7 = (bf16[2,32,1024]{2,1,0:T(8,128)(2,1)S(1)}, bf16[2,32,1024]{2,1,0:T(8,128)(2,1)S(1)}, u32[]{:S(2)}, u32[]{:S(2)}) collective-permute-start(bf16[2,32,1024]{2,1,0:T(8,128)(2,1)S(1)} %pad_maximum_fusion.1.refs_4_.refs_2_), channel_id=1, source_target_pairs={{0,8},{8,0},{16,24},{24,16},{1,9},{9,1},{17,25},{25,17},{2,10},{10... | collective-permute-start | bytes 393224 | tf_op jit(solution)/shard_map/ppermute | solution.py:197
  15.4 2.3 %collective-permute-start.6 = (bf16[2,32,1024]{2,1,0:T(8,128)(2,1)S(1)}, bf16[2,32,1024]{2,1,0:T(8,128)(2,1)S(1)}, u32[]{:S(2)}, u32[]{:S(2)}) collective-permute-start(bf16[2,32,1024]{2,1,0:T(8,128)(2,1)S(1)} %pad_maximum_fusion.refs_0_.refs_3_.refs_1_), channel_id=1, source_target_pairs={{0,8},{8,0},{16,24},{24,16},{1,9},{9,1},{17,25},{25,17},{2,10},{10... | collective-permute-start | bytes 393224 | tf_op jit(solution)/shard_map/ppermute | solution.py:197
  15.9 0.7 %copy-start = (f32[2]{0:T(128)S(1)}, f32[2]{0:T(128)}, u32[]{:S(2)}) copy-start(f32[2]{0:T(128)} %param.5) | copy-start | bytes 28
  15.9 1.8 %collective-permute-start.11 = (bf16[2,32,1024]{2,1,0:T(8,128)(2,1)S(1)}, bf16[2,32,1024]{2,1,0:T(8,128)(2,1)S(1)}, u32[]{:S(2)}, u32[]{:S(2)}) collective-permute-start(bf16[2,32,1024]{2,1,0:T(8,128)(2,1)S(1)} %pad_maximum_fusion.2.refs_7_), channel_id=1, source_target_pairs={{0,8},{8,0},{16,24},{24,16},{1,9},{9,1},{17,25},{25,17},{2,10},{10... | collective-permute-start | bytes 393224 | tf_op jit(solution)/shard_map/ppermute | solution.py:197
  16.0 1.7 %collective-permute-start.8 = (bf16[2,32,1024]{2,1,0:T(8,128)(2,1)S(1)}, bf16[2,32,1024]{2,1,0:T(8,128)(2,1)S(1)}, u32[]{:S(2)}, u32[]{:S(2)}) collective-permute-start(bf16[2,32,1024]{2,1,0:T(8,128)(2,1)S(1)} %collective-permute-done.4.refs_5_.refs_3_), channel_id=1, source_target_pairs={{0,8},{8,0},{16,24},{24,16},{1,9},{9,1},{17,25},{25,17},{2,10},{10... | collective-permute-start | bytes 393224 | tf_op jit(solution)/shard_map/ppermute | solution.py:197
  18.9 7.3 %collective-permute-start.14 = (f16[65,8,128]{2,1,0:T(8,128)(2,1)S(1)}, f16[65,8,128]{2,1,0:T(8,128)(2,1)S(1)}, u32[]{:S(2)}, u32[]{:S(2)}) collective-permute-start(f16[65,8,128]{2,1,0:T(8,128)(2,1)S(1)} %convert_element_type.22), channel_id=1, source_target_pairs={{0,17},{1,16},{2,19},{3,18},{4,21},{5,20},{6,23},{7,22},{8,25},{9,... | collective-permute-start | bytes 399368 | tf_op jit(solution)/shard_map/ppermute | solution.py:231
  21.8 6.4 %collective-permute-start.13 = (f16[65,8,128]{2,1,0:T(8,128)(2,1)S(1)}, f16[65,8,128]{2,1,0:T(8,128)(2,1)S(1)}, u32[]{:S(2)}, u32[]{:S(2)}) collective-permute-start(f16[65,8,128]{2,1,0:T(8,128)(2,1)S(1)} %convert_element_type.20), channel_id=1, source_target_pairs={{0,1},{1,0},{2,3},{3,2},{4,5},{5,4},{6,7},{7,6},{8,9},{9,8},{10,11... | collective-permute-start | bytes 399368 | tf_op jit(solution)/shard_map/ppermute | solution.py:231
  22.4 5.9 %collective-permute-start.12 = (f16[65,8,128]{2,1,0:T(8,128)(2,1)S(1)}, f16[65,8,128]{2,1,0:T(8,128)(2,1)S(1)}, u32[]{:S(2)}, u32[]{:S(2)}) collective-permute-start(f16[65,8,128]{2,1,0:T(8,128)(2,1)S(1)} %convert_element_type.18), channel_id=1, source_target_pairs={{0,16},{1,17},{2,18},{3,19},{4,20},{5,21},{6,22},{7,23},{8,24},{9,... | collective-permute-start | bytes 399368 | tf_op jit(solution)/shard_map/ppermute | solution.py:231

commit v21 on v17

--- a/solution.py
+++ b/solution.py
@@ -180,7 +180,7 @@
     factors = jnp.broadcast_to((loss_weights * (1.0 / math.sqrt(width * batch)))[:, None], (2, 128))
     both = ("row", "col")
     square = [(j, k) for j in range(halves(n_row)[0]) for k in range(halves(n_col)[1])]
-    square = square[2:] + square[1:2]
+    square = square[1:2] + square[3:] + square[2:3]
     own = jnp.stack([images, texts])
 
     mine = [own] + [lax.ppermute(own, both, square_shift(n_row, n_col, j, k)) for j, k in square]

time: 29.3 us -> 29.7 us (1.014)
  waiting for transfers between devices: 6.89 us -> 7.59 us
  starting transfers between devices: 17.6 us -> 17.3 us
    ppermute x3, waiting for transfers between devices: 1.01 us -> 1.73 us  [local(): lax.ppermute(own, both, square_shift(n_row, n_col, j, k))]
    ppermute x4, waiting for transfers between devices: 0.05 us -> 0.66 us  [local(): apart[step] = [lax.ppermute(half, 'col', perm) for half in apart[which]]]
    ppermute x3, waiting for transfers between devices: 5.73 us -> 5.16 us  [local(): lax.ppermute(part.astype(jnp.float16), both, square_shift(n_row, n_col, -...]
    ppermute x4, starting transfers between devices: 1.09 us -> 0.62 us  [pair(): lax.ppermute(block, 'row', inner_shift(n_row, k))]
where the time goes in v21:
time: 29.7 us; the launch traced here: 29.5 us
  starting transfers between devices  17.3 us (58%)
  waiting for transfers between devices  7.59 us (26%)
  Pallas kernels  2.74 us (9%)
  other arithmetic  1.04 us (4%)
  between operations  0.73 us (2%)
    ppermute x4, starting transfers between devices, local(): apart[step] = [lax.ppermute(half, 'col', perm) for half in apart[which]]  6.2 us
    ppermute x3, waiting for transfers between devices, local(): lax.ppermute(part.astype(jnp.float16), both, square_shift(n_row, n_col, -...  5.16 us
    ppermute x3, starting transfers between devices, local(): lax.ppermute(own, both, square_shift(n_row, n_col, j, k))  4.93 us
    ppermute x3, starting transfers between devices, local(): lax.ppermute(part.astype(jnp.float16), both, square_shift(n_row, n_col, -...  3.62 us
    pallas_call x3, Pallas kernels, call(): pl.pallas_call(kernel, out_shape=out_shape, in_specs=[vmem] * len(operand...  2.74 us
    ppermute x1, starting transfers between devices, local(): line.append(lax.ppermute(line[which], 'col', perm))  1.9 us
    ppermute x3, waiting for transfers between devices, local(): lax.ppermute(own, both, square_shift(n_row, n_col, j, k))  1.73 us
    another operation x1, other arithmetic, local(): own = jnp.stack([images, texts])  0.89 us
  transfers between devices with their start and end apart: 15, of which 6 were waited for; matrix products, arithmetic and copies ran while one was open for 4% of the time, Pallas kernels for 3%

profile of v21, /device:TPU:0, one launch (start us, length us, event | category | flops | bytes accessed | tf_op | source)
XLA Modules:
  0.0 29.5 jit_solution(12582154714090927784)
XLA Ops:
  0.6 4.1 %collective-permute-start.2 = (bf16[32,1024]{1,0:T(8,128)(2,1)}, bf16[32,1024]{1,0:T(8,128)(2,1)S(1)}, u32[]{:S(2)}, u32[]{:S(2)}) collective-permute-start(bf16[32,1024]{1,0:T(8,128)(2,1)} %param.3), channel_id=1, source_target_pairs={{0,4},{1,5},{2,6},{3,7},{4,0},{5,1},{6,2},{7,3},{8,12},{9,13},{10,... | collective-permute-start | bytes 196616 | tf_op jit(solution)/shard_map/ppermute | solution.py:191
  4.7 0.1 collective-permute-start.3
  4.8 0.9 %pad_maximum_fusion.refs_0_.refs_3_.refs_1_ = bf16[2,32,1024]{2,1,0:T(8,128)(2,1)S(1)} fusion(bf16[1,32,1024]{2,1,0:T(8,128)(2,1)} %bitcast.7, bf16[1,32,1024]{2,1,0:T(8,128)(2,1)} %bitcast.6), kind=kLoop, calls=%fused_computation | loop fusion | flops 65536 | bytes 262144 | tf_op jit(solution)/shard_map/stack | solution.py:184
  5.7 1.9 %collective-permute-start.4 = (bf16[2,32,1024]{2,1,0:T(8,128)(2,1)S(1)}, bf16[2,32,1024]{2,1,0:T(8,128)(2,1)S(1)}, u32[]{:S(2)}, u32[]{:S(2)}) collective-permute-start(bf16[2,32,1024]{2,1,0:T(8,128)(2,1)S(1)} %pad_maximum_fusion.refs_0_.refs_3_.refs_1_), channel_id=1, source_target_pairs={{0,2},{1,3},{2,0},{3,1},{4,6},{5,7},{6,4},{7,5},{8,10},{9,11},{10,... | collective-permute-start | bytes 393224 | tf_op jit(solution)/shard_map/ppermute | solution.py:194
  7.6 1.5 %collective-permute-start = (bf16[2,32,1024]{2,1,0:T(8,128)(2,1)S(1)}, bf16[2,32,1024]{2,1,0:T(8,128)(2,1)S(1)}, u32[]{:S(2)}, u32[]{:S(2)}) collective-permute-start(bf16[2,32,1024]{2,1,0:T(8,128)(2,1)S(1)} %pad_maximum_fusion.refs_0_.refs_3_.refs_1_), channel_id=1, source_target_pairs={{0,1},{1,0},{2,3},{3,2},{4,5},{5,4},{6,7},{7,6},{8,9},{9,8},{10,11... | collective-permute-start | bytes 393224 | tf_op jit(solution)/shard_map/ppermute | solution.py:186
  9.1 1.5 %collective-permute-start.1 = (bf16[2,32,1024]{2,1,0:T(8,128)(2,1)S(1)}, bf16[2,32,1024]{2,1,0:T(8,128)(2,1)S(1)}, u32[]{:S(2)}, u32[]{:S(2)}) collective-permute-start(bf16[2,32,1024]{2,1,0:T(8,128)(2,1)S(1)} %pad_maximum_fusion.refs_0_.refs_3_.refs_1_), channel_id=1, source_target_pairs={{0,17},{1,16},{2,19},{3,18},{4,21},{5,20},{6,23},{7,22},{8,25},{9,... | collective-permute-start | bytes 393224 | tf_op jit(solution)/shard_map/ppermute | solution.py:186
  10.6 0.0 collective-permute-done.2
  10.6 0.5 %collective-permute-start.9 = (bf16[32,1024]{1,0:T(8,128)(2,1)S(1)}, bf16[32,1024]{1,0:T(8,128)(2,1)S(1)}, u32[]{:S(2)}, u32[]{:S(2)}) collective-permute-start(bf16[32,1024]{1,0:T(8,128)(2,1)S(1)} %collective-permute-done.2), channel_id=1, source_target_pairs={{0,2},{1,3},{2,0},{3,1},{4,6},{5,7},{6,4},{7,5},{8,10},{9,11},{10,... | collective-permute-start | bytes 196616 | tf_op jit(solution)/shard_map/ppermute | solution.py:191
  11.0 0.0 collective-permute-done.3
  11.0 1.6 %collective-permute-start.10 = (bf16[32,1024]{1,0:T(8,128)(2,1)S(1)}, bf16[32,1024]{1,0:T(8,128)(2,1)S(1)}, u32[]{:S(2)}, u32[]{:S(2)}) collective-permute-start(bf16[32,1024]{1,0:T(8,128)(2,1)S(1)} %collective-permute-done.3), channel_id=1, source_target_pairs={{0,2},{1,3},{2,0},{3,1},{4,6},{5,7},{6,4},{7,5},{8,10},{9,11},{10,... | collective-permute-start | bytes 196616 | tf_op jit(solution)/shard_map/ppermute | solution.py:191
  12.6 0.0 collective-permute-done.4.refs_5_.refs_3_
  12.7 1.9 %collective-permute-start.5 = (bf16[2,32,1024]{2,1,0:T(8,128)(2,1)S(1)}, bf16[2,32,1024]{2,1,0:T(8,128)(2,1)S(1)}, u32[]{:S(2)}, u32[]{:S(2)}) collective-permute-start(bf16[2,32,1024]{2,1,0:T(8,128)(2,1)S(1)} %pad_maximum_fusion.refs_0_.refs_3_.refs_1_), channel_id=1, source_target_pairs={{0,16},{1,17},{2,18},{3,19},{4,20},{5,21},{6,22},{7,23},{8,24},{9,... | collective-permute-start | bytes 393224 | tf_op jit(solution)/shard_map/ppermute | solution.py:186
  14.6 0.0 collective-permute-done.refs_1_
  14.6 0.0 collective-permute-start.7
  14.6 0.2 collective-permute-done.9
  14.9 0.3 collective-permute-start.6
  15.1 0.4 %collective-permute-done.10 = bf16[32,1024]{1,0:T(8,128)(2,1)S(1)} collective-permute-done((bf16[32,1024]{1,0:T(8,128)(2,1)S(1)}, bf16[32,1024]{1,0:T(8,128)(2,1)S(1)}, u32[]{:S(2)}, u32[]{:S(2)}) %collective-permute-start.10) | collective-permute-done | bytes 65568 | tf_op jit(solution)/shard_map/ppermute | solution.py:191
  15.6 0.0 copy-start
  15.6 0.1 collective-permute-start.11
  15.7 0.2 collective-permute-done.1.refs_2_
  15.9 0.3 collective-permute-start.8
  16.2 0.1 copy-done
  16.2 0.1 broadcast_in_dim.2.factors
  16.3 0.8 %shard_map.50 = (bf16[192,1024]{1,0:T(8,128)(2,1)S(1)}, f32[192,1024]{1,0:T(8,128)S(1)}, f32[192,128]{1,0:T(8,128)S(1)}, f32[32,128]{1,0:T(8,128)S(1)}, f32[8,128]{1,0:T(8,128)S(1)}) custom-call(f32[2,128]{1,0:T(2,128)S(1)} %broadcast_in_dim.2.factors, bf16[2,32,1024]{2,1,0:T(8,128)(2,1)S(1)} %pad_maximum_fusion.refs_0_.refs_3_.refs_1_, ...), custom_call_target="tpu_custom_call" | custom-call | flops 150994944 | bytes 2085888 | tf_op jit(solution)/shard_map/pallas_call | solution.py:165
  17.1 1.5 %collective-permute-done.5.refs_0_ = bf16[2,32,1024]{2,1,0:T(8,128)(2,1)S(1)} collective-permute-done((bf16[2,32,1024]{2,1,0:T(8,128)(2,1)S(1)}, bf16[2,32,1024]{2,1,0:T(8,128)(2,1)S(1)}, u32[]{:S(2)}, u32[]{:S(2)}) %collective-permute-start.5) | collective-permute-done | bytes 131104 | tf_op jit(solution)/shard_map/ppermute | solution.py:186
  18.6 0.0 collective-permute-done.7.refs_5_
  18.6 0.0 collective-permute-done.8.refs_6_
  18.6 0.0 collective-permute-done.6.refs_4_
  18.6 0.0 collective-permute-done.11.refs_8_
  18.6 1.1 %shard_map.51 = (f32[2,32,1024]{2,1,0:T(8,128)S(1)}, f32[65,8,128]{2,1,0:T(8,128)S(1)}, f32[65,8,128]{2,1,0:T(8,128)S(1)}, f32[65,8,128]{2,1,0:T(8,128)S(1)}) custom-call(f32[2,128]{1,0:T(2,128)S(1)} %broadcast_in_dim.2.factors, bf16[192,1024]{1,0:T(8,128)(2,1)S(1)} %get-tuple-element.17.own, f32[192,1024]{1,0:T(8,128)S(1)} %get-tuple-element.18.acc, ...), custom_call_target="tpu_custom_call" | custom-call | flops 385875968 | bytes 3523584 | tf_op jit(solution)/shard_map/pallas_call | solution.py:165
  19.8 2.0 %collective-permute-start.14 = (f16[65,8,128]{2,1,0:T(8,128)(2,1)S(1)}, f16[65,8,128]{2,1,0:T(8,128)(2,1)S(1)}, u32[]{:S(2)}, u32[]{:S(2)}) collective-permute-start(f16[65,8,128]{2,1,0:T(8,128)(2,1)S(1)} %convert_element_type.22), channel_id=1, source_target_pairs={{0,17},{1,16},{2,19},{3,18},{4,21},{5,20},{6,23},{7,22},{8,25},{9,... | collective-permute-start | bytes 399368 | tf_op jit(solution)/shard_map/ppermute | solution.py:231
  21.8 1.0 %collective-permute-start.13 = (f16[65,8,128]{2,1,0:T(8,128)(2,1)S(1)}, f16[65,8,128]{2,1,0:T(8,128)(2,1)S(1)}, u32[]{:S(2)}, u32[]{:S(2)}) collective-permute-start(f16[65,8,128]{2,1,0:T(8,128)(2,1)S(1)} %convert_element_type.20), channel_id=1, source_target_pairs={{0,16},{1,17},{2,18},{3,19},{4,20},{5,21},{6,22},{7,23},{8,24},{9,... | collective-permute-start | bytes 399368 | tf_op jit(solution)/shard_map/ppermute | solution.py:231
  22.9 0.6 %collective-permute-start.12 = (f16[65,8,128]{2,1,0:T(8,128)(2,1)S(1)}, f16[65,8,128]{2,1,0:T(8,128)(2,1)S(1)}, u32[]{:S(2)}, u32[]{:S(2)}) collective-permute-start(f16[65,8,128]{2,1,0:T(8,128)(2,1)S(1)} %convert_element_type.18), channel_id=1, source_target_pairs={{0,1},{1,0},{2,3},{3,2},{4,5},{5,4},{6,7},{7,6},{8,9},{9,8},{10,11... | collective-permute-start | bytes 399368 | tf_op jit(solution)/shard_map/ppermute | solution.py:231
  23.5 3.2 %collective-permute-done.14 = f16[65,8,128]{2,1,0:T(8,128)(2,1)S(1)} collective-permute-done((f16[65,8,128]{2,1,0:T(8,128)(2,1)S(1)}, f16[65,8,128]{2,1,0:T(8,128)(2,1)S(1)}, u32[]{:S(2)}, u32[]{:S(2)}) %collective-permute-start.14) | collective-permute-done | bytes 133152 | tf_op jit(solution)/shard_map/ppermute | solution.py:231
  26.7 2.0 %collective-permute-done.13 = f16[65,8,128]{2,1,0:T(8,128)(2,1)S(1)} collective-permute-done((f16[65,8,128]{2,1,0:T(8,128)(2,1)S(1)}, f16[65,8,128]{2,1,0:T(8,128)(2,1)S(1)}, u32[]{:S(2)}, u32[]{:S(2)}) %collective-permute-start.13) | collective-permute-done | bytes 133152 | tf_op jit(solution)/shard_map/ppermute | solution.py:231
  28.7 0.0 collective-permute-done.12
  28.7 0.8 %shard_map.52 = (f32[32,1024]{1,0:T(8,128)}, f32[32,1024]{1,0:T(8,128)}) custom-call(f32[2,32,1024]{2,1,0:T(8,128)S(1)} %get-tuple-element.23.own, f32[32,128]{1,0:T(8,128)S(1)} %get-tuple-element.24.down, f32[65,8,128]{2,1,0:T(8,128)S(1)} %convert_element_type.19.refs_0_, f32[65,8,128]{2,1,0:T(8,128)S(1)} %convert_element_type.21.refs_1_, ...), custom_call_target="tpu_custom_call" | custom-call | flops 524288 | bytes 1339392 | tf_op jit(solution)/shard_map/pallas_call | solution.py:165
  (9 shorter events, 0.2 us)
Async XLA Ops:
  0.6 10.0 %collective-permute-start.2 = (bf16[32,1024]{1,0:T(8,128)(2,1)}, bf16[32,1024]{1,0:T(8,128)(2,1)S(1)}, u32[]{:S(2)}, u32[]{:S(2)}) collective-permute-start(bf16[32,1024]{1,0:T(8,128)(2,1)} %param.3), channel_id=1, source_target_pairs={{0,4},{1,5},{2,6},{3,7},{4,0},{5,1},{6,2},{7,3},{8,12},{9,13},{10,... | collective-permute-start | bytes 196616 | tf_op jit(solution)/shard_map/ppermute | solution.py:191
  4.7 6.3 %collective-permute-start.3 = (bf16[32,1024]{1,0:T(8,128)(2,1)}, bf16[32,1024]{1,0:T(8,128)(2,1)S(1)}, u32[]{:S(2)}, u32[]{:S(2)}) collective-permute-start(bf16[32,1024]{1,0:T(8,128)(2,1)} %param.4), channel_id=1, source_target_pairs={{0,4},{1,5},{2,6},{3,7},{4,0},{5,1},{6,2},{7,3},{8,12},{9,13},{10,... | collective-permute-start | bytes 196616 | tf_op jit(solution)/shard_map/ppermute | solution.py:191
  5.7 7.0 %collective-permute-start.4 = (bf16[2,32,1024]{2,1,0:T(8,128)(2,1)S(1)}, bf16[2,32,1024]{2,1,0:T(8,128)(2,1)S(1)}, u32[]{:S(2)}, u32[]{:S(2)}) collective-permute-start(bf16[2,32,1024]{2,1,0:T(8,128)(2,1)S(1)} %pad_maximum_fusion.refs_0_.refs_3_.refs_1_), channel_id=1, source_target_pairs={{0,2},{1,3},{2,0},{3,1},{4,6},{5,7},{6,4},{7,5},{8,10},{9,11},{10,... | collective-permute-start | bytes 393224 | tf_op jit(solution)/shard_map/ppermute | solution.py:194
  7.6 7.0 %collective-permute-start = (bf16[2,32,1024]{2,1,0:T(8,128)(2,1)S(1)}, bf16[2,32,1024]{2,1,0:T(8,128)(2,1)S(1)}, u32[]{:S(2)}, u32[]{:S(2)}) collective-permute-start(bf16[2,32,1024]{2,1,0:T(8,128)(2,1)S(1)} %pad_maximum_fusion.refs_0_.refs_3_.refs_1_), channel_id=1, source_target_pairs={{0,1},{1,0},{2,3},{3,2},{4,5},{5,4},{6,7},{7,6},{8,9},{9,8},{10,11... | collective-permute-start | bytes 393224 | tf_op jit(solution)/shard_map/ppermute | solution.py:186
  9.1 6.8 %collective-permute-start.1 = (bf16[2,32,1024]{2,1,0:T(8,128)(2,1)S(1)}, bf16[2,32,1024]{2,1,0:T(8,128)(2,1)S(1)}, u32[]{:S(2)}, u32[]{:S(2)}) collective-permute-start(bf16[2,32,1024]{2,1,0:T(8,128)(2,1)S(1)} %pad_maximum_fusion.refs_0_.refs_3_.refs_1_), channel_id=1, source_target_pairs={{0,17},{1,16},{2,19},{3,18},{4,21},{5,20},{6,23},{7,22},{8,25},{9,... | collective-permute-start | bytes 393224 | tf_op jit(solution)/shard_map/ppermute | solution.py:186
  10.6 4.3 %collective-permute-start.9 = (bf16[32,1024]{1,0:T(8,128)(2,1)S(1)}, bf16[32,1024]{1,0:T(8,128)(2,1)S(1)}, u32[]{:S(2)}, u32[]{:S(2)}) collective-permute-start(bf16[32,1024]{1,0:T(8,128)(2,1)S(1)} %collective-permute-done.2), channel_id=1, source_target_pairs={{0,2},{1,3},{2,0},{3,1},{4,6},{5,7},{6,4},{7,5},{8,10},{9,11},{10,... | collective-permute-start | bytes 196616 | tf_op jit(solution)/shard_map/ppermute | solution.py:191
  11.0 4.5 %collective-permute-start.10 = (bf16[32,1024]{1,0:T(8,128)(2,1)S(1)}, bf16[32,1024]{1,0:T(8,128)(2,1)S(1)}, u32[]{:S(2)}, u32[]{:S(2)}) collective-permute-start(bf16[32,1024]{1,0:T(8,128)(2,1)S(1)} %collective-permute-done.3), channel_id=1, source_target_pairs={{0,2},{1,3},{2,0},{3,1},{4,6},{5,7},{6,4},{7,5},{8,10},{9,11},{10,... | collective-permute-start | bytes 196616 | tf_op jit(solution)/shard_map/ppermute | solution.py:191
  12.7 5.9 %collective-permute-start.5 = (bf16[2,32,1024]{2,1,0:T(8,128)(2,1)S(1)}, bf16[2,32,1024]{2,1,0:T(8,128)(2,1)S(1)}, u32[]{:S(2)}, u32[]{:S(2)}) collective-permute-start(bf16[2,32,1024]{2,1,0:T(8,128)(2,1)S(1)} %pad_maximum_fusion.refs_0_.refs_3_.refs_1_), channel_id=1, source_target_pairs={{0,16},{1,17},{2,18},{3,19},{4,20},{5,21},{6,22},{7,23},{8,24},{9,... | collective-permute-start | bytes 393224 | tf_op jit(solution)/shard_map/ppermute | solution.py:186
  14.6 4.0 %collective-permute-start.7 = (bf16[2,32,1024]{2,1,0:T(8,128)(2,1)S(1)}, bf16[2,32,1024]{2,1,0:T(8,128)(2,1)S(1)}, u32[]{:S(2)}, u32[]{:S(2)}) collective-permute-start(bf16[2,32,1024]{2,1,0:T(8,128)(2,1)S(1)} %pad_maximum_fusion.1.refs_4_.refs_2_), channel_id=1, source_target_pairs={{0,8},{8,0},{16,24},{24,16},{1,9},{9,1},{17,25},{25,17},{2,10},{10... | collective-permute-start | bytes 393224 | tf_op jit(solution)/shard_map/ppermute | solution.py:197
  14.9 3.7 %collective-permute-start.6 = (bf16[2,32,1024]{2,1,0:T(8,128)(2,1)S(1)}, bf16[2,32,1024]{2,1,0:T(8,128)(2,1)S(1)}, u32[]{:S(2)}, u32[]{:S(2)}) collective-permute-start(bf16[2,32,1024]{2,1,0:T(8,128)(2,1)S(1)} %pad_maximum_fusion.refs_0_.refs_3_.refs_1_), channel_id=1, source_target_pairs={{0,8},{8,0},{16,24},{24,16},{1,9},{9,1},{17,25},{25,17},{2,10},{10... | collective-permute-start | bytes 393224 | tf_op jit(solution)/shard_map/ppermute | solution.py:197
  15.6 0.7 %copy-start = (f32[2]{0:T(128)S(1)}, f32[2]{0:T(128)}, u32[]{:S(2)}) copy-start(f32[2]{0:T(128)} %param.5) | copy-start | bytes 28
  15.6 3.0 %collective-permute-start.11 = (bf16[2,32,1024]{2,1,0:T(8,128)(2,1)S(1)}, bf16[2,32,1024]{2,1,0:T(8,128)(2,1)S(1)}, u32[]{:S(2)}, u32[]{:S(2)}) collective-permute-start(bf16[2,32,1024]{2,1,0:T(8,128)(2,1)S(1)} %pad_maximum_fusion.2.refs_7_), channel_id=1, source_target_pairs={{0,8},{8,0},{16,24},{24,16},{1,9},{9,1},{17,25},{25,17},{2,10},{10... | collective-permute-start | bytes 393224 | tf_op jit(solution)/shard_map/ppermute | solution.py:197
  15.9 2.7 %collective-permute-start.8 = (bf16[2,32,1024]{2,1,0:T(8,128)(2,1)S(1)}, bf16[2,32,1024]{2,1,0:T(8,128)(2,1)S(1)}, u32[]{:S(2)}, u32[]{:S(2)}) collective-permute-start(bf16[2,32,1024]{2,1,0:T(8,128)(2,1)S(1)} %collective-permute-done.4.refs_5_.refs_3_), channel_id=1, source_target_pairs={{0,8},{8,0},{16,24},{24,16},{1,9},{9,1},{17,25},{25,17},{2,10},{10... | collective-permute-start | bytes 393224 | tf_op jit(solution)/shard_map/ppermute | solution.py:197
  19.8 6.8 %collective-permute-start.14 = (f16[65,8,128]{2,1,0:T(8,128)(2,1)S(1)}, f16[65,8,128]{2,1,0:T(8,128)(2,1)S(1)}, u32[]{:S(2)}, u32[]{:S(2)}) collective-permute-start(f16[65,8,128]{2,1,0:T(8,128)(2,1)S(1)} %convert_element_type.22), channel_id=1, source_target_pairs={{0,17},{1,16},{2,19},{3,18},{4,21},{5,20},{6,23},{7,22},{8,25},{9,... | collective-permute-start | bytes 399368 | tf_op jit(solution)/shard_map/ppermute | solution.py:231
  21.8 6.8 %collective-permute-start.13 = (f16[65,8,128]{2,1,0:T(8,128)(2,1)S(1)}, f16[65,8,128]{2,1,0:T(8,128)(2,1)S(1)}, u32[]{:S(2)}, u32[]{:S(2)}) collective-permute-start(f16[65,8,128]{2,1,0:T(8,128)(2,1)S(1)} %convert_element_type.20), channel_id=1, source_target_pairs={{0,16},{1,17},{2,18},{3,19},{4,20},{5,21},{6,22},{7,23},{8,24},{9,... | collective-permute-start | bytes 399368 | tf_op jit(solution)/shard_map/ppermute | solution.py:231
  22.9 5.8 %collective-permute-start.12 = (f16[65,8,128]{2,1,0:T(8,128)(2,1)S(1)}, f16[65,8,128]{2,1,0:T(8,128)(2,1)S(1)}, u32[]{:S(2)}, u32[]{:S(2)}) collective-permute-start(f16[65,8,128]{2,1,0:T(8,128)(2,1)S(1)} %convert_element_type.18), channel_id=1, source_target_pairs={{0,1},{1,0},{2,3},{3,2},{4,5},{5,4},{6,7},{7,6},{8,9},{9,8},{10,11... | collective-permute-start | bytes 399368 | tf_op jit(solution)/shard_map/ppermute | solution.py:231

commit v22 on v21

--- a/solution.py
+++ b/solution.py
@@ -180,7 +180,7 @@
     factors = jnp.broadcast_to((loss_weights * (1.0 / math.sqrt(width * batch)))[:, None], (2, 128))
     both = ("row", "col")
     square = [(j, k) for j in range(halves(n_row)[0]) for k in range(halves(n_col)[1])]
-    square = square[1:2] + square[3:] + square[2:3]
+    square = sorted(square[1:], key=lambda place: (all(place), not place[0]))
     own = jnp.stack([images, texts])
 
     mine = [own] + [lax.ppermute(own, both, square_shift(n_row, n_col, j, k)) for j, k in square]
@@ -200,8 +200,6 @@
     for i, block in enumerate(line[:-1]):
         if i == 0 and len(mine) > 1:
             block, mine[1] = lax.optimization_barrier((block, mine[1]))
-        if i == 1 and len(early) > 2:
-            block, early[2] = lax.optimization_barrier((block, early[2]))
         copies += pair(block)
     total = rows * len(line) * row_inner
     f32 = jnp.float32

time: 29.7 us -> 29.4 us (0.990)
    ppermute x3, starting transfers between devices: 4.93 us -> 5.58 us  [local(): lax.ppermute(own, both, square_shift(n_row, n_col, j, k))]
    ppermute x4, waiting for transfers between devices: 0.66 us -> 1.29 us  [local(): apart[step] = [lax.ppermute(half, 'col', perm) for half in apart[which]]]
    ppermute x3, waiting for transfers between devices: 1.73 us -> 1.25 us  [local(): lax.ppermute(own, both, square_shift(n_row, n_col, j, k))]
    ppermute x4, starting transfers between devices: 6.2 us -> 5.77 us  [local(): apart[step] = [lax.ppermute(half, 'col', perm) for half in apart[which]]]
    ppermute x1, starting transfers between devices: 1.9 us -> 1.58 us  [local(): line.append(lax.ppermute(line[which], 'col', perm))]
where the time goes in v22:
time: 29.4 us; the launch traced here: 29.3 us
  starting transfers between devices  17.2 us (59%)
  waiting for transfers between devices  7.48 us (25%)
  Pallas kernels  2.74 us (9%)
  other arithmetic  1.04 us (4%)
  between operations  0.72 us (2%)
    ppermute x4, starting transfers between devices, local(): apart[step] = [lax.ppermute(half, 'col', perm) for half in apart[which]]  5.77 us
    ppermute x3, starting transfers between devices, local(): lax.ppermute(own, both, square_shift(n_row, n_col, j, k))  5.58 us
    ppermute x3, waiting for transfers between devices, local(): lax.ppermute(part.astype(jnp.float16), both, square_shift(n_row, n_col, -...  4.93 us
    ppermute x3, starting transfers between devices, local(): lax.ppermute(part.astype(jnp.float16), both, square_shift(n_row, n_col, -...  3.62 us
    pallas_call x3, Pallas kernels, call(): pl.pallas_call(kernel, out_shape=out_shape, in_specs=[vmem] * len(operand...  2.74 us
    ppermute x1, starting transfers between devices, local(): line.append(lax.ppermute(line[which], 'col', perm))  1.58 us
    ppermute x4, waiting for transfers between devices, local(): apart[step] = [lax.ppermute(half, 'col', perm) for half in apart[which]]  1.29 us
    ppermute x3, waiting for transfers between devices, local(): lax.ppermute(own, both, square_shift(n_row, n_col, j, k))  1.25 us
  transfers between devices with their start and end apart: 15, of which 6 were waited for; matrix products, arithmetic and copies ran while one was open for 4% of the time, Pallas kernels for 3%

profile of v22, /device:TPU:0, one launch (start us, length us, event | category | flops | bytes accessed | tf_op | source)
XLA Modules:
  0.0 29.3 jit_solution(13038191963535233070)
XLA Ops:
  0.6 4.1 %collective-permute-start.2 = (bf16[32,1024]{1,0:T(8,128)(2,1)}, bf16[32,1024]{1,0:T(8,128)(2,1)S(1)}, u32[]{:S(2)}, u32[]{:S(2)}) collective-permute-start(bf16[32,1024]{1,0:T(8,128)(2,1)} %param.3), channel_id=1, source_target_pairs={{0,4},{1,5},{2,6},{3,7},{4,0},{5,1},{6,2},{7,3},{8,12},{9,13},{10,... | collective-permute-start | bytes 196616 | tf_op jit(solution)/shard_map/ppermute | solution.py:191
  4.7 0.1 collective-permute-start.3
  4.8 0.9 %pad_maximum_fusion.refs_0_.refs_3_.refs_1_ = bf16[2,32,1024]{2,1,0:T(8,128)(2,1)S(1)} fusion(bf16[1,32,1024]{2,1,0:T(8,128)(2,1)} %bitcast.7, bf16[1,32,1024]{2,1,0:T(8,128)(2,1)} %bitcast.6), kind=kLoop, calls=%fused_computation | loop fusion | flops 65536 | bytes 262144 | tf_op jit(solution)/shard_map/stack | solution.py:184
  5.7 1.8 %collective-permute-start = (bf16[2,32,1024]{2,1,0:T(8,128)(2,1)S(1)}, bf16[2,32,1024]{2,1,0:T(8,128)(2,1)S(1)}, u32[]{:S(2)}, u32[]{:S(2)}) collective-permute-start(bf16[2,32,1024]{2,1,0:T(8,128)(2,1)S(1)} %pad_maximum_fusion.refs_0_.refs_3_.refs_1_), channel_id=1, source_target_pairs={{0,16},{1,17},{2,18},{3,19},{4,20},{5,21},{6,22},{7,23},{8,24},{9,... | collective-permute-start | bytes 393224 | tf_op jit(solution)/shard_map/ppermute | solution.py:186
  7.5 1.6 %collective-permute-start.4 = (bf16[2,32,1024]{2,1,0:T(8,128)(2,1)S(1)}, bf16[2,32,1024]{2,1,0:T(8,128)(2,1)S(1)}, u32[]{:S(2)}, u32[]{:S(2)}) collective-permute-start(bf16[2,32,1024]{2,1,0:T(8,128)(2,1)S(1)} %pad_maximum_fusion.refs_0_.refs_3_.refs_1_), channel_id=1, source_target_pairs={{0,2},{1,3},{2,0},{3,1},{4,6},{5,7},{6,4},{7,5},{8,10},{9,11},{10,... | collective-permute-start | bytes 393224 | tf_op jit(solution)/shard_map/ppermute | solution.py:194
  9.1 1.5 %collective-permute-start.1 = (bf16[2,32,1024]{2,1,0:T(8,128)(2,1)S(1)}, bf16[2,32,1024]{2,1,0:T(8,128)(2,1)S(1)}, u32[]{:S(2)}, u32[]{:S(2)}) collective-permute-start(bf16[2,32,1024]{2,1,0:T(8,128)(2,1)S(1)} %pad_maximum_fusion.refs_0_.refs_3_.refs_1_), channel_id=1, source_target_pairs={{0,1},{1,0},{2,3},{3,2},{4,5},{5,4},{6,7},{7,6},{8,9},{9,8},{10,11... | collective-permute-start | bytes 393224 | tf_op jit(solution)/shard_map/ppermute | solution.py:186
  10.6 0.0 collective-permute-done.2
  10.6 0.5 %collective-permute-start.9 = (bf16[32,1024]{1,0:T(8,128)(2,1)S(1)}, bf16[32,1024]{1,0:T(8,128)(2,1)S(1)}, u32[]{:S(2)}, u32[]{:S(2)}) collective-permute-start(bf16[32,1024]{1,0:T(8,128)(2,1)S(1)} %collective-permute-done.2), channel_id=1, source_target_pairs={{0,2},{1,3},{2,0},{3,1},{4,6},{5,7},{6,4},{7,5},{8,10},{9,11},{10,... | collective-permute-start | bytes 196616 | tf_op jit(solution)/shard_map/ppermute | solution.py:191
  11.1 0.4 %collective-permute-done.3 = bf16[32,1024]{1,0:T(8,128)(2,1)S(1)} collective-permute-done((bf16[32,1024]{1,0:T(8,128)(2,1)}, bf16[32,1024]{1,0:T(8,128)(2,1)S(1)}, u32[]{:S(2)}, u32[]{:S(2)}) %collective-permute-start.3) | collective-permute-done | bytes 65568 | tf_op jit(solution)/shard_map/ppermute | solution.py:191
  11.5 1.1 %collective-permute-start.10 = (bf16[32,1024]{1,0:T(8,128)(2,1)S(1)}, bf16[32,1024]{1,0:T(8,128)(2,1)S(1)}, u32[]{:S(2)}, u32[]{:S(2)}) collective-permute-start(bf16[32,1024]{1,0:T(8,128)(2,1)S(1)} %collective-permute-done.3), channel_id=1, source_target_pairs={{0,2},{1,3},{2,0},{3,1},{4,6},{5,7},{6,4},{7,5},{8,10},{9,11},{10,... | collective-permute-start | bytes 196616 | tf_op jit(solution)/shard_map/ppermute | solution.py:191
  12.7 0.0 collective-permute-done.refs_1_
  12.7 2.2 %collective-permute-start.5 = (bf16[2,32,1024]{2,1,0:T(8,128)(2,1)S(1)}, bf16[2,32,1024]{2,1,0:T(8,128)(2,1)S(1)}, u32[]{:S(2)}, u32[]{:S(2)}) collective-permute-start(bf16[2,32,1024]{2,1,0:T(8,128)(2,1)S(1)} %pad_maximum_fusion.refs_0_.refs_3_.refs_1_), channel_id=1, source_target_pairs={{0,17},{1,16},{2,19},{3,18},{4,21},{5,20},{6,23},{7,22},{8,25},{9,... | collective-permute-start | bytes 393224 | tf_op jit(solution)/shard_map/ppermute | solution.py:186
  14.9 0.0 collective-permute-done.9
  15.0 0.0 collective-permute-start.7
  15.0 0.8 %collective-permute-done.10 = bf16[32,1024]{1,0:T(8,128)(2,1)S(1)} collective-permute-done((bf16[32,1024]{1,0:T(8,128)(2,1)S(1)}, bf16[32,1024]{1,0:T(8,128)(2,1)S(1)}, u32[]{:S(2)}, u32[]{:S(2)}) %collective-permute-start.10) | collective-permute-done | bytes 65568 | tf_op jit(solution)/shard_map/ppermute | solution.py:191
  15.8 0.0 collective-permute-start.6
  15.8 0.0 copy-start
  15.8 0.0 collective-permute-done.4.refs_5_.refs_3_
  15.8 0.6 %collective-permute-start.11 = (bf16[2,32,1024]{2,1,0:T(8,128)(2,1)S(1)}, bf16[2,32,1024]{2,1,0:T(8,128)(2,1)S(1)}, u32[]{:S(2)}, u32[]{:S(2)}) collective-permute-start(bf16[2,32,1024]{2,1,0:T(8,128)(2,1)S(1)} %pad_maximum_fusion.2.refs_7_), channel_id=1, source_target_pairs={{0,8},{8,0},{16,24},{24,16},{1,9},{9,1},{17,25},{25,17},{2,10},{10... | collective-permute-start | bytes 393224 | tf_op jit(solution)/shard_map/ppermute | solution.py:197
  16.4 0.0 collective-permute-done.1.refs_2_
  16.4 0.1 collective-permute-start.8
  16.5 0.0 copy-done
  16.5 0.1 broadcast_in_dim.2.factors
  16.5 0.8 %shard_map.50 = (bf16[192,1024]{1,0:T(8,128)(2,1)S(1)}, f32[192,1024]{1,0:T(8,128)S(1)}, f32[192,128]{1,0:T(8,128)S(1)}, f32[32,128]{1,0:T(8,128)S(1)}, f32[8,128]{1,0:T(8,128)S(1)}) custom-call(f32[2,128]{1,0:T(2,128)S(1)} %broadcast_in_dim.2.factors, bf16[2,32,1024]{2,1,0:T(8,128)(2,1)S(1)} %pad_maximum_fusion.refs_0_.refs_3_.refs_1_, ...), custom_call_target="tpu_custom_call" | custom-call | flops 150994944 | bytes 2085888 | tf_op jit(solution)/shard_map/pallas_call | solution.py:165
  17.4 1.2 %collective-permute-done.5.refs_0_ = bf16[2,32,1024]{2,1,0:T(8,128)(2,1)S(1)} collective-permute-done((bf16[2,32,1024]{2,1,0:T(8,128)(2,1)S(1)}, bf16[2,32,1024]{2,1,0:T(8,128)(2,1)S(1)}, u32[]{:S(2)}, u32[]{:S(2)}) %collective-permute-start.5) | collective-permute-done | bytes 131104 | tf_op jit(solution)/shard_map/ppermute | solution.py:186
  18.6 0.0 collective-permute-done.7.refs_5_
  18.6 0.0 collective-permute-done.8.refs_6_
  18.6 0.0 collective-permute-done.6.refs_4_
  18.6 0.0 collective-permute-done.11.refs_8_
  18.6 1.1 %shard_map.51 = (f32[2,32,1024]{2,1,0:T(8,128)S(1)}, f32[65,8,128]{2,1,0:T(8,128)S(1)}, f32[65,8,128]{2,1,0:T(8,128)S(1)}, f32[65,8,128]{2,1,0:T(8,128)S(1)}) custom-call(f32[2,128]{1,0:T(2,128)S(1)} %broadcast_in_dim.2.factors, bf16[192,1024]{1,0:T(8,128)(2,1)S(1)} %get-tuple-element.14.own, f32[192,1024]{1,0:T(8,128)S(1)} %get-tuple-element.15.acc, ...), custom_call_target="tpu_custom_call" | custom-call | flops 385875968 | bytes 3523584 | tf_op jit(solution)/shard_map/pallas_call | solution.py:165
  19.8 2.2 %collective-permute-start.14 = (f16[65,8,128]{2,1,0:T(8,128)(2,1)S(1)}, f16[65,8,128]{2,1,0:T(8,128)(2,1)S(1)}, u32[]{:S(2)}, u32[]{:S(2)}) collective-permute-start(f16[65,8,128]{2,1,0:T(8,128)(2,1)S(1)} %convert_element_type.22), channel_id=1, source_target_pairs={{0,17},{1,16},{2,19},{3,18},{4,21},{5,20},{6,23},{7,22},{8,25},{9,... | collective-permute-start | bytes 399368 | tf_op jit(solution)/shard_map/ppermute | solution.py:229
  22.1 0.5 %collective-permute-start.13 = (f16[65,8,128]{2,1,0:T(8,128)(2,1)S(1)}, f16[65,8,128]{2,1,0:T(8,128)(2,1)S(1)}, u32[]{:S(2)}, u32[]{:S(2)}) collective-permute-start(f16[65,8,128]{2,1,0:T(8,128)(2,1)S(1)} %convert_element_type.20), channel_id=1, source_target_pairs={{0,1},{1,0},{2,3},{3,2},{4,5},{5,4},{6,7},{7,6},{8,9},{9,8},{10,11... | collective-permute-start | bytes 399368 | tf_op jit(solution)/shard_map/ppermute | solution.py:229
  22.7 0.8 %collective-permute-start.12 = (f16[65,8,128]{2,1,0:T(8,128)(2,1)S(1)}, f16[65,8,128]{2,1,0:T(8,128)(2,1)S(1)}, u32[]{:S(2)}, u32[]{:S(2)}) collective-permute-start(f16[65,8,128]{2,1,0:T(8,128)(2,1)S(1)} %convert_element_type.18), channel_id=1, source_target_pairs={{0,16},{1,17},{2,18},{3,19},{4,20},{5,21},{6,22},{7,23},{8,24},{9,... | collective-permute-start | bytes 399368 | tf_op jit(solution)/shard_map/ppermute | solution.py:229
  23.5 3.6 %collective-permute-done.14 = f16[65,8,128]{2,1,0:T(8,128)(2,1)S(1)} collective-permute-done((f16[65,8,128]{2,1,0:T(8,128)(2,1)S(1)}, f16[65,8,128]{2,1,0:T(8,128)(2,1)S(1)}, u32[]{:S(2)}, u32[]{:S(2)}) %collective-permute-start.14) | collective-permute-done | bytes 133152 | tf_op jit(solution)/shard_map/ppermute | solution.py:229
  27.1 1.2 %collective-permute-done.13 = f16[65,8,128]{2,1,0:T(8,128)(2,1)S(1)} collective-permute-done((f16[65,8,128]{2,1,0:T(8,128)(2,1)S(1)}, f16[65,8,128]{2,1,0:T(8,128)(2,1)S(1)}, u32[]{:S(2)}, u32[]{:S(2)}) %collective-permute-start.13) | collective-permute-done | bytes 133152 | tf_op jit(solution)/shard_map/ppermute | solution.py:229
  28.4 0.1 collective-permute-done.12
  28.5 0.8 %shard_map.52 = (f32[32,1024]{1,0:T(8,128)}, f32[32,1024]{1,0:T(8,128)}) custom-call(f32[2,32,1024]{2,1,0:T(8,128)S(1)} %get-tuple-element.19.own, f32[32,128]{1,0:T(8,128)S(1)} %get-tuple-element.20.down, f32[65,8,128]{2,1,0:T(8,128)S(1)} %convert_element_type.19.refs_0_, f32[65,8,128]{2,1,0:T(8,128)S(1)} %convert_element_type.21.refs_1_, ...), custom_call_target="tpu_custom_call" | custom-call | flops 524288 | bytes 1339392 | tf_op jit(solution)/shard_map/pallas_call | solution.py:165
  (9 shorter events, 0.2 us)
Async XLA Ops:
  0.6 10.0 %collective-permute-start.2 = (bf16[32,1024]{1,0:T(8,128)(2,1)}, bf16[32,1024]{1,0:T(8,128)(2,1)S(1)}, u32[]{:S(2)}, u32[]{:S(2)}) collective-permute-start(bf16[32,1024]{1,0:T(8,128)(2,1)} %param.3), channel_id=1, source_target_pairs={{0,4},{1,5},{2,6},{3,7},{4,0},{5,1},{6,2},{7,3},{8,12},{9,13},{10,... | collective-permute-start | bytes 196616 | tf_op jit(solution)/shard_map/ppermute | solution.py:191
  4.7 6.8 %collective-permute-start.3 = (bf16[32,1024]{1,0:T(8,128)(2,1)}, bf16[32,1024]{1,0:T(8,128)(2,1)S(1)}, u32[]{:S(2)}, u32[]{:S(2)}) collective-permute-start(bf16[32,1024]{1,0:T(8,128)(2,1)} %param.4), channel_id=1, source_target_pairs={{0,4},{1,5},{2,6},{3,7},{4,0},{5,1},{6,2},{7,3},{8,12},{9,13},{10,... | collective-permute-start | bytes 196616 | tf_op jit(solution)/shard_map/ppermute | solution.py:191
  5.7 7.0 %collective-permute-start = (bf16[2,32,1024]{2,1,0:T(8,128)(2,1)S(1)}, bf16[2,32,1024]{2,1,0:T(8,128)(2,1)S(1)}, u32[]{:S(2)}, u32[]{:S(2)}) collective-permute-start(bf16[2,32,1024]{2,1,0:T(8,128)(2,1)S(1)} %pad_maximum_fusion.refs_0_.refs_3_.refs_1_), channel_id=1, source_target_pairs={{0,16},{1,17},{2,18},{3,19},{4,20},{5,21},{6,22},{7,23},{8,24},{9,... | collective-permute-start | bytes 393224 | tf_op jit(solution)/shard_map/ppermute | solution.py:186
  7.5 8.3 %collective-permute-start.4 = (bf16[2,32,1024]{2,1,0:T(8,128)(2,1)S(1)}, bf16[2,32,1024]{2,1,0:T(8,128)(2,1)S(1)}, u32[]{:S(2)}, u32[]{:S(2)}) collective-permute-start(bf16[2,32,1024]{2,1,0:T(8,128)(2,1)S(1)} %pad_maximum_fusion.refs_0_.refs_3_.refs_1_), channel_id=1, source_target_pairs={{0,2},{1,3},{2,0},{3,1},{4,6},{5,7},{6,4},{7,5},{8,10},{9,11},{10,... | collective-permute-start | bytes 393224 | tf_op jit(solution)/shard_map/ppermute | solution.py:194
  9.1 7.3 %collective-permute-start.1 = (bf16[2,32,1024]{2,1,0:T(8,128)(2,1)S(1)}, bf16[2,32,1024]{2,1,0:T(8,128)(2,1)S(1)}, u32[]{:S(2)}, u32[]{:S(2)}) collective-permute-start(bf16[2,32,1024]{2,1,0:T(8,128)(2,1)S(1)} %pad_maximum_fusion.refs_0_.refs_3_.refs_1_), channel_id=1, source_target_pairs={{0,1},{1,0},{2,3},{3,2},{4,5},{5,4},{6,7},{7,6},{8,9},{9,8},{10,11... | collective-permute-start | bytes 393224 | tf_op jit(solution)/shard_map/ppermute | solution.py:186
  10.6 4.3 %collective-permute-start.9 = (bf16[32,1024]{1,0:T(8,128)(2,1)S(1)}, bf16[32,1024]{1,0:T(8,128)(2,1)S(1)}, u32[]{:S(2)}, u32[]{:S(2)}) collective-permute-start(bf16[32,1024]{1,0:T(8,128)(2,1)S(1)} %collective-permute-done.2), channel_id=1, source_target_pairs={{0,2},{1,3},{2,0},{3,1},{4,6},{5,7},{6,4},{7,5},{8,10},{9,11},{10,... | collective-permute-start | bytes 196616 | tf_op jit(solution)/shard_map/ppermute | solution.py:191
  11.5 4.3 %collective-permute-start.10 = (bf16[32,1024]{1,0:T(8,128)(2,1)S(1)}, bf16[32,1024]{1,0:T(8,128)(2,1)S(1)}, u32[]{:S(2)}, u32[]{:S(2)}) collective-permute-start(bf16[32,1024]{1,0:T(8,128)(2,1)S(1)} %collective-permute-done.3), channel_id=1, source_target_pairs={{0,2},{1,3},{2,0},{3,1},{4,6},{5,7},{6,4},{7,5},{8,10},{9,11},{10,... | collective-permute-start | bytes 196616 | tf_op jit(solution)/shard_map/ppermute | solution.py:191
  12.7 5.9 %collective-permute-start.5 = (bf16[2,32,1024]{2,1,0:T(8,128)(2,1)S(1)}, bf16[2,32,1024]{2,1,0:T(8,128)(2,1)S(1)}, u32[]{:S(2)}, u32[]{:S(2)}) collective-permute-start(bf16[2,32,1024]{2,1,0:T(8,128)(2,1)S(1)} %pad_maximum_fusion.refs_0_.refs_3_.refs_1_), channel_id=1, source_target_pairs={{0,17},{1,16},{2,19},{3,18},{4,21},{5,20},{6,23},{7,22},{8,25},{9,... | collective-permute-start | bytes 393224 | tf_op jit(solution)/shard_map/ppermute | solution.py:186
  15.0 3.6 %collective-permute-start.7 = (bf16[2,32,1024]{2,1,0:T(8,128)(2,1)S(1)}, bf16[2,32,1024]{2,1,0:T(8,128)(2,1)S(1)}, u32[]{:S(2)}, u32[]{:S(2)}) collective-permute-start(bf16[2,32,1024]{2,1,0:T(8,128)(2,1)S(1)} %pad_maximum_fusion.1.refs_4_.refs_2_), channel_id=1, source_target_pairs={{0,8},{8,0},{16,24},{24,16},{1,9},{9,1},{17,25},{25,17},{2,10},{10... | collective-permute-start | bytes 393224 | tf_op jit(solution)/shard_map/ppermute | solution.py:197
  15.8 2.8 %collective-permute-start.6 = (bf16[2,32,1024]{2,1,0:T(8,128)(2,1)S(1)}, bf16[2,32,1024]{2,1,0:T(8,128)(2,1)S(1)}, u32[]{:S(2)}, u32[]{:S(2)}) collective-permute-start(bf16[2,32,1024]{2,1,0:T(8,128)(2,1)S(1)} %pad_maximum_fusion.refs_0_.refs_3_.refs_1_), channel_id=1, source_target_pairs={{0,8},{8,0},{16,24},{24,16},{1,9},{9,1},{17,25},{25,17},{2,10},{10... | collective-permute-start | bytes 393224 | tf_op jit(solution)/shard_map/ppermute | solution.py:197
  15.8 0.7 %copy-start = (f32[2]{0:T(128)S(1)}, f32[2]{0:T(128)}, u32[]{:S(2)}) copy-start(f32[2]{0:T(128)} %param.5) | copy-start | bytes 28
  15.8 2.8 %collective-permute-start.11 = (bf16[2,32,1024]{2,1,0:T(8,128)(2,1)S(1)}, bf16[2,32,1024]{2,1,0:T(8,128)(2,1)S(1)}, u32[]{:S(2)}, u32[]{:S(2)}) collective-permute-start(bf16[2,32,1024]{2,1,0:T(8,128)(2,1)S(1)} %pad_maximum_fusion.2.refs_7_), channel_id=1, source_target_pairs={{0,8},{8,0},{16,24},{24,16},{1,9},{9,1},{17,25},{25,17},{2,10},{10... | collective-permute-start | bytes 393224 | tf_op jit(solution)/shard_map/ppermute | solution.py:197
  16.4 2.2 %collective-permute-start.8 = (bf16[2,32,1024]{2,1,0:T(8,128)(2,1)S(1)}, bf16[2,32,1024]{2,1,0:T(8,128)(2,1)S(1)}, u32[]{:S(2)}, u32[]{:S(2)}) collective-permute-start(bf16[2,32,1024]{2,1,0:T(8,128)(2,1)S(1)} %collective-permute-done.4.refs_5_.refs_3_), channel_id=1, source_target_pairs={{0,8},{8,0},{16,24},{24,16},{1,9},{9,1},{17,25},{25,17},{2,10},{10... | collective-permute-start | bytes 393224 | tf_op jit(solution)/shard_map/ppermute | solution.py:197
  19.8 7.2 %collective-permute-start.14 = (f16[65,8,128]{2,1,0:T(8,128)(2,1)S(1)}, f16[65,8,128]{2,1,0:T(8,128)(2,1)S(1)}, u32[]{:S(2)}, u32[]{:S(2)}) collective-permute-start(f16[65,8,128]{2,1,0:T(8,128)(2,1)S(1)} %convert_element_type.22), channel_id=1, source_target_pairs={{0,17},{1,16},{2,19},{3,18},{4,21},{5,20},{6,23},{7,22},{8,25},{9,... | collective-permute-start | bytes 399368 | tf_op jit(solution)/shard_map/ppermute | solution.py:229
  22.1 6.2 %collective-permute-start.13 = (f16[65,8,128]{2,1,0:T(8,128)(2,1)S(1)}, f16[65,8,128]{2,1,0:T(8,128)(2,1)S(1)}, u32[]{:S(2)}, u32[]{:S(2)}) collective-permute-start(f16[65,8,128]{2,1,0:T(8,128)(2,1)S(1)} %convert_element_type.20), channel_id=1, source_target_pairs={{0,1},{1,0},{2,3},{3,2},{4,5},{5,4},{6,7},{7,6},{8,9},{9,8},{10,11... | collective-permute-start | bytes 399368 | tf_op jit(solution)/shard_map/ppermute | solution.py:229
  22.7 5.8 %collective-permute-start.12 = (f16[65,8,128]{2,1,0:T(8,128)(2,1)S(1)}, f16[65,8,128]{2,1,0:T(8,128)(2,1)S(1)}, u32[]{:S(2)}, u32[]{:S(2)}) collective-permute-start(f16[65,8,128]{2,1,0:T(8,128)(2,1)S(1)} %convert_element_type.18), channel_id=1, source_target_pairs={{0,16},{1,17},{2,18},{3,19},{4,20},{5,21},{6,22},{7,23},{8,24},{9,... | collective-permute-start | bytes 399368 | tf_op jit(solution)/shard_map/ppermute | solution.py:229

commit v23 on v22

--- a/solution.py
+++ b/solution.py
@@ -200,6 +200,8 @@
     for i, block in enumerate(line[:-1]):
         if i == 0 and len(mine) > 1:
             block, mine[1] = lax.optimization_barrier((block, mine[1]))
+        if i == 1 and len(early) > 2:
+            block, mine[1], early[2] = lax.optimization_barrier((block, mine[1], early[2]))
         copies += pair(block)
     total = rows * len(line) * row_inner
     f32 = jnp.float32

time: 29.4 us -> 29.3 us (level)
  waiting for transfers between devices: 7.48 us -> 6.87 us
  starting transfers between devices: 17.2 us -> 17.6 us
    ppermute x4, waiting for transfers between devices: 1.29 us -> 0.81 us  [local(): apart[step] = [lax.ppermute(half, 'col', perm) for half in apart[which]]]
    ppermute x4, starting transfers between devices: 0.66 us -> 1.04 us  [pair(): lax.ppermute(block, 'row', inner_shift(n_row, k))]
where the time goes in v23:
time: 29.3 us; the launch traced here: 29.1 us
  starting transfers between devices  17.6 us (60%)
  waiting for transfers between devices  6.87 us (23%)
  Pallas kernels  2.74 us (9%)
  other arithmetic  1.04 us (4%)
  between operations  0.73 us (2%)
    ppermute x4, starting transfers between devices, local(): apart[step] = [lax.ppermute(half, 'col', perm) for half in apart[which]]  5.77 us
    ppermute x3, starting transfers between devices, local(): lax.ppermute(own, both, square_shift(n_row, n_col, j, k))  5.58 us
    ppermute x3, waiting for transfers between devices, local(): lax.ppermute(part.astype(jnp.float16), both, square_shift(n_row, n_col, -...  4.75 us
    ppermute x3, starting transfers between devices, local(): lax.ppermute(part.astype(jnp.float16), both, square_shift(n_row, n_col, -...  3.62 us
    pallas_call x3, Pallas kernels, call(): pl.pallas_call(kernel, out_shape=out_shape, in_specs=[vmem] * len(operand...  2.74 us
    ppermute x1, starting transfers between devices, local(): line.append(lax.ppermute(line[which], 'col', perm))  1.58 us
    ppermute x3, waiting for transfers between devices, local(): lax.ppermute(own, both, square_shift(n_row, n_col, j, k))  1.29 us
    ppermute x4, starting transfers between devices, pair(): lax.ppermute(block, 'row', inner_shift(n_row, k))  1.04 us
  transfers between devices with their start and end apart: 15, of which 6 were waited for; matrix products, arithmetic and copies ran while one was open for 4% of the time, Pallas kernels for 3%

profile of v23, /device:TPU:0, one launch (start us, length us, event | category | flops | bytes accessed | tf_op | source)
XLA Modules:
  0.0 29.1 jit_solution(10713595728035740838)
XLA Ops:
  0.6 4.1 %collective-permute-start = (bf16[32,1024]{1,0:T(8,128)(2,1)}, bf16[32,1024]{1,0:T(8,128)(2,1)S(1)}, u32[]{:S(2)}, u32[]{:S(2)}) collective-permute-start(bf16[32,1024]{1,0:T(8,128)(2,1)} %param.3), channel_id=1, source_target_pairs={{0,4},{1,5},{2,6},{3,7},{4,0},{5,1},{6,2},{7,3},{8,12},{9,13},{10,... | collective-permute-start | bytes 196616 | tf_op jit(solution)/shard_map/ppermute | solution.py:191
  4.7 0.1 collective-permute-start.1
  4.8 0.9 %pad_maximum_fusion.refs_0_.refs_3_.refs_1_ = bf16[2,32,1024]{2,1,0:T(8,128)(2,1)S(1)} fusion(bf16[1,32,1024]{2,1,0:T(8,128)(2,1)} %bitcast.7, bf16[1,32,1024]{2,1,0:T(8,128)(2,1)} %bitcast.6), kind=kLoop, calls=%fused_computation | loop fusion | flops 65536 | bytes 262144 | tf_op jit(solution)/shard_map/stack | solution.py:184
  5.7 1.8 %collective-permute-start.2 = (bf16[2,32,1024]{2,1,0:T(8,128)(2,1)S(1)}, bf16[2,32,1024]{2,1,0:T(8,128)(2,1)S(1)}, u32[]{:S(2)}, u32[]{:S(2)}) collective-permute-start(bf16[2,32,1024]{2,1,0:T(8,128)(2,1)S(1)} %pad_maximum_fusion.refs_0_.refs_3_.refs_1_), channel_id=1, source_target_pairs={{0,16},{1,17},{2,18},{3,19},{4,20},{5,21},{6,22},{7,23},{8,24},{9,... | collective-permute-start | bytes 393224 | tf_op jit(solution)/shard_map/ppermute | solution.py:186
  7.5 1.6 %collective-permute-start.3 = (bf16[2,32,1024]{2,1,0:T(8,128)(2,1)S(1)}, bf16[2,32,1024]{2,1,0:T(8,128)(2,1)S(1)}, u32[]{:S(2)}, u32[]{:S(2)}) collective-permute-start(bf16[2,32,1024]{2,1,0:T(8,128)(2,1)S(1)} %pad_maximum_fusion.refs_0_.refs_3_.refs_1_), channel_id=1, source_target_pairs={{0,2},{1,3},{2,0},{3,1},{4,6},{5,7},{6,4},{7,5},{8,10},{9,11},{10,... | collective-permute-start | bytes 393224 | tf_op jit(solution)/shard_map/ppermute | solution.py:194
  9.1 1.5 %collective-permute-start.4 = (bf16[2,32,1024]{2,1,0:T(8,128)(2,1)S(1)}, bf16[2,32,1024]{2,1,0:T(8,128)(2,1)S(1)}, u32[]{:S(2)}, u32[]{:S(2)}) collective-permute-start(bf16[2,32,1024]{2,1,0:T(8,128)(2,1)S(1)} %pad_maximum_fusion.refs_0_.refs_3_.refs_1_), channel_id=1, source_target_pairs={{0,1},{1,0},{2,3},{3,2},{4,5},{5,4},{6,7},{7,6},{8,9},{9,8},{10,11... | collective-permute-start | bytes 393224 | tf_op jit(solution)/shard_map/ppermute | solution.py:186
  10.6 0.0 collective-permute-done
  10.6 0.5 %collective-permute-start.9 = (bf16[32,1024]{1,0:T(8,128)(2,1)S(1)}, bf16[32,1024]{1,0:T(8,128)(2,1)S(1)}, u32[]{:S(2)}, u32[]{:S(2)}) collective-permute-start(bf16[32,1024]{1,0:T(8,128)(2,1)S(1)} %collective-permute-done), channel_id=1, source_target_pairs={{0,2},{1,3},{2,0},{3,1},{4,6},{5,7},{6,4},{7,5},{8,10},{9,11},{10,... | collective-permute-start | bytes 196616 | tf_op jit(solution)/shard_map/ppermute | solution.py:191
  11.1 0.4 %collective-permute-done.1 = bf16[32,1024]{1,0:T(8,128)(2,1)S(1)} collective-permute-done((bf16[32,1024]{1,0:T(8,128)(2,1)}, bf16[32,1024]{1,0:T(8,128)(2,1)S(1)}, u32[]{:S(2)}, u32[]{:S(2)}) %collective-permute-start.1) | collective-permute-done | bytes 65568 | tf_op jit(solution)/shard_map/ppermute | solution.py:191
  11.5 1.1 %collective-permute-start.10 = (bf16[32,1024]{1,0:T(8,128)(2,1)S(1)}, bf16[32,1024]{1,0:T(8,128)(2,1)S(1)}, u32[]{:S(2)}, u32[]{:S(2)}) collective-permute-start(bf16[32,1024]{1,0:T(8,128)(2,1)S(1)} %collective-permute-done.1), channel_id=1, source_target_pairs={{0,2},{1,3},{2,0},{3,1},{4,6},{5,7},{6,4},{7,5},{8,10},{9,11},{10,... | collective-permute-start | bytes 196616 | tf_op jit(solution)/shard_map/ppermute | solution.py:191
  12.7 0.0 collective-permute-done.2.refs_1_
  12.7 2.2 %collective-permute-start.5 = (bf16[2,32,1024]{2,1,0:T(8,128)(2,1)S(1)}, bf16[2,32,1024]{2,1,0:T(8,128)(2,1)S(1)}, u32[]{:S(2)}, u32[]{:S(2)}) collective-permute-start(bf16[2,32,1024]{2,1,0:T(8,128)(2,1)S(1)} %pad_maximum_fusion.refs_0_.refs_3_.refs_1_), channel_id=1, source_target_pairs={{0,17},{1,16},{2,19},{3,18},{4,21},{5,20},{6,23},{7,22},{8,25},{9,... | collective-permute-start | bytes 393224 | tf_op jit(solution)/shard_map/ppermute | solution.py:186
  14.9 0.0 collective-permute-done.3.refs_5_.refs_3_
  14.9 0.0 collective-permute-start.7
  14.9 0.0 collective-permute-done.9
  15.0 0.5 %collective-permute-start.6 = (bf16[2,32,1024]{2,1,0:T(8,128)(2,1)S(1)}, bf16[2,32,1024]{2,1,0:T(8,128)(2,1)S(1)}, u32[]{:S(2)}, u32[]{:S(2)}) collective-permute-start(bf16[2,32,1024]{2,1,0:T(8,128)(2,1)S(1)} %pad_maximum_fusion.refs_0_.refs_3_.refs_1_), channel_id=1, source_target_pairs={{0,8},{8,0},{16,24},{24,16},{1,9},{9,1},{17,25},{25,17},{2,10},{10... | collective-permute-start | bytes 393224 | tf_op jit(solution)/shard_map/ppermute | solution.py:197
  15.4 0.3 %collective-permute-done.10 = bf16[32,1024]{1,0:T(8,128)(2,1)S(1)} collective-permute-done((bf16[32,1024]{1,0:T(8,128)(2,1)S(1)}, bf16[32,1024]{1,0:T(8,128)(2,1)S(1)}, u32[]{:S(2)}, u32[]{:S(2)}) %collective-permute-start.10) | collective-permute-done | bytes 65568 | tf_op jit(solution)/shard_map/ppermute | solution.py:191
  15.8 0.0 copy-start
  15.8 0.1 collective-permute-start.11
  15.9 0.0 collective-permute-done.4.refs_2_
  15.9 0.5 %collective-permute-start.8 = (bf16[2,32,1024]{2,1,0:T(8,128)(2,1)S(1)}, bf16[2,32,1024]{2,1,0:T(8,128)(2,1)S(1)}, u32[]{:S(2)}, u32[]{:S(2)}) collective-permute-start(bf16[2,32,1024]{2,1,0:T(8,128)(2,1)S(1)} %collective-permute-done.3.refs_5_.refs_3_), channel_id=1, source_target_pairs={{0,8},{8,0},{16,24},{24,16},{1,9},{9,1},{17,25},{25,17},{2,10},{10... | collective-permute-start | bytes 393224 | tf_op jit(solution)/shard_map/ppermute | solution.py:197
  16.4 0.1 copy-done
  16.4 0.1 broadcast_in_dim.2.factors
  16.5 0.8 %shard_map.50 = (bf16[192,1024]{1,0:T(8,128)(2,1)S(1)}, f32[192,1024]{1,0:T(8,128)S(1)}, f32[192,128]{1,0:T(8,128)S(1)}, f32[32,128]{1,0:T(8,128)S(1)}, f32[8,128]{1,0:T(8,128)S(1)}) custom-call(f32[2,128]{1,0:T(2,128)S(1)} %broadcast_in_dim.2.factors, bf16[2,32,1024]{2,1,0:T(8,128)(2,1)S(1)} %pad_maximum_fusion.refs_0_.refs_3_.refs_1_, ...), custom_call_target="tpu_custom_call" | custom-call | flops 150994944 | bytes 2085888 | tf_op jit(solution)/shard_map/pallas_call | solution.py:165
  17.3 1.3 %collective-permute-done.5.refs_0_ = bf16[2,32,1024]{2,1,0:T(8,128)(2,1)S(1)} collective-permute-done((bf16[2,32,1024]{2,1,0:T(8,128)(2,1)S(1)}, bf16[2,32,1024]{2,1,0:T(8,128)(2,1)S(1)}, u32[]{:S(2)}, u32[]{:S(2)}) %collective-permute-start.5) | collective-permute-done | bytes 131104 | tf_op jit(solution)/shard_map/ppermute | solution.py:186
  18.6 0.0 collective-permute-done.8.refs_6_
  18.6 0.0 collective-permute-done.7.refs_5_
  18.6 0.0 collective-permute-done.6.refs_4_
  18.6 0.0 collective-permute-done.11.refs_8_
  18.6 1.1 %shard_map.51 = (f32[2,32,1024]{2,1,0:T(8,128)S(1)}, f32[65,8,128]{2,1,0:T(8,128)S(1)}, f32[65,8,128]{2,1,0:T(8,128)S(1)}, f32[65,8,128]{2,1,0:T(8,128)S(1)}) custom-call(f32[2,128]{1,0:T(2,128)S(1)} %broadcast_in_dim.2.factors, bf16[192,1024]{1,0:T(8,128)(2,1)S(1)} %get-tuple-element.19.own, f32[192,1024]{1,0:T(8,128)S(1)} %get-tuple-element.20.acc, ...), custom_call_target="tpu_custom_call" | custom-call | flops 385875968 | bytes 3523584 | tf_op jit(solution)/shard_map/pallas_call | solution.py:165
  19.8 2.2 %collective-permute-start.14 = (f16[65,8,128]{2,1,0:T(8,128)(2,1)S(1)}, f16[65,8,128]{2,1,0:T(8,128)(2,1)S(1)}, u32[]{:S(2)}, u32[]{:S(2)}) collective-permute-start(f16[65,8,128]{2,1,0:T(8,128)(2,1)S(1)} %convert_element_type.22), channel_id=1, source_target_pairs={{0,17},{1,16},{2,19},{3,18},{4,21},{5,20},{6,23},{7,22},{8,25},{9,... | collective-permute-start | bytes 399368 | tf_op jit(solution)/shard_map/ppermute | solution.py:231
  22.1 0.5 %collective-permute-start.13 = (f16[65,8,128]{2,1,0:T(8,128)(2,1)S(1)}, f16[65,8,128]{2,1,0:T(8,128)(2,1)S(1)}, u32[]{:S(2)}, u32[]{:S(2)}) collective-permute-start(f16[65,8,128]{2,1,0:T(8,128)(2,1)S(1)} %convert_element_type.20), channel_id=1, source_target_pairs={{0,1},{1,0},{2,3},{3,2},{4,5},{5,4},{6,7},{7,6},{8,9},{9,8},{10,11... | collective-permute-start | bytes 399368 | tf_op jit(solution)/shard_map/ppermute | solution.py:231
  22.7 0.8 %collective-permute-start.12 = (f16[65,8,128]{2,1,0:T(8,128)(2,1)S(1)}, f16[65,8,128]{2,1,0:T(8,128)(2,1)S(1)}, u32[]{:S(2)}, u32[]{:S(2)}) collective-permute-start(f16[65,8,128]{2,1,0:T(8,128)(2,1)S(1)} %convert_element_type.18), channel_id=1, source_target_pairs={{0,16},{1,17},{2,18},{3,19},{4,20},{5,21},{6,22},{7,23},{8,24},{9,... | collective-permute-start | bytes 399368 | tf_op jit(solution)/shard_map/ppermute | solution.py:231
  23.5 3.4 %collective-permute-done.14 = f16[65,8,128]{2,1,0:T(8,128)(2,1)S(1)} collective-permute-done((f16[65,8,128]{2,1,0:T(8,128)(2,1)S(1)}, f16[65,8,128]{2,1,0:T(8,128)(2,1)S(1)}, u32[]{:S(2)}, u32[]{:S(2)}) %collective-permute-start.14) | collective-permute-done | bytes 133152 | tf_op jit(solution)/shard_map/ppermute | solution.py:231
  26.9 1.2 %collective-permute-done.13 = f16[65,8,128]{2,1,0:T(8,128)(2,1)S(1)} collective-permute-done((f16[65,8,128]{2,1,0:T(8,128)(2,1)S(1)}, f16[65,8,128]{2,1,0:T(8,128)(2,1)S(1)}, u32[]{:S(2)}, u32[]{:S(2)}) %collective-permute-start.13) | collective-permute-done | bytes 133152 | tf_op jit(solution)/shard_map/ppermute | solution.py:231
  28.2 0.1 collective-permute-done.12
  28.3 0.8 %shard_map.52 = (f32[32,1024]{1,0:T(8,128)}, f32[32,1024]{1,0:T(8,128)}) custom-call(f32[2,32,1024]{2,1,0:T(8,128)S(1)} %get-tuple-element.25.own, f32[32,128]{1,0:T(8,128)S(1)} %get-tuple-element.26.down, f32[65,8,128]{2,1,0:T(8,128)S(1)} %convert_element_type.19.refs_0_, f32[65,8,128]{2,1,0:T(8,128)S(1)} %convert_element_type.21.refs_1_, ...), custom_call_target="tpu_custom_call" | custom-call | flops 524288 | bytes 1339392 | tf_op jit(solution)/shard_map/pallas_call | solution.py:165
  (9 shorter events, 0.2 us)
Async XLA Ops:
  0.6 10.0 %collective-permute-start = (bf16[32,1024]{1,0:T(8,128)(2,1)}, bf16[32,1024]{1,0:T(8,128)(2,1)S(1)}, u32[]{:S(2)}, u32[]{:S(2)}) collective-permute-start(bf16[32,1024]{1,0:T(8,128)(2,1)} %param.3), channel_id=1, source_target_pairs={{0,4},{1,5},{2,6},{3,7},{4,0},{5,1},{6,2},{7,3},{8,12},{9,13},{10,... | collective-permute-start | bytes 196616 | tf_op jit(solution)/shard_map/ppermute | solution.py:191
  4.7 6.8 %collective-permute-start.1 = (bf16[32,1024]{1,0:T(8,128)(2,1)}, bf16[32,1024]{1,0:T(8,128)(2,1)S(1)}, u32[]{:S(2)}, u32[]{:S(2)}) collective-permute-start(bf16[32,1024]{1,0:T(8,128)(2,1)} %param.4), channel_id=1, source_target_pairs={{0,4},{1,5},{2,6},{3,7},{4,0},{5,1},{6,2},{7,3},{8,12},{9,13},{10,... | collective-permute-start | bytes 196616 | tf_op jit(solution)/shard_map/ppermute | solution.py:191
  5.7 7.0 %collective-permute-start.2 = (bf16[2,32,1024]{2,1,0:T(8,128)(2,1)S(1)}, bf16[2,32,1024]{2,1,0:T(8,128)(2,1)S(1)}, u32[]{:S(2)}, u32[]{:S(2)}) collective-permute-start(bf16[2,32,1024]{2,1,0:T(8,128)(2,1)S(1)} %pad_maximum_fusion.refs_0_.refs_3_.refs_1_), channel_id=1, source_target_pairs={{0,16},{1,17},{2,18},{3,19},{4,20},{5,21},{6,22},{7,23},{8,24},{9,... | collective-permute-start | bytes 393224 | tf_op jit(solution)/shard_map/ppermute | solution.py:186
  7.5 7.4 %collective-permute-start.3 = (bf16[2,32,1024]{2,1,0:T(8,128)(2,1)S(1)}, bf16[2,32,1024]{2,1,0:T(8,128)(2,1)S(1)}, u32[]{:S(2)}, u32[]{:S(2)}) collective-permute-start(bf16[2,32,1024]{2,1,0:T(8,128)(2,1)S(1)} %pad_maximum_fusion.refs_0_.refs_3_.refs_1_), channel_id=1, source_target_pairs={{0,2},{1,3},{2,0},{3,1},{4,6},{5,7},{6,4},{7,5},{8,10},{9,11},{10,... | collective-permute-start | bytes 393224 | tf_op jit(solution)/shard_map/ppermute | solution.py:194
  9.1 6.8 %collective-permute-start.4 = (bf16[2,32,1024]{2,1,0:T(8,128)(2,1)S(1)}, bf16[2,32,1024]{2,1,0:T(8,128)(2,1)S(1)}, u32[]{:S(2)}, u32[]{:S(2)}) collective-permute-start(bf16[2,32,1024]{2,1,0:T(8,128)(2,1)S(1)} %pad_maximum_fusion.refs_0_.refs_3_.refs_1_), channel_id=1, source_target_pairs={{0,1},{1,0},{2,3},{3,2},{4,5},{5,4},{6,7},{7,6},{8,9},{9,8},{10,11... | collective-permute-start | bytes 393224 | tf_op jit(solution)/shard_map/ppermute | solution.py:186
  10.6 4.3 %collective-permute-start.9 = (bf16[32,1024]{1,0:T(8,128)(2,1)S(1)}, bf16[32,1024]{1,0:T(8,128)(2,1)S(1)}, u32[]{:S(2)}, u32[]{:S(2)}) collective-permute-start(bf16[32,1024]{1,0:T(8,128)(2,1)S(1)} %collective-permute-done), channel_id=1, source_target_pairs={{0,2},{1,3},{2,0},{3,1},{4,6},{5,7},{6,4},{7,5},{8,10},{9,11},{10,... | collective-permute-start | bytes 196616 | tf_op jit(solution)/shard_map/ppermute | solution.py:191
  11.5 4.3 %collective-permute-start.10 = (bf16[32,1024]{1,0:T(8,128)(2,1)S(1)}, bf16[32,1024]{1,0:T(8,128)(2,1)S(1)}, u32[]{:S(2)}, u32[]{:S(2)}) collective-permute-start(bf16[32,1024]{1,0:T(8,128)(2,1)S(1)} %collective-permute-done.1), channel_id=1, source_target_pairs={{0,2},{1,3},{2,0},{3,1},{4,6},{5,7},{6,4},{7,5},{8,10},{9,11},{10,... | collective-permute-start | bytes 196616 | tf_op jit(solution)/shard_map/ppermute | solution.py:191
  12.7 5.9 %collective-permute-start.5 = (bf16[2,32,1024]{2,1,0:T(8,128)(2,1)S(1)}, bf16[2,32,1024]{2,1,0:T(8,128)(2,1)S(1)}, u32[]{:S(2)}, u32[]{:S(2)}) collective-permute-start(bf16[2,32,1024]{2,1,0:T(8,128)(2,1)S(1)} %pad_maximum_fusion.refs_0_.refs_3_.refs_1_), channel_id=1, source_target_pairs={{0,17},{1,16},{2,19},{3,18},{4,21},{5,20},{6,23},{7,22},{8,25},{9,... | collective-permute-start | bytes 393224 | tf_op jit(solution)/shard_map/ppermute | solution.py:186
  14.9 3.7 %collective-permute-start.7 = (bf16[2,32,1024]{2,1,0:T(8,128)(2,1)S(1)}, bf16[2,32,1024]{2,1,0:T(8,128)(2,1)S(1)}, u32[]{:S(2)}, u32[]{:S(2)}) collective-permute-start(bf16[2,32,1024]{2,1,0:T(8,128)(2,1)S(1)} %pad_maximum_fusion.1.refs_4_.refs_2_), channel_id=1, source_target_pairs={{0,8},{8,0},{16,24},{24,16},{1,9},{9,1},{17,25},{25,17},{2,10},{10... | collective-permute-start | bytes 393224 | tf_op jit(solution)/shard_map/ppermute | solution.py:197
  15.0 3.7 %collective-permute-start.6 = (bf16[2,32,1024]{2,1,0:T(8,128)(2,1)S(1)}, bf16[2,32,1024]{2,1,0:T(8,128)(2,1)S(1)}, u32[]{:S(2)}, u32[]{:S(2)}) collective-permute-start(bf16[2,32,1024]{2,1,0:T(8,128)(2,1)S(1)} %pad_maximum_fusion.refs_0_.refs_3_.refs_1_), channel_id=1, source_target_pairs={{0,8},{8,0},{16,24},{24,16},{1,9},{9,1},{17,25},{25,17},{2,10},{10... | collective-permute-start | bytes 393224 | tf_op jit(solution)/shard_map/ppermute | solution.py:197
  15.8 0.7 %copy-start = (f32[2]{0:T(128)S(1)}, f32[2]{0:T(128)}, u32[]{:S(2)}) copy-start(f32[2]{0:T(128)} %param.5) | copy-start | bytes 28
  15.8 2.8 %collective-permute-start.11 = (bf16[2,32,1024]{2,1,0:T(8,128)(2,1)S(1)}, bf16[2,32,1024]{2,1,0:T(8,128)(2,1)S(1)}, u32[]{:S(2)}, u32[]{:S(2)}) collective-permute-start(bf16[2,32,1024]{2,1,0:T(8,128)(2,1)S(1)} %pad_maximum_fusion.2.refs_7_), channel_id=1, source_target_pairs={{0,8},{8,0},{16,24},{24,16},{1,9},{9,1},{17,25},{25,17},{2,10},{10... | collective-permute-start | bytes 393224 | tf_op jit(solution)/shard_map/ppermute | solution.py:197
  15.9 2.7 %collective-permute-start.8 = (bf16[2,32,1024]{2,1,0:T(8,128)(2,1)S(1)}, bf16[2,32,1024]{2,1,0:T(8,128)(2,1)S(1)}, u32[]{:S(2)}, u32[]{:S(2)}) collective-permute-start(bf16[2,32,1024]{2,1,0:T(8,128)(2,1)S(1)} %collective-permute-done.3.refs_5_.refs_3_), channel_id=1, source_target_pairs={{0,8},{8,0},{16,24},{24,16},{1,9},{9,1},{17,25},{25,17},{2,10},{10... | collective-permute-start | bytes 393224 | tf_op jit(solution)/shard_map/ppermute | solution.py:197
  19.8 7.1 %collective-permute-start.14 = (f16[65,8,128]{2,1,0:T(8,128)(2,1)S(1)}, f16[65,8,128]{2,1,0:T(8,128)(2,1)S(1)}, u32[]{:S(2)}, u32[]{:S(2)}) collective-permute-start(f16[65,8,128]{2,1,0:T(8,128)(2,1)S(1)} %convert_element_type.22), channel_id=1, source_target_pairs={{0,17},{1,16},{2,19},{3,18},{4,21},{5,20},{6,23},{7,22},{8,25},{9,... | collective-permute-start | bytes 399368 | tf_op jit(solution)/shard_map/ppermute | solution.py:231
  22.1 6.1 %collective-permute-start.13 = (f16[65,8,128]{2,1,0:T(8,128)(2,1)S(1)}, f16[65,8,128]{2,1,0:T(8,128)(2,1)S(1)}, u32[]{:S(2)}, u32[]{:S(2)}) collective-permute-start(f16[65,8,128]{2,1,0:T(8,128)(2,1)S(1)} %convert_element_type.20), channel_id=1, source_target_pairs={{0,1},{1,0},{2,3},{3,2},{4,5},{5,4},{6,7},{7,6},{8,9},{9,8},{10,11... | collective-permute-start | bytes 399368 | tf_op jit(solution)/shard_map/ppermute | solution.py:231
  22.7 5.6 %collective-permute-start.12 = (f16[65,8,128]{2,1,0:T(8,128)(2,1)S(1)}, f16[65,8,128]{2,1,0:T(8,128)(2,1)S(1)}, u32[]{:S(2)}, u32[]{:S(2)}) collective-permute-start(f16[65,8,128]{2,1,0:T(8,128)(2,1)S(1)} %convert_element_type.18), channel_id=1, source_target_pairs={{0,16},{1,17},{2,18},{3,19},{4,20},{5,21},{6,22},{7,23},{8,24},{9,... | collective-permute-start | bytes 399368 | tf_op jit(solution)/shard_map/ppermute | solution.py:231

commit v24 on v23

--- a/solution.py
+++ b/solution.py
@@ -218,7 +218,7 @@
         + [jax.ShapeDtypeStruct(s, f32) for s in [(2 * many, width), (2 * many, 128), (rows, 128), (8, 128)]],
         flops(len(first), len(early)),
     )
-    late = copies + [line[-1]] + pair(line[-1])
+    late = copies + [line[-1]] + [jnp.stack(halves) for halves in zip(*map(pair, apart.get(len(line) - 1, line[-1])))]
     parts = call(
         functools.partial(late_kernel, total, len(first), len(early)),
         [factors, mine_joined, acc, up, most_key, last] + early + late,

time: 29.3 us -> 33 us (1.13)
  waiting for transfers between devices: 6.87 us -> 10.7 us
    ppermute x4, waiting for transfers between devices: 0.81 us -> 2.65 us  [local(): apart[step] = [lax.ppermute(half, 'col', perm) for half in apart[which]]]
    ppermute x3, waiting for transfers between devices: 1.29 us -> 2.71 us  [local(): lax.ppermute(own, both, square_shift(n_row, n_col, j, k))]
    ppermute x3, waiting for transfers between devices: 4.75 us -> 5.3 us  [local(): lax.ppermute(part.astype(jnp.float16), both, square_shift(n_row, n_col, -...]
    ppermute x4 -> x5, starting transfers between devices: 1.04 us -> 1.02 us  [pair(): lax.ppermute(block, 'row', inner_shift(n_row, k))]
  transfers between devices with their start and end apart: 15 -> 16, of which waited for: 6 -> 6; matrix products, arithmetic and copies ran while one was open for 4% -> 3% of each run, Pallas kernels for 3% -> 2%
where the time goes in v24:
time: 33 us; the launch traced here: 32.9 us
  starting transfers between devices  17.5 us (53%)
  waiting for transfers between devices  10.7 us (32%)
  Pallas kernels  2.75 us (8%)
  other arithmetic  1.07 us (3%)
  between operations  0.71 us (2%)
    ppermute x4, starting transfers between devices, local(): apart[step] = [lax.ppermute(half, 'col', perm) for half in apart[which]]  5.85 us
    ppermute x3, starting transfers between devices, local(): lax.ppermute(own, both, square_shift(n_row, n_col, j, k))  5.47 us
    ppermute x3, waiting for transfers between devices, local(): lax.ppermute(part.astype(jnp.float16), both, square_shift(n_row, n_col, -...  5.3 us
    ppermute x3, starting transfers between devices, local(): lax.ppermute(part.astype(jnp.float16), both, square_shift(n_row, n_col, -...  3.62 us
    pallas_call x3, Pallas kernels, call(): pl.pallas_call(kernel, out_shape=out_shape, in_specs=[vmem] * len(operand...  2.75 us
    ppermute x3, waiting for transfers between devices, local(): lax.ppermute(own, both, square_shift(n_row, n_col, j, k))  2.71 us
    ppermute x4, waiting for transfers between devices, local(): apart[step] = [lax.ppermute(half, 'col', perm) for half in apart[which]]  2.65 us
    ppermute x1, starting transfers between devices, local(): line.append(lax.ppermute(line[which], 'col', perm))  1.58 us
  transfers between devices with their start and end apart: 16, of which 6 were waited for; matrix products, arithmetic and copies ran while one was open for 3% of the time, Pallas kernels for 2%

profile of v24, /device:TPU:0, one launch (start us, length us, event | category | flops | bytes accessed | tf_op | source)
XLA Modules:
  0.0 32.9 jit_solution(7334147716081289840)
XLA Ops:
  0.6 4.1 %collective-permute-start = (bf16[32,1024]{1,0:T(8,128)(2,1)}, bf16[32,1024]{1,0:T(8,128)(2,1)S(1)}, u32[]{:S(2)}, u32[]{:S(2)}) collective-permute-start(bf16[32,1024]{1,0:T(8,128)(2,1)} %param.3), channel_id=1, source_target_pairs={{0,4},{1,5},{2,6},{3,7},{4,0},{5,1},{6,2},{7,3},{8,12},{9,13},{10,... | collective-permute-start | bytes 196616 | tf_op jit(solution)/shard_map/ppermute | solution.py:191
  4.7 0.1 collective-permute-start.1
  4.8 0.0 copy-start
  4.8 0.9 %pad_maximum_fusion.refs_0_.refs_3_.refs_1_ = bf16[2,32,1024]{2,1,0:T(8,128)(2,1)S(1)} fusion(bf16[1,32,1024]{2,1,0:T(8,128)(2,1)} %bitcast.9, bf16[1,32,1024]{2,1,0:T(8,128)(2,1)} %bitcast.8), kind=kLoop, calls=%fused_computation | loop fusion | flops 65536 | bytes 262144 | tf_op jit(solution)/shard_map/stack | solution.py:184
  5.7 1.8 %collective-permute-start.4 = (bf16[2,32,1024]{2,1,0:T(8,128)(2,1)S(1)}, bf16[2,32,1024]{2,1,0:T(8,128)(2,1)S(1)}, u32[]{:S(2)}, u32[]{:S(2)}) collective-permute-start(bf16[2,32,1024]{2,1,0:T(8,128)(2,1)S(1)} %pad_maximum_fusion.refs_0_.refs_3_.refs_1_), channel_id=1, source_target_pairs={{0,1},{1,0},{2,3},{3,2},{4,5},{5,4},{6,7},{7,6},{8,9},{9,8},{10,11... | collective-permute-start | bytes 393224 | tf_op jit(solution)/shard_map/ppermute | solution.py:186
  7.5 1.6 %collective-permute-start.3 = (bf16[2,32,1024]{2,1,0:T(8,128)(2,1)S(1)}, bf16[2,32,1024]{2,1,0:T(8,128)(2,1)S(1)}, u32[]{:S(2)}, u32[]{:S(2)}) collective-permute-start(bf16[2,32,1024]{2,1,0:T(8,128)(2,1)S(1)} %pad_maximum_fusion.refs_0_.refs_3_.refs_1_), channel_id=1, source_target_pairs={{0,2},{1,3},{2,0},{3,1},{4,6},{5,7},{6,4},{7,5},{8,10},{9,11},{10,... | collective-permute-start | bytes 393224 | tf_op jit(solution)/shard_map/ppermute | solution.py:194
  9.1 1.5 %collective-permute-start.2 = (bf16[2,32,1024]{2,1,0:T(8,128)(2,1)S(1)}, bf16[2,32,1024]{2,1,0:T(8,128)(2,1)S(1)}, u32[]{:S(2)}, u32[]{:S(2)}) collective-permute-start(bf16[2,32,1024]{2,1,0:T(8,128)(2,1)S(1)} %pad_maximum_fusion.refs_0_.refs_3_.refs_1_), channel_id=1, source_target_pairs={{0,16},{1,17},{2,18},{3,19},{4,20},{5,21},{6,22},{7,23},{8,24},{9,... | collective-permute-start | bytes 393224 | tf_op jit(solution)/shard_map/ppermute | solution.py:186
  10.6 0.0 collective-permute-done
  10.6 0.5 %collective-permute-start.9 = (bf16[32,1024]{1,0:T(8,128)(2,1)S(1)}, bf16[32,1024]{1,0:T(8,128)(2,1)S(1)}, u32[]{:S(2)}, u32[]{:S(2)}) collective-permute-start(bf16[32,1024]{1,0:T(8,128)(2,1)S(1)} %collective-permute-done), channel_id=1, source_target_pairs={{0,2},{1,3},{2,0},{3,1},{4,6},{5,7},{6,4},{7,5},{8,10},{9,11},{10,... | collective-permute-start | bytes 196616 | tf_op jit(solution)/shard_map/ppermute | solution.py:191
  11.1 0.0 copy-done
  11.1 0.4 %collective-permute-done.1 = bf16[32,1024]{1,0:T(8,128)(2,1)S(1)} collective-permute-done((bf16[32,1024]{1,0:T(8,128)(2,1)}, bf16[32,1024]{1,0:T(8,128)(2,1)S(1)}, u32[]{:S(2)}, u32[]{:S(2)}) %collective-permute-start.1) | collective-permute-done | bytes 65568 | tf_op jit(solution)/shard_map/ppermute | solution.py:191
  11.5 1.2 %collective-permute-start.10 = (bf16[32,1024]{1,0:T(8,128)(2,1)S(1)}, bf16[32,1024]{1,0:T(8,128)(2,1)S(1)}, u32[]{:S(2)}, u32[]{:S(2)}) collective-permute-start(bf16[32,1024]{1,0:T(8,128)(2,1)S(1)} %collective-permute-done.1), channel_id=1, source_target_pairs={{0,2},{1,3},{2,0},{3,1},{4,6},{5,7},{6,4},{7,5},{8,10},{9,11},{10,... | collective-permute-start | bytes 196616 | tf_op jit(solution)/shard_map/ppermute | solution.py:191
  12.7 2.2 %collective-permute-done.9 = bf16[32,1024]{1,0:T(8,128)(2,1)S(1)} collective-permute-done((bf16[32,1024]{1,0:T(8,128)(2,1)S(1)}, bf16[32,1024]{1,0:T(8,128)(2,1)S(1)}, u32[]{:S(2)}, u32[]{:S(2)}) %collective-permute-start.9) | collective-permute-done | bytes 65568 | tf_op jit(solution)/shard_map/ppermute | solution.py:191
  14.9 0.0 collective-permute-start.11
  15.0 0.0 collective-permute-done.2.refs_1_
  15.0 2.1 %collective-permute-start.5 = (bf16[2,32,1024]{2,1,0:T(8,128)(2,1)S(1)}, bf16[2,32,1024]{2,1,0:T(8,128)(2,1)S(1)}, u32[]{:S(2)}, u32[]{:S(2)}) collective-permute-start(bf16[2,32,1024]{2,1,0:T(8,128)(2,1)S(1)} %pad_maximum_fusion.refs_0_.refs_3_.refs_1_), channel_id=1, source_target_pairs={{0,17},{1,16},{2,19},{3,18},{4,21},{5,20},{6,23},{7,22},{8,25},{9,... | collective-permute-start | bytes 393224 | tf_op jit(solution)/shard_map/ppermute | solution.py:186
  17.1 0.0 collective-permute-done.3.refs_5_.refs_3_
  17.1 0.2 collective-permute-start.7
  17.3 0.0 collective-permute-done.10
  17.4 0.3 collective-permute-start.6
  17.6 0.0 collective-permute-done.4.refs_2_
  17.6 0.2 collective-permute-start.8
  17.9 0.0 collective-permute-done.11
  17.9 0.3 collective-permute-start.12
  18.2 0.1 broadcast_in_dim.2.factors
  18.2 0.8 %shard_map.50 = (bf16[192,1024]{1,0:T(8,128)(2,1)S(1)}, f32[192,1024]{1,0:T(8,128)S(1)}, f32[192,128]{1,0:T(8,128)S(1)}, f32[32,128]{1,0:T(8,128)S(1)}, f32[8,128]{1,0:T(8,128)S(1)}) custom-call(f32[2,128]{1,0:T(2,128)S(1)} %broadcast_in_dim.2.factors, bf16[2,32,1024]{2,1,0:T(8,128)(2,1)S(1)} %pad_maximum_fusion.refs_0_.refs_3_.refs_1_, ...), custom_call_target="tpu_custom_call" | custom-call | flops 150994944 | bytes 2085888 | tf_op jit(solution)/shard_map/pallas_call | solution.py:165
  19.1 0.1 collective-permute-done.12
  19.1 2.7 %collective-permute-done.5.refs_0_ = bf16[2,32,1024]{2,1,0:T(8,128)(2,1)S(1)} collective-permute-done((bf16[2,32,1024]{2,1,0:T(8,128)(2,1)S(1)}, bf16[2,32,1024]{2,1,0:T(8,128)(2,1)S(1)}, u32[]{:S(2)}, u32[]{:S(2)}) %collective-permute-start.5) | collective-permute-done | bytes 131104 | tf_op jit(solution)/shard_map/ppermute | solution.py:186
  21.9 0.0 collective-permute-done.8.refs_6_
  21.9 0.0 collective-permute-done.7.refs_5_
  21.9 0.0 collective-permute-done.6.refs_4_
  21.9 1.2 %shard_map.51 = (f32[2,32,1024]{2,1,0:T(8,128)S(1)}, f32[65,8,128]{2,1,0:T(8,128)S(1)}, f32[65,8,128]{2,1,0:T(8,128)S(1)}, f32[65,8,128]{2,1,0:T(8,128)S(1)}) custom-call(f32[2,128]{1,0:T(2,128)S(1)} %broadcast_in_dim.2.factors, bf16[192,1024]{1,0:T(8,128)(2,1)S(1)} %get-tuple-element.19.own, f32[192,1024]{1,0:T(8,128)S(1)} %get-tuple-element.20.acc, ...), custom_call_target="tpu_custom_call" | custom-call | flops 385875968 | bytes 3523584 | tf_op jit(solution)/shard_map/pallas_call | solution.py:165
  23.1 2.1 %collective-permute-start.15 = (f16[65,8,128]{2,1,0:T(8,128)(2,1)S(1)}, f16[65,8,128]{2,1,0:T(8,128)(2,1)S(1)}, u32[]{:S(2)}, u32[]{:S(2)}) collective-permute-start(f16[65,8,128]{2,1,0:T(8,128)(2,1)S(1)} %convert_element_type.22), channel_id=1, source_target_pairs={{0,17},{1,16},{2,19},{3,18},{4,21},{5,20},{6,23},{7,22},{8,25},{9,... | collective-permute-start | bytes 399368 | tf_op jit(solution)/shard_map/ppermute | solution.py:231
  25.2 0.8 %collective-permute-start.14 = (f16[65,8,128]{2,1,0:T(8,128)(2,1)S(1)}, f16[65,8,128]{2,1,0:T(8,128)(2,1)S(1)}, u32[]{:S(2)}, u32[]{:S(2)}) collective-permute-start(f16[65,8,128]{2,1,0:T(8,128)(2,1)S(1)} %convert_element_type.20), channel_id=1, source_target_pairs={{0,1},{1,0},{2,3},{3,2},{4,5},{5,4},{6,7},{7,6},{8,9},{9,8},{10,11... | collective-permute-start | bytes 399368 | tf_op jit(solution)/shard_map/ppermute | solution.py:231
  26.0 0.7 %collective-permute-start.13 = (f16[65,8,128]{2,1,0:T(8,128)(2,1)S(1)}, f16[65,8,128]{2,1,0:T(8,128)(2,1)S(1)}, u32[]{:S(2)}, u32[]{:S(2)}) collective-permute-start(f16[65,8,128]{2,1,0:T(8,128)(2,1)S(1)} %convert_element_type.18), channel_id=1, source_target_pairs={{0,16},{1,17},{2,18},{3,19},{4,20},{5,21},{6,22},{7,23},{8,24},{9,... | collective-permute-start | bytes 399368 | tf_op jit(solution)/shard_map/ppermute | solution.py:231
  26.7 3.8 %collective-permute-done.15 = f16[65,8,128]{2,1,0:T(8,128)(2,1)S(1)} collective-permute-done((f16[65,8,128]{2,1,0:T(8,128)(2,1)S(1)}, f16[65,8,128]{2,1,0:T(8,128)(2,1)S(1)}, u32[]{:S(2)}, u32[]{:S(2)}) %collective-permute-start.15) | collective-permute-done | bytes 133152 | tf_op jit(solution)/shard_map/ppermute | solution.py:231
  30.5 1.5 %collective-permute-done.14 = f16[65,8,128]{2,1,0:T(8,128)(2,1)S(1)} collective-permute-done((f16[65,8,128]{2,1,0:T(8,128)(2,1)S(1)}, f16[65,8,128]{2,1,0:T(8,128)(2,1)S(1)}, u32[]{:S(2)}, u32[]{:S(2)}) %collective-permute-start.14) | collective-permute-done | bytes 133152 | tf_op jit(solution)/shard_map/ppermute | solution.py:231
  32.0 0.0 collective-permute-done.13
  32.1 0.8 %shard_map.52 = (f32[32,1024]{1,0:T(8,128)}, f32[32,1024]{1,0:T(8,128)}) custom-call(f32[2,32,1024]{2,1,0:T(8,128)S(1)} %get-tuple-element.25.own, f32[32,128]{1,0:T(8,128)S(1)} %get-tuple-element.26.down, f32[65,8,128]{2,1,0:T(8,128)S(1)} %convert_element_type.19.refs_0_, f32[65,8,128]{2,1,0:T(8,128)S(1)} %convert_element_type.21.refs_1_, ...), custom_call_target="tpu_custom_call" | custom-call | flops 524288 | bytes 1339392 | tf_op jit(solution)/shard_map/pallas_call | solution.py:165
  (10 shorter events, 0.2 us)
Async XLA Ops:
  0.6 10.0 %collective-permute-start = (bf16[32,1024]{1,0:T(8,128)(2,1)}, bf16[32,1024]{1,0:T(8,128)(2,1)S(1)}, u32[]{:S(2)}, u32[]{:S(2)}) collective-permute-start(bf16[32,1024]{1,0:T(8,128)(2,1)} %param.3), channel_id=1, source_target_pairs={{0,4},{1,5},{2,6},{3,7},{4,0},{5,1},{6,2},{7,3},{8,12},{9,13},{10,... | collective-permute-start | bytes 196616 | tf_op jit(solution)/shard_map/ppermute | solution.py:191
  4.7 6.8 %collective-permute-start.1 = (bf16[32,1024]{1,0:T(8,128)(2,1)}, bf16[32,1024]{1,0:T(8,128)(2,1)S(1)}, u32[]{:S(2)}, u32[]{:S(2)}) collective-permute-start(bf16[32,1024]{1,0:T(8,128)(2,1)} %param.4), channel_id=1, source_target_pairs={{0,4},{1,5},{2,6},{3,7},{4,0},{5,1},{6,2},{7,3},{8,12},{9,13},{10,... | collective-permute-start | bytes 196616 | tf_op jit(solution)/shard_map/ppermute | solution.py:191
  4.8 6.3 %copy-start = (f32[2]{0:T(128)S(1)}, f32[2]{0:T(128)}, u32[]{:S(2)}) copy-start(f32[2]{0:T(128)} %param.5) | copy-start | bytes 28
  5.7 11.9 %collective-permute-start.4 = (bf16[2,32,1024]{2,1,0:T(8,128)(2,1)S(1)}, bf16[2,32,1024]{2,1,0:T(8,128)(2,1)S(1)}, u32[]{:S(2)}, u32[]{:S(2)}) collective-permute-start(bf16[2,32,1024]{2,1,0:T(8,128)(2,1)S(1)} %pad_maximum_fusion.refs_0_.refs_3_.refs_1_), channel_id=1, source_target_pairs={{0,1},{1,0},{2,3},{3,2},{4,5},{5,4},{6,7},{7,6},{8,9},{9,8},{10,11... | collective-permute-start | bytes 393224 | tf_op jit(solution)/shard_map/ppermute | solution.py:186
  7.5 9.6 %collective-permute-start.3 = (bf16[2,32,1024]{2,1,0:T(8,128)(2,1)S(1)}, bf16[2,32,1024]{2,1,0:T(8,128)(2,1)S(1)}, u32[]{:S(2)}, u32[]{:S(2)}) collective-permute-start(bf16[2,32,1024]{2,1,0:T(8,128)(2,1)S(1)} %pad_maximum_fusion.refs_0_.refs_3_.refs_1_), channel_id=1, source_target_pairs={{0,2},{1,3},{2,0},{3,1},{4,6},{5,7},{6,4},{7,5},{8,10},{9,11},{10,... | collective-permute-start | bytes 393224 | tf_op jit(solution)/shard_map/ppermute | solution.py:194
  9.1 5.9 %collective-permute-start.2 = (bf16[2,32,1024]{2,1,0:T(8,128)(2,1)S(1)}, bf16[2,32,1024]{2,1,0:T(8,128)(2,1)S(1)}, u32[]{:S(2)}, u32[]{:S(2)}) collective-permute-start(bf16[2,32,1024]{2,1,0:T(8,128)(2,1)S(1)} %pad_maximum_fusion.refs_0_.refs_3_.refs_1_), channel_id=1, source_target_pairs={{0,16},{1,17},{2,18},{3,19},{4,20},{5,21},{6,22},{7,23},{8,24},{9,... | collective-permute-start | bytes 393224 | tf_op jit(solution)/shard_map/ppermute | solution.py:186
  10.6 4.3 %collective-permute-start.9 = (bf16[32,1024]{1,0:T(8,128)(2,1)S(1)}, bf16[32,1024]{1,0:T(8,128)(2,1)S(1)}, u32[]{:S(2)}, u32[]{:S(2)}) collective-permute-start(bf16[32,1024]{1,0:T(8,128)(2,1)S(1)} %collective-permute-done), channel_id=1, source_target_pairs={{0,2},{1,3},{2,0},{3,1},{4,6},{5,7},{6,4},{7,5},{8,10},{9,11},{10,... | collective-permute-start | bytes 196616 | tf_op jit(solution)/shard_map/ppermute | solution.py:191
  11.5 5.8 %collective-permute-start.10 = (bf16[32,1024]{1,0:T(8,128)(2,1)S(1)}, bf16[32,1024]{1,0:T(8,128)(2,1)S(1)}, u32[]{:S(2)}, u32[]{:S(2)}) collective-permute-start(bf16[32,1024]{1,0:T(8,128)(2,1)S(1)} %collective-permute-done.1), channel_id=1, source_target_pairs={{0,2},{1,3},{2,0},{3,1},{4,6},{5,7},{6,4},{7,5},{8,10},{9,11},{10,... | collective-permute-start | bytes 196616 | tf_op jit(solution)/shard_map/ppermute | solution.py:191
  14.9 2.9 %collective-permute-start.11 = (bf16[32,1024]{1,0:T(8,128)(2,1)S(1)}, bf16[32,1024]{1,0:T(8,128)(2,1)S(1)}, u32[]{:S(2)}, u32[]{:S(2)}) collective-permute-start(bf16[32,1024]{1,0:T(8,128)(2,1)S(1)} %collective-permute-done.9), channel_id=1, source_target_pairs={{0,8},{8,0},{16,24},{24,16},{1,9},{9,1},{17,25},{25,17},{2,10},{10... | collective-permute-start | bytes 196616 | tf_op jit(solution)/shard_map/ppermute | solution.py:197
  15.0 6.9 %collective-permute-start.5 = (bf16[2,32,1024]{2,1,0:T(8,128)(2,1)S(1)}, bf16[2,32,1024]{2,1,0:T(8,128)(2,1)S(1)}, u32[]{:S(2)}, u32[]{:S(2)}) collective-permute-start(bf16[2,32,1024]{2,1,0:T(8,128)(2,1)S(1)} %pad_maximum_fusion.refs_0_.refs_3_.refs_1_), channel_id=1, source_target_pairs={{0,17},{1,16},{2,19},{3,18},{4,21},{5,20},{6,23},{7,22},{8,25},{9,... | collective-permute-start | bytes 393224 | tf_op jit(solution)/shard_map/ppermute | solution.py:186
  17.1 4.7 %collective-permute-start.7 = (bf16[2,32,1024]{2,1,0:T(8,128)(2,1)S(1)}, bf16[2,32,1024]{2,1,0:T(8,128)(2,1)S(1)}, u32[]{:S(2)}, u32[]{:S(2)}) collective-permute-start(bf16[2,32,1024]{2,1,0:T(8,128)(2,1)S(1)} %pad_maximum_fusion.1.refs_4_.refs_2_), channel_id=1, source_target_pairs={{0,8},{8,0},{16,24},{24,16},{1,9},{9,1},{17,25},{25,17},{2,10},{10... | collective-permute-start | bytes 393224 | tf_op jit(solution)/shard_map/ppermute | solution.py:197
  17.4 4.5 %collective-permute-start.6 = (bf16[2,32,1024]{2,1,0:T(8,128)(2,1)S(1)}, bf16[2,32,1024]{2,1,0:T(8,128)(2,1)S(1)}, u32[]{:S(2)}, u32[]{:S(2)}) collective-permute-start(bf16[2,32,1024]{2,1,0:T(8,128)(2,1)S(1)} %pad_maximum_fusion.refs_0_.refs_3_.refs_1_), channel_id=1, source_target_pairs={{0,8},{8,0},{16,24},{24,16},{1,9},{9,1},{17,25},{25,17},{2,10},{10... | collective-permute-start | bytes 393224 | tf_op jit(solution)/shard_map/ppermute | solution.py:197
  17.6 4.2 %collective-permute-start.8 = (bf16[2,32,1024]{2,1,0:T(8,128)(2,1)S(1)}, bf16[2,32,1024]{2,1,0:T(8,128)(2,1)S(1)}, u32[]{:S(2)}, u32[]{:S(2)}) collective-permute-start(bf16[2,32,1024]{2,1,0:T(8,128)(2,1)S(1)} %collective-permute-done.3.refs_5_.refs_3_), channel_id=1, source_target_pairs={{0,8},{8,0},{16,24},{24,16},{1,9},{9,1},{17,25},{25,17},{2,10},{10... | collective-permute-start | bytes 393224 | tf_op jit(solution)/shard_map/ppermute | solution.py:197
  17.9 1.3 %collective-permute-start.12 = (bf16[32,1024]{1,0:T(8,128)(2,1)S(1)}, bf16[32,1024]{1,0:T(8,128)(2,1)S(1)}, u32[]{:S(2)}, u32[]{:S(2)}) collective-permute-start(bf16[32,1024]{1,0:T(8,128)(2,1)S(1)} %collective-permute-done.10), channel_id=1, source_target_pairs={{0,8},{8,0},{16,24},{24,16},{1,9},{9,1},{17,25},{25,17},{2,10},{10... | collective-permute-start | bytes 196616 | tf_op jit(solution)/shard_map/ppermute | solution.py:197
  23.1 7.4 %collective-permute-start.15 = (f16[65,8,128]{2,1,0:T(8,128)(2,1)S(1)}, f16[65,8,128]{2,1,0:T(8,128)(2,1)S(1)}, u32[]{:S(2)}, u32[]{:S(2)}) collective-permute-start(f16[65,8,128]{2,1,0:T(8,128)(2,1)S(1)} %convert_element_type.22), channel_id=1, source_target_pairs={{0,17},{1,16},{2,19},{3,18},{4,21},{5,20},{6,23},{7,22},{8,25},{9,... | collective-permute-start | bytes 399368 | tf_op jit(solution)/shard_map/ppermute | solution.py:231
  25.2 6.8 %collective-permute-start.14 = (f16[65,8,128]{2,1,0:T(8,128)(2,1)S(1)}, f16[65,8,128]{2,1,0:T(8,128)(2,1)S(1)}, u32[]{:S(2)}, u32[]{:S(2)}) collective-permute-start(f16[65,8,128]{2,1,0:T(8,128)(2,1)S(1)} %convert_element_type.20), channel_id=1, source_target_pairs={{0,1},{1,0},{2,3},{3,2},{4,5},{5,4},{6,7},{7,6},{8,9},{9,8},{10,11... | collective-permute-start | bytes 399368 | tf_op jit(solution)/shard_map/ppermute | solution.py:231
  26.0 6.0 %collective-permute-start.13 = (f16[65,8,128]{2,1,0:T(8,128)(2,1)S(1)}, f16[65,8,128]{2,1,0:T(8,128)(2,1)S(1)}, u32[]{:S(2)}, u32[]{:S(2)}) collective-permute-start(f16[65,8,128]{2,1,0:T(8,128)(2,1)S(1)} %convert_element_type.18), channel_id=1, source_target_pairs={{0,16},{1,17},{2,18},{3,19},{4,20},{5,21},{6,22},{7,23},{8,24},{9,... | collective-permute-start | bytes 399368 | tf_op jit(solution)/shard_map/ppermute | solution.py:231
